TPU v7x, 256 devices: a whole 4x4x8 slice. The times are simulated.
256 devices in a mesh: node: 16 (over y, x), feat: 16 (over z, core).
Axes of the slice: x: 4, y: 4, z: 8, core: 2. Of those that a mesh axis runs over, the one named last changes fastest.
Arguments:
- features: bfloat16 [131072, 4096], P('node', 'feat'), may hold values from -6 to 6
- adjacency: bfloat16 [4096, 128, 128], P('node'), may hold values from 0 to 0.039794922
- target_block: int32 [4096], P('node'), may hold values from 0 to 127
- source_block: int32 [4096], P('node'), may hold values from 0 to 63
- block_count: int32 [16], P('node'), may hold values from 64 to 256, as said below
- layer_one: bfloat16 [4096, 256], P('feat'), may hold values from -0.09375 to 0.09375
- bias_one: float32 [256], replicated, may hold values from -3 to 3
- self_weight: bfloat16 [256, 172], replicated, may hold values from -0.375 to 0.375
- neigh_weight: bfloat16 [256, 172], replicated, may hold values from -0.375 to 0.375
- bias_two: float32 [172], replicated, may hold values from -4 to 4
- seed_ids: int32 [8192], P(('node', 'feat')), may hold values from 0 to 63
- neighbor_ids: int32 [8192, 8], P(('node', 'feat')), may hold values from 0 to 63
Outputs:
- logits: float32 [8192, 172], P(('node', 'feat'))
Inputs may be any that keep to these rules, and one draw needn't show every extreme that they name: Only the first block_count[n] slots of node shard n are live; some node shard has all 256 live.
All inputs are finite; a program needn't handle non-finite values.
Results may differ from a plain program's by a relative error of at most 0.0028.
Values sent between devices are 32-bit elements; how exact they have to be, the bound alone decides.
No kernel may reach another device: no remote copies, remote signals or barrier semaphores. Data moves between devices by JAX's collectives and lax.ppermute only.
A program may use at most 192 MiB of HBM per device.

v0:
```python
import jax
import jax.numpy as jnp
from jax import lax
from jax.sharding import PartitionSpec as P

T_DEV = 64


def projector(source_rows, layer_one):
    return jnp.dot(source_rows, layer_one, preferred_element_type=jnp.float32)


def on_device(
    features,
    adjacency,
    target_block,
    source_block,
    block_count,
    layer_one,
    bias_one,
    self_weight,
    neigh_weight,
    bias_two,
    seed_ids,
    neighbor_ids,
):
    block_size = adjacency.shape[1]
    blocks_held = adjacency.shape[0]
    columns = features.shape[1]
    node_count = lax.axis_size("node")
    feat_count = lax.axis_size("feat")
    per_device = T_DEV
    all_targets = per_device * node_count * feat_count
    target_blocks = all_targets // block_size
    sources = features.reshape(-1, block_size, columns)[source_block]
    products = jnp.einsum("bij,bjf->bif", adjacency, sources, preferred_element_type=jnp.float32)
    live_mask = (jnp.arange(blocks_held, dtype=jnp.int32) < block_count[0]).astype(jnp.float32)
    summed = (
        jnp.zeros((target_blocks, block_size, columns), jnp.float32)
        .at[target_block]
        .add(products * live_mask[:, None, None])
    )
    aggregated = summed.reshape(all_targets, columns).astype(jnp.bfloat16)
    hidden_sum = lax.psum_scatter(
        projector(aggregated, layer_one), ("node", "feat"), scatter_dimension=0, tiled=True
    )
    hidden_one = jnp.maximum(hidden_sum + bias_one[None, :], 0.0).astype(jnp.bfloat16)
    positions = jnp.arange(per_device, dtype=jnp.int32)
    pick_self = (seed_ids[:, None] == positions[None, :]).astype(jnp.bfloat16)
    self_rows = jnp.dot(pick_self, hidden_one, preferred_element_type=jnp.float32).astype(
        jnp.bfloat16
    )
    weights_mean = (
        jnp.sum((neighbor_ids[:, :, None] == positions[None, None, :]).astype(jnp.float32), axis=1)
        / neighbor_ids.shape[1]
    )
    neigh_mean = jnp.dot(
        weights_mean, hidden_one.astype(jnp.float32), precision=lax.Precision.HIGHEST
    ).astype(jnp.bfloat16)
    logits = jnp.dot(self_rows, self_weight, preferred_element_type=jnp.float32) + jnp.dot(
        neigh_mean, neigh_weight, preferred_element_type=jnp.float32
    )
    return logits + bias_two[None, :]


def solution(mesh):
    placed = (
        P("node", "feat"),
        P("node", None, None),
        P("node"),
        P("node"),
        P("node"),
        P("feat", None),
        P(),
        P(),
        P(),
        P(),
        P(("node", "feat")),
        P(("node", "feat"), None),
    )
    return jax.shard_map(
        on_device, mesh=mesh, in_specs=placed, out_specs=P(("node", "feat"), None), check_vma=False
    )
```

profile of v0, /device:TPU:1, one launch (start us, length us, event | category | flops | bytes accessed | tf_op | source)
XLA Modules:
  0.0 1476.3 jit_solution(5244050670209363681)
XLA Ops:
  6.5 0.0 copy-start
  6.5 0.0 reduce-scatter.2.cloned.1.call-start
  6.5 0.7 compare_select_fusion
  7.9 12.0 gather_fusion
  19.9 21.6 %multiply_bitcast_fusion = f32[256,128,256]{1,2,0:T(8,128)} fusion(f32[256]{0:T(256)S(1)} %compare_convert_fusion, bf16[256,128,256]{2,1,0:T(8,128)(2,1)} %gather_fusion, bf16[256,128,128]{2,1,0:T(8,128)(2,1)} %param.13), kind=kOutput, calls=%fused_computation.2 | convolution fusion | flops 2155872256 | bytes 58721280 | tf_op jit(solution)/shard_map/bij,bjf->bif/dot_general | solution.py:36
  41.5 0.0 copy-start.6
  41.5 33.5 %copy.19 = f32[256,128,256]{2,1,0:T(8,128)} copy(f32[256,128,256]{1,2,0:T(8,128)} %multiply_bitcast_fusion) | data formatting | bytes 67108864 | tf_op jit(solution)/shard_map/mul | solution.py:41
  75.0 0.0 copy-done.6
  75.0 7.8 broadcast_in_dim.6
  82.8 76.3 %scatter_fusion = f32[128,128,256]{2,1,0:T(8,128)} fusion(f32[128,128,256]{2,1,0:T(8,128)} %broadcast_in_dim.6, s32[256]{0:T(256)S(1)} %compare_select_fusion.1, f32[256,128,256]{2,1,0:T(8,128)} %copy.19), kind=kCustom, calls=%fused_computation.1 | custom fusion | flops 8388608 | bytes 100664320 | tf_op jit(solution)/shard_map/scatter-add | solution.py:41
  159.1 6.5 convert_element_type.28
  165.6 0.0 copy-done
  165.6 8.1 fusion.10
  173.7 0.0 copy-start.4
  173.7 0.0 copy-start.3
  173.7 0.0 copy-start.1
  173.7 0.0 copy-start.7
  173.7 0.0 copy-start.2
  173.7 0.0 copy-start.5
  173.7 0.0 reduce-scatter.2.cloned.1.call-update
  173.7 0.6 copy-done.4
  174.4 0.1 copy.20
  174.4 0.1 convert_reduce_fusion
  174.6 1291.9 %reduce-scatter.2.cloned.1.call-done = f32[64,256]{1,0:T(8,128)} async-done(((f32[16384,256]{1,0:T(8,128)}), f32[64,256]{1,0:T(8,128)}) %reduce-scatter.2.cloned.1.call-update) | async-done | bytes 65552 | tf_op jit(solution)/shard_map/reduce_scatter | solution.py:44
  1466.5 0.0 copy-done.3
  1466.5 1.0 convolution_convert_fusion
  1467.5 0.0 copy-done.1
  1467.5 0.0 copy-done.7
  1467.5 1.1 fusion.1
  1468.6 0.0 copy-done.2
  1468.6 0.0 copy-done.5
  1468.6 0.8 fusion
  (3 shorter events, 0.0 us)
Async XLA Ops:
  6.5 159.1 %copy-start = (bf16[256,256]{1,0:T(8,128)(2,1)S(1)}, bf16[256,256]{1,0:T(8,128)(2,1)}, u32[]{:S(2)}) copy-start(bf16[256,256]{1,0:T(8,128)(2,1)} %param.17) | copy-start | bytes 393220
  6.5 1459.9 %reduce-scatter.2.cloned.1.call-start = ((), (), s32[]{:S(2)}) async-start(), calls=%async_computation.1 | async-start | bytes 16842752 | tf_op jit(solution)/shard_map/reduce_scatter | solution.py:44
  41.5 33.5 %copy-start.6 = (s32[256]{0:T(256)S(1)}, s32[256]{0:T(256)}, u32[]{:S(2)}) copy-start(s32[256]{0:T(256)} %param.14) | copy-start | bytes 3076
  173.7 0.7 copy-start.4
  173.7 1292.8 %copy-start.3 = (f32[256]{0:T(256)S(1)}, f32[256]{0:T(256)}, u32[]{:S(2)}) copy-start(f32[256]{0:T(256)} %param.18) | copy-start | bytes 3076
  173.7 1293.8 %copy-start.1 = (bf16[256,172]{0,1:T(8,128)(2,1)S(1)}, bf16[256,172]{0,1:T(8,128)(2,1)}, u32[]{:S(2)}) copy-start(bf16[256,172]{0,1:T(8,128)(2,1)} %param.19) | copy-start | bytes 264196
  173.7 1293.8 %copy-start.7 = (s32[32]{0:T(128)S(1)}, s32[32]{0:T(128)}, u32[]{:S(2)}) copy-start(s32[32]{0:T(128)} %param.22) | copy-start | bytes 388
  173.7 1294.9 %copy-start.2 = (bf16[256,172]{0,1:T(8,128)(2,1)S(1)}, bf16[256,172]{0,1:T(8,128)(2,1)}, u32[]{:S(2)}) copy-start(bf16[256,172]{0,1:T(8,128)(2,1)} %param.20) | copy-start | bytes 264196
  173.7 1294.9 %copy-start.5 = (f32[172]{0:T(256)S(1)}, f32[172]{0:T(256)}, u32[]{:S(2)}) copy-start(f32[172]{0:T(256)} %param.21) | copy-start | bytes 2068
Sparse Core Ops, SparseCore 0:
  173.9 1292.5 reduce-scatter.1
where the time goes:
time: 1480 us
  waiting for transfers between devices  1290 us (87%)
  other arithmetic  83.7 us (6%)
  local copies, waits for them, and re-layouts  54 us (4%)
  matrix products  32.6 us (2%)
    reduce_scatter x1, waiting for transfers between devices, on_device(): lax.psum_scatter(projector(aggregated, layer_one), ('node', 'feat'), scat...  1290 us
    scatter-add x1, other arithmetic, on_device(): summed = jnp.zeros((target_blocks, block_size, columns), jnp.float32).at[...  76.3 us
    mul x1, local copies, waits for them, and re-layouts, on_device(): products * live_mask[:, None, None]  33.5 us
  transfers between devices with their start and end apart: 1, of which 1 were waited for; matrix products, arithmetic and copies ran while one was open for 0% of the time, Pallas kernels for 0%

commit v1 on v0

v1 whole, which is shorter than its diff:
```python
import functools

import jax
import jax.numpy as jnp
from jax import lax
from jax.experimental import pallas as pl
from jax.experimental.pallas import tpu as pltpu
from jax.sharding import PartitionSpec as P

T_DEV = 64
NT = (((1,), (1,)), ((), ()))


def project_kernel(where, layer_one, features, *refs):
    *outs, ordered = refs
    chips = where[2]
    width = outs[0].shape[1]
    hidden = layer_one.shape[1]

    @pl.when(pl.program_id(0) == 0)
    def _():
        row = lax.broadcasted_iota(jnp.int32, (hidden, hidden), 0)
        column = lax.broadcasted_iota(jnp.int32, (hidden, hidden), 1)
        half = hidden // 2
        other = (row < half).astype(jnp.int32)
        place = (row % half) // width
        hop = (place + 1) // 2
        hop = chips // 2 + jnp.where(place % 2 == 1, -hop, hop)
        chip = (where[0] + hop) % chips
        core = (where[1] + other) % 2
        wanted = (chip * 2 + core) * width + row % width
        pick = (column == wanted).astype(jnp.bfloat16)
        ordered[...] = lax.dot_general(
            pick, layer_one[...], NT, preferred_element_type=jnp.float32
        ).astype(jnp.bfloat16)

    product = lax.dot_general(ordered[...], features[...], NT, preferred_element_type=jnp.float32)
    at = 0
    for out in outs:
        for k in range(out.shape[0]):
            out[k] = product[at : at + width]
            at += width


def project(where, layer_one, features, chips, width):
    rows, columns = features.shape
    hidden = layer_one.shape[1]
    tile = min(1024, rows)
    groups = [1] + [2] * (chips // 2 - 1) + [1]
    shapes = [jax.ShapeDtypeStruct((g, width, rows), jnp.float32) for g in groups] * 2
    return pl.pallas_call(
        project_kernel,
        grid_spec=pltpu.PrefetchScalarGridSpec(
            num_scalar_prefetch=1,
            grid=(rows // tile,),
            in_specs=[
                pl.BlockSpec((columns, hidden), lambda i, w: (0, 0)),
                pl.BlockSpec((tile, columns), lambda i, w: (i, 0)),
            ],
            out_specs=[pl.BlockSpec((g, width, tile), lambda i, w: (0, 0, i)) for g in groups] * 2,
            scratch_shapes=[pltpu.VMEM((hidden, columns), jnp.bfloat16)],
        ),
        out_shape=shapes,
        name="project",
        compiler_params=pltpu.CompilerParams(vmem_limit_bytes=24 * 2**20),
        cost_estimate=pl.CostEstimate(
            flops=2 * rows * columns * hidden,
            bytes_accessed=rows * columns * 2 + rows * hidden * 4,
            transcendentals=0,
        ),
    )(where, layer_one, features)


def blocks_kernel(target, source, count, own, paired, forward, backward, adjacency, out, held):
    step = pl.program_id(0)
    group = adjacency.shape[0]
    size = adjacency.shape[1]

    @pl.when(step == 0)
    def _():
        out[...] = jnp.zeros_like(out)
        for b in range(held.shape[0]):
            at = slice(b * size, (b + 1) * size)
            held[b] = (
                (own[0, :, at] + paired[0, :, at]) + (forward[0, :, at] + backward[0, :, at])
            ).astype(held.dtype)

    first = step * group
    live = count[0]

    @pl.when(first + group <= live)
    def _():
        products = []
        for k in range(group):
            products.append(
                lax.dot_general(
                    held[source[first + k]], adjacency[k], NT, preferred_element_type=jnp.float32
                )
            )
        for k in range(group):
            out[target[first + k]] += products[k]

    @pl.when((first < live) & (first + group > live))
    def _():
        for k in range(group):

            @pl.when(first + k < live)
            def _():
                out[target[first + k]] += lax.dot_general(
                    held[source[first + k]], adjacency[k], NT, preferred_element_type=jnp.float32
                )


def blocks(target, source, count, own, paired, forward, backward, adjacency, target_blocks):
    slots, size, _ = adjacency.shape
    width, rows = own.shape[1:]
    group = 16

    def last_live(i, t, s, c):
        return jnp.minimum(i, (c[0] - 1) // group), 0, 0

    whole = pl.BlockSpec((1, width, rows), lambda i, t, s, c: (0, 0, 0))
    return pl.pallas_call(
        blocks_kernel,
        grid_spec=pltpu.PrefetchScalarGridSpec(
            num_scalar_prefetch=3,
            grid=(slots // group,),
            in_specs=[whole] * 4 + [pl.BlockSpec((group, size, size), last_live)],
            out_specs=pl.BlockSpec((target_blocks, width, size), lambda i, t, s, c: (0, 0, 0)),
            scratch_shapes=[pltpu.VMEM((rows // size, width, size), jnp.bfloat16)],
        ),
        out_shape=jax.ShapeDtypeStruct((target_blocks, width, size), jnp.float32),
        name="blocks",
        compiler_params=pltpu.CompilerParams(vmem_limit_bytes=24 * 2**20),
        cost_estimate=pl.CostEstimate(
            flops=2 * slots * size * size * width,
            bytes_accessed=slots * size * size * 2,
            transcendentals=0,
        ),
    )(target, source, count, own, paired, forward, backward, adjacency)


def second_kernel(where, sums, bias_one, self_weight, neigh_weight, bias_two, seeds, neighbors, out):
    hidden = jnp.maximum(sums[...] + bias_one[...], 0.0).astype(jnp.bfloat16)
    count, fan = neighbors.shape
    positions = lax.broadcasted_iota(jnp.int32, (count, hidden.shape[1]), 1) - where[1] * T_DEV
    pick_self = (positions == seeds[...]).astype(jnp.bfloat16)
    tally = jnp.zeros(positions.shape, jnp.float32)
    for k in range(fan):
        tally += (positions == neighbors[:, k : k + 1]).astype(jnp.float32)
    weights_mean = (tally / fan).astype(jnp.bfloat16)
    self_rows = lax.dot_general(pick_self, hidden, NT, preferred_element_type=jnp.float32)
    neigh_mean = lax.dot_general(weights_mean, hidden, NT, preferred_element_type=jnp.float32)
    out[...] = (
        jnp.dot(
            self_rows.astype(jnp.bfloat16), self_weight[...], preferred_element_type=jnp.float32
        )
        + jnp.dot(
            neigh_mean.astype(jnp.bfloat16), neigh_weight[...], preferred_element_type=jnp.float32
        )
        + bias_two[...]
    )


def second(where, sums, bias_one, self_weight, neigh_weight, bias_two, seeds, neighbors):
    vmem = pl.BlockSpec(memory_space=pltpu.VMEM)
    return pl.pallas_call(
        second_kernel,
        in_specs=[pl.BlockSpec(memory_space=pltpu.SMEM)] + [vmem] * 7,
        out_specs=vmem,
        out_shape=jax.ShapeDtypeStruct((seeds.shape[0], bias_two.shape[0]), jnp.float32),
        name="second",
        compiler_params=pltpu.CompilerParams(vmem_limit_bytes=16 * 2**20),
    )(
        where,
        sums,
        bias_one[:, None],
        self_weight,
        neigh_weight,
        bias_two[None, :],
        seeds[:, None],
        neighbors,
    )


def on_device(
    features,
    adjacency,
    target_block,
    source_block,
    block_count,
    layer_one,
    bias_one,
    self_weight,
    neigh_weight,
    bias_two,
    seed_ids,
    neighbor_ids,
):
    size = adjacency.shape[1]
    node_count = lax.axis_size("node")
    feat_count = lax.axis_size("feat")
    chips = feat_count // 2
    hidden = layer_one.shape[1]
    width = hidden // feat_count
    target_blocks = T_DEV * node_count * feat_count // size
    feat = lax.axis_index("feat")
    where = jnp.stack([feat // 2, feat % 2, jnp.int32(chips)]).astype(jnp.int32)

    pair = [(i, i ^ 1) for i in range(feat_count)]
    up = [(i, (i + 2) % feat_count) for i in range(feat_count)]
    down = [((i + 2) % feat_count, i) for i in range(feat_count)]

    def send(value, route):
        return lax.ppermute(value, "feat", route)

    *parts, = project(where, layer_one, features, chips, width)
    groups = len(parts) // 2
    paired = [send(part, pair) for part in parts[:groups]]
    kept = parts[groups:]

    half = width // 2
    opposite = kept[0][0] + paired[0][0]
    forward = send(opposite[:half], up)
    backward = send(opposite[half:], down)
    for g in range(1, groups - 1):
        onward = kept[g][0] + paired[g][0]
        back = kept[g][1] + paired[g][1]
        if g == 1:
            onward = jnp.concatenate([onward[:half] + forward, onward[half:]])
            back = jnp.concatenate([back[:half], back[half:] + backward])
        else:
            onward = onward + forward
            back = back + backward
        forward = send(onward, up)
        backward = send(back, down)

    partial = blocks(
        target_block,
        source_block,
        block_count,
        kept[-1],
        paired[-1],
        forward[None],
        backward[None],
        adjacency,
        target_blocks,
    )

    partial = partial.reshape(node_count, chips, width, size)
    summed = jnp.sum(lax.all_to_all(partial, "node", 0, 0), axis=0)
    doubled = jnp.broadcast_to(summed[:, None], (chips, 2, width, size))
    sums = lax.all_to_all(doubled.reshape(feat_count, width, size), "feat", 0, 0)
    return second(
        where,
        sums.reshape(hidden, size),
        bias_one,
        self_weight,
        neigh_weight,
        bias_two,
        seed_ids,
        neighbor_ids,
    )


def solution(mesh):
    placed = (
        P("node", "feat"),
        P("node", None, None),
        P("node"),
        P("node"),
        P("node"),
        P("feat", None),
        P(),
        P(),
        P(),
        P(),
        P(("node", "feat")),
        P(("node", "feat"), None),
    )
    return jax.shard_map(
        on_device, mesh=mesh, in_specs=placed, out_specs=P(("node", "feat"), None), check_vma=False
    )
```

time: 1480 us -> 112 us (0.08)
  waiting for transfers between devices: 1290 us -> 42.2 us
  other arithmetic: 83.7 us -> 0.94 us
  local copies, waits for them, and re-layouts: 54 us -> 4.38 us
  matrix products: 32.6 us -> 0 us
  starting transfers between devices: 0.01 us -> 29.3 us
  blocking collectives: 0 us -> 19.4 us
    reduce_scatter x1 -> x0, waiting for transfers between devices: 1290 us -> none  [on_device(): lax.psum_scatter(projector(aggregated, layer_one), ('node', 'feat'), scat...]
    scatter-add x1 -> x0, other arithmetic: 76.3 us -> none  [on_device(): summed = jnp.zeros((target_blocks, block_size, columns), jnp.float32).at[...]
    ppermute x0 -> x13, waiting for transfers between devices: none -> 33.6 us  [send(): return lax.ppermute(value, 'feat', route)]
    mul x1 -> x0, local copies, waits for them, and re-layouts: 33.5 us -> none  [on_device(): products * live_mask[:, None, None]]
    dot_general x5 -> x0, matrix products: 32.6 us -> none  [the longest x1 21.6 us: on_device(): jnp.einsum('bij,bjf->bif', adjacency, sources, preferred_element_type=jnp...]
    ppermute x0 -> x13, starting transfers between devices: none -> 20.1 us  [send(): return lax.ppermute(value, 'feat', route)]
    all_to_all x0 -> x1, blocking collectives: none -> 19.4 us  [on_device(): summed = jnp.sum(lax.all_to_all(partial, 'node', 0, 0), axis=0)]
  transfers between devices with their start and end apart: 1 -> 14, of which waited for: 1 -> 8; matrix products, arithmetic and copies ran while one was open for 0% -> 1% of each run, Pallas kernels for 0% -> 0%
where the time goes in v1:
time: 112 us; the launch traced here: 111 us
  waiting for transfers between devices  42.2 us (38%)
  starting transfers between devices  29.3 us (26%)
  blocking collectives  19.4 us (17%)
  Pallas kernels  13.8 us (12%)
  local copies, waits for them, and re-layouts  4.38 us (4%)
    ppermute x13, waiting for transfers between devices, send(): return lax.ppermute(value, 'feat', route)  33.6 us
    ppermute x13, starting transfers between devices, send(): return lax.ppermute(value, 'feat', route)  20.1 us
    all_to_all x1, blocking collectives, on_device(): summed = jnp.sum(lax.all_to_all(partial, 'node', 0, 0), axis=0)  19.4 us
    all_to_all x1, starting transfers between devices, on_device(): lax.all_to_all(doubled.reshape(feat_count, width, size), 'feat', 0, 0)  9.13 us
    all_to_all x1, waiting for transfers between devices, on_device(): lax.all_to_all(doubled.reshape(feat_count, width, size), 'feat', 0, 0)  8.61 us
    pallas_call x1, Pallas kernels, blocks(): pl.pallas_call(blocks_kernel, grid_spec=pltpu.PrefetchScalarGridSpec(num_...  6.69 us
    pallas_call x1, Pallas kernels, project(): pl.pallas_call(project_kernel, grid_spec=pltpu.PrefetchScalarGridSpec(num...  5.55 us
    unnamed x27, local copies, waits for them, and re-layouts  3.43 us
  transfers between devices with their start and end apart: 14, of which 8 were waited for; matrix products, arithmetic and copies ran while one was open for 1% of the time, Pallas kernels for 0%

profile of v1, /device:TPU:1, one launch (start us, length us, event | category | flops | bytes accessed | tf_op | source)
XLA Modules:
  0.0 110.9 jit_solution(7089168421135888258)
XLA Ops:
  0.1 2.2 %copy-done = bf16[8192,256]{1,0:T(8,128)(2,1)S(1)} copy-done((bf16[8192,256]{1,0:T(8,128)(2,1)S(1)}, bf16[8192,256]{1,0:T(8,128)(2,1)}, u32[]{:S(2)}) %copy-start) | copy-done | bytes 4194328
  2.3 0.9 copy-done.1
  3.2 5.6 %project.1 = (f32[1,16,8192]{2,1,0:T(8,128)S(1)}, f32[2,16,8192]{2,1,0:T(8,128)S(1)}, f32[2,16,8192]{2,1,0:T(8,128)S(1)}, f32[2,16,8192]{2,1,0:T(8,128)S(1)}, f3...) custom-call(s32[3]{0:T(128)S(1)} %pad_add_fusion.where, ...), custom_call_target="tpu_custom_call" | custom-call | flops 1073741824 | bytes 12582912 | tf_op jit(solution)/shard_map/project/pallas_call | solution.py:51
  8.7 3.3 %collective-permute-start.4 = (f32[1,16,8192]{2,1,0:T(8,128)S(1)}, f32[1,16,8192]{2,1,0:T(8,128)S(1)}, u32[]{:S(2)}, u32[]{:S(2)}) collective-permute-start(f32[1,16,8192]{2,1,0:T(8,128)S(1)} %get-tuple-element.24), channel_id=1, source_target_pairs={{0,1},{1,0},{2,3},{3,2},{4,5},{5,4},{6,7},{7,6},{8,9},{9,8},{10,11... | collective-permute-start | bytes 1572872 | tf_op jit(solution)/shard_map/ppermute | solution.py:215
  12.1 0.1 collective-permute-start.3
  12.2 0.4 collective-permute-start.2
  12.6 1.0 collective-permute-done.4
  13.8 3.9 %collective-permute-start.9 = (f32[8,8192]{1,0:T(8,128)S(1)}, f32[8,8192]{1,0:T(8,128)S(1)}, u32[]{:S(2)}, u32[]{:S(2)}) collective-permute-start(f32[8,8192]{1,0:T(8,128)S(1)} %get-tuple-element.31), channel_id=1, source_target_pairs={{2,0},{3,1},{4,2},{5,3},{6,4},{7,5},{8,6},{9,7},{10,8},{11,9},{12,... | collective-permute-start | bytes 786440 | tf_op jit(solution)/shard_map/ppermute | solution.py:215
  17.7 0.2 slice_add_fusion
  17.9 5.1 %collective-permute-done.9 = f32[8,8192]{1,0:T(8,128)S(1)} collective-permute-done((f32[8,8192]{1,0:T(8,128)S(1)}, f32[8,8192]{1,0:T(8,128)S(1)}, u32[]{:S(2)}, u32[]{:S(2)}) %collective-permute-start.9) | collective-permute-done | bytes 262176 | tf_op jit(solution)/shard_map/ppermute | solution.py:215
  23.1 3.5 %collective-permute-start.10 = (f32[16,8192]{1,0:T(8,128)S(1)}, f32[16,8192]{1,0:T(8,128)S(1)}, u32[]{:S(2)}, u32[]{:S(2)}) collective-permute-start(f32[16,8192]{1,0:T(8,128)S(1)} %pad_maximum_fusion.1), channel_id=1, source_target_pairs={{2,0},{3,1},{4,2},{5,3},{6,4},{7,5},{8,6},{9,7},{10,8},{11,9},{12,... | collective-permute-start | bytes 1572872 | tf_op jit(solution)/shard_map/ppermute | solution.py:215
  26.8 1.6 %collective-permute-start.1 = (f32[2,16,8192]{2,1,0:T(8,128)S(1)}, f32[2,16,8192]{2,1,0:T(8,128)S(1)}, u32[]{:S(2)}, u32[]{:S(2)}) collective-permute-start(f32[2,16,8192]{2,1,0:T(8,128)S(1)} %get-tuple-element.18), channel_id=1, source_target_pairs={{0,1},{1,0},{2,3},{3,2},{4,5},{5,4},{6,7},{7,6},{8,9},{9,8},{10,11... | collective-permute-start | bytes 3145736 | tf_op jit(solution)/shard_map/ppermute | solution.py:215
  28.3 8.2 %collective-permute-done.10 = f32[16,8192]{1,0:T(8,128)S(1)} collective-permute-done((f32[16,8192]{1,0:T(8,128)S(1)}, f32[16,8192]{1,0:T(8,128)S(1)}, u32[]{:S(2)}, u32[]{:S(2)}) %collective-permute-start.10) | collective-permute-done | bytes 524320 | tf_op jit(solution)/shard_map/ppermute | solution.py:215
  36.6 3.3 %collective-permute-done.6 = f32[16,8192]{1,0:T(8,128)S(1)} collective-permute-done((f32[16,8192]{1,0:T(8,128)S(1)}, f32[16,8192]{1,0:T(8,128)S(1)}, u32[]{:S(2)}, u32[]{:S(2)}) %collective-permute-start.6) | collective-permute-done | bytes 524320 | tf_op jit(solution)/shard_map/ppermute | solution.py:215
  39.9 0.2 fusion.1
  40.1 0.2 collective-permute-start.11
  40.3 1.4 %collective-permute-start.7 = (f32[16,8192]{1,0:T(8,128)S(1)}, f32[16,8192]{1,0:T(8,128)S(1)}, u32[]{:S(2)}, u32[]{:S(2)}) collective-permute-start(f32[16,8192]{1,0:T(8,128)S(1)} %get-tuple-element.28), channel_id=1, source_target_pairs={{0,2},{1,3},{2,4},{3,5},{4,6},{5,7},{6,8},{7,9},{8,10},{9,11},{10,... | collective-permute-start | bytes 1572872 | tf_op jit(solution)/shard_map/ppermute | solution.py:215
  41.7 3.0 %collective-permute-start = (f32[1,16,8192]{2,1,0:T(8,128)S(1)}, f32[1,16,8192]{2,1,0:T(8,128)S(1)}, u32[]{:S(2)}, u32[]{:S(2)}) collective-permute-start(f32[1,16,8192]{2,1,0:T(8,128)S(1)} %get-tuple-element.16), channel_id=1, source_target_pairs={{0,1},{1,0},{2,3},{3,2},{4,5},{5,4},{6,7},{7,6},{8,9},{9,8},{10,11... | collective-permute-start | bytes 1572872 | tf_op jit(solution)/shard_map/ppermute | solution.py:215
  44.6 6.6 %collective-permute-done.11 = f32[16,8192]{1,0:T(8,128)S(1)} collective-permute-done((f32[16,8192]{1,0:T(8,128)S(1)}, f32[16,8192]{1,0:T(8,128)S(1)}, u32[]{:S(2)}, u32[]{:S(2)}) %collective-permute-start.11) | collective-permute-done | bytes 524320 | tf_op jit(solution)/shard_map/ppermute | solution.py:215
  51.2 1.3 %collective-permute-done.7 = f32[16,8192]{1,0:T(8,128)S(1)} collective-permute-done((f32[16,8192]{1,0:T(8,128)S(1)}, f32[16,8192]{1,0:T(8,128)S(1)}, u32[]{:S(2)}, u32[]{:S(2)}) %collective-permute-start.7) | collective-permute-done | bytes 524320 | tf_op jit(solution)/shard_map/ppermute | solution.py:215
  52.5 0.2 fusion.3
  52.9 2.7 %collective-permute-start.12 = (f32[16,8192]{1,0:T(8,128)S(1)}, f32[16,8192]{1,0:T(8,128)S(1)}, u32[]{:S(2)}, u32[]{:S(2)}) collective-permute-start(f32[16,8192]{1,0:T(8,128)S(1)} %get-tuple-element.25), channel_id=1, source_target_pairs={{2,0},{3,1},{4,2},{5,3},{6,4},{7,5},{8,6},{9,7},{10,8},{11,9},{12,... | collective-permute-start | bytes 1572872 | tf_op jit(solution)/shard_map/ppermute | solution.py:215
  56.2 8.0 %collective-permute-done.8 = f32[16,8192]{1,0:T(8,128)S(1)} collective-permute-done((f32[16,8192]{1,0:T(8,128)S(1)}, f32[16,8192]{1,0:T(8,128)S(1)}, u32[]{:S(2)}, u32[]{:S(2)}) %collective-permute-start.8) | collective-permute-done | bytes 524320 | tf_op jit(solution)/shard_map/ppermute | solution.py:215
  64.2 6.7 %blocks.1 = f32[128,16,128]{2,1,0:T(8,128)S(1)} custom-call(s32[256]{0:T(256)S(1)} %copy-done.2, s32[256]{0:T(256)S(1)} %copy-done.3, s32[1]{0:T(128)S(6)} %copy.22.count, f32[1,16,8192]{2,1,0:T(8,128)S(1)} %get-tuple-element.15.own, f32[1,16,8192]{2,1,0:T(8,128)S(1)} %collective-permute-done.paired, f32[1,16,8192]{2,1,0:T(8,128)S(1)} %bitcast.45, ...), custom_call_target="tpu_custom_call" | custom-call | flops 134217728 | bytes 8388608 | tf_op jit(solution)/shard_map/blocks/pallas_call | solution.py:123
  70.9 19.4 %all_to_all.10 = f32[16,8,16,128]{3,2,1,0:T(8,128)S(1)} all-to-all(f32[16,8,16,128]{3,2,1,0:T(8,128)S(1)} %bitcast.44), channel_id=1, replica_groups=mesh['node'=16,'feat'=16] {'node'}, dimensions={0} | all-to-all | bytes 2097152 | tf_op jit(solution)/shard_map/all_to_all | solution.py:251
  90.4 0.7 broadcast_in_dim.23
  91.1 9.1 %all-to-all-start.1 = ((f32[16,16,128]{2,1,0:T(8,128)}), f32[16,16,128]{2,1,0:T(8,128)S(1)}, u32[]{:S(2)}, u32[]{:S(2)}) async-start(f32[16,16,128]{2,1,0:T(8,128)} %bitcast.15), calls=%async_computation.1 | async-start | bytes 262144 | tf_op jit(solution)/shard_map/all_to_all | solution.py:253
  100.2 0.1 copy.17.bias_one
  100.4 0.1 copy.18.self_weight
  100.5 0.1 copy.19.neigh_weight
  100.8 8.6 %all-to-all-done.1 = f32[16,16,128]{2,1,0:T(8,128)S(1)} async-done(((f32[16,16,128]{2,1,0:T(8,128)}), f32[16,16,128]{2,1,0:T(8,128)S(1)}, u32[]{:S(2)}, u32[]{:S(2)}) %all-to-all-start.1) | async-done | bytes 131104 | tf_op jit(solution)/shard_map/all_to_all | solution.py:253
  109.4 1.6 %second.1 = f32[32,172]{1,0:T(8,128)} custom-call(s32[3]{0:T(128)S(1)} %pad_add_fusion.where, f32[256,128]{1,0:T(8,128)S(1)} %bitcast.47, f32[256,1]{1,0:T(8,128)S(1)} %copy.17.bias_one, bf16[256,172]{1,0:T(8,128)(2,1)S(1)} %copy.18.self_weight, bf16[256,172]{1,0:T(8,128)(2,1)S(1)} %copy.19.neigh_weight, f32[1,172]{1,0:T(1,128)S(1)} %bitcast.48, ...), custom_call_target="tpu_custom_call" | custom-call | tf_op jit(solution)/shard_map/second/pallas_call | solution.py:167
  (44 shorter events, 0.8 us)
Async XLA Ops:
  0.1 2.2 %copy-start = (bf16[8192,256]{1,0:T(8,128)(2,1)S(1)}, bf16[8192,256]{1,0:T(8,128)(2,1)}, u32[]{:S(2)}) copy-start(bf16[8192,256]{1,0:T(8,128)(2,1)} %features.1) | copy-start | bytes 12582916
  2.3 0.9 copy-start.1
  8.7 4.9 %collective-permute-start.4 = (f32[1,16,8192]{2,1,0:T(8,128)S(1)}, f32[1,16,8192]{2,1,0:T(8,128)S(1)}, u32[]{:S(2)}, u32[]{:S(2)}) collective-permute-start(f32[1,16,8192]{2,1,0:T(8,128)S(1)} %get-tuple-element.24), channel_id=1, source_target_pairs={{0,1},{1,0},{2,3},{3,2},{4,5},{5,4},{6,7},{7,6},{8,9},{9,8},{10,11... | collective-permute-start | bytes 1572872 | tf_op jit(solution)/shard_map/ppermute | solution.py:215
  12.1 5.6 %collective-permute-start.3 = (f32[2,16,8192]{2,1,0:T(8,128)S(1)}, f32[2,16,8192]{2,1,0:T(8,128)S(1)}, u32[]{:S(2)}, u32[]{:S(2)}) collective-permute-start(f32[2,16,8192]{2,1,0:T(8,128)S(1)} %get-tuple-element.22), channel_id=1, source_target_pairs={{0,1},{1,0},{2,3},{3,2},{4,5},{5,4},{6,7},{7,6},{8,9},{9,8},{10,11... | collective-permute-start | bytes 3145736 | tf_op jit(solution)/shard_map/ppermute | solution.py:215
  12.2 16.2 %collective-permute-start.2 = (f32[2,16,8192]{2,1,0:T(8,128)S(1)}, f32[2,16,8192]{2,1,0:T(8,128)S(1)}, u32[]{:S(2)}, u32[]{:S(2)}) collective-permute-start(f32[2,16,8192]{2,1,0:T(8,128)S(1)} %get-tuple-element.20), channel_id=1, source_target_pairs={{0,1},{1,0},{2,3},{3,2},{4,5},{5,4},{6,7},{7,6},{8,9},{9,8},{10,11... | collective-permute-start | bytes 3145736 | tf_op jit(solution)/shard_map/ppermute | solution.py:215
  13.7 50.5 %slice-start = ((s8[8388608]{0:T(1024)(128)(4,1)}), s8[4194304]{0:T(1024)(128)(4,1)S(1)}, s32[]{:S(2)}) async-start(s8[8388608]{0:T(1024)(128)(4,1)} %bitcast.42), calls=%async_computation.2 | async-start | bytes 8388608
  13.7 50.5 %copy-start.2 = (s32[256]{0:T(256)S(1)}, s32[256]{0:T(256)}, u32[]{:S(2)}) copy-start(s32[256]{0:T(256)} %target.1) | copy-start | bytes 3076
  13.7 50.5 %copy-start.3 = (s32[256]{0:T(256)S(1)}, s32[256]{0:T(256)}, u32[]{:S(2)}) copy-start(s32[256]{0:T(256)} %source.1) | copy-start | bytes 3076
  13.8 9.2 %collective-permute-start.9 = (f32[8,8192]{1,0:T(8,128)S(1)}, f32[8,8192]{1,0:T(8,128)S(1)}, u32[]{:S(2)}, u32[]{:S(2)}) collective-permute-start(f32[8,8192]{1,0:T(8,128)S(1)} %get-tuple-element.31), channel_id=1, source_target_pairs={{2,0},{3,1},{4,2},{5,3},{6,4},{7,5},{8,6},{9,7},{10,8},{11,9},{12,... | collective-permute-start | bytes 786440 | tf_op jit(solution)/shard_map/ppermute | solution.py:215
  17.7 8.9 %collective-permute-start.5 = (f32[8,8192]{1,0:T(8,128)S(1)}, f32[8,8192]{1,0:T(8,128)S(1)}, u32[]{:S(2)}, u32[]{:S(2)}) collective-permute-start(f32[8,8192]{1,0:T(8,128)S(1)} %get-tuple-element.32), channel_id=1, source_target_pairs={{0,2},{1,3},{2,4},{3,5},{4,6},{5,7},{6,8},{7,9},{8,10},{9,11},{10,... | collective-permute-start | bytes 786440 | tf_op jit(solution)/shard_map/ppermute | solution.py:215
  23.1 13.5 %collective-permute-start.10 = (f32[16,8192]{1,0:T(8,128)S(1)}, f32[16,8192]{1,0:T(8,128)S(1)}, u32[]{:S(2)}, u32[]{:S(2)}) collective-permute-start(f32[16,8192]{1,0:T(8,128)S(1)} %pad_maximum_fusion.1), channel_id=1, source_target_pairs={{2,0},{3,1},{4,2},{5,3},{6,4},{7,5},{8,6},{9,7},{10,8},{11,9},{12,... | collective-permute-start | bytes 1572872 | tf_op jit(solution)/shard_map/ppermute | solution.py:215
  26.7 13.2 %collective-permute-start.6 = (f32[16,8192]{1,0:T(8,128)S(1)}, f32[16,8192]{1,0:T(8,128)S(1)}, u32[]{:S(2)}, u32[]{:S(2)}) collective-permute-start(f32[16,8192]{1,0:T(8,128)S(1)} %pad_maximum_fusion), channel_id=1, source_target_pairs={{0,2},{1,3},{2,4},{3,5},{4,6},{5,7},{6,8},{7,9},{8,10},{9,11},{10,... | collective-permute-start | bytes 1572872 | tf_op jit(solution)/shard_map/ppermute | solution.py:215
  26.8 17.9 %collective-permute-start.1 = (f32[2,16,8192]{2,1,0:T(8,128)S(1)}, f32[2,16,8192]{2,1,0:T(8,128)S(1)}, u32[]{:S(2)}, u32[]{:S(2)}) collective-permute-start(f32[2,16,8192]{2,1,0:T(8,128)S(1)} %get-tuple-element.18), channel_id=1, source_target_pairs={{0,1},{1,0},{2,3},{3,2},{4,5},{5,4},{6,7},{7,6},{8,9},{9,8},{10,11... | collective-permute-start | bytes 3145736 | tf_op jit(solution)/shard_map/ppermute | solution.py:215
  39.9 24.3 %slice-start.1 = ((s8[8388608]{0:T(1024)(128)(4,1)}), s8[4194304]{0:T(1024)(128)(4,1)S(1)}, s32[]{:S(2)}) async-start(s8[8388608]{0:T(1024)(128)(4,1)} %bitcast.42), calls=%async_computation.3 | async-start | bytes 8388608
  40.1 11.1 %collective-permute-start.11 = (f32[16,8192]{1,0:T(8,128)S(1)}, f32[16,8192]{1,0:T(8,128)S(1)}, u32[]{:S(2)}, u32[]{:S(2)}) collective-permute-start(f32[16,8192]{1,0:T(8,128)S(1)} %get-tuple-element.27), channel_id=1, source_target_pairs={{2,0},{3,1},{4,2},{5,3},{6,4},{7,5},{8,6},{9,7},{10,8},{11,9},{12,... | collective-permute-start | bytes 1572872 | tf_op jit(solution)/shard_map/ppermute | solution.py:215
  40.3 12.2 %collective-permute-start.7 = (f32[16,8192]{1,0:T(8,128)S(1)}, f32[16,8192]{1,0:T(8,128)S(1)}, u32[]{:S(2)}, u32[]{:S(2)}) collective-permute-start(f32[16,8192]{1,0:T(8,128)S(1)} %get-tuple-element.28), channel_id=1, source_target_pairs={{0,2},{1,3},{2,4},{3,5},{4,6},{5,7},{6,8},{7,9},{8,10},{9,11},{10,... | collective-permute-start | bytes 1572872 | tf_op jit(solution)/shard_map/ppermute | solution.py:215
  41.7 14.5 %collective-permute-start = (f32[1,16,8192]{2,1,0:T(8,128)S(1)}, f32[1,16,8192]{2,1,0:T(8,128)S(1)}, u32[]{:S(2)}, u32[]{:S(2)}) collective-permute-start(f32[1,16,8192]{2,1,0:T(8,128)S(1)} %get-tuple-element.16), channel_id=1, source_target_pairs={{0,1},{1,0},{2,3},{3,2},{4,5},{5,4},{6,7},{7,6},{8,9},{9,8},{10,11... | collective-permute-start | bytes 1572872 | tf_op jit(solution)/shard_map/ppermute | solution.py:215
  52.7 47.5 %copy-start.8 = (f32[256]{0:T(256)S(1)}, f32[256]{0:T(256)}, u32[]{:S(2)}) copy-start(f32[256]{0:T(256)} %param.18) | copy-start | bytes 3076
  52.7 47.6 %copy-start.5 = (bf16[256,172]{0,1:T(8,128)(2,1)S(1)}, bf16[256,172]{0,1:T(8,128)(2,1)}, u32[]{:S(2)}) copy-start(bf16[256,172]{0,1:T(8,128)(2,1)} %param.19) | copy-start | bytes 264196
  52.8 47.7 %copy-start.6 = (bf16[256,172]{0,1:T(8,128)(2,1)S(1)}, bf16[256,172]{0,1:T(8,128)(2,1)}, u32[]{:S(2)}) copy-start(bf16[256,172]{0,1:T(8,128)(2,1)} %param.20) | copy-start | bytes 264196
  52.8 47.8 %copy-start.9 = (s32[32]{0:T(128)S(1)}, s32[32]{0:T(128)}, u32[]{:S(2)}) copy-start(s32[32]{0:T(128)} %param.22) | copy-start | bytes 388
  52.8 47.9 %copy-start.7 = (s32[32,8]{0,1:T(8,128)S(1)}, s32[32,8]{0,1:T(8,128)}, u32[]{:S(2)}) copy-start(s32[32,8]{0,1:T(8,128)} %param.23) | copy-start | bytes 3076
  52.8 56.6 %copy-start.4 = (f32[172]{0:T(256)S(1)}, f32[172]{0:T(256)}, u32[]{:S(2)}) copy-start(f32[172]{0:T(256)} %param.21) | copy-start | bytes 2068
  52.8 11.4 %collective-permute-start.8 = (f32[16,8192]{1,0:T(8,128)S(1)}, f32[16,8192]{1,0:T(8,128)S(1)}, u32[]{:S(2)}, u32[]{:S(2)}) collective-permute-start(f32[16,8192]{1,0:T(8,128)S(1)} %get-tuple-element.26), channel_id=1, source_target_pairs={{0,2},{1,3},{2,4},{3,5},{4,6},{5,7},{6,8},{7,9},{8,10},{9,11},{10,... | collective-permute-start | bytes 1572872 | tf_op jit(solution)/shard_map/ppermute | solution.py:215
  52.9 11.3 %collective-permute-start.12 = (f32[16,8192]{1,0:T(8,128)S(1)}, f32[16,8192]{1,0:T(8,128)S(1)}, u32[]{:S(2)}, u32[]{:S(2)}) collective-permute-start(f32[16,8192]{1,0:T(8,128)S(1)} %get-tuple-element.25), channel_id=1, source_target_pairs={{2,0},{3,1},{4,2},{5,3},{6,4},{7,5},{8,6},{9,7},{10,8},{11,9},{12,... | collective-permute-start | bytes 1572872 | tf_op jit(solution)/shard_map/ppermute | solution.py:215
  91.1 18.3 %all-to-all-start.1 = ((f32[16,16,128]{2,1,0:T(8,128)}), f32[16,16,128]{2,1,0:T(8,128)S(1)}, u32[]{:S(2)}, u32[]{:S(2)}) async-start(f32[16,16,128]{2,1,0:T(8,128)} %bitcast.15), calls=%async_computation.1 | async-start | bytes 262144 | tf_op jit(solution)/shard_map/all_to_all | solution.py:253

commit v2 on v1

v2 whole, which is shorter than its diff:
```python
import jax
import jax.numpy as jnp
from jax import lax
from jax.experimental import pallas as pl
from jax.experimental.pallas import tpu as pltpu
from jax.sharding import PartitionSpec as P

T_DEV = 64
NT = (((1,), (1,)), ((), ()))


VMEM = pl.BlockSpec(memory_space=pltpu.VMEM)
SMEM = pl.BlockSpec(memory_space=pltpu.SMEM)


def project_kernel(where, layer_one, features, *outs):
    chips, streams = 8, 2
    strip = outs[0].shape[1]
    width = streams * strip
    hidden = layer_one.shape[1]
    row = lax.broadcasted_iota(jnp.int32, (hidden, hidden), 0)
    column = lax.broadcasted_iota(jnp.int32, (hidden, hidden), 1)
    half = hidden // 2
    core = (where[1] + (row < half).astype(jnp.int32)) % 2
    place = (row % half) // width
    hop = (place + 1) // 2
    hop = chips // 2 + jnp.where(place % 2 == 1, -hop, hop)
    chip = (where[0] + hop) % chips
    wanted = (chip * 2 + core) * width + row % width
    pick = (column == wanted).astype(jnp.bfloat16)
    ordered = lax.dot_general(
        pick, layer_one[...], NT, preferred_element_type=jnp.float32
    ).astype(jnp.bfloat16)

    tiles = 16
    tile = features.shape[0] // tiles
    for i in range(tiles):
        rows = features[i * tile : (i + 1) * tile]
        product = lax.dot_general(ordered, rows, NT, preferred_element_type=jnp.float32)
        side, at = divmod(i, tiles // 2)
        take = 0
        for out in outs:
            for k in range(out.shape[0] // 2):
                out[2 * k + side, :, at * tile : (at + 1) * tile] = product[take : take + strip]
                take += strip


def project(where, layer_one, features):
    rows, columns = features.shape
    hidden = layer_one.shape[1]
    strip = hidden // 32
    shapes = [
        jax.ShapeDtypeStruct((4 * hops, strip, rows // 2), jnp.float32) for hops in (1, 2, 5)
    ] * 2
    return pl.pallas_call(
        project_kernel,
        in_specs=[SMEM, VMEM, VMEM],
        out_specs=[VMEM] * 6,
        out_shape=shapes,
        name="project",
        compiler_params=pltpu.CompilerParams(vmem_limit_bytes=8 * 2**20),
        cost_estimate=pl.CostEstimate(
            flops=2 * rows * columns * hidden,
            bytes_accessed=rows * columns * 2 + rows * hidden * 4,
            transcendentals=0,
        ),
    )(where, layer_one, features)


def blocks_kernel(target, source, count, own, paired, up_a, down_a, up_b, down_b, adjacency, out, held):
    size = adjacency.shape[1]
    strip = own.shape[1]
    out[...] = jnp.zeros_like(out)
    blocks = held.shape[0]
    for b in range(blocks):
        side, at = divmod(b, blocks // 2)
        at = slice(at * size, (at + 1) * size)
        totals = [
            (own[2 * k + side, :, at] + paired[2 * k + side, :, at])
            + (up[side, :, at] + down[side, :, at])
            for k, (up, down) in enumerate(((up_a, down_a), (up_b, down_b)))
        ]
        total = jnp.concatenate(totals, axis=0)
        upper = total.astype(jnp.bfloat16)
        held[b, : 2 * strip] = upper
        held[b, 2 * strip :] = (total - upper.astype(jnp.float32)).astype(jnp.bfloat16)

    def product(s):
        value = lax.dot_general(
            held[source[s]], adjacency[s], NT, preferred_element_type=jnp.float32
        )
        return value[: 2 * strip] + value[2 * strip :]

    group = 16
    live = count[0]
    full = live // group

    def whole(i, before):
        products = [product(i * group + k) for k in range(group)]
        for k in range(group):
            out[target[(i - 1) * group + k]] += before[k]
        return products

    last = lax.fori_loop(1, full, whole, [product(k) for k in range(group)])
    for k in range(group):
        out[target[(full - 1) * group + k]] += last[k]

    def single(s, carry):
        out[target[s]] += product(s)
        return carry

    lax.fori_loop(full * group, live, single, 0)


def blocks(target, source, count, own, paired, streams, adjacency, target_blocks):
    slots, size, _ = adjacency.shape
    parts, strip, half_rows = own.shape
    width = parts // 2 * strip
    return pl.pallas_call(
        blocks_kernel,
        in_specs=[SMEM] * 3 + [VMEM] * 7,
        out_specs=VMEM,
        out_shape=jax.ShapeDtypeStruct((target_blocks, width, size), jnp.float32),
        scratch_shapes=[pltpu.VMEM((2 * half_rows // size, 2 * width, size), jnp.bfloat16)],
        name="blocks",
        compiler_params=pltpu.CompilerParams(vmem_limit_bytes=8 * 2**20),
        cost_estimate=pl.CostEstimate(
            flops=2 * slots * size * size * width,
            bytes_accessed=slots * size * size * 2,
            transcendentals=0,
        ),
    )(target, source, count, own, paired, *streams[0], *streams[1], adjacency)


def second_kernel(where, sums, bias_one, self_weight, neigh_weight, bias_two, seeds, neighbors, out):
    hidden = jnp.maximum(sums[...] + bias_one[...], 0.0).astype(jnp.bfloat16)
    count, fan = neighbors.shape
    positions = lax.broadcasted_iota(jnp.int32, (count, hidden.shape[1]), 1) - where[1] * T_DEV
    pick_self = (positions == seeds[...]).astype(jnp.bfloat16)
    tally = jnp.zeros(positions.shape, jnp.float32)
    for k in range(fan):
        tally += (positions == neighbors[:, k : k + 1]).astype(jnp.float32)
    weights_mean = (tally / fan).astype(jnp.bfloat16)
    self_rows = lax.dot_general(pick_self, hidden, NT, preferred_element_type=jnp.float32)
    neigh_mean = lax.dot_general(weights_mean, hidden, NT, preferred_element_type=jnp.float32)
    out[...] = (
        jnp.dot(
            self_rows.astype(jnp.bfloat16), self_weight[...], preferred_element_type=jnp.float32
        )
        + jnp.dot(
            neigh_mean.astype(jnp.bfloat16), neigh_weight[...], preferred_element_type=jnp.float32
        )
        + bias_two[...]
    )


def second(where, sums, bias_one, self_weight, neigh_weight, bias_two, seeds, neighbors):
    vmem = pl.BlockSpec(memory_space=pltpu.VMEM)
    return pl.pallas_call(
        second_kernel,
        in_specs=[pl.BlockSpec(memory_space=pltpu.SMEM)] + [vmem] * 7,
        out_specs=vmem,
        out_shape=jax.ShapeDtypeStruct((seeds.shape[0], bias_two.shape[0]), jnp.float32),
        name="second",
        compiler_params=pltpu.CompilerParams(vmem_limit_bytes=16 * 2**20),
    )(
        where,
        sums,
        bias_one[:, None],
        self_weight,
        neigh_weight,
        bias_two[None, :],
        seeds[:, None],
        neighbors,
    )


def on_device(
    features,
    adjacency,
    target_block,
    source_block,
    block_count,
    layer_one,
    bias_one,
    self_weight,
    neigh_weight,
    bias_two,
    seed_ids,
    neighbor_ids,
):
    size = adjacency.shape[1]
    node_count = lax.axis_size("node")
    feat_count = lax.axis_size("feat")
    chips = feat_count // 2
    hidden = layer_one.shape[1]
    width = hidden // feat_count
    target_blocks = T_DEV * node_count * feat_count // size
    feat = lax.axis_index("feat")
    where = jnp.stack([feat >> 1, feat & 1]).astype(jnp.int32)

    pair = [(i, i ^ 1) for i in range(feat_count)]
    up = [(i, (i + 2) % feat_count) for i in range(feat_count)]
    down = [((i + 2) % feat_count, i) for i in range(feat_count)]

    def send(value, route):
        return lax.ppermute(value, "feat", route)

    parts = project(where, layer_one, features)
    opposite, three, rest = [send(part, pair) for part in parts[:3]]
    opposite_own, three_own, rest_own = parts[3:]
    strip, half_rows = opposite.shape[1:]

    tie = lax.optimization_barrier
    opposite = (opposite_own + opposite).reshape(2, 2, strip, half_rows)
    zero = jnp.float32(0)
    streams = []
    for k in range(2):
        onward, back, opposite = tie((opposite[k, 0], opposite[k, 1], opposite))
        streams.append((send(onward, up), send(back, down)))
    three = three.reshape(2, 2, 2, strip, half_rows)
    three_own = three_own.reshape(2, 2, 2, strip, half_rows)
    for k, (onward, back) in enumerate(streams):
        onward = lax.pad(onward[None], zero, ((0, 1, 0), (0, 0, 0), (0, 0, 0)))
        back = lax.pad(back[None], zero, ((1, 0, 0), (0, 0, 0), (0, 0, 0)))
        onward, back, three, three_own = tie(
            (
                three_own[0, k] + three[0, k] + onward,
                three_own[1, k] + three[1, k] + back,
                three,
                three_own,
            )
        )
        streams[k] = send(onward, up), send(back, down)
    rest = rest.reshape(5, 2, 2, strip, half_rows)
    rest_own = rest_own.reshape(5, 2, 2, strip, half_rows)
    for hop in (0, 2):
        for k, (onward, back) in enumerate(streams):
            onward, back, rest, rest_own = tie(
                (
                    rest_own[hop, k] + rest[hop, k] + onward,
                    rest_own[hop + 1, k] + rest[hop + 1, k] + back,
                    rest,
                    rest_own,
                )
            )
            streams[k] = send(onward, up), send(back, down)

    partial = blocks(
        target_block,
        source_block,
        block_count,
        rest_own[4].reshape(4, strip, half_rows),
        rest[4].reshape(4, strip, half_rows),
        streams,
        adjacency,
        target_blocks,
    )

    partial = partial.reshape(node_count, chips, width, size)
    summed = jnp.sum(lax.all_to_all(partial, "node", 0, 0), axis=0)
    doubled = jnp.broadcast_to(summed[:, None], (chips, 2, width, size))
    sums = lax.all_to_all(doubled.reshape(feat_count, width, size), "feat", 0, 0)
    return second(
        where,
        sums.reshape(hidden, size),
        bias_one,
        self_weight,
        neigh_weight,
        bias_two,
        seed_ids,
        neighbor_ids,
    )


def solution(mesh):
    placed = (
        P("node", "feat"),
        P("node", None, None),
        P("node"),
        P("node"),
        P("node"),
        P("feat", None),
        P(),
        P(),
        P(),
        P(),
        P(("node", "feat")),
        P(("node", "feat"), None),
    )
    return jax.shard_map(
        on_device, mesh=mesh, in_specs=placed, out_specs=P(("node", "feat"), None), check_vma=False
    )
```

time: 112 us -> 106 us (0.946); the launches traced: 111 us -> 106 us
  waiting for transfers between devices: 42.2 us -> 33.2 us
  starting transfers between devices: 29.3 us -> 35.9 us
  Pallas kernels: 13.8 us -> 8.23 us
  blocking collectives: 19.4 us -> 22.8 us
    ppermute x13 -> x19, waiting for transfers between devices: 33.6 us -> 24.6 us  [send(): return lax.ppermute(value, 'feat', route)]
    pallas_call x2, Pallas kernels: 12.2 us -> 6.66 us  [the longest x1 4.57 us: blocks(): pl.pallas_call(blocks_kernel, in_specs=[SMEM] * 3 + [VMEM] * 7, out_specs...]
    ppermute x13 -> x19, starting transfers between devices: 20.1 us -> 24.8 us  [send(): return lax.ppermute(value, 'feat', route)]
    all_to_all x1, blocking collectives: 19.4 us -> 22.8 us  [on_device(): summed = jnp.sum(lax.all_to_all(partial, 'node', 0, 0), axis=0)]
    all_to_all x1, starting transfers between devices: 9.13 us -> 11.2 us  [on_device(): lax.all_to_all(doubled.reshape(feat_count, width, size), 'feat', 0, 0)]
  transfers between devices with their start and end apart: 14 -> 20, of which waited for: 8 -> 14; matrix products, arithmetic and copies ran while one was open for 1% -> 1% of each run, Pallas kernels for 0% -> 0%
where the time goes in v2:
time: 106 us
  starting transfers between devices  35.9 us (34%)
  waiting for transfers between devices  33.2 us (31%)
  blocking collectives  22.8 us (22%)
  Pallas kernels  8.23 us (8%)
  local copies, waits for them, and re-layouts  4.43 us (4%)
    ppermute x19, starting transfers between devices, send(): return lax.ppermute(value, 'feat', route)  24.8 us
    ppermute x19, waiting for transfers between devices, send(): return lax.ppermute(value, 'feat', route)  24.6 us
    all_to_all x1, blocking collectives, on_device(): summed = jnp.sum(lax.all_to_all(partial, 'node', 0, 0), axis=0)  22.8 us
    all_to_all x1, starting transfers between devices, on_device(): lax.all_to_all(doubled.reshape(feat_count, width, size), 'feat', 0, 0)  11.2 us
    all_to_all x1, waiting for transfers between devices, on_device(): lax.all_to_all(doubled.reshape(feat_count, width, size), 'feat', 0, 0)  8.61 us
    pallas_call x1, Pallas kernels, blocks(): pl.pallas_call(blocks_kernel, in_specs=[SMEM] * 3 + [VMEM] * 7, out_specs...  4.57 us
    unnamed x27, local copies, waits for them, and re-layouts  3.45 us
  transfers between devices with their start and end apart: 20, of which 14 were waited for; matrix products, arithmetic and copies ran while one was open for 1% of the time, Pallas kernels for 0%

profile of v2, /device:TPU:1, one launch (start us, length us, event | category | flops | bytes accessed | tf_op | source)
XLA Modules:
  0.0 106.2 jit_solution(5939124562079122605)
XLA Ops:
  0.1 2.2 %copy-done = bf16[8192,256]{1,0:T(8,128)(2,1)S(1)} copy-done((bf16[8192,256]{1,0:T(8,128)(2,1)S(1)}, bf16[8192,256]{1,0:T(8,128)(2,1)}, u32[]{:S(2)}) %copy-start) | copy-done | bytes 4194328
  2.3 0.9 copy-done.1
  3.2 2.1 %project.1 = (f32[4,8,4096]{2,1,0:T(8,128)S(1)}, f32[8,8,4096]{2,1,0:T(8,128)S(1)}, f32[20,8,4096]{2,1,0:T(8,128)S(1)}, f32[4,8,4096]{2,1,0:T(8,128)S(1)}, f32[8...) custom-call(s32[2]{0:T(128)S(1)} %pad_add_fusion.where, bf16[256,256]{1,0:T(8,128)(2,1)S(1)} %copy-done.1, ...), custom_call_target="tpu_custom_call" | custom-call | flops 1073741824 | bytes 12582912 | tf_op jit(solution)/shard_map/project/pallas_call | solution.py:55
  5.3 3.3 %collective-permute-start.2 = (f32[4,8,4096]{2,1,0:T(8,128)S(1)}, f32[4,8,4096]{2,1,0:T(8,128)S(1)}, u32[]{:S(2)}, u32[]{:S(2)}) collective-permute-start(f32[4,8,4096]{2,1,0:T(8,128)S(1)} %get-tuple-element.43), channel_id=1, source_target_pairs={{0,1},{1,0},{2,3},{3,2},{4,5},{5,4},{6,7},{7,6},{8,9},{9,8},{10,11... | collective-permute-start | bytes 1572872 | tf_op jit(solution)/shard_map/ppermute | solution.py:207
  9.1 1.0 collective-permute-done.2
  10.2 3.9 %collective-permute-start.4 = (f32[8,4096]{1,0:T(8,128)S(1)}, f32[8,4096]{1,0:T(8,128)S(1)}, u32[]{:S(2)}, u32[]{:S(2)}) collective-permute-start(f32[8,4096]{1,0:T(8,128)S(1)} %get-tuple-element.45), channel_id=1, source_target_pairs={{2,0},{3,1},{4,2},{5,3},{6,4},{7,5},{8,6},{9,7},{10,8},{11,9},{12,... | collective-permute-start | bytes 393224 | tf_op jit(solution)/shard_map/ppermute | solution.py:207
  14.2 2.7 %collective-permute-start.8 = (f32[8,4096]{1,0:T(8,128)S(1)}, f32[8,4096]{1,0:T(8,128)S(1)}, u32[]{:S(2)}, u32[]{:S(2)}) collective-permute-start(f32[8,4096]{1,0:T(8,128)S(1)} %get-tuple-element.54), channel_id=1, source_target_pairs={{2,0},{3,1},{4,2},{5,3},{6,4},{7,5},{8,6},{9,7},{10,8},{11,9},{12,... | collective-permute-start | bytes 393224 | tf_op jit(solution)/shard_map/ppermute | solution.py:207
  16.9 2.8 %collective-permute-done.3 = f32[8,4096]{1,0:T(8,128)S(1)} collective-permute-done((f32[8,4096]{1,0:T(8,128)S(1)}, f32[8,4096]{1,0:T(8,128)S(1)}, u32[]{:S(2)}, u32[]{:S(2)}) %collective-permute-start.3) | collective-permute-done | bytes 131104 | tf_op jit(solution)/shard_map/ppermute | solution.py:207
  19.8 0.4 collective-permute-start.6
  20.2 1.1 %collective-permute-start.5 = (f32[2,8,4096]{2,1,0:T(8,128)S(1)}, f32[2,8,4096]{2,1,0:T(8,128)S(1)}, u32[]{:S(2)}, u32[]{:S(2)}) collective-permute-start(f32[2,8,4096]{2,1,0:T(8,128)S(1)} %get-tuple-element.46), channel_id=1, source_target_pairs={{0,2},{1,3},{2,4},{3,5},{4,6},{5,7},{6,8},{7,9},{8,10},{9,11},{10,... | collective-permute-start | bytes 786440 | tf_op jit(solution)/shard_map/ppermute | solution.py:207
  21.4 1.1 collective-permute-done.7
  22.5 1.5 %collective-permute-start.10 = (f32[2,8,4096]{2,1,0:T(8,128)S(1)}, f32[2,8,4096]{2,1,0:T(8,128)S(1)}, u32[]{:S(2)}, u32[]{:S(2)}) collective-permute-start(f32[2,8,4096]{2,1,0:T(8,128)S(1)} %get-tuple-element.56), channel_id=1, source_target_pairs={{2,0},{3,1},{4,2},{5,3},{6,4},{7,5},{8,6},{9,7},{10,8},{11,9},{12,... | collective-permute-start | bytes 786440 | tf_op jit(solution)/shard_map/ppermute | solution.py:207
  24.0 2.1 %collective-permute-done.6 = f32[2,8,4096]{2,1,0:T(8,128)S(1)} collective-permute-done((f32[2,8,4096]{2,1,0:T(8,128)S(1)}, f32[2,8,4096]{2,1,0:T(8,128)S(1)}, u32[]{:S(2)}, u32[]{:S(2)}) %collective-permute-start.6) | collective-permute-done | bytes 262176 | tf_op jit(solution)/shard_map/ppermute | solution.py:207
  26.2 1.6 %collective-permute-done.5 = f32[2,8,4096]{2,1,0:T(8,128)S(1)} collective-permute-done((f32[2,8,4096]{2,1,0:T(8,128)S(1)}, f32[2,8,4096]{2,1,0:T(8,128)S(1)}, u32[]{:S(2)}, u32[]{:S(2)}) %collective-permute-start.5) | collective-permute-done | bytes 262176 | tf_op jit(solution)/shard_map/ppermute | solution.py:207
  27.9 2.3 %collective-permute-start.12 = (f32[2,8,4096]{2,1,0:T(8,128)S(1)}, f32[2,8,4096]{2,1,0:T(8,128)S(1)}, u32[]{:S(2)}, u32[]{:S(2)}) collective-permute-start(f32[2,8,4096]{2,1,0:T(8,128)S(1)} %get-tuple-element.60), channel_id=1, source_target_pairs={{2,0},{3,1},{4,2},{5,3},{6,4},{7,5},{8,6},{9,7},{10,8},{11,9},{12,... | collective-permute-start | bytes 786440 | tf_op jit(solution)/shard_map/ppermute | solution.py:207
  30.1 1.6 %collective-permute-done.10 = f32[2,8,4096]{2,1,0:T(8,128)S(1)} collective-permute-done((f32[2,8,4096]{2,1,0:T(8,128)S(1)}, f32[2,8,4096]{2,1,0:T(8,128)S(1)}, u32[]{:S(2)}, u32[]{:S(2)}) %collective-permute-start.10) | collective-permute-done | bytes 262176 | tf_op jit(solution)/shard_map/ppermute | solution.py:207
  31.8 0.9 collective-permute-done.9
  32.7 3.0 %collective-permute-start.14 = (f32[2,8,4096]{2,1,0:T(8,128)S(1)}, f32[2,8,4096]{2,1,0:T(8,128)S(1)}, u32[]{:S(2)}, u32[]{:S(2)}) collective-permute-start(f32[2,8,4096]{2,1,0:T(8,128)S(1)} %get-tuple-element.64), channel_id=1, source_target_pairs={{2,0},{3,1},{4,2},{5,3},{6,4},{7,5},{8,6},{9,7},{10,8},{11,9},{12,... | collective-permute-start | bytes 786440 | tf_op jit(solution)/shard_map/ppermute | solution.py:207
  35.8 1.6 %collective-permute-done.12 = f32[2,8,4096]{2,1,0:T(8,128)S(1)} collective-permute-done((f32[2,8,4096]{2,1,0:T(8,128)S(1)}, f32[2,8,4096]{2,1,0:T(8,128)S(1)}, u32[]{:S(2)}, u32[]{:S(2)}) %collective-permute-start.12) | collective-permute-done | bytes 262176 | tf_op jit(solution)/shard_map/ppermute | solution.py:207
  37.4 0.8 collective-permute-done.11
  38.4 4.7 %collective-permute-done.14 = f32[2,8,4096]{2,1,0:T(8,128)S(1)} collective-permute-done((f32[2,8,4096]{2,1,0:T(8,128)S(1)}, f32[2,8,4096]{2,1,0:T(8,128)S(1)}, u32[]{:S(2)}, u32[]{:S(2)}) %collective-permute-start.14) | collective-permute-done | bytes 262176 | tf_op jit(solution)/shard_map/ppermute | solution.py:207
  43.0 0.8 collective-permute-done.13
  43.9 0.4 collective-permute-start.15
  44.4 2.7 %collective-permute-start.16 = (f32[2,8,4096]{2,1,0:T(8,128)S(1)}, f32[2,8,4096]{2,1,0:T(8,128)S(1)}, u32[]{:S(2)}, u32[]{:S(2)}) collective-permute-start(f32[2,8,4096]{2,1,0:T(8,128)S(1)} %get-tuple-element.68), channel_id=1, source_target_pairs={{2,0},{3,1},{4,2},{5,3},{6,4},{7,5},{8,6},{9,7},{10,8},{11,9},{12,... | collective-permute-start | bytes 786440 | tf_op jit(solution)/shard_map/ppermute | solution.py:207
  47.1 2.7 %collective-permute-start.18 = (f32[2,8,4096]{2,1,0:T(8,128)S(1)}, f32[2,8,4096]{2,1,0:T(8,128)S(1)}, u32[]{:S(2)}, u32[]{:S(2)}) collective-permute-start(f32[2,8,4096]{2,1,0:T(8,128)S(1)} %get-tuple-element.70), channel_id=1, source_target_pairs={{2,0},{3,1},{4,2},{5,3},{6,4},{7,5},{8,6},{9,7},{10,8},{11,9},{12,... | collective-permute-start | bytes 786440 | tf_op jit(solution)/shard_map/ppermute | solution.py:207
  50.8 5.3 %collective-permute-done.17.up_b = f32[2,8,4096]{2,1,0:T(8,128)S(1)} collective-permute-done((f32[2,8,4096]{2,1,0:T(8,128)S(1)}, f32[2,8,4096]{2,1,0:T(8,128)S(1)}, u32[]{:S(2)}, u32[]{:S(2)}) %collective-permute-start.17) | collective-permute-done | bytes 262176 | tf_op jit(solution)/shard_map/ppermute | solution.py:207
  56.1 4.6 %blocks.1 = f32[128,16,128]{2,1,0:T(8,128)S(1)} custom-call(s32[256]{0:T(256)S(1)} %copy-done.2, s32[256]{0:T(256)S(1)} %copy-done.3, s32[1]{0:T(128)S(6)} %copy.22.count, f32[4,8,4096]{2,1,0:T(8,128)S(1)} %bitcast.67, f32[4,8,4096]{2,1,0:T(8,128)S(1)} %bitcast.68, f32[2,8,4096]{2,1,0:T(8,128)S(1)} %collective-permute-done.15.up_a, ...), custom_call_target="tpu_custom_call" | custom-call | flops 134217728 | bytes 8388608 | tf_op jit(solution)/shard_map/blocks/pallas_call | solution.py:119
  60.8 22.8 %all_to_all.10 = f32[16,8,16,128]{3,2,1,0:T(8,128)S(1)} all-to-all(f32[16,8,16,128]{3,2,1,0:T(8,128)S(1)} %bitcast.61), channel_id=1, replica_groups=mesh['node'=16,'feat'=16] {'node'}, dimensions={0} | all-to-all | bytes 2097152 | tf_op jit(solution)/shard_map/all_to_all | solution.py:261
  83.6 0.7 broadcast_in_dim.31
  84.3 11.2 %all-to-all-start.1 = ((f32[16,16,128]{2,1,0:T(8,128)}), f32[16,16,128]{2,1,0:T(8,128)S(1)}, u32[]{:S(2)}, u32[]{:S(2)}) async-start(f32[16,16,128]{2,1,0:T(8,128)} %bitcast.30), calls=%async_computation.1 | async-start | bytes 262144 | tf_op jit(solution)/shard_map/all_to_all | solution.py:263
  96.0 8.6 %all-to-all-done.1 = f32[16,16,128]{2,1,0:T(8,128)S(1)} async-done(((f32[16,16,128]{2,1,0:T(8,128)}), f32[16,16,128]{2,1,0:T(8,128)S(1)}, u32[]{:S(2)}, u32[]{:S(2)}) %all-to-all-start.1) | async-done | bytes 131104 | tf_op jit(solution)/shard_map/all_to_all | solution.py:263
  104.6 1.6 %second.1 = f32[32,172]{1,0:T(8,128)} custom-call(s32[2]{0:T(128)S(1)} %pad_add_fusion.where, f32[256,128]{1,0:T(8,128)S(1)} %bitcast.71, f32[256,1]{1,0:T(8,128)S(1)} %copy.17.bias_one, bf16[256,172]{1,0:T(8,128)(2,1)S(1)} %copy.18.self_weight, bf16[256,172]{1,0:T(8,128)(2,1)S(1)} %copy.19.neigh_weight, f32[1,172]{1,0:T(1,128)S(1)} %bitcast.72, ...), custom_call_target="tpu_custom_call" | custom-call | tf_op jit(solution)/shard_map/second/pallas_call | solution.py:159
  (56 shorter events, 2.2 us)
Async XLA Ops:
  0.1 2.2 %copy-start = (bf16[8192,256]{1,0:T(8,128)(2,1)S(1)}, bf16[8192,256]{1,0:T(8,128)(2,1)}, u32[]{:S(2)}) copy-start(bf16[8192,256]{1,0:T(8,128)(2,1)} %features.1) | copy-start | bytes 12582916
  2.3 0.9 copy-start.1
  5.3 4.9 %collective-permute-start.2 = (f32[4,8,4096]{2,1,0:T(8,128)S(1)}, f32[4,8,4096]{2,1,0:T(8,128)S(1)}, u32[]{:S(2)}, u32[]{:S(2)}) collective-permute-start(f32[4,8,4096]{2,1,0:T(8,128)S(1)} %get-tuple-element.43), channel_id=1, source_target_pairs={{0,1},{1,0},{2,3},{3,2},{4,5},{5,4},{6,7},{7,6},{8,9},{9,8},{10,11... | collective-permute-start | bytes 1572872 | tf_op jit(solution)/shard_map/ppermute | solution.py:207
  8.6 11.2 %collective-permute-start.1 = (f32[8,8,4096]{2,1,0:T(8,128)S(1)}, f32[8,8,4096]{2,1,0:T(8,128)S(1)}, u32[]{:S(2)}, u32[]{:S(2)}) collective-permute-start(f32[8,8,4096]{2,1,0:T(8,128)S(1)} %get-tuple-element.41), channel_id=1, source_target_pairs={{0,1},{1,0},{2,3},{3,2},{4,5},{5,4},{6,7},{7,6},{8,9},{9,8},{10,11... | collective-permute-start | bytes 3145736 | tf_op jit(solution)/shard_map/ppermute | solution.py:207
  8.7 19.1 %collective-permute-start = (f32[20,8,4096]{2,1,0:T(8,128)S(1)}, f32[20,8,4096]{2,1,0:T(8,128)S(1)}, u32[]{:S(2)}, u32[]{:S(2)}) collective-permute-start(f32[20,8,4096]{2,1,0:T(8,128)S(1)} %get-tuple-element.39), channel_id=1, source_target_pairs={{0,1},{1,0},{2,3},{3,2},{4,5},{5,4},{6,7},{7,6},{8,9},{9,8},{10,11... | collective-permute-start | bytes 7864328 | tf_op jit(solution)/shard_map/ppermute | solution.py:207
  10.2 45.9 %slice-start = ((s8[8388608]{0:T(1024)(128)(4,1)}), s8[4194304]{0:T(1024)(128)(4,1)S(1)}, s32[]{:S(2)}) async-start(s8[8388608]{0:T(1024)(128)(4,1)} %bitcast.59), calls=%async_computation.2 | async-start | bytes 8388608
  10.2 6.7 %collective-permute-start.4 = (f32[8,4096]{1,0:T(8,128)S(1)}, f32[8,4096]{1,0:T(8,128)S(1)}, u32[]{:S(2)}, u32[]{:S(2)}) collective-permute-start(f32[8,4096]{1,0:T(8,128)S(1)} %get-tuple-element.45), channel_id=1, source_target_pairs={{2,0},{3,1},{4,2},{5,3},{6,4},{7,5},{8,6},{9,7},{10,8},{11,9},{12,... | collective-permute-start | bytes 393224 | tf_op jit(solution)/shard_map/ppermute | solution.py:207
  14.1 5.6 %collective-permute-start.3 = (f32[8,4096]{1,0:T(8,128)S(1)}, f32[8,4096]{1,0:T(8,128)S(1)}, u32[]{:S(2)}, u32[]{:S(2)}) collective-permute-start(f32[8,4096]{1,0:T(8,128)S(1)} %get-tuple-element.44), channel_id=1, source_target_pairs={{0,2},{1,3},{2,4},{3,5},{4,6},{5,7},{6,8},{7,9},{8,10},{9,11},{10,... | collective-permute-start | bytes 393224 | tf_op jit(solution)/shard_map/ppermute | solution.py:207
  14.2 7.2 %collective-permute-start.8 = (f32[8,4096]{1,0:T(8,128)S(1)}, f32[8,4096]{1,0:T(8,128)S(1)}, u32[]{:S(2)}, u32[]{:S(2)}) collective-permute-start(f32[8,4096]{1,0:T(8,128)S(1)} %get-tuple-element.54), channel_id=1, source_target_pairs={{2,0},{3,1},{4,2},{5,3},{6,4},{7,5},{8,6},{9,7},{10,8},{11,9},{12,... | collective-permute-start | bytes 393224 | tf_op jit(solution)/shard_map/ppermute | solution.py:207
  16.9 5.5 %collective-permute-start.7 = (f32[8,4096]{1,0:T(8,128)S(1)}, f32[8,4096]{1,0:T(8,128)S(1)}, u32[]{:S(2)}, u32[]{:S(2)}) collective-permute-start(f32[8,4096]{1,0:T(8,128)S(1)} %get-tuple-element.53), channel_id=1, source_target_pairs={{0,2},{1,3},{2,4},{3,5},{4,6},{5,7},{6,8},{7,9},{8,10},{9,11},{10,... | collective-permute-start | bytes 393224 | tf_op jit(solution)/shard_map/ppermute | solution.py:207
  19.8 6.4 %collective-permute-start.6 = (f32[2,8,4096]{2,1,0:T(8,128)S(1)}, f32[2,8,4096]{2,1,0:T(8,128)S(1)}, u32[]{:S(2)}, u32[]{:S(2)}) collective-permute-start(f32[2,8,4096]{2,1,0:T(8,128)S(1)} %get-tuple-element.47), channel_id=1, source_target_pairs={{2,0},{3,1},{4,2},{5,3},{6,4},{7,5},{8,6},{9,7},{10,8},{11,9},{12,... | collective-permute-start | bytes 786440 | tf_op jit(solution)/shard_map/ppermute | solution.py:207
  20.2 7.5 %collective-permute-start.5 = (f32[2,8,4096]{2,1,0:T(8,128)S(1)}, f32[2,8,4096]{2,1,0:T(8,128)S(1)}, u32[]{:S(2)}, u32[]{:S(2)}) collective-permute-start(f32[2,8,4096]{2,1,0:T(8,128)S(1)} %get-tuple-element.46), channel_id=1, source_target_pairs={{0,2},{1,3},{2,4},{3,5},{4,6},{5,7},{6,8},{7,9},{8,10},{9,11},{10,... | collective-permute-start | bytes 786440 | tf_op jit(solution)/shard_map/ppermute | solution.py:207
  22.5 9.3 %collective-permute-start.10 = (f32[2,8,4096]{2,1,0:T(8,128)S(1)}, f32[2,8,4096]{2,1,0:T(8,128)S(1)}, u32[]{:S(2)}, u32[]{:S(2)}) collective-permute-start(f32[2,8,4096]{2,1,0:T(8,128)S(1)} %get-tuple-element.56), channel_id=1, source_target_pairs={{2,0},{3,1},{4,2},{5,3},{6,4},{7,5},{8,6},{9,7},{10,8},{11,9},{12,... | collective-permute-start | bytes 786440 | tf_op jit(solution)/shard_map/ppermute | solution.py:207
  24.0 8.6 %collective-permute-start.9 = (f32[2,8,4096]{2,1,0:T(8,128)S(1)}, f32[2,8,4096]{2,1,0:T(8,128)S(1)}, u32[]{:S(2)}, u32[]{:S(2)}) collective-permute-start(f32[2,8,4096]{2,1,0:T(8,128)S(1)} %get-tuple-element.55), channel_id=1, source_target_pairs={{0,2},{1,3},{2,4},{3,5},{4,6},{5,7},{6,8},{7,9},{8,10},{9,11},{10,... | collective-permute-start | bytes 786440 | tf_op jit(solution)/shard_map/ppermute | solution.py:207
  27.8 28.2 %slice-start.1 = ((s8[8388608]{0:T(1024)(128)(4,1)}), s8[4194304]{0:T(1024)(128)(4,1)S(1)}, s32[]{:S(2)}) async-start(s8[8388608]{0:T(1024)(128)(4,1)} %bitcast.59), calls=%async_computation.3 | async-start | bytes 8388608
  27.9 9.5 %collective-permute-start.12 = (f32[2,8,4096]{2,1,0:T(8,128)S(1)}, f32[2,8,4096]{2,1,0:T(8,128)S(1)}, u32[]{:S(2)}, u32[]{:S(2)}) collective-permute-start(f32[2,8,4096]{2,1,0:T(8,128)S(1)} %get-tuple-element.60), channel_id=1, source_target_pairs={{2,0},{3,1},{4,2},{5,3},{6,4},{7,5},{8,6},{9,7},{10,8},{11,9},{12,... | collective-permute-start | bytes 786440 | tf_op jit(solution)/shard_map/ppermute | solution.py:207
  30.1 8.1 %collective-permute-start.11 = (f32[2,8,4096]{2,1,0:T(8,128)S(1)}, f32[2,8,4096]{2,1,0:T(8,128)S(1)}, u32[]{:S(2)}, u32[]{:S(2)}) collective-permute-start(f32[2,8,4096]{2,1,0:T(8,128)S(1)} %get-tuple-element.59), channel_id=1, source_target_pairs={{0,2},{1,3},{2,4},{3,5},{4,6},{5,7},{6,8},{7,9},{8,10},{9,11},{10,... | collective-permute-start | bytes 786440 | tf_op jit(solution)/shard_map/ppermute | solution.py:207
  32.7 10.3 %collective-permute-start.14 = (f32[2,8,4096]{2,1,0:T(8,128)S(1)}, f32[2,8,4096]{2,1,0:T(8,128)S(1)}, u32[]{:S(2)}, u32[]{:S(2)}) collective-permute-start(f32[2,8,4096]{2,1,0:T(8,128)S(1)} %get-tuple-element.64), channel_id=1, source_target_pairs={{2,0},{3,1},{4,2},{5,3},{6,4},{7,5},{8,6},{9,7},{10,8},{11,9},{12,... | collective-permute-start | bytes 786440 | tf_op jit(solution)/shard_map/ppermute | solution.py:207
  35.8 8.1 %collective-permute-start.13 = (f32[2,8,4096]{2,1,0:T(8,128)S(1)}, f32[2,8,4096]{2,1,0:T(8,128)S(1)}, u32[]{:S(2)}, u32[]{:S(2)}) collective-permute-start(f32[2,8,4096]{2,1,0:T(8,128)S(1)} %get-tuple-element.63), channel_id=1, source_target_pairs={{0,2},{1,3},{2,4},{3,5},{4,6},{5,7},{6,8},{7,9},{8,10},{9,11},{10,... | collective-permute-start | bytes 786440 | tf_op jit(solution)/shard_map/ppermute | solution.py:207
  38.3 17.8 %copy-start.2 = (s32[256]{0:T(256)S(1)}, s32[256]{0:T(256)}, u32[]{:S(2)}) copy-start(s32[256]{0:T(256)} %target.1) | copy-start | bytes 3076
  38.3 17.8 %copy-start.3 = (s32[256]{0:T(256)S(1)}, s32[256]{0:T(256)}, u32[]{:S(2)}) copy-start(s32[256]{0:T(256)} %source.1) | copy-start | bytes 3076
  43.9 6.8 %collective-permute-start.15 = (f32[2,8,4096]{2,1,0:T(8,128)S(1)}, f32[2,8,4096]{2,1,0:T(8,128)S(1)}, u32[]{:S(2)}, u32[]{:S(2)}) collective-permute-start(f32[2,8,4096]{2,1,0:T(8,128)S(1)} %get-tuple-element.67), channel_id=1, source_target_pairs={{0,2},{1,3},{2,4},{3,5},{4,6},{5,7},{6,8},{7,9},{8,10},{9,11},{10,... | collective-permute-start | bytes 786440 | tf_op jit(solution)/shard_map/ppermute | solution.py:207
  44.4 6.4 %collective-permute-start.16 = (f32[2,8,4096]{2,1,0:T(8,128)S(1)}, f32[2,8,4096]{2,1,0:T(8,128)S(1)}, u32[]{:S(2)}, u32[]{:S(2)}) collective-permute-start(f32[2,8,4096]{2,1,0:T(8,128)S(1)} %get-tuple-element.68), channel_id=1, source_target_pairs={{2,0},{3,1},{4,2},{5,3},{6,4},{7,5},{8,6},{9,7},{10,8},{11,9},{12,... | collective-permute-start | bytes 786440 | tf_op jit(solution)/shard_map/ppermute | solution.py:207
  47.1 9.0 %collective-permute-start.17 = (f32[2,8,4096]{2,1,0:T(8,128)S(1)}, f32[2,8,4096]{2,1,0:T(8,128)S(1)}, u32[]{:S(2)}, u32[]{:S(2)}) collective-permute-start(f32[2,8,4096]{2,1,0:T(8,128)S(1)} %get-tuple-element.69), channel_id=1, source_target_pairs={{0,2},{1,3},{2,4},{3,5},{4,6},{5,7},{6,8},{7,9},{8,10},{9,11},{10,... | collective-permute-start | bytes 786440 | tf_op jit(solution)/shard_map/ppermute | solution.py:207
  47.1 9.0 %collective-permute-start.18 = (f32[2,8,4096]{2,1,0:T(8,128)S(1)}, f32[2,8,4096]{2,1,0:T(8,128)S(1)}, u32[]{:S(2)}, u32[]{:S(2)}) collective-permute-start(f32[2,8,4096]{2,1,0:T(8,128)S(1)} %get-tuple-element.70), channel_id=1, source_target_pairs={{2,0},{3,1},{4,2},{5,3},{6,4},{7,5},{8,6},{9,7},{10,8},{11,9},{12,... | collective-permute-start | bytes 786440 | tf_op jit(solution)/shard_map/ppermute | solution.py:207
  60.7 34.8 %copy-start.8 = (f32[256]{0:T(256)S(1)}, f32[256]{0:T(256)}, u32[]{:S(2)}) copy-start(f32[256]{0:T(256)} %param.18) | copy-start | bytes 3076
  60.7 34.9 %copy-start.5 = (bf16[256,172]{0,1:T(8,128)(2,1)S(1)}, bf16[256,172]{0,1:T(8,128)(2,1)}, u32[]{:S(2)}) copy-start(bf16[256,172]{0,1:T(8,128)(2,1)} %param.19) | copy-start | bytes 264196
  60.7 35.0 %copy-start.6 = (bf16[256,172]{0,1:T(8,128)(2,1)S(1)}, bf16[256,172]{0,1:T(8,128)(2,1)}, u32[]{:S(2)}) copy-start(bf16[256,172]{0,1:T(8,128)(2,1)} %param.20) | copy-start | bytes 264196
  60.7 35.1 %copy-start.9 = (s32[32]{0:T(128)S(1)}, s32[32]{0:T(128)}, u32[]{:S(2)}) copy-start(s32[32]{0:T(128)} %param.22) | copy-start | bytes 388
  60.7 35.2 %copy-start.7 = (s32[32,8]{0,1:T(8,128)S(1)}, s32[32,8]{0,1:T(8,128)}, u32[]{:S(2)}) copy-start(s32[32,8]{0,1:T(8,128)} %param.23) | copy-start | bytes 3076
  60.8 43.9 %copy-start.4 = (f32[172]{0:T(256)S(1)}, f32[172]{0:T(256)}, u32[]{:S(2)}) copy-start(f32[172]{0:T(256)} %param.21) | copy-start | bytes 2068
  84.3 20.3 %all-to-all-start.1 = ((f32[16,16,128]{2,1,0:T(8,128)}), f32[16,16,128]{2,1,0:T(8,128)S(1)}, u32[]{:S(2)}, u32[]{:S(2)}) async-start(f32[16,16,128]{2,1,0:T(8,128)} %bitcast.30), calls=%async_computation.1 | async-start | bytes 262144 | tf_op jit(solution)/shard_map/all_to_all | solution.py:263

commit v3 on v2

--- a/solution.py
+++ b/solution.py
@@ -13,9 +13,18 @@
 SMEM = pl.BlockSpec(memory_space=pltpu.SMEM)
 
 
-def project_kernel(where, layer_one, features, *outs):
+def project_kernel(where, layer_one, features, *refs):
+    outs, (held, landed) = refs[:6], refs[6:]
     chips, streams = 8, 2
     strip = outs[0].shape[1]
+    tiles, tile = held.shape[:2]
+    copies = [
+        pltpu.make_async_copy(features.at[pl.ds(i * tile, tile)], held.at[i], landed.at[i])
+        for i in range(tiles)
+    ]
+    for copy in copies:
+        copy.start()
+
     width = streams * strip
     hidden = layer_one.shape[1]
     row = lax.broadcasted_iota(jnp.int32, (hidden, hidden), 0)
@@ -32,11 +41,9 @@
         pick, layer_one[...], NT, preferred_element_type=jnp.float32
     ).astype(jnp.bfloat16)
 
-    tiles = 16
-    tile = features.shape[0] // tiles
     for i in range(tiles):
-        rows = features[i * tile : (i + 1) * tile]
-        product = lax.dot_general(ordered, rows, NT, preferred_element_type=jnp.float32)
+        copies[i].wait()
+        product = lax.dot_general(ordered, held[i], NT, preferred_element_type=jnp.float32)
         side, at = divmod(i, tiles // 2)
         take = 0
         for out in outs:
@@ -49,16 +56,21 @@
     rows, columns = features.shape
     hidden = layer_one.shape[1]
     strip = hidden // 32
+    tiles = 16
     shapes = [
         jax.ShapeDtypeStruct((4 * hops, strip, rows // 2), jnp.float32) for hops in (1, 2, 5)
     ] * 2
     return pl.pallas_call(
         project_kernel,
-        in_specs=[SMEM, VMEM, VMEM],
+        in_specs=[SMEM, VMEM, pl.BlockSpec(memory_space=pl.ANY)],
         out_specs=[VMEM] * 6,
         out_shape=shapes,
+        scratch_shapes=[
+            pltpu.VMEM((tiles, rows // tiles, columns), jnp.bfloat16),
+            pltpu.SemaphoreType.DMA((tiles,)),
+        ],
         name="project",
-        compiler_params=pltpu.CompilerParams(vmem_limit_bytes=8 * 2**20),
+        compiler_params=pltpu.CompilerParams(vmem_limit_bytes=44 * 2**20),
         cost_estimate=pl.CostEstimate(
             flops=2 * rows * columns * hidden,
             bytes_accessed=rows * columns * 2 + rows * hidden * 4,
@@ -67,7 +79,7 @@
     )(where, layer_one, features)
 
 
-def blocks_kernel(target, source, count, own, paired, up_a, down_a, up_b, down_b, adjacency, out, held):
+def blocks_kernel(lists, first, own, paired, up, down, adjacency, out, held):
     size = adjacency.shape[1]
     strip = own.shape[1]
     out[...] = jnp.zeros_like(out)
@@ -75,50 +87,48 @@
     for b in range(blocks):
         side, at = divmod(b, blocks // 2)
         at = slice(at * size, (at + 1) * size)
-        totals = [
-            (own[2 * k + side, :, at] + paired[2 * k + side, :, at])
-            + (up[side, :, at] + down[side, :, at])
-            for k, (up, down) in enumerate(((up_a, down_a), (up_b, down_b)))
-        ]
-        total = jnp.concatenate(totals, axis=0)
+        other = (own[side, :, at] + paired[side, :, at]) + (up[side, :, at] + down[side, :, at])
+        total = jnp.concatenate([first[side, :, at], other], axis=0)
         upper = total.astype(jnp.bfloat16)
         held[b, : 2 * strip] = upper
         held[b, 2 * strip :] = (total - upper.astype(jnp.float32)).astype(jnp.bfloat16)
 
+    slots = adjacency.shape[0]
+
     def product(s):
         value = lax.dot_general(
-            held[source[s]], adjacency[s], NT, preferred_element_type=jnp.float32
+            held[lists[1 + slots + s]], adjacency[s], NT, preferred_element_type=jnp.float32
         )
         return value[: 2 * strip] + value[2 * strip :]
 
     group = 16
-    live = count[0]
+    live = lists[0]
     full = live // group
 
     def whole(i, before):
         products = [product(i * group + k) for k in range(group)]
         for k in range(group):
-            out[target[(i - 1) * group + k]] += before[k]
+            out[lists[1 + (i - 1) * group + k]] += before[k]
         return products
 
     last = lax.fori_loop(1, full, whole, [product(k) for k in range(group)])
     for k in range(group):
-        out[target[(full - 1) * group + k]] += last[k]
+        out[lists[1 + (full - 1) * group + k]] += last[k]
 
     def single(s, carry):
-        out[target[s]] += product(s)
+        out[lists[1 + s]] += product(s)
         return carry
 
     lax.fori_loop(full * group, live, single, 0)
 
 
-def blocks(target, source, count, own, paired, streams, adjacency, target_blocks):
+def blocks(lists, first, own, paired, up, down, adjacency, target_blocks):
     slots, size, _ = adjacency.shape
-    parts, strip, half_rows = own.shape
-    width = parts // 2 * strip
+    _, strip, half_rows = own.shape
+    width = 2 * strip
     return pl.pallas_call(
         blocks_kernel,
-        in_specs=[SMEM] * 3 + [VMEM] * 7,
+        in_specs=[SMEM] + [VMEM] * 6,
         out_specs=VMEM,
         out_shape=jax.ShapeDtypeStruct((target_blocks, width, size), jnp.float32),
         scratch_shapes=[pltpu.VMEM((2 * half_rows // size, 2 * width, size), jnp.bfloat16)],
@@ -129,7 +139,7 @@
             bytes_accessed=slots * size * size * 2,
             transcendentals=0,
         ),
-    )(target, source, count, own, paired, *streams[0], *streams[1], adjacency)
+    )(lists, first, own, paired, up, down, adjacency)
 
 
 def second_kernel(where, sums, bias_one, self_weight, neigh_weight, bias_two, seeds, neighbors, out):
@@ -207,54 +217,48 @@
         return lax.ppermute(value, "feat", route)
 
     parts = project(where, layer_one, features)
-    opposite, three, rest = [send(part, pair) for part in parts[:3]]
-    opposite_own, three_own, rest_own = parts[3:]
+    tie = lax.optimization_barrier
+    opposite, *others = tie((send(parts[0], pair), *parts[1:3]))
+    opposite_own = parts[3]
     strip, half_rows = opposite.shape[1:]
 
-    tie = lax.optimization_barrier
+    zero = jnp.float32(0)
     opposite = (opposite_own + opposite).reshape(2, 2, strip, half_rows)
-    zero = jnp.float32(0)
-    streams = []
-    for k in range(2):
-        onward, back, opposite = tie((opposite[k, 0], opposite[k, 1], opposite))
-        streams.append((send(onward, up), send(back, down)))
-    three = three.reshape(2, 2, 2, strip, half_rows)
-    three_own = three_own.reshape(2, 2, 2, strip, half_rows)
-    for k, (onward, back) in enumerate(streams):
-        onward = lax.pad(onward[None], zero, ((0, 1, 0), (0, 0, 0), (0, 0, 0)))
-        back = lax.pad(back[None], zero, ((1, 0, 0), (0, 0, 0), (0, 0, 0)))
-        onward, back, three, three_own = tie(
-            (
-                three_own[0, k] + three[0, k] + onward,
-                three_own[1, k] + three[1, k] + back,
-                three,
-                three_own,
-            )
-        )
-        streams[k] = send(onward, up), send(back, down)
-    rest = rest.reshape(5, 2, 2, strip, half_rows)
-    rest_own = rest_own.reshape(5, 2, 2, strip, half_rows)
-    for hop in (0, 2):
-        for k, (onward, back) in enumerate(streams):
-            onward, back, rest, rest_own = tie(
-                (
-                    rest_own[hop, k] + rest[hop, k] + onward,
-                    rest_own[hop + 1, k] + rest[hop + 1, k] + back,
-                    rest,
-                    rest_own,
-                )
-            )
+    three, rest = [send(part, pair).reshape(-1, 2, 2, strip, half_rows) for part in others]
+    three_own, rest_own = [part.reshape(-1, 2, 2, strip, half_rows) for part in parts[4:]]
+    lists = jnp.concatenate([block_count, target_block, source_block])
+
+    streams = [None, None]
+    for step in range(5):
+        for k in range(2):
+            turn = step - k
+            if not 0 <= turn <= 3:
+                continue
+            if turn == 0:
+                opposite, lists = tie((opposite, lists))
+                onward, back = opposite[k, 0], opposite[k, 1]
+            else:
+                onward, back = streams[k]
+                if turn == 1:
+                    three, three_own, lists = tie((three, three_own, lists))
+                    onward = lax.pad(onward[None], zero, ((0, 1, 0), (0, 0, 0), (0, 0, 0)))
+                    back = lax.pad(back[None], zero, ((1, 0, 0), (0, 0, 0), (0, 0, 0)))
+                    onward = three_own[0, k] + three[0, k] + onward
+                    back = three_own[1, k] + three[1, k] + back
+                else:
+                    if step == 4:
+                        rest, rest_own, *streams[0] = tie((rest, rest_own, *streams[0]))
+                    rest, rest_own, lists = tie((rest, rest_own, lists))
+                    at = 2 * turn - 4
+                    onward = rest_own[at, k] + rest[at, k] + onward
+                    back = rest_own[at + 1, k] + rest[at + 1, k] + back
+            onward, back, lists = tie((onward, back, lists))
             streams[k] = send(onward, up), send(back, down)
 
+    onward, back = streams[0]
+    first = rest_own[4, 0] + rest[4, 0] + onward + back
     partial = blocks(
-        target_block,
-        source_block,
-        block_count,
-        rest_own[4].reshape(4, strip, half_rows),
-        rest[4].reshape(4, strip, half_rows),
-        streams,
-        adjacency,
-        target_blocks,
+        lists, first, rest_own[4, 1], rest[4, 1], *streams[1], adjacency, target_blocks
     )
 
     partial = partial.reshape(node_count, chips, width, size)

time: 106 us -> 112 us (1.057)
  starting transfers between devices: 35.9 us -> 41.2 us
  Pallas kernels: 8.23 us -> 10.8 us
  local copies, waits for them, and re-layouts: 4.43 us -> 2.19 us
    all_to_all x1, starting transfers between devices: 11.2 us -> 14.1 us  [on_device(): lax.all_to_all(doubled.reshape(feat_count, width, size), 'feat', 0, 0)]
    pallas_call x2, Pallas kernels: 6.66 us -> 9.21 us  [the longest x1 5.84 us: project(): pl.pallas_call(project_kernel, in_specs=[SMEM, VMEM, pl.BlockSpec(memory_...]
    ppermute x19, starting transfers between devices: 24.8 us -> 27.1 us  [send(): return lax.ppermute(value, 'feat', route)]
    unnamed x27 -> x25, local copies, waits for them, and re-layouts: 3.45 us -> 1.25 us
  transfers between devices with their start and end apart: 20 -> 20, of which waited for: 14 -> 11; matrix products, arithmetic and copies ran while one was open for 1% -> 1% of each run, Pallas kernels for 0% -> 0%
where the time goes in v3:
time: 112 us; the launch traced here: 111 us
  starting transfers between devices  41.2 us (37%)
  waiting for transfers between devices  33.7 us (30%)
  blocking collectives  21.7 us (19%)
  Pallas kernels  10.8 us (10%)
  local copies, waits for them, and re-layouts  2.19 us (2%)
    ppermute x19, starting transfers between devices, send(): return lax.ppermute(value, 'feat', route)  27.1 us
    ppermute x19, waiting for transfers between devices, send(): return lax.ppermute(value, 'feat', route)  25.1 us
    all_to_all x1, blocking collectives, on_device(): summed = jnp.sum(lax.all_to_all(partial, 'node', 0, 0), axis=0)  21.7 us
    all_to_all x1, starting transfers between devices, on_device(): lax.all_to_all(doubled.reshape(feat_count, width, size), 'feat', 0, 0)  14.1 us
    all_to_all x1, waiting for transfers between devices, on_device(): lax.all_to_all(doubled.reshape(feat_count, width, size), 'feat', 0, 0)  8.61 us
    pallas_call x1, Pallas kernels, project(): pl.pallas_call(project_kernel, in_specs=[SMEM, VMEM, pl.BlockSpec(memory_...  5.84 us
    pallas_call x1, Pallas kernels, blocks(): pl.pallas_call(blocks_kernel, in_specs=[SMEM] + [VMEM] * 6, out_specs=VME...  3.37 us
  transfers between devices with their start and end apart: 20, of which 11 were waited for; matrix products, arithmetic and copies ran while one was open for 1% of the time, Pallas kernels for 0%

profile of v3, /device:TPU:1, one launch (start us, length us, event | category | flops | bytes accessed | tf_op | source)
XLA Modules:
  0.0 111.3 jit_solution(167446107911271400)
XLA Ops:
  0.1 0.9 copy-done
  1.0 5.8 %project.1 = (f32[4,8,4096]{2,1,0:T(8,128)S(1)}, f32[8,8,4096]{2,1,0:T(8,128)S(1)}, f32[20,8,4096]{2,1,0:T(8,128)S(1)}, f32[4,8,4096]{2,1,0:T(8,128)S(1)}, f32[8...) custom-call(s32[2]{0:T(128)S(1)} %pad_add_fusion.1.where, bf16[256,256]{1,0:T(8,128)(2,1)S(1)} %copy-done, ...), custom_call_target="tpu_custom_call" | custom-call | flops 1073741824 | bytes 12582912 | tf_op jit(solution)/shard_map/project/pallas_call | solution.py:63
  6.8 3.3 %collective-permute-start = (f32[4,8,4096]{2,1,0:T(8,128)S(1)}, f32[4,8,4096]{2,1,0:T(8,128)S(1)}, u32[]{:S(2)}, u32[]{:S(2)}) collective-permute-start(f32[4,8,4096]{2,1,0:T(8,128)S(1)} %get-tuple-element.64), channel_id=1, source_target_pairs={{0,1},{1,0},{2,3},{3,2},{4,5},{5,4},{6,7},{7,6},{8,9},{9,8},{10,11... | collective-permute-start | bytes 1572872 | tf_op jit(solution)/shard_map/ppermute | solution.py:217
  10.8 0.9 collective-permute-done
  11.7 0.4 collective-permute-start.2
  12.6 3.9 %collective-permute-start.4 = (f32[8,4096]{1,0:T(8,128)S(1)}, f32[8,4096]{1,0:T(8,128)S(1)}, u32[]{:S(2)}, u32[]{:S(2)}) collective-permute-start(f32[8,4096]{1,0:T(8,128)S(1)} %get-tuple-element.79), channel_id=1, source_target_pairs={{2,0},{3,1},{4,2},{5,3},{6,4},{7,5},{8,6},{9,7},{10,8},{11,9},{12,... | collective-permute-start | bytes 393224 | tf_op jit(solution)/shard_map/ppermute | solution.py:217
  16.5 3.5 %collective-permute-done.3 = f32[8,4096]{1,0:T(8,128)S(1)} collective-permute-done((f32[8,4096]{1,0:T(8,128)S(1)}, f32[8,4096]{1,0:T(8,128)S(1)}, u32[]{:S(2)}, u32[]{:S(2)}) %collective-permute-start.3) | collective-permute-done | bytes 131104 | tf_op jit(solution)/shard_map/ppermute | solution.py:217
  20.1 2.7 %collective-permute-start.6 = (f32[2,8,4096]{2,1,0:T(8,128)S(1)}, f32[2,8,4096]{2,1,0:T(8,128)S(1)}, u32[]{:S(2)}, u32[]{:S(2)}) collective-permute-start(f32[2,8,4096]{2,1,0:T(8,128)S(1)} %get-tuple-element.88), channel_id=1, source_target_pairs={{2,0},{3,1},{4,2},{5,3},{6,4},{7,5},{8,6},{9,7},{10,8},{11,9},{12,... | collective-permute-start | bytes 786440 | tf_op jit(solution)/shard_map/ppermute | solution.py:217
  22.9 2.7 %collective-permute-start.8 = (f32[8,4096]{1,0:T(8,128)S(1)}, f32[8,4096]{1,0:T(8,128)S(1)}, u32[]{:S(2)}, u32[]{:S(2)}) collective-permute-start(f32[8,4096]{1,0:T(8,128)S(1)} %get-tuple-element.94), channel_id=1, source_target_pairs={{2,0},{3,1},{4,2},{5,3},{6,4},{7,5},{8,6},{9,7},{10,8},{11,9},{12,... | collective-permute-start | bytes 393224 | tf_op jit(solution)/shard_map/ppermute | solution.py:217
  25.6 2.7 %collective-permute-done.5 = f32[2,8,4096]{2,1,0:T(8,128)S(1)} collective-permute-done((f32[2,8,4096]{2,1,0:T(8,128)S(1)}, f32[2,8,4096]{2,1,0:T(8,128)S(1)}, u32[]{:S(2)}, u32[]{:S(2)}) %collective-permute-start.5) | collective-permute-done | bytes 262176 | tf_op jit(solution)/shard_map/ppermute | solution.py:217
  28.4 2.4 %collective-permute-start.10 = (f32[2,8,4096]{2,1,0:T(8,128)S(1)}, f32[2,8,4096]{2,1,0:T(8,128)S(1)}, u32[]{:S(2)}, u32[]{:S(2)}) collective-permute-start(f32[2,8,4096]{2,1,0:T(8,128)S(1)} %get-tuple-element.100), channel_id=1, source_target_pairs={{2,0},{3,1},{4,2},{5,3},{6,4},{7,5},{8,6},{9,7},{10,8},{11,9},{12,... | collective-permute-start | bytes 786440 | tf_op jit(solution)/shard_map/ppermute | solution.py:217
  30.8 0.3 collective-permute-done.7
  31.2 1.0 collective-permute-start.13
  32.1 1.8 %collective-permute-start.14 = (f32[2,8,4096]{2,1,0:T(8,128)S(1)}, f32[2,8,4096]{2,1,0:T(8,128)S(1)}, u32[]{:S(2)}, u32[]{:S(2)}) collective-permute-start(f32[2,8,4096]{2,1,0:T(8,128)S(1)} %get-tuple-element.110), channel_id=1, source_target_pairs={{2,0},{3,1},{4,2},{5,3},{6,4},{7,5},{8,6},{9,7},{10,8},{11,9},{12,... | collective-permute-start | bytes 786440 | tf_op jit(solution)/shard_map/ppermute | solution.py:217
  33.9 0.6 collective-permute-done.10
  34.5 2.7 %collective-permute-done.9 = f32[2,8,4096]{2,1,0:T(8,128)S(1)} collective-permute-done((f32[2,8,4096]{2,1,0:T(8,128)S(1)}, f32[2,8,4096]{2,1,0:T(8,128)S(1)}, u32[]{:S(2)}, u32[]{:S(2)}) %collective-permute-start.9) | collective-permute-done | bytes 262176 | tf_op jit(solution)/shard_map/ppermute | solution.py:217
  37.3 0.3 collective-permute-start.11
  37.6 2.7 %collective-permute-start.12 = (f32[2,8,4096]{2,1,0:T(8,128)S(1)}, f32[2,8,4096]{2,1,0:T(8,128)S(1)}, u32[]{:S(2)}, u32[]{:S(2)}) collective-permute-start(f32[2,8,4096]{2,1,0:T(8,128)S(1)} %get-tuple-element.106), channel_id=1, source_target_pairs={{2,0},{3,1},{4,2},{5,3},{6,4},{7,5},{8,6},{9,7},{10,8},{11,9},{12,... | collective-permute-start | bytes 786440 | tf_op jit(solution)/shard_map/ppermute | solution.py:217
  40.3 1.4 %collective-permute-done.13 = f32[2,8,4096]{2,1,0:T(8,128)S(1)} collective-permute-done((f32[2,8,4096]{2,1,0:T(8,128)S(1)}, f32[2,8,4096]{2,1,0:T(8,128)S(1)}, u32[]{:S(2)}, u32[]{:S(2)}) %collective-permute-start.13) | collective-permute-done | bytes 262176 | tf_op jit(solution)/shard_map/ppermute | solution.py:217
  41.8 0.7 collective-permute-start.15
  42.5 2.0 %collective-permute-start.16 = (f32[2,8,4096]{2,1,0:T(8,128)S(1)}, f32[2,8,4096]{2,1,0:T(8,128)S(1)}, u32[]{:S(2)}, u32[]{:S(2)}) collective-permute-start(f32[2,8,4096]{2,1,0:T(8,128)S(1)} %get-tuple-element.116), channel_id=1, source_target_pairs={{2,0},{3,1},{4,2},{5,3},{6,4},{7,5},{8,6},{9,7},{10,8},{11,9},{12,... | collective-permute-start | bytes 786440 | tf_op jit(solution)/shard_map/ppermute | solution.py:217
  44.5 2.7 %collective-permute-done.11 = f32[2,8,4096]{2,1,0:T(8,128)S(1)} collective-permute-done((f32[2,8,4096]{2,1,0:T(8,128)S(1)}, f32[2,8,4096]{2,1,0:T(8,128)S(1)}, u32[]{:S(2)}, u32[]{:S(2)}) %collective-permute-start.11) | collective-permute-done | bytes 262176 | tf_op jit(solution)/shard_map/ppermute | solution.py:217
  47.3 5.6 %collective-permute-done.15 = f32[2,8,4096]{2,1,0:T(8,128)S(1)} collective-permute-done((f32[2,8,4096]{2,1,0:T(8,128)S(1)}, f32[2,8,4096]{2,1,0:T(8,128)S(1)}, u32[]{:S(2)}, u32[]{:S(2)}) %collective-permute-start.15) | collective-permute-done | bytes 262176 | tf_op jit(solution)/shard_map/ppermute | solution.py:217
  53.1 0.7 collective-permute-start.17
  53.8 2.0 %collective-permute-start.18 = (f32[2,8,4096]{2,1,0:T(8,128)S(1)}, f32[2,8,4096]{2,1,0:T(8,128)S(1)}, u32[]{:S(2)}, u32[]{:S(2)}) collective-permute-start(f32[2,8,4096]{2,1,0:T(8,128)S(1)} %get-tuple-element.122), channel_id=1, source_target_pairs={{2,0},{3,1},{4,2},{5,3},{6,4},{7,5},{8,6},{9,7},{10,8},{11,9},{12,... | collective-permute-start | bytes 786440 | tf_op jit(solution)/shard_map/ppermute | solution.py:217
  55.9 4.7 %collective-permute-done.17.up = f32[2,8,4096]{2,1,0:T(8,128)S(1)} collective-permute-done((f32[2,8,4096]{2,1,0:T(8,128)S(1)}, f32[2,8,4096]{2,1,0:T(8,128)S(1)}, u32[]{:S(2)}, u32[]{:S(2)}) %collective-permute-start.17) | collective-permute-done | bytes 262176 | tf_op jit(solution)/shard_map/ppermute | solution.py:217
  60.6 3.4 %blocks.1 = f32[128,16,128]{2,1,0:T(8,128)S(1)} custom-call(s32[513]{0:T(1024)S(1)} %pad_add_fusion.lists, f32[2,8,4096]{2,1,0:T(8,128)S(1)} %get-tuple-element.123.first, f32[2,8,4096]{2,1,0:T(8,128)S(1)} %get-tuple-element.141.own, f32[2,8,4096]{2,1,0:T(8,128)S(1)} %get-tuple-element.140.paired, f32[2,8,4096]{2,1,0:T(8,128)S(1)} %collective-permute-done.17.up, ...), custom_call_target="tpu_custom_call" | custom-call | flops 134217728 | bytes 8388608 | tf_op jit(solution)/shard_map/blocks/pallas_call | solution.py:129
  64.0 21.7 %all_to_all.10 = f32[16,8,16,128]{3,2,1,0:T(8,128)S(1)} all-to-all(f32[16,8,16,128]{3,2,1,0:T(8,128)S(1)} %bitcast.59), channel_id=1, replica_groups=mesh['node'=16,'feat'=16] {'node'}, dimensions={0} | all-to-all | bytes 2097152 | tf_op jit(solution)/shard_map/all_to_all | solution.py:265
  85.8 0.7 broadcast_in_dim.31
  86.4 14.1 %all-to-all-start.1 = ((f32[16,16,128]{2,1,0:T(8,128)}), f32[16,16,128]{2,1,0:T(8,128)S(1)}, u32[]{:S(2)}, u32[]{:S(2)}) async-start(f32[16,16,128]{2,1,0:T(8,128)} %bitcast.31), calls=%async_computation.1 | async-start | bytes 262144 | tf_op jit(solution)/shard_map/all_to_all | solution.py:267
  101.1 8.6 %all-to-all-done.1 = f32[16,16,128]{2,1,0:T(8,128)S(1)} async-done(((f32[16,16,128]{2,1,0:T(8,128)}), f32[16,16,128]{2,1,0:T(8,128)S(1)}, u32[]{:S(2)}, u32[]{:S(2)}) %all-to-all-start.1) | async-done | bytes 131104 | tf_op jit(solution)/shard_map/all_to_all | solution.py:267
  109.7 1.6 %second.1 = f32[32,172]{1,0:T(8,128)} custom-call(s32[2]{0:T(128)S(1)} %pad_add_fusion.1.where, f32[256,128]{1,0:T(8,128)S(1)} %bitcast.67, f32[256,1]{1,0:T(8,128)S(1)} %copy.17.bias_one, bf16[256,172]{1,0:T(8,128)(2,1)S(1)} %copy.18.self_weight, bf16[256,172]{1,0:T(8,128)(2,1)S(1)} %copy.19.neigh_weight, f32[1,172]{1,0:T(1,128)S(1)} %bitcast.68, ...), custom_call_target="tpu_custom_call" | custom-call | tf_op jit(solution)/shard_map/second/pallas_call | solution.py:169
  (54 shorter events, 2.1 us)
Async XLA Ops:
  0.0 12.1 %copy-start.7 = (s32[256]{0:T(256)S(1)}, s32[256]{0:T(256)}, u32[]{:S(2)}) copy-start(s32[256]{0:T(256)} %param.14) | copy-start | bytes 3076
  0.0 12.1 %copy-start.6 = (s32[256]{0:T(256)S(1)}, s32[256]{0:T(256)}, u32[]{:S(2)}) copy-start(s32[256]{0:T(256)} %param.15) | copy-start | bytes 3076
  0.1 0.9 copy-start
  6.8 4.9 %collective-permute-start = (f32[4,8,4096]{2,1,0:T(8,128)S(1)}, f32[4,8,4096]{2,1,0:T(8,128)S(1)}, u32[]{:S(2)}, u32[]{:S(2)}) collective-permute-start(f32[4,8,4096]{2,1,0:T(8,128)S(1)} %get-tuple-element.64), channel_id=1, source_target_pairs={{0,1},{1,0},{2,3},{3,2},{4,5},{5,4},{6,7},{7,6},{8,9},{9,8},{10,11... | collective-permute-start | bytes 1572872 | tf_op jit(solution)/shard_map/ppermute | solution.py:217
  11.7 4.8 %collective-permute-start.2 = (f32[8,8,4096]{2,1,0:T(8,128)S(1)}, f32[8,8,4096]{2,1,0:T(8,128)S(1)}, u32[]{:S(2)}, u32[]{:S(2)}) collective-permute-start(f32[8,8,4096]{2,1,0:T(8,128)S(1)} %get-tuple-element.72), channel_id=1, source_target_pairs={{0,1},{1,0},{2,3},{3,2},{4,5},{5,4},{6,7},{7,6},{8,9},{9,8},{10,11... | collective-permute-start | bytes 3145736 | tf_op jit(solution)/shard_map/ppermute | solution.py:217
  12.2 13.4 %collective-permute-start.1 = (f32[20,8,4096]{2,1,0:T(8,128)S(1)}, f32[20,8,4096]{2,1,0:T(8,128)S(1)}, u32[]{:S(2)}, u32[]{:S(2)}) collective-permute-start(f32[20,8,4096]{2,1,0:T(8,128)S(1)} %get-tuple-element.67), channel_id=1, source_target_pairs={{0,1},{1,0},{2,3},{3,2},{4,5},{5,4},{6,7},{7,6},{8,9},{9,8},{10,11... | collective-permute-start | bytes 7864328 | tf_op jit(solution)/shard_map/ppermute | solution.py:217
  12.4 48.1 %slice-start = ((s8[8388608]{0:T(1024)(128)(4,1)}), s8[4194304]{0:T(1024)(128)(4,1)S(1)}, s32[]{:S(2)}) async-start(s8[8388608]{0:T(1024)(128)(4,1)} %bitcast.57), calls=%async_computation.2 | async-start | bytes 8388608
  12.5 7.5 %collective-permute-start.3 = (f32[8,4096]{1,0:T(8,128)S(1)}, f32[8,4096]{1,0:T(8,128)S(1)}, u32[]{:S(2)}, u32[]{:S(2)}) collective-permute-start(f32[8,4096]{1,0:T(8,128)S(1)} %get-tuple-element.78), channel_id=1, source_target_pairs={{0,2},{1,3},{2,4},{3,5},{4,6},{5,7},{6,8},{7,9},{8,10},{9,11},{10,... | collective-permute-start | bytes 393224 | tf_op jit(solution)/shard_map/ppermute | solution.py:217
  12.6 7.4 %collective-permute-start.4 = (f32[8,4096]{1,0:T(8,128)S(1)}, f32[8,4096]{1,0:T(8,128)S(1)}, u32[]{:S(2)}, u32[]{:S(2)}) collective-permute-start(f32[8,4096]{1,0:T(8,128)S(1)} %get-tuple-element.79), channel_id=1, source_target_pairs={{2,0},{3,1},{4,2},{5,3},{6,4},{7,5},{8,6},{9,7},{10,8},{11,9},{12,... | collective-permute-start | bytes 393224 | tf_op jit(solution)/shard_map/ppermute | solution.py:217
  20.0 8.2 %collective-permute-start.5 = (f32[2,8,4096]{2,1,0:T(8,128)S(1)}, f32[2,8,4096]{2,1,0:T(8,128)S(1)}, u32[]{:S(2)}, u32[]{:S(2)}) collective-permute-start(f32[2,8,4096]{2,1,0:T(8,128)S(1)} %get-tuple-element.87), channel_id=1, source_target_pairs={{0,2},{1,3},{2,4},{3,5},{4,6},{5,7},{6,8},{7,9},{8,10},{9,11},{10,... | collective-permute-start | bytes 786440 | tf_op jit(solution)/shard_map/ppermute | solution.py:217
  20.1 8.1 %collective-permute-start.6 = (f32[2,8,4096]{2,1,0:T(8,128)S(1)}, f32[2,8,4096]{2,1,0:T(8,128)S(1)}, u32[]{:S(2)}, u32[]{:S(2)}) collective-permute-start(f32[2,8,4096]{2,1,0:T(8,128)S(1)} %get-tuple-element.88), channel_id=1, source_target_pairs={{2,0},{3,1},{4,2},{5,3},{6,4},{7,5},{8,6},{9,7},{10,8},{11,9},{12,... | collective-permute-start | bytes 786440 | tf_op jit(solution)/shard_map/ppermute | solution.py:217
  22.8 8.3 %collective-permute-start.7 = (f32[8,4096]{1,0:T(8,128)S(1)}, f32[8,4096]{1,0:T(8,128)S(1)}, u32[]{:S(2)}, u32[]{:S(2)}) collective-permute-start(f32[8,4096]{1,0:T(8,128)S(1)} %get-tuple-element.93), channel_id=1, source_target_pairs={{0,2},{1,3},{2,4},{3,5},{4,6},{5,7},{6,8},{7,9},{8,10},{9,11},{10,... | collective-permute-start | bytes 393224 | tf_op jit(solution)/shard_map/ppermute | solution.py:217
  22.9 8.2 %collective-permute-start.8 = (f32[8,4096]{1,0:T(8,128)S(1)}, f32[8,4096]{1,0:T(8,128)S(1)}, u32[]{:S(2)}, u32[]{:S(2)}) collective-permute-start(f32[8,4096]{1,0:T(8,128)S(1)} %get-tuple-element.94), channel_id=1, source_target_pairs={{2,0},{3,1},{4,2},{5,3},{6,4},{7,5},{8,6},{9,7},{10,8},{11,9},{12,... | collective-permute-start | bytes 393224 | tf_op jit(solution)/shard_map/ppermute | solution.py:217
  28.4 6.2 %collective-permute-start.10 = (f32[2,8,4096]{2,1,0:T(8,128)S(1)}, f32[2,8,4096]{2,1,0:T(8,128)S(1)}, u32[]{:S(2)}, u32[]{:S(2)}) collective-permute-start(f32[2,8,4096]{2,1,0:T(8,128)S(1)} %get-tuple-element.100), channel_id=1, source_target_pairs={{2,0},{3,1},{4,2},{5,3},{6,4},{7,5},{8,6},{9,7},{10,8},{11,9},{12,... | collective-permute-start | bytes 786440 | tf_op jit(solution)/shard_map/ppermute | solution.py:217
  30.8 6.4 %collective-permute-start.9 = (f32[2,8,4096]{2,1,0:T(8,128)S(1)}, f32[2,8,4096]{2,1,0:T(8,128)S(1)}, u32[]{:S(2)}, u32[]{:S(2)}) collective-permute-start(f32[2,8,4096]{2,1,0:T(8,128)S(1)} %get-tuple-element.99), channel_id=1, source_target_pairs={{0,2},{1,3},{2,4},{3,5},{4,6},{5,7},{6,8},{7,9},{8,10},{9,11},{10,... | collective-permute-start | bytes 786440 | tf_op jit(solution)/shard_map/ppermute | solution.py:217
  31.2 29.4 %slice-start.1 = ((s8[8388608]{0:T(1024)(128)(4,1)}), s8[4194304]{0:T(1024)(128)(4,1)S(1)}, s32[]{:S(2)}) async-start(s8[8388608]{0:T(1024)(128)(4,1)} %bitcast.57), calls=%async_computation.3 | async-start | bytes 8388608
  31.2 10.5 %collective-permute-start.13 = (f32[2,8,4096]{2,1,0:T(8,128)S(1)}, f32[2,8,4096]{2,1,0:T(8,128)S(1)}, u32[]{:S(2)}, u32[]{:S(2)}) collective-permute-start(f32[2,8,4096]{2,1,0:T(8,128)S(1)} %get-tuple-element.109), channel_id=1, source_target_pairs={{0,2},{1,3},{2,4},{3,5},{4,6},{5,7},{6,8},{7,9},{8,10},{9,11},{10,... | collective-permute-start | bytes 786440 | tf_op jit(solution)/shard_map/ppermute | solution.py:217
  32.1 9.5 %collective-permute-start.14 = (f32[2,8,4096]{2,1,0:T(8,128)S(1)}, f32[2,8,4096]{2,1,0:T(8,128)S(1)}, u32[]{:S(2)}, u32[]{:S(2)}) collective-permute-start(f32[2,8,4096]{2,1,0:T(8,128)S(1)} %get-tuple-element.110), channel_id=1, source_target_pairs={{2,0},{3,1},{4,2},{5,3},{6,4},{7,5},{8,6},{9,7},{10,8},{11,9},{12,... | collective-permute-start | bytes 786440 | tf_op jit(solution)/shard_map/ppermute | solution.py:217
  37.3 9.9 %collective-permute-start.11 = (f32[2,8,4096]{2,1,0:T(8,128)S(1)}, f32[2,8,4096]{2,1,0:T(8,128)S(1)}, u32[]{:S(2)}, u32[]{:S(2)}) collective-permute-start(f32[2,8,4096]{2,1,0:T(8,128)S(1)} %get-tuple-element.105), channel_id=1, source_target_pairs={{0,2},{1,3},{2,4},{3,5},{4,6},{5,7},{6,8},{7,9},{8,10},{9,11},{10,... | collective-permute-start | bytes 786440 | tf_op jit(solution)/shard_map/ppermute | solution.py:217
  37.6 9.7 %collective-permute-start.12 = (f32[2,8,4096]{2,1,0:T(8,128)S(1)}, f32[2,8,4096]{2,1,0:T(8,128)S(1)}, u32[]{:S(2)}, u32[]{:S(2)}) collective-permute-start(f32[2,8,4096]{2,1,0:T(8,128)S(1)} %get-tuple-element.106), channel_id=1, source_target_pairs={{2,0},{3,1},{4,2},{5,3},{6,4},{7,5},{8,6},{9,7},{10,8},{11,9},{12,... | collective-permute-start | bytes 786440 | tf_op jit(solution)/shard_map/ppermute | solution.py:217
  41.8 11.1 %collective-permute-start.15 = (f32[2,8,4096]{2,1,0:T(8,128)S(1)}, f32[2,8,4096]{2,1,0:T(8,128)S(1)}, u32[]{:S(2)}, u32[]{:S(2)}) collective-permute-start(f32[2,8,4096]{2,1,0:T(8,128)S(1)} %get-tuple-element.115), channel_id=1, source_target_pairs={{0,2},{1,3},{2,4},{3,5},{4,6},{5,7},{6,8},{7,9},{8,10},{9,11},{10,... | collective-permute-start | bytes 786440 | tf_op jit(solution)/shard_map/ppermute | solution.py:217
  42.5 10.4 %collective-permute-start.16 = (f32[2,8,4096]{2,1,0:T(8,128)S(1)}, f32[2,8,4096]{2,1,0:T(8,128)S(1)}, u32[]{:S(2)}, u32[]{:S(2)}) collective-permute-start(f32[2,8,4096]{2,1,0:T(8,128)S(1)} %get-tuple-element.116), channel_id=1, source_target_pairs={{2,0},{3,1},{4,2},{5,3},{6,4},{7,5},{8,6},{9,7},{10,8},{11,9},{12,... | collective-permute-start | bytes 786440 | tf_op jit(solution)/shard_map/ppermute | solution.py:217
  53.1 7.4 %collective-permute-start.17 = (f32[2,8,4096]{2,1,0:T(8,128)S(1)}, f32[2,8,4096]{2,1,0:T(8,128)S(1)}, u32[]{:S(2)}, u32[]{:S(2)}) collective-permute-start(f32[2,8,4096]{2,1,0:T(8,128)S(1)} %get-tuple-element.121), channel_id=1, source_target_pairs={{0,2},{1,3},{2,4},{3,5},{4,6},{5,7},{6,8},{7,9},{8,10},{9,11},{10,... | collective-permute-start | bytes 786440 | tf_op jit(solution)/shard_map/ppermute | solution.py:217
  53.8 6.7 %collective-permute-start.18 = (f32[2,8,4096]{2,1,0:T(8,128)S(1)}, f32[2,8,4096]{2,1,0:T(8,128)S(1)}, u32[]{:S(2)}, u32[]{:S(2)}) collective-permute-start(f32[2,8,4096]{2,1,0:T(8,128)S(1)} %get-tuple-element.122), channel_id=1, source_target_pairs={{2,0},{3,1},{4,2},{5,3},{6,4},{7,5},{8,6},{9,7},{10,8},{11,9},{12,... | collective-permute-start | bytes 786440 | tf_op jit(solution)/shard_map/ppermute | solution.py:217
  63.9 36.6 %copy-start.5 = (f32[256]{0:T(256)S(1)}, f32[256]{0:T(256)}, u32[]{:S(2)}) copy-start(f32[256]{0:T(256)} %param.18) | copy-start | bytes 3076
  63.9 36.8 %copy-start.2 = (bf16[256,172]{0,1:T(8,128)(2,1)S(1)}, bf16[256,172]{0,1:T(8,128)(2,1)}, u32[]{:S(2)}) copy-start(bf16[256,172]{0,1:T(8,128)(2,1)} %param.19) | copy-start | bytes 264196
  63.9 36.9 %copy-start.3 = (bf16[256,172]{0,1:T(8,128)(2,1)S(1)}, bf16[256,172]{0,1:T(8,128)(2,1)}, u32[]{:S(2)}) copy-start(bf16[256,172]{0,1:T(8,128)(2,1)} %param.20) | copy-start | bytes 264196
  64.0 37.0 %copy-start.8 = (s32[32]{0:T(128)S(1)}, s32[32]{0:T(128)}, u32[]{:S(2)}) copy-start(s32[32]{0:T(128)} %param.22) | copy-start | bytes 388
  64.0 37.0 %copy-start.4 = (s32[32,8]{0,1:T(8,128)S(1)}, s32[32,8]{0,1:T(8,128)}, u32[]{:S(2)}) copy-start(s32[32,8]{0,1:T(8,128)} %param.23) | copy-start | bytes 3076
  64.0 45.7 %copy-start.1 = (f32[172]{0:T(256)S(1)}, f32[172]{0:T(256)}, u32[]{:S(2)}) copy-start(f32[172]{0:T(256)} %param.21) | copy-start | bytes 2068
  86.4 23.3 %all-to-all-start.1 = ((f32[16,16,128]{2,1,0:T(8,128)}), f32[16,16,128]{2,1,0:T(8,128)S(1)}, u32[]{:S(2)}, u32[]{:S(2)}) async-start(f32[16,16,128]{2,1,0:T(8,128)} %bitcast.31), calls=%async_computation.1 | async-start | bytes 262144 | tf_op jit(solution)/shard_map/all_to_all | solution.py:267

commit v4 on v0

v4 whole, which is shorter than its diff:
```python
import jax
import jax.numpy as jnp
from jax import lax
from jax.experimental import pallas as pl
from jax.experimental.pallas import tpu as pltpu
from jax.sharding import PartitionSpec as P

T_DEV = 64
CHIPS = 8
TILE = 8
RUNS = 8
SPANS = ((0, 10), (10, 16))
NT = (((1,), (1,)), ((), ()))
VMEM = pl.BlockSpec(memory_space=pltpu.VMEM)

UNITS = 2 * RUNS


def project_kernel(ordered, features, *outs):
    lanes = outs[0].shape[2]
    tile = min(512, lanes)
    for i in range(features.shape[0] // tile):
        rows = features[i * tile : (i + 1) * tile]
        product = lax.dot_general(ordered[...], rows, NT, preferred_element_type=jnp.float32)
        run, at = divmod(i * tile, lanes)
        take = 0
        for out in outs:
            for k in range(out.shape[0] // RUNS):
                out[k * RUNS + run, :, at : at + tile] = product[take : take + TILE]
                take += TILE


def project(ordered, features):
    rows, columns = features.shape
    hidden = ordered.shape[0]
    shapes = [
        jax.ShapeDtypeStruct((strips * UNITS, TILE, rows // RUNS), jnp.float32)
        for strips in (1, CHIPS - 1)
    ] * 2
    return pl.pallas_call(
        project_kernel,
        in_specs=[VMEM] * 2,
        out_specs=[VMEM] * 4,
        out_shape=shapes,
        name="project",
        compiler_params=pltpu.CompilerParams(vmem_limit_bytes=8 * 2**20),
        cost_estimate=pl.CostEstimate(
            flops=2 * rows * columns * hidden,
            bytes_accessed=rows * columns * 2 + rows * hidden * 4,
            transcendentals=0,
        ),
    )(ordered, features)


def in_hop_order(layer_one):
    hidden = layer_one.shape[1]
    feat = lax.axis_index("feat")
    row = jnp.arange(hidden, dtype=jnp.int32)
    place = row % (hidden // 2) // (2 * TILE)
    hop = (place + 1) // 2
    hop = CHIPS // 2 + jnp.where(place % 2 == 1, -hop, hop)
    chip = ((feat >> 1) + hop) % CHIPS
    core = ((feat & 1) + (row < hidden // 2)) % 2
    wanted = (chip * 2 + core) * (2 * TILE) + row % (2 * TILE)
    pick = (jnp.arange(hidden, dtype=jnp.int32)[None, :] == wanted[:, None]).astype(jnp.bfloat16)
    return lax.dot_general(pick, layer_one, NT, preferred_element_type=jnp.float32).astype(
        jnp.bfloat16
    )


def blocks_kernel(
    lists, own, paired, up_a, down_a, up_b, down_b, adjacency, out, held, table, landed
):
    copy = pltpu.make_async_copy(lists, table, landed)
    copy.start()
    slots, size, _ = adjacency.shape
    lanes = own.shape[2]
    out[...] = jnp.zeros_like(out)
    for b in range(held.shape[0]):
        run, at = divmod(b * size, lanes)
        at = slice(at, at + size)
        totals = []
        for unit in (run, RUNS + run):
            ups, downs, begin = (up_a, down_a, 0) if unit < SPANS[0][1] else (up_b, down_b, SPANS[1][0])
            totals.append(
                (own[unit, :, at] + paired[unit, :, at])
                + (ups[unit - begin, :, at] + downs[unit - begin, :, at])
            )
        total = jnp.concatenate(totals, axis=0)
        upper = total.astype(jnp.bfloat16)
        held[b, : 2 * TILE] = upper
        held[b, 2 * TILE :] = (total - upper.astype(jnp.float32)).astype(jnp.bfloat16)
    copy.wait()

    def product(s):
        value = lax.dot_general(
            held[table[slots + s]], adjacency[s], NT, preferred_element_type=jnp.float32
        )
        return value[: 2 * TILE] + value[2 * TILE :]

    def add(s, value):
        block = table[s]
        place = 2 * block - block % CHIPS
        out[place] += value[:TILE]
        out[place + CHIPS] += value[TILE:]

    group = 16
    live = table[2 * slots]
    full = live // group

    def whole(i, before):
        products = [product(i * group + k) for k in range(group)]
        for k in range(group):
            add((i - 1) * group + k, before[k])
        return products

    last = lax.fori_loop(1, full, whole, [product(k) for k in range(group)])
    for k in range(group):
        add((full - 1) * group + k, last[k])

    def single(s, carry):
        add(s, product(s))
        return carry

    lax.fori_loop(full * group, live, single, 0)


def blocks(lists, own, paired, streams, adjacency, target_blocks):
    slots, size, _ = adjacency.shape
    rows = RUNS * own.shape[2]
    return pl.pallas_call(
        blocks_kernel,
        in_specs=[pl.BlockSpec(memory_space=pl.ANY)] + [VMEM] * 7,
        out_specs=VMEM,
        out_shape=jax.ShapeDtypeStruct((2 * target_blocks, TILE, size), jnp.float32),
        scratch_shapes=[
            pltpu.VMEM((rows // size, 4 * TILE, size), jnp.bfloat16),
            pltpu.SMEM(lists.shape, jnp.int32),
            pltpu.SemaphoreType.DMA,
        ],
        name="blocks",
        compiler_params=pltpu.CompilerParams(vmem_limit_bytes=8 * 2**20),
        cost_estimate=pl.CostEstimate(
            flops=4 * slots * size * size * UNITS,
            bytes_accessed=slots * size * size * 2,
            transcendentals=0,
        ),
    )(lists, own, paired, *streams[0], *streams[1], adjacency)


def combine_kernel(parts, out):
    size = parts.shape[3]
    low = lax.broadcasted_iota(jnp.int32, (TILE, size), 1) < T_DEV
    for chip in range(CHIPS):
        left, right = parts[0, chip], parts[0, CHIPS + chip]
        for n in range(1, parts.shape[0]):
            left += parts[n, chip]
            right += parts[n, CHIPS + chip]
        out[2 * chip] = jnp.where(low, left, pltpu.roll(right, T_DEV, 1))
        out[2 * chip + 1] = jnp.where(low, pltpu.roll(left, T_DEV, 1), right)


def combine(parts):
    return pl.pallas_call(
        combine_kernel,
        in_specs=[VMEM],
        out_specs=VMEM,
        out_shape=jax.ShapeDtypeStruct(parts.shape[1:], jnp.float32),
        name="combine",
        compiler_params=pltpu.CompilerParams(vmem_limit_bytes=4 * 2**20),
    )(parts)


def second_kernel(parts, bias_one, self_weight, neigh_weight, bias_two, seeds, neighbors, out):
    rows = []
    for k in range(parts.shape[0]):
        rows += [parts[k], pltpu.roll(parts[k], T_DEV, 1)]
    sums = jnp.concatenate(rows, axis=0)
    hidden = jnp.maximum(sums + bias_one[...], 0.0).astype(jnp.bfloat16)
    count, fan = neighbors.shape
    positions = lax.broadcasted_iota(jnp.int32, (count, hidden.shape[1]), 1)
    pick_self = (positions == seeds[...]).astype(jnp.float32)
    tally = jnp.zeros(positions.shape, jnp.float32)
    for k in range(fan):
        tally += (positions == neighbors[:, k : k + 1]).astype(jnp.float32)
    picked = lax.dot_general(
        jnp.concatenate([pick_self, tally / fan], axis=0).astype(jnp.bfloat16),
        hidden,
        NT,
        preferred_element_type=jnp.float32,
    ).astype(jnp.bfloat16)
    out[...] = (
        lax.dot_general(
            picked[:count], self_weight[...], NT, preferred_element_type=jnp.float32
        )
        + lax.dot_general(
            picked[count:], neigh_weight[...], NT, preferred_element_type=jnp.float32
        )
        + bias_two[...]
    )


def second(parts, bias_one, self_weight, neigh_weight, bias_two, seeds, neighbors):
    return pl.pallas_call(
        second_kernel,
        in_specs=[VMEM] * 7,
        out_specs=VMEM,
        out_shape=jax.ShapeDtypeStruct((seeds.shape[0], bias_two.shape[0]), jnp.float32),
        name="second",
        compiler_params=pltpu.CompilerParams(vmem_limit_bytes=8 * 2**20),
    )(
        parts,
        bias_one[:, None],
        self_weight.T,
        neigh_weight.T,
        bias_two[None, :],
        seeds[:, None],
        neighbors,
    )


def on_device(
    features,
    adjacency,
    target_block,
    source_block,
    block_count,
    layer_one,
    bias_one,
    self_weight,
    neigh_weight,
    bias_two,
    seed_ids,
    neighbor_ids,
):
    size = adjacency.shape[1]
    node_count = lax.axis_size("node")
    feat_count = lax.axis_size("feat")
    target_blocks = T_DEV * node_count * feat_count // size

    pair = [(i, i ^ 1) for i in range(feat_count)]
    up = [(i, (i + 2) % feat_count) for i in range(feat_count)]
    down = [((i + 2) % feat_count, i) for i in range(feat_count)]

    def send(value, route):
        return lax.ppermute(value, "feat", route)

    tie = lax.optimization_barrier
    opposite, rest, opposite_own, rest_own = project(in_hop_order(layer_one), features)
    opposite, rest = tie((send(opposite, pair), rest))
    rest = send(rest, pair)

    order = block_count
    streams = []
    for begin, end in SPANS:
        middle = (end - begin) // 2
        opposite, opposite_own, order = tie((opposite, opposite_own, order))
        onward = opposite_own[begin : begin + middle] + opposite[begin : begin + middle]
        back = opposite_own[begin + middle : end] + opposite[begin + middle : end]
        onward, back, order = tie((onward, back, order))
        streams.append((send(onward, up), send(back, down)))
    for turn in range(3):
        for k, (begin, end) in enumerate(SPANS):
            onward, back = streams[k]
            if turn == 0:
                zero = jnp.float32(0)
                onward = lax.pad(onward, zero, ((0, (end - begin) // 2, 0), (0, 0, 0), (0, 0, 0)))
                back = lax.pad(back, zero, (((end - begin) // 2, 0, 0), (0, 0, 0), (0, 0, 0)))
            rest, rest_own, order = tie((rest, rest_own, order))
            at = 2 * turn * UNITS
            onward = rest_own[at + begin : at + end] + rest[at + begin : at + end] + onward
            at += UNITS
            back = rest_own[at + begin : at + end] + rest[at + begin : at + end] + back
            onward, back, order = tie((onward, back, order))
            streams[k] = send(onward, up), send(back, down)

    lists = jnp.concatenate([target_block, source_block, block_count])
    partial = blocks(
        lists, rest_own[6 * UNITS :], rest[6 * UNITS :], streams, adjacency, target_blocks
    )

    partial = partial.reshape(node_count, 2 * CHIPS, TILE, size)
    parts = combine(lax.all_to_all(partial, "node", 0, 0))
    parts = lax.all_to_all(parts, "feat", 0, 0)
    return second(
        parts, bias_one, self_weight, neigh_weight, bias_two, seed_ids, neighbor_ids
    )


def solution(mesh):
    placed = (
        P("node", "feat"),
        P("node", None, None),
        P("node"),
        P("node"),
        P("node"),
        P("feat", None),
        P(),
        P(),
        P(),
        P(),
        P(("node", "feat")),
        P(("node", "feat"), None),
    )
    return jax.shard_map(
        on_device, mesh=mesh, in_specs=placed, out_specs=P(("node", "feat"), None), check_vma=False
    )
```

time: 1480 us -> 99.4 us (0.07)
  waiting for transfers between devices: 1290 us -> 26.9 us
  other arithmetic: 83.7 us -> 0.76 us
  local copies, waits for them, and re-layouts: 54 us -> 3.49 us
  starting transfers between devices: 0.01 us -> 37 us
  matrix products: 32.6 us -> 0.23 us
  blocking collectives: 0 us -> 24.5 us
    reduce_scatter x1 -> x0, waiting for transfers between devices: 1290 us -> none  [on_device(): lax.psum_scatter(projector(aggregated, layer_one), ('node', 'feat'), scat...]
    scatter-add x1 -> x0, other arithmetic: 76.3 us -> none  [on_device(): summed = jnp.zeros((target_blocks, block_size, columns), jnp.float32).at[...]
    mul x1 -> x0, local copies, waits for them, and re-layouts: 33.5 us -> none  [on_device(): products * live_mask[:, None, None]]
    dot_general x5 -> x1, matrix products: 32.6 us -> 0.23 us  [in_hop_order(): lax.dot_general(pick, layer_one, NT, preferred_element_type=jnp.float32)]
    ppermute x0 -> x18, starting transfers between devices: none -> 27 us  [send(): return lax.ppermute(value, 'feat', route)]
    all_to_all x0 -> x1, blocking collectives: none -> 24.5 us  [on_device(): parts = combine(lax.all_to_all(partial, 'node', 0, 0))]
    ppermute x0 -> x18, waiting for transfers between devices: none -> 19.4 us  [send(): return lax.ppermute(value, 'feat', route)]
  transfers between devices with their start and end apart: 1 -> 19, of which waited for: 1 -> 8; matrix products, arithmetic and copies ran while one was open for 0% -> 1% of each run, Pallas kernels for 0% -> 0%
where the time goes in v4:
time: 99.4 us; the launch traced here: 99.1 us
  starting transfers between devices  37 us (37%)
  waiting for transfers between devices  26.9 us (27%)
  blocking collectives  24.5 us (25%)
  Pallas kernels  5.37 us (5%)
  local copies, waits for them, and re-layouts  3.49 us (4%)
    ppermute x18, starting transfers between devices, send(): return lax.ppermute(value, 'feat', route)  27 us
    all_to_all x1, blocking collectives, on_device(): parts = combine(lax.all_to_all(partial, 'node', 0, 0))  24.5 us
    ppermute x18, waiting for transfers between devices, send(): return lax.ppermute(value, 'feat', route)  19.4 us
    all_to_all x1, starting transfers between devices, on_device(): parts = lax.all_to_all(parts, 'feat', 0, 0)  10 us
    all_to_all x1, waiting for transfers between devices, on_device(): parts = lax.all_to_all(parts, 'feat', 0, 0)  7.49 us
    unnamed x25, local copies, waits for them, and re-layouts  3.19 us
    pallas_call x1, Pallas kernels, blocks(): pl.pallas_call(blocks_kernel, in_specs=[pl.BlockSpec(memory_space=pl.ANY)...  2.31 us
  transfers between devices with their start and end apart: 19, of which 8 were waited for; matrix products, arithmetic and copies ran while one was open for 1% of the time, Pallas kernels for 0%

profile of v4, /device:TPU:1, one launch (start us, length us, event | category | flops | bytes accessed | tf_op | source)
XLA Modules:
  0.0 99.1 jit_solution(14648988210822680550)
XLA Ops:
  0.0 0.9 copy-done
  0.9 0.2 convolution_convert_fusion.ordered
  1.2 2.2 %copy-done.1 = bf16[8192,256]{1,0:T(8,128)(2,1)S(1)} copy-done((bf16[8192,256]{1,0:T(8,128)(2,1)S(1)}, bf16[8192,256]{1,0:T(8,128)(2,1)}, u32[]{:S(2)}) %copy-start.1) | copy-done | bytes 4194328
  3.3 1.3 %project.1 = (f32[16,8,1024]{2,1,0:T(8,128)S(1)}, f32[112,8,1024]{2,1,0:T(8,128)S(1)}, f32[16,8,1024]{2,1,0:T(8,128)S(1)}, f32[112,8,1024]{2,1,0:T(8,128)S(1)}) custom-call(bf16[256,256]{1,0:T(8,128)(2,1)S(1)} %convolution_convert_fusion.ordered, bf16[8192,256]{1,0:T(8,128)(2,1)S(1)} %copy-done.1), custom_call_target="tpu_custom_call" | custom-call | flops 1073741824 | bytes 12582912 | tf_op jit(solution)/shard_map/project/pallas_call | solution.py:40
  4.6 3.3 %collective-permute-start = (f32[16,8,1024]{2,1,0:T(8,128)S(1)}, f32[16,8,1024]{2,1,0:T(8,128)S(1)}, u32[]{:S(2)}, u32[]{:S(2)}) collective-permute-start(f32[16,8,1024]{2,1,0:T(8,128)S(1)} %get-tuple-element.44), channel_id=1, source_target_pairs={{0,1},{1,0},{2,3},{3,2},{4,5},{5,4},{6,7},{7,6},{8,9},{9,8},{10,11... | collective-permute-start | bytes 1572872 | tf_op jit(solution)/shard_map/ppermute | solution.py:246
  7.9 1.5 %collective-permute-done = f32[16,8,1024]{2,1,0:T(8,128)S(1)} collective-permute-done((f32[16,8,1024]{2,1,0:T(8,128)S(1)}, f32[16,8,1024]{2,1,0:T(8,128)S(1)}, u32[]{:S(2)}, u32[]{:S(2)}) %collective-permute-start) | collective-permute-done | bytes 524320 | tf_op jit(solution)/shard_map/ppermute | solution.py:246
  9.5 0.4 collective-permute-start.1
  10.0 3.9 %collective-permute-start.3 = (f32[5,8,1024]{2,1,0:T(8,128)S(1)}, f32[5,8,1024]{2,1,0:T(8,128)S(1)}, u32[]{:S(2)}, u32[]{:S(2)}) collective-permute-start(f32[5,8,1024]{2,1,0:T(8,128)S(1)} %get-tuple-element.62), channel_id=1, source_target_pairs={{2,0},{3,1},{4,2},{5,3},{6,4},{7,5},{8,6},{9,7},{10,8},{11,9},{12,... | collective-permute-start | bytes 491528 | tf_op jit(solution)/shard_map/ppermute | solution.py:246
  14.0 2.7 %collective-permute-start.11 = (f32[3,8,1024]{2,1,0:T(8,128)S(1)}, f32[3,8,1024]{2,1,0:T(8,128)S(1)}, u32[]{:S(2)}, u32[]{:S(2)}) collective-permute-start(f32[3,8,1024]{2,1,0:T(8,128)S(1)} %get-tuple-element.76), channel_id=1, source_target_pairs={{2,0},{3,1},{4,2},{5,3},{6,4},{7,5},{8,6},{9,7},{10,8},{11,9},{12,... | collective-permute-start | bytes 294920 | tf_op jit(solution)/shard_map/ppermute | solution.py:246
  16.7 1.6 %collective-permute-done.2 = f32[5,8,1024]{2,1,0:T(8,128)S(1)} collective-permute-done((f32[5,8,1024]{2,1,0:T(8,128)S(1)}, f32[5,8,1024]{2,1,0:T(8,128)S(1)}, u32[]{:S(2)}, u32[]{:S(2)}) %collective-permute-start.2) | collective-permute-done | bytes 163872 | tf_op jit(solution)/shard_map/ppermute | solution.py:246
  18.5 2.7 %collective-permute-start.5 = (f32[10,8,1024]{2,1,0:T(8,128)S(1)}, f32[10,8,1024]{2,1,0:T(8,128)S(1)}, u32[]{:S(2)}, u32[]{:S(2)}) collective-permute-start(f32[10,8,1024]{2,1,0:T(8,128)S(1)} %get-tuple-element.64), channel_id=1, source_target_pairs={{2,0},{3,1},{4,2},{5,3},{6,4},{7,5},{8,6},{9,7},{10,8},{11,9},{12,... | collective-permute-start | bytes 983048 | tf_op jit(solution)/shard_map/ppermute | solution.py:246
  21.3 2.7 %collective-permute-start.13 = (f32[6,8,1024]{2,1,0:T(8,128)S(1)}, f32[6,8,1024]{2,1,0:T(8,128)S(1)}, u32[]{:S(2)}, u32[]{:S(2)}) collective-permute-start(f32[6,8,1024]{2,1,0:T(8,128)S(1)} %get-tuple-element.78), channel_id=1, source_target_pairs={{2,0},{3,1},{4,2},{5,3},{6,4},{7,5},{8,6},{9,7},{10,8},{11,9},{12,... | collective-permute-start | bytes 589832 | tf_op jit(solution)/shard_map/ppermute | solution.py:246
  24.0 3.8 %collective-permute-done.4 = f32[10,8,1024]{2,1,0:T(8,128)S(1)} collective-permute-done((f32[10,8,1024]{2,1,0:T(8,128)S(1)}, f32[10,8,1024]{2,1,0:T(8,128)S(1)}, u32[]{:S(2)}, u32[]{:S(2)}) %collective-permute-start.4) | collective-permute-done | bytes 327712 | tf_op jit(solution)/shard_map/ppermute | solution.py:246
  28.0 0.8 collective-permute-start.6
  28.8 1.9 %collective-permute-start.7 = (f32[10,8,1024]{2,1,0:T(8,128)S(1)}, f32[10,8,1024]{2,1,0:T(8,128)S(1)}, u32[]{:S(2)}, u32[]{:S(2)}) collective-permute-start(f32[10,8,1024]{2,1,0:T(8,128)S(1)} %get-tuple-element.66), channel_id=1, source_target_pairs={{2,0},{3,1},{4,2},{5,3},{6,4},{7,5},{8,6},{9,7},{10,8},{11,9},{12,... | collective-permute-start | bytes 983048 | tf_op jit(solution)/shard_map/ppermute | solution.py:246
  30.7 1.3 %collective-permute-done.12 = f32[6,8,1024]{2,1,0:T(8,128)S(1)} collective-permute-done((f32[6,8,1024]{2,1,0:T(8,128)S(1)}, f32[6,8,1024]{2,1,0:T(8,128)S(1)}, u32[]{:S(2)}, u32[]{:S(2)}) %collective-permute-start.12) | collective-permute-done | bytes 196640 | tf_op jit(solution)/shard_map/ppermute | solution.py:246
  32.1 0.8 collective-permute-start.14
  32.9 1.9 %collective-permute-start.15 = (f32[6,8,1024]{2,1,0:T(8,128)S(1)}, f32[6,8,1024]{2,1,0:T(8,128)S(1)}, u32[]{:S(2)}, u32[]{:S(2)}) collective-permute-start(f32[6,8,1024]{2,1,0:T(8,128)S(1)} %get-tuple-element.80), channel_id=1, source_target_pairs={{2,0},{3,1},{4,2},{5,3},{6,4},{7,5},{8,6},{9,7},{10,8},{11,9},{12,... | collective-permute-start | bytes 589832 | tf_op jit(solution)/shard_map/ppermute | solution.py:246
  34.8 3.2 %collective-permute-done.6 = f32[10,8,1024]{2,1,0:T(8,128)S(1)} collective-permute-done((f32[10,8,1024]{2,1,0:T(8,128)S(1)}, f32[10,8,1024]{2,1,0:T(8,128)S(1)}, u32[]{:S(2)}, u32[]{:S(2)}) %collective-permute-start.6) | collective-permute-done | bytes 327712 | tf_op jit(solution)/shard_map/ppermute | solution.py:246
  38.1 0.2 add_add_fusion
  38.2 0.8 collective-permute-start.8
  39.0 2.0 %collective-permute-start.9 = (f32[10,8,1024]{2,1,0:T(8,128)S(1)}, f32[10,8,1024]{2,1,0:T(8,128)S(1)}, u32[]{:S(2)}, u32[]{:S(2)}) collective-permute-start(f32[10,8,1024]{2,1,0:T(8,128)S(1)} %get-tuple-element.68), channel_id=1, source_target_pairs={{2,0},{3,1},{4,2},{5,3},{6,4},{7,5},{8,6},{9,7},{10,8},{11,9},{12,... | collective-permute-start | bytes 983048 | tf_op jit(solution)/shard_map/ppermute | solution.py:246
  41.0 1.3 %collective-permute-done.14 = f32[6,8,1024]{2,1,0:T(8,128)S(1)} collective-permute-done((f32[6,8,1024]{2,1,0:T(8,128)S(1)}, f32[6,8,1024]{2,1,0:T(8,128)S(1)}, u32[]{:S(2)}, u32[]{:S(2)}) %collective-permute-start.14) | collective-permute-done | bytes 196640 | tf_op jit(solution)/shard_map/ppermute | solution.py:246
  42.4 0.7 collective-permute-start.16
  43.1 2.0 %collective-permute-start.17 = (f32[6,8,1024]{2,1,0:T(8,128)S(1)}, f32[6,8,1024]{2,1,0:T(8,128)S(1)}, u32[]{:S(2)}, u32[]{:S(2)}) collective-permute-start(f32[6,8,1024]{2,1,0:T(8,128)S(1)} %get-tuple-element.82), channel_id=1, source_target_pairs={{2,0},{3,1},{4,2},{5,3},{6,4},{7,5},{8,6},{9,7},{10,8},{11,9},{12,... | collective-permute-start | bytes 589832 | tf_op jit(solution)/shard_map/ppermute | solution.py:246
  46.0 6.7 %collective-permute-done.16.up_b = f32[6,8,1024]{2,1,0:T(8,128)S(1)} collective-permute-done((f32[6,8,1024]{2,1,0:T(8,128)S(1)}, f32[6,8,1024]{2,1,0:T(8,128)S(1)}, u32[]{:S(2)}, u32[]{:S(2)}) %collective-permute-start.16) | collective-permute-done | bytes 196640 | tf_op jit(solution)/shard_map/ppermute | solution.py:246
  52.7 2.3 %blocks.1 = f32[256,8,128]{2,1,0:T(8,128)S(1)} custom-call(s32[513]{0:T(1024)S(1)} %pad_add_fusion.4.lists, f32[16,8,1024]{2,1,0:T(8,128)S(1)} %slice.102.own, f32[16,8,1024]{2,1,0:T(8,128)S(1)} %slice.103.paired, f32[10,8,1024]{2,1,0:T(8,128)S(1)} %collective-permute-done.8.up_a, f32[10,8,1024]{2,1,0:T(8,128)S(1)} %collective-permute-done.9.down_a, ...), custom_call_target="tpu_custom_call" | custom-call | flops 268435456 | bytes 8388608 | tf_op jit(solution)/shard_map/blocks/pallas_call | solution.py:131
  55.0 24.5 %all_to_all.10.parts = f32[16,16,8,128]{3,2,1,0:T(8,128)S(1)} all-to-all(f32[16,16,8,128]{3,2,1,0:T(8,128)S(1)} %bitcast.9), channel_id=1, replica_groups=mesh['node'=16,'feat'=16] {'node'}, dimensions={0} | all-to-all | bytes 2097152 | tf_op jit(solution)/shard_map/all_to_all | solution.py:283
  79.5 0.7 combine.1
  80.3 10.0 %all-to-all-start.1 = ((f32[16,8,128]{2,1,0:T(8,128)}), f32[16,8,128]{2,1,0:T(8,128)S(1)}, u32[]{:S(2)}, u32[]{:S(2)}) async-start(f32[16,8,128]{2,1,0:T(8,128)} %combine.1), calls=%async_computation.1 | async-start | bytes 131072 | tf_op jit(solution)/shard_map/all_to_all | solution.py:284
  90.6 7.5 %all-to-all-done.1.parts = f32[16,8,128]{2,1,0:T(8,128)S(1)} async-done(((f32[16,8,128]{2,1,0:T(8,128)}), f32[16,8,128]{2,1,0:T(8,128)S(1)}, u32[]{:S(2)}, u32[]{:S(2)}) %all-to-all-start.1) | async-done | bytes 65568 | tf_op jit(solution)/shard_map/all_to_all | solution.py:284
  98.1 1.0 %second.1 = f32[32,172]{1,0:T(8,128)} custom-call(f32[16,8,128]{2,1,0:T(8,128)S(1)} %all-to-all-done.1.parts, f32[256,1]{1,0:T(8,128)S(1)} %copy.15.bias_one, bf16[172,256]{1,0:T(8,128)(2,1)S(1)} %bitcast.10, bf16[172,256]{1,0:T(8,128)(2,1)S(1)} %bitcast.11, f32[1,172]{1,0:T(1,128)S(1)} %bitcast.12, s32[32,1]{1,0:T(8,128)S(1)} %copy.16.seeds, ...), custom_call_target="tpu_custom_call" | custom-call | tf_op jit(solution)/shard_map/second/pallas_call | solution.py:204
  (52 shorter events, 1.4 us)
Async XLA Ops:
  0.0 0.9 copy-start
  1.1 2.2 %copy-start.1 = (bf16[8192,256]{1,0:T(8,128)(2,1)S(1)}, bf16[8192,256]{1,0:T(8,128)(2,1)}, u32[]{:S(2)}) copy-start(bf16[8192,256]{1,0:T(8,128)(2,1)} %features.1) | copy-start | bytes 12582916
  4.6 4.9 %collective-permute-start = (f32[16,8,1024]{2,1,0:T(8,128)S(1)}, f32[16,8,1024]{2,1,0:T(8,128)S(1)}, u32[]{:S(2)}, u32[]{:S(2)}) collective-permute-start(f32[16,8,1024]{2,1,0:T(8,128)S(1)} %get-tuple-element.44), channel_id=1, source_target_pairs={{0,1},{1,0},{2,3},{3,2},{4,5},{5,4},{6,7},{7,6},{8,9},{9,8},{10,11... | collective-permute-start | bytes 1572872 | tf_op jit(solution)/shard_map/ppermute | solution.py:246
  9.5 7.2 %collective-permute-start.1 = (f32[112,8,1024]{2,1,0:T(8,128)S(1)}, f32[112,8,1024]{2,1,0:T(8,128)S(1)}, u32[]{:S(2)}, u32[]{:S(2)}) collective-permute-start(f32[112,8,1024]{2,1,0:T(8,128)S(1)} %get-tuple-element.46), channel_id=1, source_target_pairs={{0,1},{1,0},{2,3},{3,2},{4,5},{5,4},{6,7},{7,6},{8,9},{9,8},{10,11... | collective-permute-start | bytes 11010056 | tf_op jit(solution)/shard_map/ppermute | solution.py:246
  9.9 42.8 %slice-start = ((s8[8388608]{0:T(1024)(128)(4,1)}), s8[4194304]{0:T(1024)(128)(4,1)S(1)}, s32[]{:S(2)}) async-start(s8[8388608]{0:T(1024)(128)(4,1)} %bitcast.7), calls=%async_computation.2 | async-start | bytes 8388608
  9.9 8.4 %collective-permute-start.2 = (f32[5,8,1024]{2,1,0:T(8,128)S(1)}, f32[5,8,1024]{2,1,0:T(8,128)S(1)}, u32[]{:S(2)}, u32[]{:S(2)}) collective-permute-start(f32[5,8,1024]{2,1,0:T(8,128)S(1)} %get-tuple-element.61), channel_id=1, source_target_pairs={{0,2},{1,3},{2,4},{3,5},{4,6},{5,7},{6,8},{7,9},{8,10},{9,11},{10,... | collective-permute-start | bytes 491528 | tf_op jit(solution)/shard_map/ppermute | solution.py:246
  10.0 8.3 %collective-permute-start.3 = (f32[5,8,1024]{2,1,0:T(8,128)S(1)}, f32[5,8,1024]{2,1,0:T(8,128)S(1)}, u32[]{:S(2)}, u32[]{:S(2)}) collective-permute-start(f32[5,8,1024]{2,1,0:T(8,128)S(1)} %get-tuple-element.62), channel_id=1, source_target_pairs={{2,0},{3,1},{4,2},{5,3},{6,4},{7,5},{8,6},{9,7},{10,8},{11,9},{12,... | collective-permute-start | bytes 491528 | tf_op jit(solution)/shard_map/ppermute | solution.py:246
  13.9 7.2 %collective-permute-start.10 = (f32[3,8,1024]{2,1,0:T(8,128)S(1)}, f32[3,8,1024]{2,1,0:T(8,128)S(1)}, u32[]{:S(2)}, u32[]{:S(2)}) collective-permute-start(f32[3,8,1024]{2,1,0:T(8,128)S(1)} %get-tuple-element.75), channel_id=1, source_target_pairs={{0,2},{1,3},{2,4},{3,5},{4,6},{5,7},{6,8},{7,9},{8,10},{9,11},{10,... | collective-permute-start | bytes 294920 | tf_op jit(solution)/shard_map/ppermute | solution.py:246
  14.0 7.1 %collective-permute-start.11 = (f32[3,8,1024]{2,1,0:T(8,128)S(1)}, f32[3,8,1024]{2,1,0:T(8,128)S(1)}, u32[]{:S(2)}, u32[]{:S(2)}) collective-permute-start(f32[3,8,1024]{2,1,0:T(8,128)S(1)} %get-tuple-element.76), channel_id=1, source_target_pairs={{2,0},{3,1},{4,2},{5,3},{6,4},{7,5},{8,6},{9,7},{10,8},{11,9},{12,... | collective-permute-start | bytes 294920 | tf_op jit(solution)/shard_map/ppermute | solution.py:246
  18.4 9.4 %collective-permute-start.4 = (f32[10,8,1024]{2,1,0:T(8,128)S(1)}, f32[10,8,1024]{2,1,0:T(8,128)S(1)}, u32[]{:S(2)}, u32[]{:S(2)}) collective-permute-start(f32[10,8,1024]{2,1,0:T(8,128)S(1)} %get-tuple-element.63), channel_id=1, source_target_pairs={{0,2},{1,3},{2,4},{3,5},{4,6},{5,7},{6,8},{7,9},{8,10},{9,11},{10,... | collective-permute-start | bytes 983048 | tf_op jit(solution)/shard_map/ppermute | solution.py:246
  18.5 9.3 %collective-permute-start.5 = (f32[10,8,1024]{2,1,0:T(8,128)S(1)}, f32[10,8,1024]{2,1,0:T(8,128)S(1)}, u32[]{:S(2)}, u32[]{:S(2)}) collective-permute-start(f32[10,8,1024]{2,1,0:T(8,128)S(1)} %get-tuple-element.64), channel_id=1, source_target_pairs={{2,0},{3,1},{4,2},{5,3},{6,4},{7,5},{8,6},{9,7},{10,8},{11,9},{12,... | collective-permute-start | bytes 983048 | tf_op jit(solution)/shard_map/ppermute | solution.py:246
  21.2 24.6 %copy-start.7 = (s32[256]{0:T(256)S(1)}, s32[256]{0:T(256)}, u32[]{:S(2)}) copy-start(s32[256]{0:T(256)} %param.15) | copy-start | bytes 3076
  21.2 24.6 %copy-start.8 = (s32[256]{0:T(256)S(1)}, s32[256]{0:T(256)}, u32[]{:S(2)}) copy-start(s32[256]{0:T(256)} %param.14) | copy-start | bytes 3076
  21.2 10.8 %collective-permute-start.12 = (f32[6,8,1024]{2,1,0:T(8,128)S(1)}, f32[6,8,1024]{2,1,0:T(8,128)S(1)}, u32[]{:S(2)}, u32[]{:S(2)}) collective-permute-start(f32[6,8,1024]{2,1,0:T(8,128)S(1)} %get-tuple-element.77), channel_id=1, source_target_pairs={{0,2},{1,3},{2,4},{3,5},{4,6},{5,7},{6,8},{7,9},{8,10},{9,11},{10,... | collective-permute-start | bytes 589832 | tf_op jit(solution)/shard_map/ppermute | solution.py:246
  21.3 10.7 %collective-permute-start.13 = (f32[6,8,1024]{2,1,0:T(8,128)S(1)}, f32[6,8,1024]{2,1,0:T(8,128)S(1)}, u32[]{:S(2)}, u32[]{:S(2)}) collective-permute-start(f32[6,8,1024]{2,1,0:T(8,128)S(1)} %get-tuple-element.78), channel_id=1, source_target_pairs={{2,0},{3,1},{4,2},{5,3},{6,4},{7,5},{8,6},{9,7},{10,8},{11,9},{12,... | collective-permute-start | bytes 589832 | tf_op jit(solution)/shard_map/ppermute | solution.py:246
  28.0 24.7 %slice-start.1 = ((s8[8388608]{0:T(1024)(128)(4,1)}), s8[4194304]{0:T(1024)(128)(4,1)S(1)}, s32[]{:S(2)}) async-start(s8[8388608]{0:T(1024)(128)(4,1)} %bitcast.7), calls=%async_computation.3 | async-start | bytes 8388608
  28.0 10.1 %collective-permute-start.6 = (f32[10,8,1024]{2,1,0:T(8,128)S(1)}, f32[10,8,1024]{2,1,0:T(8,128)S(1)}, u32[]{:S(2)}, u32[]{:S(2)}) collective-permute-start(f32[10,8,1024]{2,1,0:T(8,128)S(1)} %get-tuple-element.65), channel_id=1, source_target_pairs={{0,2},{1,3},{2,4},{3,5},{4,6},{5,7},{6,8},{7,9},{8,10},{9,11},{10,... | collective-permute-start | bytes 983048 | tf_op jit(solution)/shard_map/ppermute | solution.py:246
  28.8 9.2 %collective-permute-start.7 = (f32[10,8,1024]{2,1,0:T(8,128)S(1)}, f32[10,8,1024]{2,1,0:T(8,128)S(1)}, u32[]{:S(2)}, u32[]{:S(2)}) collective-permute-start(f32[10,8,1024]{2,1,0:T(8,128)S(1)} %get-tuple-element.66), channel_id=1, source_target_pairs={{2,0},{3,1},{4,2},{5,3},{6,4},{7,5},{8,6},{9,7},{10,8},{11,9},{12,... | collective-permute-start | bytes 983048 | tf_op jit(solution)/shard_map/ppermute | solution.py:246
  32.1 10.2 %collective-permute-start.14 = (f32[6,8,1024]{2,1,0:T(8,128)S(1)}, f32[6,8,1024]{2,1,0:T(8,128)S(1)}, u32[]{:S(2)}, u32[]{:S(2)}) collective-permute-start(f32[6,8,1024]{2,1,0:T(8,128)S(1)} %get-tuple-element.79), channel_id=1, source_target_pairs={{0,2},{1,3},{2,4},{3,5},{4,6},{5,7},{6,8},{7,9},{8,10},{9,11},{10,... | collective-permute-start | bytes 589832 | tf_op jit(solution)/shard_map/ppermute | solution.py:246
  32.9 9.4 %collective-permute-start.15 = (f32[6,8,1024]{2,1,0:T(8,128)S(1)}, f32[6,8,1024]{2,1,0:T(8,128)S(1)}, u32[]{:S(2)}, u32[]{:S(2)}) collective-permute-start(f32[6,8,1024]{2,1,0:T(8,128)S(1)} %get-tuple-element.80), channel_id=1, source_target_pairs={{2,0},{3,1},{4,2},{5,3},{6,4},{7,5},{8,6},{9,7},{10,8},{11,9},{12,... | collective-permute-start | bytes 589832 | tf_op jit(solution)/shard_map/ppermute | solution.py:246
  38.2 14.4 %collective-permute-start.8 = (f32[10,8,1024]{2,1,0:T(8,128)S(1)}, f32[10,8,1024]{2,1,0:T(8,128)S(1)}, u32[]{:S(2)}, u32[]{:S(2)}) collective-permute-start(f32[10,8,1024]{2,1,0:T(8,128)S(1)} %get-tuple-element.67), channel_id=1, source_target_pairs={{0,2},{1,3},{2,4},{3,5},{4,6},{5,7},{6,8},{7,9},{8,10},{9,11},{10,... | collective-permute-start | bytes 983048 | tf_op jit(solution)/shard_map/ppermute | solution.py:246
  39.0 13.7 %collective-permute-start.9 = (f32[10,8,1024]{2,1,0:T(8,128)S(1)}, f32[10,8,1024]{2,1,0:T(8,128)S(1)}, u32[]{:S(2)}, u32[]{:S(2)}) collective-permute-start(f32[10,8,1024]{2,1,0:T(8,128)S(1)} %get-tuple-element.68), channel_id=1, source_target_pairs={{2,0},{3,1},{4,2},{5,3},{6,4},{7,5},{8,6},{9,7},{10,8},{11,9},{12,... | collective-permute-start | bytes 983048 | tf_op jit(solution)/shard_map/ppermute | solution.py:246
  42.4 10.3 %collective-permute-start.16 = (f32[6,8,1024]{2,1,0:T(8,128)S(1)}, f32[6,8,1024]{2,1,0:T(8,128)S(1)}, u32[]{:S(2)}, u32[]{:S(2)}) collective-permute-start(f32[6,8,1024]{2,1,0:T(8,128)S(1)} %get-tuple-element.81), channel_id=1, source_target_pairs={{0,2},{1,3},{2,4},{3,5},{4,6},{5,7},{6,8},{7,9},{8,10},{9,11},{10,... | collective-permute-start | bytes 589832 | tf_op jit(solution)/shard_map/ppermute | solution.py:246
  43.1 9.5 %collective-permute-start.17 = (f32[6,8,1024]{2,1,0:T(8,128)S(1)}, f32[6,8,1024]{2,1,0:T(8,128)S(1)}, u32[]{:S(2)}, u32[]{:S(2)}) collective-permute-start(f32[6,8,1024]{2,1,0:T(8,128)S(1)} %get-tuple-element.82), channel_id=1, source_target_pairs={{2,0},{3,1},{4,2},{5,3},{6,4},{7,5},{8,6},{9,7},{10,8},{11,9},{12,... | collective-permute-start | bytes 589832 | tf_op jit(solution)/shard_map/ppermute | solution.py:246
  45.9 44.4 %copy-start.9 = (s32[32]{0:T(128)S(1)}, s32[32]{0:T(128)}, u32[]{:S(2)}) copy-start(s32[32]{0:T(128)} %param.22) | copy-start | bytes 388
  45.9 44.5 %copy-start.5 = (s32[32,8]{0,1:T(8,128)S(1)}, s32[32,8]{0,1:T(8,128)}, u32[]{:S(2)}) copy-start(s32[32,8]{0,1:T(8,128)} %param.23) | copy-start | bytes 3076
  45.9 44.6 %copy-start.6 = (f32[256]{0:T(256)S(1)}, f32[256]{0:T(256)}, u32[]{:S(2)}) copy-start(f32[256]{0:T(256)} %param.18) | copy-start | bytes 3076
  45.9 52.2 %copy-start.2 = (bf16[256,172]{0,1:T(8,128)(2,1)S(1)}, bf16[256,172]{0,1:T(8,128)(2,1)}, u32[]{:S(2)}) copy-start(bf16[256,172]{0,1:T(8,128)(2,1)} %param.19) | copy-start | bytes 264196
  45.9 52.2 %copy-start.3 = (bf16[256,172]{0,1:T(8,128)(2,1)S(1)}, bf16[256,172]{0,1:T(8,128)(2,1)}, u32[]{:S(2)}) copy-start(bf16[256,172]{0,1:T(8,128)(2,1)} %param.20) | copy-start | bytes 264196
  45.9 52.2 %copy-start.4 = (f32[172]{0:T(256)S(1)}, f32[172]{0:T(256)}, u32[]{:S(2)}) copy-start(f32[172]{0:T(256)} %param.21) | copy-start | bytes 2068
  80.3 17.8 %all-to-all-start.1 = ((f32[16,8,128]{2,1,0:T(8,128)}), f32[16,8,128]{2,1,0:T(8,128)S(1)}, u32[]{:S(2)}, u32[]{:S(2)}) async-start(f32[16,8,128]{2,1,0:T(8,128)} %combine.1), calls=%async_computation.1 | async-start | bytes 131072 | tf_op jit(solution)/shard_map/all_to_all | solution.py:284

commit v5 on v4

--- a/solution.py
+++ b/solution.py
@@ -10,6 +10,7 @@
 TILE = 8
 RUNS = 8
 SPANS = ((0, 10), (10, 16))
+GROUP = 16
 NT = (((1,), (1,)), ((), ()))
 VMEM = pl.BlockSpec(memory_space=pltpu.VMEM)
 
@@ -26,7 +27,8 @@
         take = 0
         for out in outs:
             for k in range(out.shape[0] // RUNS):
-                out[k * RUNS + run, :, at : at + tile] = product[take : take + TILE]
+                unit = k // 2 * UNITS + 2 * run + k % 2
+                out[unit, :, at : at + tile] = product[take : take + TILE]
                 take += TILE
 
 
@@ -68,69 +70,101 @@
     )
 
 
-def blocks_kernel(
-    lists, own, paired, up_a, down_a, up_b, down_b, adjacency, out, held, table, landed
-):
+def block_lists(target_block, source_block, block_count, early):
+    place = 2 * target_block - target_block % CHIPS
+    slots = target_block.shape[0]
+    slot = jnp.arange(slots, dtype=jnp.int32)
+    live = slot < block_count[0]
+    key = jnp.where(live, (source_block >= early).astype(jnp.int32), 2)
+    key = key * slots + slot
+    rank = jnp.sum((key[None, :] < key[:, None]).astype(jnp.int32), axis=1)
+    at = rank[None, :] == slot[:, None]
+    lists = [
+        jnp.sum(jnp.where(at, values[None, :], 0), axis=1)
+        for values in (place, source_block, slot)
+    ]
+    first = jnp.sum((key < slots).astype(jnp.int32))[None]
+    spare = jnp.zeros((GROUP,), jnp.int32)
+    pieces = [piece for values in lists for piece in (values, spare)]
+    return jnp.concatenate([*pieces, first, block_count])
+
+
+def block_products(late, lists, own, paired, up, down, adjacency, out, held, table, landed):
     copy = pltpu.make_async_copy(lists, table, landed)
     copy.start()
     slots, size, _ = adjacency.shape
     lanes = own.shape[2]
-    out[...] = jnp.zeros_like(out)
-    for b in range(held.shape[0]):
+    begin = SPANS[late][0]
+    for b in range(begin // 2 * lanes // size, SPANS[late][1] // 2 * lanes // size):
         run, at = divmod(b * size, lanes)
         at = slice(at, at + size)
-        totals = []
-        for unit in (run, RUNS + run):
-            ups, downs, begin = (up_a, down_a, 0) if unit < SPANS[0][1] else (up_b, down_b, SPANS[1][0])
-            totals.append(
+        total = jnp.concatenate(
+            [
                 (own[unit, :, at] + paired[unit, :, at])
-                + (ups[unit - begin, :, at] + downs[unit - begin, :, at])
-            )
-        total = jnp.concatenate(totals, axis=0)
+                + (up[unit - begin, :, at] + down[unit - begin, :, at])
+                for unit in (2 * run, 2 * run + 1)
+            ],
+            axis=0,
+        )
         upper = total.astype(jnp.bfloat16)
         held[b, : 2 * TILE] = upper
         held[b, 2 * TILE :] = (total - upper.astype(jnp.float32)).astype(jnp.bfloat16)
     copy.wait()
-
-    def product(s):
-        value = lax.dot_general(
-            held[table[slots + s]], adjacency[s], NT, preferred_element_type=jnp.float32
-        )
-        return value[: 2 * TILE] + value[2 * TILE :]
-
-    def add(s, value):
-        block = table[s]
-        place = 2 * block - block % CHIPS
-        out[place] += value[:TILE]
-        out[place + CHIPS] += value[TILE:]
-
-    group = 16
-    live = table[2 * slots]
-    full = live // group
+    step = slots + GROUP
+    counts = table[3 * step], table[3 * step + 1]
+    start = counts[0] if late else 0
+    end = counts[late]
+
+    def products(first):
+        values = []
+        for k in range(0, GROUP, 2):
+            left = [held[table[step + first + k + j]] for j in range(2)]
+            right = [adjacency[table[2 * step + first + k + j]] for j in range(2)]
+            value = lax.dot_general(
+                jnp.concatenate(left, axis=0),
+                jnp.concatenate(right, axis=0),
+                NT,
+                preferred_element_type=jnp.float32,
+            )
+            rows = 2 * TILE
+            values.append(value[:rows, :size] + value[rows : 2 * rows, :size])
+            values.append(value[2 * rows : 3 * rows, size:] + value[3 * rows :, size:])
+        return values
+
+    def add(first, values):
+        for k in range(GROUP):
+            place = table[first + k]
+            value = jnp.where(first + k < end, values[k], 0.0)
+            out[place] += value[:TILE]
+            out[place + CHIPS] += value[TILE:]
 
     def whole(i, before):
-        products = [product(i * group + k) for k in range(group)]
-        for k in range(group):
-            add((i - 1) * group + k, before[k])
-        return products
-
-    last = lax.fori_loop(1, full, whole, [product(k) for k in range(group)])
-    for k in range(group):
-        add((full - 1) * group + k, last[k])
-
-    def single(s, carry):
-        add(s, product(s))
-        return carry
-
-    lax.fori_loop(full * group, live, single, 0)
-
-
-def blocks(lists, own, paired, streams, adjacency, target_blocks):
+        after = products(start + i * GROUP)
+        add(start + (i - 1) * GROUP, before)
+        return after
+
+    groups = (end - start + GROUP - 1) // GROUP
+    last = lax.fori_loop(1, groups, whole, products(start))
+    add(start + (jnp.maximum(groups, 1) - 1) * GROUP, last)
+
+
+def early_kernel(lists, own, paired, up, down, adjacency, out, held, table, landed):
+    out[...] = jnp.zeros_like(out)
+    block_products(0, lists, own, paired, up, down, adjacency, out, held, table, landed)
+
+
+def late_kernel(before, lists, own, paired, up, down, adjacency, out, held, table, landed):
+    out[...] = before[...]
+    block_products(1, lists, own, paired, up, down, adjacency, out, held, table, landed)
+
+
+def blocks(before, lists, own, paired, stream, adjacency, target_blocks):
     slots, size, _ = adjacency.shape
     rows = RUNS * own.shape[2]
+    late = before is not None
     return pl.pallas_call(
-        blocks_kernel,
-        in_specs=[pl.BlockSpec(memory_space=pl.ANY)] + [VMEM] * 7,
+        late_kernel if late else early_kernel,
+        in_specs=[VMEM] * late + [pl.BlockSpec(memory_space=pl.ANY)] + [VMEM] * 5,
         out_specs=VMEM,
         out_shape=jax.ShapeDtypeStruct((2 * target_blocks, TILE, size), jnp.float32),
         scratch_shapes=[
@@ -138,14 +172,14 @@
             pltpu.SMEM(lists.shape, jnp.int32),
             pltpu.SemaphoreType.DMA,
         ],
-        name="blocks",
+        name="late_blocks" if late else "early_blocks",
         compiler_params=pltpu.CompilerParams(vmem_limit_bytes=8 * 2**20),
         cost_estimate=pl.CostEstimate(
             flops=4 * slots * size * size * UNITS,
-            bytes_accessed=slots * size * size * 2,
+            bytes_accessed=slots * size * size,
             transcendentals=0,
         ),
-    )(lists, own, paired, *streams[0], *streams[1], adjacency)
+    )(*([before] if late else []), lists, own, paired, *stream, adjacency)
 
 
 def combine_kernel(parts, out):
@@ -274,10 +308,11 @@
             onward, back, order = tie((onward, back, order))
             streams[k] = send(onward, up), send(back, down)
 
-    lists = jnp.concatenate([target_block, source_block, block_count])
-    partial = blocks(
-        lists, rest_own[6 * UNITS :], rest[6 * UNITS :], streams, adjacency, target_blocks
-    )
+    early = SPANS[0][1] // 2 * (features.shape[0] // RUNS) // size
+    lists = block_lists(target_block, source_block, block_count, early)
+    near = rest_own[6 * UNITS :], rest[6 * UNITS :]
+    partial = blocks(None, lists, *near, streams[0], adjacency, target_blocks)
+    partial = blocks(partial, lists, *near, streams[1], adjacency, target_blocks)
 
     partial = partial.reshape(node_count, 2 * CHIPS, TILE, size)
     parts = combine(lax.all_to_all(partial, "node", 0, 0))

time: 99.4 us -> 100 us (level)
  waiting for transfers between devices: 26.9 us -> 19.1 us
  local copies, waits for them, and re-layouts: 3.49 us -> 9.82 us
  blocking collectives: 24.5 us -> 19 us
  Pallas kernels: 5.37 us -> 8.71 us
  starting transfers between devices: 37 us -> 40 us
    ppermute x18, waiting for transfers between devices: 19.4 us -> 11.6 us  [send(): return lax.ppermute(value, 'feat', route)]
    all_to_all x1, blocking collectives: 24.5 us -> 19 us  [on_device(): parts = combine(lax.all_to_all(partial, 'node', 0, 0))]
    unnamed x25 -> x29, local copies, waits for them, and re-layouts: 3.19 us -> 6.72 us
    pallas_call x1 -> x2, Pallas kernels: 2.31 us -> 5.65 us  [blocks(): pl.pallas_call(late_kernel if late else early_kernel, in_specs=[VMEM] * l...]
    all_to_all x1, starting transfers between devices: 10 us -> 13 us  [on_device(): parts = lax.all_to_all(parts, 'feat', 0, 0)]
    slice x2, local copies, waits for them, and re-layouts: 0.07 us -> 2.15 us  [on_device(): near = (rest_own[6 * UNITS:], rest[6 * UNITS:])]
    reduce_sum x0 -> x3, other arithmetic: none -> 1.07 us  [the longest x1 0.66 us: block_lists(): first = jnp.sum((key < slots).astype(jnp.int32))[None]]
  transfers between devices with their start and end apart: 19 -> 19, of which waited for: 8 -> 7; matrix products, arithmetic and copies ran while one was open for 1% -> 5% of each run, Pallas kernels for 0% -> 3%
where the time goes in v5:
time: 100 us; the launch traced here: 99.4 us
  starting transfers between devices  40 us (40%)
  waiting for transfers between devices  19.1 us (19%)
  blocking collectives  19 us (19%)
  local copies, waits for them, and re-layouts  9.82 us (10%)
  Pallas kernels  8.71 us (9%)
  other arithmetic  1.72 us (2%)
    ppermute x18, starting transfers between devices, send(): return lax.ppermute(value, 'feat', route)  27 us
    all_to_all x1, blocking collectives, on_device(): parts = combine(lax.all_to_all(partial, 'node', 0, 0))  19 us
    all_to_all x1, starting transfers between devices, on_device(): parts = lax.all_to_all(parts, 'feat', 0, 0)  13 us
    ppermute x18, waiting for transfers between devices, send(): return lax.ppermute(value, 'feat', route)  11.6 us
    all_to_all x1, waiting for transfers between devices, on_device(): parts = lax.all_to_all(parts, 'feat', 0, 0)  7.49 us
    unnamed x29, local copies, waits for them, and re-layouts  6.72 us
    pallas_call x2, Pallas kernels, blocks(): pl.pallas_call(late_kernel if late else early_kernel, in_specs=[VMEM] * l...  5.65 us
    slice x2, local copies, waits for them, and re-layouts, on_device(): near = (rest_own[6 * UNITS:], rest[6 * UNITS:])  2.15 us
  transfers between devices with their start and end apart: 19, of which 7 were waited for; matrix products, arithmetic and copies ran while one was open for 5% of the time, Pallas kernels for 3%

profile of v5, /device:TPU:1, one launch (start us, length us, event | category | flops | bytes accessed | tf_op | source)
XLA Modules:
  0.0 99.4 jit_solution(6407950044650244256)
XLA Ops:
  0.0 0.9 copy-done
  1.2 2.2 %copy-done.3 = bf16[8192,256]{1,0:T(8,128)(2,1)S(1)} copy-done((bf16[8192,256]{1,0:T(8,128)(2,1)S(1)}, bf16[8192,256]{1,0:T(8,128)(2,1)}, u32[]{:S(2)}) %copy-start.3) | copy-done | bytes 4194328
  3.3 1.3 %project.1 = (f32[16,8,1024]{2,1,0:T(8,128)S(1)}, f32[112,8,1024]{2,1,0:T(8,128)S(1)}, f32[16,8,1024]{2,1,0:T(8,128)S(1)}, f32[112,8,1024]{2,1,0:T(8,128)S(1)}) custom-call(bf16[256,256]{1,0:T(8,128)(2,1)S(1)} %convolution_convert_fusion.ordered, bf16[8192,256]{1,0:T(8,128)(2,1)S(1)} %copy-done.3), custom_call_target="tpu_custom_call" | custom-call | flops 1073741824 | bytes 12582912 | tf_op jit(solution)/shard_map/project/pallas_call | solution.py:42
  4.6 3.3 %collective-permute-start = (f32[16,8,1024]{2,1,0:T(8,128)S(1)}, f32[16,8,1024]{2,1,0:T(8,128)S(1)}, u32[]{:S(2)}, u32[]{:S(2)}) collective-permute-start(f32[16,8,1024]{2,1,0:T(8,128)S(1)} %get-tuple-element.44), channel_id=1, source_target_pairs={{0,1},{1,0},{2,3},{3,2},{4,5},{5,4},{6,7},{7,6},{8,9},{9,8},{10,11... | collective-permute-start | bytes 1572872 | tf_op jit(solution)/shard_map/ppermute | solution.py:280
  8.0 1.5 %collective-permute-done = f32[16,8,1024]{2,1,0:T(8,128)S(1)} collective-permute-done((f32[16,8,1024]{2,1,0:T(8,128)S(1)}, f32[16,8,1024]{2,1,0:T(8,128)S(1)}, u32[]{:S(2)}, u32[]{:S(2)}) %collective-permute-start) | collective-permute-done | bytes 524320 | tf_op jit(solution)/shard_map/ppermute | solution.py:280
  10.0 3.9 %collective-permute-start.3 = (f32[5,8,1024]{2,1,0:T(8,128)S(1)}, f32[5,8,1024]{2,1,0:T(8,128)S(1)}, u32[]{:S(2)}, u32[]{:S(2)}) collective-permute-start(f32[5,8,1024]{2,1,0:T(8,128)S(1)} %get-tuple-element.62), channel_id=1, source_target_pairs={{2,0},{3,1},{4,2},{5,3},{6,4},{7,5},{8,6},{9,7},{10,8},{11,9},{12,... | collective-permute-start | bytes 491528 | tf_op jit(solution)/shard_map/ppermute | solution.py:280
  14.1 2.7 %collective-permute-start.11 = (f32[3,8,1024]{2,1,0:T(8,128)S(1)}, f32[3,8,1024]{2,1,0:T(8,128)S(1)}, u32[]{:S(2)}, u32[]{:S(2)}) collective-permute-start(f32[3,8,1024]{2,1,0:T(8,128)S(1)} %get-tuple-element.76), channel_id=1, source_target_pairs={{2,0},{3,1},{4,2},{5,3},{6,4},{7,5},{8,6},{9,7},{10,8},{11,9},{12,... | collective-permute-start | bytes 294920 | tf_op jit(solution)/shard_map/ppermute | solution.py:280
  16.7 1.6 %collective-permute-done.2 = f32[5,8,1024]{2,1,0:T(8,128)S(1)} collective-permute-done((f32[5,8,1024]{2,1,0:T(8,128)S(1)}, f32[5,8,1024]{2,1,0:T(8,128)S(1)}, u32[]{:S(2)}, u32[]{:S(2)}) %collective-permute-start.2) | collective-permute-done | bytes 163872 | tf_op jit(solution)/shard_map/ppermute | solution.py:280
  18.5 2.7 %collective-permute-start.5 = (f32[10,8,1024]{2,1,0:T(8,128)S(1)}, f32[10,8,1024]{2,1,0:T(8,128)S(1)}, u32[]{:S(2)}, u32[]{:S(2)}) collective-permute-start(f32[10,8,1024]{2,1,0:T(8,128)S(1)} %get-tuple-element.64), channel_id=1, source_target_pairs={{2,0},{3,1},{4,2},{5,3},{6,4},{7,5},{8,6},{9,7},{10,8},{11,9},{12,... | collective-permute-start | bytes 983048 | tf_op jit(solution)/shard_map/ppermute | solution.py:280
  22.0 2.7 %collective-permute-start.13 = (f32[6,8,1024]{2,1,0:T(8,128)S(1)}, f32[6,8,1024]{2,1,0:T(8,128)S(1)}, u32[]{:S(2)}, u32[]{:S(2)}) collective-permute-start(f32[6,8,1024]{2,1,0:T(8,128)S(1)} %get-tuple-element.78), channel_id=1, source_target_pairs={{2,0},{3,1},{4,2},{5,3},{6,4},{7,5},{8,6},{9,7},{10,8},{11,9},{12,... | collective-permute-start | bytes 589832 | tf_op jit(solution)/shard_map/ppermute | solution.py:280
  24.7 3.2 %collective-permute-done.4 = f32[10,8,1024]{2,1,0:T(8,128)S(1)} collective-permute-done((f32[10,8,1024]{2,1,0:T(8,128)S(1)}, f32[10,8,1024]{2,1,0:T(8,128)S(1)}, u32[]{:S(2)}, u32[]{:S(2)}) %collective-permute-start.4) | collective-permute-done | bytes 327712 | tf_op jit(solution)/shard_map/ppermute | solution.py:280
  28.0 0.8 collective-permute-start.6
  28.8 1.9 %collective-permute-start.7 = (f32[10,8,1024]{2,1,0:T(8,128)S(1)}, f32[10,8,1024]{2,1,0:T(8,128)S(1)}, u32[]{:S(2)}, u32[]{:S(2)}) collective-permute-start(f32[10,8,1024]{2,1,0:T(8,128)S(1)} %get-tuple-element.66), channel_id=1, source_target_pairs={{2,0},{3,1},{4,2},{5,3},{6,4},{7,5},{8,6},{9,7},{10,8},{11,9},{12,... | collective-permute-start | bytes 983048 | tf_op jit(solution)/shard_map/ppermute | solution.py:280
  32.1 0.8 collective-permute-start.14
  32.9 1.9 %collective-permute-start.15 = (f32[6,8,1024]{2,1,0:T(8,128)S(1)}, f32[6,8,1024]{2,1,0:T(8,128)S(1)}, u32[]{:S(2)}, u32[]{:S(2)}) collective-permute-start(f32[6,8,1024]{2,1,0:T(8,128)S(1)} %get-tuple-element.80), channel_id=1, source_target_pairs={{2,0},{3,1},{4,2},{5,3},{6,4},{7,5},{8,6},{9,7},{10,8},{11,9},{12,... | collective-permute-start | bytes 589832 | tf_op jit(solution)/shard_map/ppermute | solution.py:280
  34.9 3.3 %collective-permute-done.6 = f32[10,8,1024]{2,1,0:T(8,128)S(1)} collective-permute-done((f32[10,8,1024]{2,1,0:T(8,128)S(1)}, f32[10,8,1024]{2,1,0:T(8,128)S(1)}, u32[]{:S(2)}, u32[]{:S(2)}) %collective-permute-start.6) | collective-permute-done | bytes 327712 | tf_op jit(solution)/shard_map/ppermute | solution.py:280
  38.3 0.7 collective-permute-start.8
  39.0 2.0 %collective-permute-start.9 = (f32[10,8,1024]{2,1,0:T(8,128)S(1)}, f32[10,8,1024]{2,1,0:T(8,128)S(1)}, u32[]{:S(2)}, u32[]{:S(2)}) collective-permute-start(f32[10,8,1024]{2,1,0:T(8,128)S(1)} %get-tuple-element.68), channel_id=1, source_target_pairs={{2,0},{3,1},{4,2},{5,3},{6,4},{7,5},{8,6},{9,7},{10,8},{11,9},{12,... | collective-permute-start | bytes 983048 | tf_op jit(solution)/shard_map/ppermute | solution.py:280
  41.0 1.3 %collective-permute-done.14 = f32[6,8,1024]{2,1,0:T(8,128)S(1)} collective-permute-done((f32[6,8,1024]{2,1,0:T(8,128)S(1)}, f32[6,8,1024]{2,1,0:T(8,128)S(1)}, u32[]{:S(2)}, u32[]{:S(2)}) %collective-permute-start.14) | collective-permute-done | bytes 196640 | tf_op jit(solution)/shard_map/ppermute | solution.py:280
  42.4 0.7 collective-permute-start.16
  43.1 2.0 %collective-permute-start.17 = (f32[6,8,1024]{2,1,0:T(8,128)S(1)}, f32[6,8,1024]{2,1,0:T(8,128)S(1)}, u32[]{:S(2)}, u32[]{:S(2)}) collective-permute-start(f32[6,8,1024]{2,1,0:T(8,128)S(1)} %get-tuple-element.82), channel_id=1, source_target_pairs={{2,0},{3,1},{4,2},{5,3},{6,4},{7,5},{8,6},{9,7},{10,8},{11,9},{12,... | collective-permute-start | bytes 589832 | tf_op jit(solution)/shard_map/ppermute | solution.py:280
  45.6 0.7 concatenate.3.lists
  46.3 1.1 %slice.102.own = f32[16,8,1024]{2,1,0:T(8,128)S(1)} slice(f32[112,8,1024]{2,1,0:T(8,128)} %copy-done.4), slice={[96:112], [0:8], [0:1024]} | slice | bytes 1048576 | tf_op jit(solution)/shard_map/slice | solution.py:313
  47.4 1.1 %slice.103.paired = f32[16,8,1024]{2,1,0:T(8,128)S(1)} slice(f32[112,8,1024]{2,1,0:T(8,128)} %copy-done.8), slice={[96:112], [0:8], [0:1024]} | slice | bytes 1048576 | tf_op jit(solution)/shard_map/slice | solution.py:313
  48.5 3.4 %copy-done.1 = bf16[256,128,128]{2,1,0:T(8,128)(2,1)S(1)} copy-done((bf16[256,128,128]{2,1,0:T(8,128)(2,1)S(1)}, bf16[256,128,128]{2,1,0:T(8,128)(2,1)}, u32[]{:S(2)}) %copy-start.1) | copy-done | bytes 8388632
  51.9 3.1 %early_blocks.1.before = f32[256,8,128]{2,1,0:T(8,128)S(1)} custom-call(s32[818]{0:T(1024)S(1)} %concatenate.3.lists, f32[16,8,1024]{2,1,0:T(8,128)S(1)} %slice.102.own, f32[16,8,1024]{2,1,0:T(8,128)S(1)} %slice.103.paired, f32[10,8,1024]{2,1,0:T(8,128)S(1)} %collective-permute-done.8.up, f32[10,8,1024]{2,1,0:T(8,128)S(1)} %collective-permute-done.9.down, ...), custom_call_target="tpu_custom_call" | custom-call | flops 268435456 | bytes 4194304 | tf_op jit(solution)/shard_map/early_blocks/pallas_call | solution.py:165
  55.3 2.5 %late_blocks.1 = f32[256,8,128]{2,1,0:T(8,128)S(1)} custom-call(f32[256,8,128]{2,1,0:T(8,128)S(1)} %early_blocks.1.before, s32[818]{0:T(1024)S(1)} %concatenate.3.lists, f32[16,8,1024]{2,1,0:T(8,128)S(1)} %slice.102.own, f32[16,8,1024]{2,1,0:T(8,128)S(1)} %slice.103.paired, f32[6,8,1024]{2,1,0:T(8,128)S(1)} %collective-permute-done.16.up, ...), custom_call_target="tpu_custom_call" | custom-call | flops 268435456 | bytes 4194304 | tf_op jit(solution)/shard_map/late_blocks/pallas_call | solution.py:165
  57.8 19.0 %all_to_all.10.parts = f32[16,16,8,128]{3,2,1,0:T(8,128)S(1)} all-to-all(f32[16,16,8,128]{3,2,1,0:T(8,128)S(1)} %bitcast.10), channel_id=1, replica_groups=mesh['node'=16,'feat'=16] {'node'}, dimensions={0} | all-to-all | bytes 2097152 | tf_op jit(solution)/shard_map/all_to_all | solution.py:318
  76.8 0.7 combine.1
  77.5 13.0 %all-to-all-start.1 = ((f32[16,8,128]{2,1,0:T(8,128)}), f32[16,8,128]{2,1,0:T(8,128)S(1)}, u32[]{:S(2)}, u32[]{:S(2)}) async-start(f32[16,8,128]{2,1,0:T(8,128)} %combine.1), calls=%async_computation.1 | async-start | bytes 131072 | tf_op jit(solution)/shard_map/all_to_all | solution.py:319
  90.9 7.5 %all-to-all-done.1.parts = f32[16,8,128]{2,1,0:T(8,128)S(1)} async-done(((f32[16,8,128]{2,1,0:T(8,128)}), f32[16,8,128]{2,1,0:T(8,128)S(1)}, u32[]{:S(2)}, u32[]{:S(2)}) %all-to-all-start.1) | async-done | bytes 65568 | tf_op jit(solution)/shard_map/all_to_all | solution.py:319
  98.4 1.0 %second.1 = f32[32,172]{1,0:T(8,128)} custom-call(f32[16,8,128]{2,1,0:T(8,128)S(1)} %all-to-all-done.1.parts, f32[256,1]{1,0:T(8,128)S(1)} %copy.18.bias_one, bf16[172,256]{1,0:T(8,128)(2,1)S(1)} %bitcast.11, bf16[172,256]{1,0:T(8,128)(2,1)S(1)} %bitcast.12, f32[1,172]{1,0:T(1,128)S(1)} %bitcast.13, s32[32,1]{1,0:T(8,128)S(1)} %copy.19.seeds, ...), custom_call_target="tpu_custom_call" | custom-call | tf_op jit(solution)/shard_map/second/pallas_call | solution.py:238
  (61 shorter events, 3.9 us)
Async XLA Ops:
  1.1 2.2 %copy-start.3 = (bf16[8192,256]{1,0:T(8,128)(2,1)S(1)}, bf16[8192,256]{1,0:T(8,128)(2,1)}, u32[]{:S(2)}) copy-start(bf16[8192,256]{1,0:T(8,128)(2,1)} %features.1) | copy-start | bytes 12582916
  3.3 17.8 %copy-start.12 = (s32[256]{0:T(256)S(1)}, s32[256]{0:T(256)}, u32[]{:S(2)}) copy-start(s32[256]{0:T(256)} %param.14) | copy-start | bytes 3076
  4.6 37.7 %copy-start.4 = (f32[112,8,1024]{2,1,0:T(8,128)}, f32[112,8,1024]{2,1,0:T(8,128)S(1)}, u32[]{:S(2)}) copy-start(f32[112,8,1024]{2,1,0:T(8,128)S(1)} %get-tuple-element.69) | copy-start | bytes 11010052
  4.6 4.9 %collective-permute-start = (f32[16,8,1024]{2,1,0:T(8,128)S(1)}, f32[16,8,1024]{2,1,0:T(8,128)S(1)}, u32[]{:S(2)}, u32[]{:S(2)}) collective-permute-start(f32[16,8,1024]{2,1,0:T(8,128)S(1)} %get-tuple-element.44), channel_id=1, source_target_pairs={{0,1},{1,0},{2,3},{3,2},{4,5},{5,4},{6,7},{7,6},{8,9},{9,8},{10,11... | collective-permute-start | bytes 1572872 | tf_op jit(solution)/shard_map/ppermute | solution.py:280
  9.5 7.2 %collective-permute-start.1 = (f32[112,8,1024]{2,1,0:T(8,128)S(1)}, f32[112,8,1024]{2,1,0:T(8,128)S(1)}, u32[]{:S(2)}, u32[]{:S(2)}) collective-permute-start(f32[112,8,1024]{2,1,0:T(8,128)S(1)} %get-tuple-element.46), channel_id=1, source_target_pairs={{0,1},{1,0},{2,3},{3,2},{4,5},{5,4},{6,7},{7,6},{8,9},{9,8},{10,11... | collective-permute-start | bytes 11010056 | tf_op jit(solution)/shard_map/ppermute | solution.py:280
  9.9 20.8 %copy-start.10 = (s32[256]{0:T(256)S(1)}, s32[256]{0:T(256)}, u32[]{:S(2)}) copy-start(s32[256]{0:T(256)} %param.15) | copy-start | bytes 3076
  9.9 8.4 %collective-permute-start.2 = (f32[5,8,1024]{2,1,0:T(8,128)S(1)}, f32[5,8,1024]{2,1,0:T(8,128)S(1)}, u32[]{:S(2)}, u32[]{:S(2)}) collective-permute-start(f32[5,8,1024]{2,1,0:T(8,128)S(1)} %get-tuple-element.61), channel_id=1, source_target_pairs={{0,2},{1,3},{2,4},{3,5},{4,6},{5,7},{6,8},{7,9},{8,10},{9,11},{10,... | collective-permute-start | bytes 491528 | tf_op jit(solution)/shard_map/ppermute | solution.py:280
  10.0 8.3 %collective-permute-start.3 = (f32[5,8,1024]{2,1,0:T(8,128)S(1)}, f32[5,8,1024]{2,1,0:T(8,128)S(1)}, u32[]{:S(2)}, u32[]{:S(2)}) collective-permute-start(f32[5,8,1024]{2,1,0:T(8,128)S(1)} %get-tuple-element.62), channel_id=1, source_target_pairs={{2,0},{3,1},{4,2},{5,3},{6,4},{7,5},{8,6},{9,7},{10,8},{11,9},{12,... | collective-permute-start | bytes 491528 | tf_op jit(solution)/shard_map/ppermute | solution.py:280
  14.0 7.9 %collective-permute-start.10 = (f32[3,8,1024]{2,1,0:T(8,128)S(1)}, f32[3,8,1024]{2,1,0:T(8,128)S(1)}, u32[]{:S(2)}, u32[]{:S(2)}) collective-permute-start(f32[3,8,1024]{2,1,0:T(8,128)S(1)} %get-tuple-element.75), channel_id=1, source_target_pairs={{0,2},{1,3},{2,4},{3,5},{4,6},{5,7},{6,8},{7,9},{8,10},{9,11},{10,... | collective-permute-start | bytes 294920 | tf_op jit(solution)/shard_map/ppermute | solution.py:280
  14.1 7.8 %collective-permute-start.11 = (f32[3,8,1024]{2,1,0:T(8,128)S(1)}, f32[3,8,1024]{2,1,0:T(8,128)S(1)}, u32[]{:S(2)}, u32[]{:S(2)}) collective-permute-start(f32[3,8,1024]{2,1,0:T(8,128)S(1)} %get-tuple-element.76), channel_id=1, source_target_pairs={{2,0},{3,1},{4,2},{5,3},{6,4},{7,5},{8,6},{9,7},{10,8},{11,9},{12,... | collective-permute-start | bytes 294920 | tf_op jit(solution)/shard_map/ppermute | solution.py:280
  16.7 28.9 %copy-start.8 = (f32[112,8,1024]{2,1,0:T(8,128)}, f32[112,8,1024]{2,1,0:T(8,128)S(1)}, u32[]{:S(2)}) copy-start(f32[112,8,1024]{2,1,0:T(8,128)S(1)} %collective-permute-done.1) | copy-start | bytes 11010052
  18.4 9.4 %collective-permute-start.4 = (f32[10,8,1024]{2,1,0:T(8,128)S(1)}, f32[10,8,1024]{2,1,0:T(8,128)S(1)}, u32[]{:S(2)}, u32[]{:S(2)}) collective-permute-start(f32[10,8,1024]{2,1,0:T(8,128)S(1)} %get-tuple-element.63), channel_id=1, source_target_pairs={{0,2},{1,3},{2,4},{3,5},{4,6},{5,7},{6,8},{7,9},{8,10},{9,11},{10,... | collective-permute-start | bytes 983048 | tf_op jit(solution)/shard_map/ppermute | solution.py:280
  18.5 9.3 %collective-permute-start.5 = (f32[10,8,1024]{2,1,0:T(8,128)S(1)}, f32[10,8,1024]{2,1,0:T(8,128)S(1)}, u32[]{:S(2)}, u32[]{:S(2)}) collective-permute-start(f32[10,8,1024]{2,1,0:T(8,128)S(1)} %get-tuple-element.64), channel_id=1, source_target_pairs={{2,0},{3,1},{4,2},{5,3},{6,4},{7,5},{8,6},{9,7},{10,8},{11,9},{12,... | collective-permute-start | bytes 983048 | tf_op jit(solution)/shard_map/ppermute | solution.py:280
  21.9 10.1 %collective-permute-start.12 = (f32[6,8,1024]{2,1,0:T(8,128)S(1)}, f32[6,8,1024]{2,1,0:T(8,128)S(1)}, u32[]{:S(2)}, u32[]{:S(2)}) collective-permute-start(f32[6,8,1024]{2,1,0:T(8,128)S(1)} %get-tuple-element.77), channel_id=1, source_target_pairs={{0,2},{1,3},{2,4},{3,5},{4,6},{5,7},{6,8},{7,9},{8,10},{9,11},{10,... | collective-permute-start | bytes 589832 | tf_op jit(solution)/shard_map/ppermute | solution.py:280
  22.0 10.0 %collective-permute-start.13 = (f32[6,8,1024]{2,1,0:T(8,128)S(1)}, f32[6,8,1024]{2,1,0:T(8,128)S(1)}, u32[]{:S(2)}, u32[]{:S(2)}) collective-permute-start(f32[6,8,1024]{2,1,0:T(8,128)S(1)} %get-tuple-element.78), channel_id=1, source_target_pairs={{2,0},{3,1},{4,2},{5,3},{6,4},{7,5},{8,6},{9,7},{10,8},{11,9},{12,... | collective-permute-start | bytes 589832 | tf_op jit(solution)/shard_map/ppermute | solution.py:280
  28.0 10.2 %collective-permute-start.6 = (f32[10,8,1024]{2,1,0:T(8,128)S(1)}, f32[10,8,1024]{2,1,0:T(8,128)S(1)}, u32[]{:S(2)}, u32[]{:S(2)}) collective-permute-start(f32[10,8,1024]{2,1,0:T(8,128)S(1)} %get-tuple-element.65), channel_id=1, source_target_pairs={{0,2},{1,3},{2,4},{3,5},{4,6},{5,7},{6,8},{7,9},{8,10},{9,11},{10,... | collective-permute-start | bytes 983048 | tf_op jit(solution)/shard_map/ppermute | solution.py:280
  28.8 9.3 %collective-permute-start.7 = (f32[10,8,1024]{2,1,0:T(8,128)S(1)}, f32[10,8,1024]{2,1,0:T(8,128)S(1)}, u32[]{:S(2)}, u32[]{:S(2)}) collective-permute-start(f32[10,8,1024]{2,1,0:T(8,128)S(1)} %get-tuple-element.66), channel_id=1, source_target_pairs={{2,0},{3,1},{4,2},{5,3},{6,4},{7,5},{8,6},{9,7},{10,8},{11,9},{12,... | collective-permute-start | bytes 983048 | tf_op jit(solution)/shard_map/ppermute | solution.py:280
  32.1 10.2 %collective-permute-start.14 = (f32[6,8,1024]{2,1,0:T(8,128)S(1)}, f32[6,8,1024]{2,1,0:T(8,128)S(1)}, u32[]{:S(2)}, u32[]{:S(2)}) collective-permute-start(f32[6,8,1024]{2,1,0:T(8,128)S(1)} %get-tuple-element.79), channel_id=1, source_target_pairs={{0,2},{1,3},{2,4},{3,5},{4,6},{5,7},{6,8},{7,9},{8,10},{9,11},{10,... | collective-permute-start | bytes 589832 | tf_op jit(solution)/shard_map/ppermute | solution.py:280
  32.9 9.4 %collective-permute-start.15 = (f32[6,8,1024]{2,1,0:T(8,128)S(1)}, f32[6,8,1024]{2,1,0:T(8,128)S(1)}, u32[]{:S(2)}, u32[]{:S(2)}) collective-permute-start(f32[6,8,1024]{2,1,0:T(8,128)S(1)} %get-tuple-element.80), channel_id=1, source_target_pairs={{2,0},{3,1},{4,2},{5,3},{6,4},{7,5},{8,6},{9,7},{10,8},{11,9},{12,... | collective-permute-start | bytes 589832 | tf_op jit(solution)/shard_map/ppermute | solution.py:280
  38.3 10.3 %collective-permute-start.8 = (f32[10,8,1024]{2,1,0:T(8,128)S(1)}, f32[10,8,1024]{2,1,0:T(8,128)S(1)}, u32[]{:S(2)}, u32[]{:S(2)}) collective-permute-start(f32[10,8,1024]{2,1,0:T(8,128)S(1)} %get-tuple-element.67), channel_id=1, source_target_pairs={{0,2},{1,3},{2,4},{3,5},{4,6},{5,7},{6,8},{7,9},{8,10},{9,11},{10,... | collective-permute-start | bytes 983048 | tf_op jit(solution)/shard_map/ppermute | solution.py:280
  39.0 9.5 %collective-permute-start.9 = (f32[10,8,1024]{2,1,0:T(8,128)S(1)}, f32[10,8,1024]{2,1,0:T(8,128)S(1)}, u32[]{:S(2)}, u32[]{:S(2)}) collective-permute-start(f32[10,8,1024]{2,1,0:T(8,128)S(1)} %get-tuple-element.68), channel_id=1, source_target_pairs={{2,0},{3,1},{4,2},{5,3},{6,4},{7,5},{8,6},{9,7},{10,8},{11,9},{12,... | collective-permute-start | bytes 983048 | tf_op jit(solution)/shard_map/ppermute | solution.py:280
  42.4 12.7 %collective-permute-start.16 = (f32[6,8,1024]{2,1,0:T(8,128)S(1)}, f32[6,8,1024]{2,1,0:T(8,128)S(1)}, u32[]{:S(2)}, u32[]{:S(2)}) collective-permute-start(f32[6,8,1024]{2,1,0:T(8,128)S(1)} %get-tuple-element.81), channel_id=1, source_target_pairs={{0,2},{1,3},{2,4},{3,5},{4,6},{5,7},{6,8},{7,9},{8,10},{9,11},{10,... | collective-permute-start | bytes 589832 | tf_op jit(solution)/shard_map/ppermute | solution.py:280
  43.1 12.0 %collective-permute-start.17 = (f32[6,8,1024]{2,1,0:T(8,128)S(1)}, f32[6,8,1024]{2,1,0:T(8,128)S(1)}, u32[]{:S(2)}, u32[]{:S(2)}) collective-permute-start(f32[6,8,1024]{2,1,0:T(8,128)S(1)} %get-tuple-element.82), channel_id=1, source_target_pairs={{2,0},{3,1},{4,2},{5,3},{6,4},{7,5},{8,6},{9,7},{10,8},{11,9},{12,... | collective-permute-start | bytes 589832 | tf_op jit(solution)/shard_map/ppermute | solution.py:280
  48.5 3.4 %copy-start.1 = (bf16[256,128,128]{2,1,0:T(8,128)(2,1)S(1)}, bf16[256,128,128]{2,1,0:T(8,128)(2,1)}, u32[]{:S(2)}) copy-start(bf16[256,128,128]{2,1,0:T(8,128)(2,1)} %adjacency.3) | copy-start | bytes 25165828
  51.9 3.4 %copy-start.2 = (bf16[256,128,128]{2,1,0:T(8,128)(2,1)S(1)}, bf16[256,128,128]{2,1,0:T(8,128)(2,1)}, u32[]{:S(2)}) copy-start(bf16[256,128,128]{2,1,0:T(8,128)(2,1)} %adjacency.3) | copy-start | bytes 25165828
  55.0 35.5 %copy-start.13 = (s32[32]{0:T(128)S(1)}, s32[32]{0:T(128)}, u32[]{:S(2)}) copy-start(s32[32]{0:T(128)} %param.22) | copy-start | bytes 388
  55.1 35.6 %copy-start.9 = (s32[32,8]{0,1:T(8,128)S(1)}, s32[32,8]{0,1:T(8,128)}, u32[]{:S(2)}) copy-start(s32[32,8]{0,1:T(8,128)} %param.23) | copy-start | bytes 3076
  55.1 35.7 %copy-start.11 = (f32[256]{0:T(256)S(1)}, f32[256]{0:T(256)}, u32[]{:S(2)}) copy-start(f32[256]{0:T(256)} %param.18) | copy-start | bytes 3076
  55.1 43.3 %copy-start.5 = (bf16[256,172]{0,1:T(8,128)(2,1)S(1)}, bf16[256,172]{0,1:T(8,128)(2,1)}, u32[]{:S(2)}) copy-start(bf16[256,172]{0,1:T(8,128)(2,1)} %param.19) | copy-start | bytes 264196
  55.1 43.3 %copy-start.6 = (bf16[256,172]{0,1:T(8,128)(2,1)S(1)}, bf16[256,172]{0,1:T(8,128)(2,1)}, u32[]{:S(2)}) copy-start(bf16[256,172]{0,1:T(8,128)(2,1)} %param.20) | copy-start | bytes 264196
  55.1 43.3 %copy-start.7 = (f32[172]{0:T(256)S(1)}, f32[172]{0:T(256)}, u32[]{:S(2)}) copy-start(f32[172]{0:T(256)} %param.21) | copy-start | bytes 2068
  77.5 20.8 %all-to-all-start.1 = ((f32[16,8,128]{2,1,0:T(8,128)}), f32[16,8,128]{2,1,0:T(8,128)S(1)}, u32[]{:S(2)}, u32[]{:S(2)}) async-start(f32[16,8,128]{2,1,0:T(8,128)} %combine.1), calls=%async_computation.1 | async-start | bytes 131072 | tf_op jit(solution)/shard_map/all_to_all | solution.py:319
  (1 other events, 0.9 us)

commit v6 on v5

--- a/solution.py
+++ b/solution.py
@@ -37,12 +37,12 @@
     hidden = ordered.shape[0]
     shapes = [
         jax.ShapeDtypeStruct((strips * UNITS, TILE, rows // RUNS), jnp.float32)
-        for strips in (1, CHIPS - 1)
+        for strips in (1, CHIPS - 2, 1)
     ] * 2
     return pl.pallas_call(
         project_kernel,
         in_specs=[VMEM] * 2,
-        out_specs=[VMEM] * 4,
+        out_specs=[VMEM] * 6,
         out_shape=shapes,
         name="project",
         compiler_params=pltpu.CompilerParams(vmem_limit_bytes=8 * 2**20),
@@ -89,10 +89,8 @@
     return jnp.concatenate([*pieces, first, block_count])
 
 
-def block_products(late, lists, own, paired, up, down, adjacency, out, held, table, landed):
-    copy = pltpu.make_async_copy(lists, table, landed)
-    copy.start()
-    slots, size, _ = adjacency.shape
+def block_products(late, own, paired, up, down, adjacency, out, held, table, start, end, loaded):
+    size = adjacency.shape[1]
     lanes = own.shape[2]
     begin = SPANS[late][0]
     for b in range(begin // 2 * lanes // size, SPANS[late][1] // 2 * lanes // size):
@@ -109,17 +107,18 @@
         upper = total.astype(jnp.bfloat16)
         held[b, : 2 * TILE] = upper
         held[b, 2 * TILE :] = (total - upper.astype(jnp.float32)).astype(jnp.bfloat16)
-    copy.wait()
-    step = slots + GROUP
-    counts = table[3 * step], table[3 * step + 1]
-    start = counts[0] if late else 0
-    end = counts[late]
+    loaded()
+    start, end = start(), end()
+    step = (table.shape[0] - 2) // 3
 
     def products(first):
         values = []
         for k in range(0, GROUP, 2):
             left = [held[table[step + first + k + j]] for j in range(2)]
-            right = [adjacency[table[2 * step + first + k + j]] for j in range(2)]
+            right = [
+                adjacency[first - start + k + j if late else table[2 * step + first + k + j]]
+                for j in range(2)
+            ]
             value = lax.dot_general(
                 jnp.concatenate(left, axis=0),
                 jnp.concatenate(right, axis=0),
@@ -148,38 +147,79 @@
     add(start + (jnp.maximum(groups, 1) - 1) * GROUP, last)
 
 
-def early_kernel(lists, own, paired, up, down, adjacency, out, held, table, landed):
+def early_kernel(lists, own, paired, up, down, adjacency, out, kept, held, table, landed):
+    copy = pltpu.make_async_copy(lists, table, landed)
+    copy.start()
     out[...] = jnp.zeros_like(out)
-    block_products(0, lists, own, paired, up, down, adjacency, out, held, table, landed)
-
-
-def late_kernel(before, lists, own, paired, up, down, adjacency, out, held, table, landed):
+    step = (table.shape[0] - 2) // 3
+    block_products(
+        0, own, paired, up, down, adjacency, out, held, table,
+        lambda: 0, lambda: table[3 * step], copy.wait,
+    )
+
+    def keep(i, carry):
+        kept[i - table[3 * step]] = adjacency[table[2 * step + i]]
+        return carry
+
+    lax.fori_loop(table[3 * step], table[3 * step + 1], keep, 0)
+
+
+def late_kernel(before, lists, own, paired, up, down, kept, out, held, table, landed):
+    copy = pltpu.make_async_copy(lists, table, landed)
+    copy.start()
     out[...] = before[...]
-    block_products(1, lists, own, paired, up, down, adjacency, out, held, table, landed)
-
-
-def blocks(before, lists, own, paired, stream, adjacency, target_blocks):
+    step = (table.shape[0] - 2) // 3
+    block_products(
+        1, own, paired, up, down, kept, out, held, table,
+        lambda: table[3 * step], lambda: table[3 * step + 1], copy.wait,
+    )
+
+
+def scratch_for(lists, own, size):
+    return [
+        pltpu.VMEM((RUNS * own.shape[2] // size, 4 * TILE, size), jnp.bfloat16),
+        pltpu.SMEM(lists.shape, jnp.int32),
+        pltpu.SemaphoreType.DMA,
+    ]
+
+
+def early_blocks(lists, own, paired, stream, adjacency, target_blocks):
     slots, size, _ = adjacency.shape
-    rows = RUNS * own.shape[2]
-    late = before is not None
-    return pl.pallas_call(
-        late_kernel if late else early_kernel,
-        in_specs=[VMEM] * late + [pl.BlockSpec(memory_space=pl.ANY)] + [VMEM] * 5,
-        out_specs=VMEM,
-        out_shape=jax.ShapeDtypeStruct((2 * target_blocks, TILE, size), jnp.float32),
-        scratch_shapes=[
-            pltpu.VMEM((rows // size, 4 * TILE, size), jnp.bfloat16),
-            pltpu.SMEM(lists.shape, jnp.int32),
-            pltpu.SemaphoreType.DMA,
+    return pl.pallas_call(
+        early_kernel,
+        in_specs=[pl.BlockSpec(memory_space=pl.ANY)] + [VMEM] * 5,
+        out_specs=[VMEM] * 2,
+        out_shape=[
+            jax.ShapeDtypeStruct((2 * target_blocks, TILE, size), jnp.float32),
+            jax.ShapeDtypeStruct((slots + GROUP, size, size), adjacency.dtype),
         ],
-        name="late_blocks" if late else "early_blocks",
+        scratch_shapes=scratch_for(lists, own, size),
+        name="early_blocks",
         compiler_params=pltpu.CompilerParams(vmem_limit_bytes=8 * 2**20),
         cost_estimate=pl.CostEstimate(
             flops=4 * slots * size * size * UNITS,
             bytes_accessed=slots * size * size,
             transcendentals=0,
         ),
-    )(*([before] if late else []), lists, own, paired, *stream, adjacency)
+    )(lists, own, paired, *stream, adjacency)
+
+
+def late_blocks(before, lists, own, paired, stream, kept):
+    slots, size, _ = kept.shape
+    return pl.pallas_call(
+        late_kernel,
+        in_specs=[VMEM, pl.BlockSpec(memory_space=pl.ANY)] + [VMEM] * 5,
+        out_specs=VMEM,
+        out_shape=jax.ShapeDtypeStruct(before.shape, jnp.float32),
+        scratch_shapes=scratch_for(lists, own, size),
+        name="late_blocks",
+        compiler_params=pltpu.CompilerParams(vmem_limit_bytes=8 * 2**20),
+        cost_estimate=pl.CostEstimate(
+            flops=4 * slots * size * size * UNITS,
+            bytes_accessed=slots * size * size,
+            transcendentals=0,
+        ),
+    )(before, lists, own, paired, *stream, kept)
 
 
 def combine_kernel(parts, out):
@@ -280,9 +320,12 @@
         return lax.ppermute(value, "feat", route)
 
     tie = lax.optimization_barrier
-    opposite, rest, opposite_own, rest_own = project(in_hop_order(layer_one), features)
+    opposite, rest, near, opposite_own, rest_own, near_own = project(
+        in_hop_order(layer_one), features
+    )
     opposite, rest = tie((send(opposite, pair), rest))
-    rest = send(rest, pair)
+    rest, near = tie((send(rest, pair), near))
+    near = send(near, pair)
 
     order = block_count
     streams = []
@@ -310,9 +353,8 @@
 
     early = SPANS[0][1] // 2 * (features.shape[0] // RUNS) // size
     lists = block_lists(target_block, source_block, block_count, early)
-    near = rest_own[6 * UNITS :], rest[6 * UNITS :]
-    partial = blocks(None, lists, *near, streams[0], adjacency, target_blocks)
-    partial = blocks(partial, lists, *near, streams[1], adjacency, target_blocks)
+    partial, kept = early_blocks(lists, near_own, near, streams[0], adjacency, target_blocks)
+    partial = late_blocks(partial, lists, near_own, near, streams[1], kept)
 
     partial = partial.reshape(node_count, 2 * CHIPS, TILE, size)
     parts = combine(lax.all_to_all(partial, "node", 0, 0))

time: 100 us -> 101 us (1.010)
  local copies, waits for them, and re-layouts: 9.82 us -> 7.42 us
  blocking collectives: 19 us -> 20.4 us
  starting transfers between devices: 40 us -> 41.3 us
    ppermute x18 -> x19, starting transfers between devices: 27 us -> 30.5 us  [send(): return lax.ppermute(value, 'feat', route)]
    all_to_all x1, starting transfers between devices: 13 us -> 10.8 us  [on_device(): parts = lax.all_to_all(parts, 'feat', 0, 0)]
    slice x2 -> x0, local copies, waits for them, and re-layouts: 2.15 us -> none  [on_device(): near = (rest_own[6 * UNITS:], rest[6 * UNITS:])]
    all_to_all x1, blocking collectives: 19 us -> 20.4 us  [on_device(): parts = combine(lax.all_to_all(partial, 'node', 0, 0))]
    unnamed x29 -> x23, local copies, waits for them, and re-layouts: 6.72 us -> 6.56 us
    ppermute x18 -> x19, waiting for transfers between devices: 11.6 us -> 11.7 us  [send(): return lax.ppermute(value, 'feat', route)]
  transfers between devices with their start and end apart: 19 -> 20, of which waited for: 7 -> 6; matrix products, arithmetic and copies ran while one was open for 5% -> 3% of each run, Pallas kernels for 3% -> 4%
where the time goes in v6:
time: 101 us
  starting transfers between devices  41.3 us (41%)
  blocking collectives  20.4 us (20%)
  waiting for transfers between devices  19.1 us (19%)
  Pallas kernels  8.98 us (9%)
  local copies, waits for them, and re-layouts  7.42 us (7%)
  other arithmetic  2.42 us (2%)
    ppermute x19, starting transfers between devices, send(): return lax.ppermute(value, 'feat', route)  30.5 us
    all_to_all x1, blocking collectives, on_device(): parts = combine(lax.all_to_all(partial, 'node', 0, 0))  20.4 us
    ppermute x19, waiting for transfers between devices, send(): return lax.ppermute(value, 'feat', route)  11.7 us
    all_to_all x1, starting transfers between devices, on_device(): parts = lax.all_to_all(parts, 'feat', 0, 0)  10.8 us
    all_to_all x1, waiting for transfers between devices, on_device(): parts = lax.all_to_all(parts, 'feat', 0, 0)  7.48 us
    unnamed x23, local copies, waits for them, and re-layouts  6.56 us
    pallas_call x1, Pallas kernels, early_blocks(): pl.pallas_call(early_kernel, in_specs=[pl.BlockSpec(memory_space=pl.ANY)]...  3.82 us
    pallas_call x1, Pallas kernels, late_blocks(): pl.pallas_call(late_kernel, in_specs=[VMEM, pl.BlockSpec(memory_space=pl....  2.11 us
  transfers between devices with their start and end apart: 20, of which 6 were waited for; matrix products, arithmetic and copies ran while one was open for 3% of the time, Pallas kernels for 4%

profile of v6, /device:TPU:1, one launch (start us, length us, event | category | flops | bytes accessed | tf_op | source)
XLA Modules:
  0.0 100.7 jit_solution(16745248511605327667)
XLA Ops:
  0.0 0.9 copy-done
  1.2 2.2 %copy-done.2 = bf16[8192,256]{1,0:T(8,128)(2,1)S(1)} copy-done((bf16[8192,256]{1,0:T(8,128)(2,1)S(1)}, bf16[8192,256]{1,0:T(8,128)(2,1)}, u32[]{:S(2)}) %copy-start.2) | copy-done | bytes 4194328
  3.3 1.3 %project.1 = (f32[16,8,1024]{2,1,0:T(8,128)S(1)}, f32[96,8,1024]{2,1,0:T(8,128)S(1)}, f32[16,8,1024]{2,1,0:T(8,128)S(1)}, f32[16,8,1024]{2,1,0:T(8,128)S(1)}, f3...) custom-call(bf16[256,256]{1,0:T(8,128)(2,1)S(1)} %convolution_convert_fusion.ordered, bf16[8192,256]{1,0:T(8,128)(2,1)S(1)} %copy-done.2), custom_call_target="tpu_custom_call" | custom-call | flops 1073741824 | bytes 12582912 | tf_op jit(solution)/shard_map/project/pallas_call | solution.py:42
  4.6 3.3 %collective-permute-start = (f32[16,8,1024]{2,1,0:T(8,128)S(1)}, f32[16,8,1024]{2,1,0:T(8,128)S(1)}, u32[]{:S(2)}, u32[]{:S(2)}) collective-permute-start(f32[16,8,1024]{2,1,0:T(8,128)S(1)} %get-tuple-element.51), channel_id=1, source_target_pairs={{0,1},{1,0},{2,3},{3,2},{4,5},{5,4},{6,7},{7,6},{8,9},{9,8},{10,11... | collective-permute-start | bytes 1572872 | tf_op jit(solution)/shard_map/ppermute | solution.py:320
  7.9 1.5 %collective-permute-done = f32[16,8,1024]{2,1,0:T(8,128)S(1)} collective-permute-done((f32[16,8,1024]{2,1,0:T(8,128)S(1)}, f32[16,8,1024]{2,1,0:T(8,128)S(1)}, u32[]{:S(2)}, u32[]{:S(2)}) %collective-permute-start) | collective-permute-done | bytes 524320 | tf_op jit(solution)/shard_map/ppermute | solution.py:320
  10.0 3.9 %collective-permute-start.4 = (f32[5,8,1024]{2,1,0:T(8,128)S(1)}, f32[5,8,1024]{2,1,0:T(8,128)S(1)}, u32[]{:S(2)}, u32[]{:S(2)}) collective-permute-start(f32[5,8,1024]{2,1,0:T(8,128)S(1)} %get-tuple-element.70), channel_id=1, source_target_pairs={{2,0},{3,1},{4,2},{5,3},{6,4},{7,5},{8,6},{9,7},{10,8},{11,9},{12,... | collective-permute-start | bytes 491528 | tf_op jit(solution)/shard_map/ppermute | solution.py:320
  14.0 2.7 %collective-permute-start.12 = (f32[3,8,1024]{2,1,0:T(8,128)S(1)}, f32[3,8,1024]{2,1,0:T(8,128)S(1)}, u32[]{:S(2)}, u32[]{:S(2)}) collective-permute-start(f32[3,8,1024]{2,1,0:T(8,128)S(1)} %get-tuple-element.87), channel_id=1, source_target_pairs={{2,0},{3,1},{4,2},{5,3},{6,4},{7,5},{8,6},{9,7},{10,8},{11,9},{12,... | collective-permute-start | bytes 294920 | tf_op jit(solution)/shard_map/ppermute | solution.py:320
  16.7 1.6 %collective-permute-done.3 = f32[5,8,1024]{2,1,0:T(8,128)S(1)} collective-permute-done((f32[5,8,1024]{2,1,0:T(8,128)S(1)}, f32[5,8,1024]{2,1,0:T(8,128)S(1)}, u32[]{:S(2)}, u32[]{:S(2)}) %collective-permute-start.3) | collective-permute-done | bytes 163872 | tf_op jit(solution)/shard_map/ppermute | solution.py:320
  18.4 2.7 %collective-permute-start.6 = (f32[10,8,1024]{2,1,0:T(8,128)S(1)}, f32[10,8,1024]{2,1,0:T(8,128)S(1)}, u32[]{:S(2)}, u32[]{:S(2)}) collective-permute-start(f32[10,8,1024]{2,1,0:T(8,128)S(1)} %get-tuple-element.72), channel_id=1, source_target_pairs={{2,0},{3,1},{4,2},{5,3},{6,4},{7,5},{8,6},{9,7},{10,8},{11,9},{12,... | collective-permute-start | bytes 983048 | tf_op jit(solution)/shard_map/ppermute | solution.py:320
  22.0 2.7 %collective-permute-start.14 = (f32[6,8,1024]{2,1,0:T(8,128)S(1)}, f32[6,8,1024]{2,1,0:T(8,128)S(1)}, u32[]{:S(2)}, u32[]{:S(2)}) collective-permute-start(f32[6,8,1024]{2,1,0:T(8,128)S(1)} %get-tuple-element.89), channel_id=1, source_target_pairs={{2,0},{3,1},{4,2},{5,3},{6,4},{7,5},{8,6},{9,7},{10,8},{11,9},{12,... | collective-permute-start | bytes 589832 | tf_op jit(solution)/shard_map/ppermute | solution.py:320
  24.6 3.2 %collective-permute-done.5 = f32[10,8,1024]{2,1,0:T(8,128)S(1)} collective-permute-done((f32[10,8,1024]{2,1,0:T(8,128)S(1)}, f32[10,8,1024]{2,1,0:T(8,128)S(1)}, u32[]{:S(2)}, u32[]{:S(2)}) %collective-permute-start.5) | collective-permute-done | bytes 327712 | tf_op jit(solution)/shard_map/ppermute | solution.py:320
  27.9 0.8 collective-permute-start.7
  28.7 1.9 %collective-permute-start.8 = (f32[10,8,1024]{2,1,0:T(8,128)S(1)}, f32[10,8,1024]{2,1,0:T(8,128)S(1)}, u32[]{:S(2)}, u32[]{:S(2)}) collective-permute-start(f32[10,8,1024]{2,1,0:T(8,128)S(1)} %get-tuple-element.74), channel_id=1, source_target_pairs={{2,0},{3,1},{4,2},{5,3},{6,4},{7,5},{8,6},{9,7},{10,8},{11,9},{12,... | collective-permute-start | bytes 983048 | tf_op jit(solution)/shard_map/ppermute | solution.py:320
  30.7 0.6 fusion.6
  31.3 4.3 %collective-permute-start.2 = (f32[16,8,1024]{2,1,0:T(8,128)S(1)}, f32[16,8,1024]{2,1,0:T(8,128)S(1)}, u32[]{:S(2)}, u32[]{:S(2)}) collective-permute-start(f32[16,8,1024]{2,1,0:T(8,128)S(1)} %get-tuple-element.55), channel_id=1, source_target_pairs={{0,1},{1,0},{2,3},{3,2},{4,5},{5,4},{6,7},{7,6},{8,9},{9,8},{10,11... | collective-permute-start | bytes 1572872 | tf_op jit(solution)/shard_map/ppermute | solution.py:320
  35.7 0.8 collective-permute-start.15
  36.5 1.9 %collective-permute-start.16 = (f32[6,8,1024]{2,1,0:T(8,128)S(1)}, f32[6,8,1024]{2,1,0:T(8,128)S(1)}, u32[]{:S(2)}, u32[]{:S(2)}) collective-permute-start(f32[6,8,1024]{2,1,0:T(8,128)S(1)} %get-tuple-element.91), channel_id=1, source_target_pairs={{2,0},{3,1},{4,2},{5,3},{6,4},{7,5},{8,6},{9,7},{10,8},{11,9},{12,... | collective-permute-start | bytes 589832 | tf_op jit(solution)/shard_map/ppermute | solution.py:320
  38.6 2.0 %collective-permute-start.10 = (f32[10,8,1024]{2,1,0:T(8,128)S(1)}, f32[10,8,1024]{2,1,0:T(8,128)S(1)}, u32[]{:S(2)}, u32[]{:S(2)}) collective-permute-start(f32[10,8,1024]{2,1,0:T(8,128)S(1)} %get-tuple-element.76), channel_id=1, source_target_pairs={{2,0},{3,1},{4,2},{5,3},{6,4},{7,5},{8,6},{9,7},{10,8},{11,9},{12,... | collective-permute-start | bytes 983048 | tf_op jit(solution)/shard_map/ppermute | solution.py:320
  40.6 3.4 %collective-permute-done.15 = f32[6,8,1024]{2,1,0:T(8,128)S(1)} collective-permute-done((f32[6,8,1024]{2,1,0:T(8,128)S(1)}, f32[6,8,1024]{2,1,0:T(8,128)S(1)}, u32[]{:S(2)}, u32[]{:S(2)}) %collective-permute-start.15) | collective-permute-done | bytes 196640 | tf_op jit(solution)/shard_map/ppermute | solution.py:320
  44.0 0.8 add_add_fusion.4
  44.8 1.1 %collective-permute-start.17 = (f32[6,8,1024]{2,1,0:T(8,128)}, f32[6,8,1024]{2,1,0:T(8,128)S(1)}, u32[]{:S(2)}, u32[]{:S(2)}) collective-permute-start(f32[6,8,1024]{2,1,0:T(8,128)} %get-tuple-element.92), channel_id=1, source_target_pairs={{0,2},{1,3},{2,4},{3,5},{4,6},{5,7},{6,8},{7,9},{8,10},{9,11},{10,... | collective-permute-start | bytes 589832 | tf_op jit(solution)/shard_map/ppermute | solution.py:320
  45.9 1.6 %collective-permute-start.18 = (f32[6,8,1024]{2,1,0:T(8,128)}, f32[6,8,1024]{2,1,0:T(8,128)S(1)}, u32[]{:S(2)}, u32[]{:S(2)}) collective-permute-start(f32[6,8,1024]{2,1,0:T(8,128)} %get-tuple-element.93), channel_id=1, source_target_pairs={{2,0},{3,1},{4,2},{5,3},{6,4},{7,5},{8,6},{9,7},{10,8},{11,9},{12,... | collective-permute-start | bytes 589832 | tf_op jit(solution)/shard_map/ppermute | solution.py:320
  47.9 0.6 concatenate.3.lists
  48.5 2.0 %collective-permute-done.10.down = f32[10,8,1024]{2,1,0:T(8,128)S(1)} collective-permute-done((f32[10,8,1024]{2,1,0:T(8,128)S(1)}, f32[10,8,1024]{2,1,0:T(8,128)S(1)}, u32[]{:S(2)}, u32[]{:S(2)}) %collective-permute-start.10) | collective-permute-done | bytes 327712 | tf_op jit(solution)/shard_map/ppermute | solution.py:320
  50.5 3.4 %copy-done.1 = bf16[256,128,128]{2,1,0:T(8,128)(2,1)S(1)} copy-done((bf16[256,128,128]{2,1,0:T(8,128)(2,1)S(1)}, bf16[256,128,128]{2,1,0:T(8,128)(2,1)}, u32[]{:S(2)}) %copy-start.1) | copy-done | bytes 8388632
  53.9 3.8 %early_blocks.1 = (f32[256,8,128]{2,1,0:T(8,128)S(1)}, bf16[272,128,128]{2,1,0:T(8,128)(2,1)S(1)}) custom-call(s32[818]{0:T(1024)S(1)} %concatenate.3.lists, f32[16,8,1024]{2,1,0:T(8,128)S(1)} %get-tuple-element.50.own, f32[16,8,1024]{2,1,0:T(8,128)S(1)} %collective-permute-done.2.paired, f32[10,8,1024]{2,1,0:T(8,128)S(1)} %collective-permute-done.9.up, ...), custom_call_target="tpu_custom_call" | custom-call | flops 268435456 | bytes 4194304 | tf_op jit(solution)/shard_map/early_blocks/pallas_call | solution.py:188
  57.8 2.1 %late_blocks.1 = f32[256,8,128]{2,1,0:T(8,128)S(1)} custom-call(f32[256,8,128]{2,1,0:T(8,128)S(1)} %get-tuple-element.77.before, s32[818]{0:T(1024)S(1)} %concatenate.3.lists, f32[16,8,1024]{2,1,0:T(8,128)S(1)} %get-tuple-element.50.own, f32[16,8,1024]{2,1,0:T(8,128)S(1)} %collective-permute-done.2.paired, f32[6,8,1024]{2,1,0:T(8,128)S(1)} %collective-permute-done.17.up, ...), custom_call_target="tpu_custom_call" | custom-call | flops 285212672 | bytes 4456448 | tf_op jit(solution)/shard_map/late_blocks/pallas_call | solution.py:209
  60.0 20.4 %all_to_all.10.parts = f32[16,16,8,128]{3,2,1,0:T(8,128)S(1)} all-to-all(f32[16,16,8,128]{3,2,1,0:T(8,128)S(1)} %bitcast.10), channel_id=1, replica_groups=mesh['node'=16,'feat'=16] {'node'}, dimensions={0} | all-to-all | bytes 2097152 | tf_op jit(solution)/shard_map/all_to_all | solution.py:360
  80.3 0.7 combine.1
  81.1 10.8 %all-to-all-start.1 = ((f32[16,8,128]{2,1,0:T(8,128)}), f32[16,8,128]{2,1,0:T(8,128)S(1)}, u32[]{:S(2)}, u32[]{:S(2)}) async-start(f32[16,8,128]{2,1,0:T(8,128)} %combine.1), calls=%async_computation.1 | async-start | bytes 131072 | tf_op jit(solution)/shard_map/all_to_all | solution.py:361
  92.2 7.5 %all-to-all-done.1.parts = f32[16,8,128]{2,1,0:T(8,128)S(1)} async-done(((f32[16,8,128]{2,1,0:T(8,128)}), f32[16,8,128]{2,1,0:T(8,128)S(1)}, u32[]{:S(2)}, u32[]{:S(2)}) %all-to-all-start.1) | async-done | bytes 65568 | tf_op jit(solution)/shard_map/all_to_all | solution.py:361
  99.7 1.0 %second.1 = f32[32,172]{1,0:T(8,128)} custom-call(f32[16,8,128]{2,1,0:T(8,128)S(1)} %all-to-all-done.1.parts, f32[256,1]{1,0:T(8,128)S(1)} %copy.18.bias_one, bf16[172,256]{1,0:T(8,128)(2,1)S(1)} %bitcast.11, bf16[172,256]{1,0:T(8,128)(2,1)S(1)} %bitcast.12, f32[1,172]{1,0:T(1,128)S(1)} %bitcast.13, s32[32,1]{1,0:T(8,128)S(1)} %copy.19.seeds, ...), custom_call_target="tpu_custom_call" | custom-call | tf_op jit(solution)/shard_map/second/pallas_call | solution.py:278
  (55 shorter events, 2.3 us)
Async XLA Ops:
  0.0 0.9 copy-start
  1.1 2.2 %copy-start.2 = (bf16[8192,256]{1,0:T(8,128)(2,1)S(1)}, bf16[8192,256]{1,0:T(8,128)(2,1)}, u32[]{:S(2)}) copy-start(bf16[8192,256]{1,0:T(8,128)(2,1)} %features.1) | copy-start | bytes 12582916
  3.3 17.8 %copy-start.9 = (s32[256]{0:T(256)S(1)}, s32[256]{0:T(256)}, u32[]{:S(2)}) copy-start(s32[256]{0:T(256)} %param.14) | copy-start | bytes 3076
  4.6 4.9 %collective-permute-start = (f32[16,8,1024]{2,1,0:T(8,128)S(1)}, f32[16,8,1024]{2,1,0:T(8,128)S(1)}, u32[]{:S(2)}, u32[]{:S(2)}) collective-permute-start(f32[16,8,1024]{2,1,0:T(8,128)S(1)} %get-tuple-element.51), channel_id=1, source_target_pairs={{0,1},{1,0},{2,3},{3,2},{4,5},{5,4},{6,7},{7,6},{8,9},{9,8},{10,11... | collective-permute-start | bytes 1572872 | tf_op jit(solution)/shard_map/ppermute | solution.py:320
  9.5 7.2 %collective-permute-start.1 = (f32[96,8,1024]{2,1,0:T(8,128)S(1)}, f32[96,8,1024]{2,1,0:T(8,128)S(1)}, u32[]{:S(2)}, u32[]{:S(2)}) collective-permute-start(f32[96,8,1024]{2,1,0:T(8,128)S(1)} %get-tuple-element.53), channel_id=1, source_target_pairs={{0,1},{1,0},{2,3},{3,2},{4,5},{5,4},{6,7},{7,6},{8,9},{9,8},{10,11... | collective-permute-start | bytes 9437192 | tf_op jit(solution)/shard_map/ppermute | solution.py:320
  9.9 8.4 %collective-permute-start.3 = (f32[5,8,1024]{2,1,0:T(8,128)S(1)}, f32[5,8,1024]{2,1,0:T(8,128)S(1)}, u32[]{:S(2)}, u32[]{:S(2)}) collective-permute-start(f32[5,8,1024]{2,1,0:T(8,128)S(1)} %get-tuple-element.69), channel_id=1, source_target_pairs={{0,2},{1,3},{2,4},{3,5},{4,6},{5,7},{6,8},{7,9},{8,10},{9,11},{10,... | collective-permute-start | bytes 491528 | tf_op jit(solution)/shard_map/ppermute | solution.py:320
  10.0 8.3 %collective-permute-start.4 = (f32[5,8,1024]{2,1,0:T(8,128)S(1)}, f32[5,8,1024]{2,1,0:T(8,128)S(1)}, u32[]{:S(2)}, u32[]{:S(2)}) collective-permute-start(f32[5,8,1024]{2,1,0:T(8,128)S(1)} %get-tuple-element.70), channel_id=1, source_target_pairs={{2,0},{3,1},{4,2},{5,3},{6,4},{7,5},{8,6},{9,7},{10,8},{11,9},{12,... | collective-permute-start | bytes 491528 | tf_op jit(solution)/shard_map/ppermute | solution.py:320
  13.9 7.8 %collective-permute-start.11 = (f32[3,8,1024]{2,1,0:T(8,128)S(1)}, f32[3,8,1024]{2,1,0:T(8,128)S(1)}, u32[]{:S(2)}, u32[]{:S(2)}) collective-permute-start(f32[3,8,1024]{2,1,0:T(8,128)S(1)} %get-tuple-element.86), channel_id=1, source_target_pairs={{0,2},{1,3},{2,4},{3,5},{4,6},{5,7},{6,8},{7,9},{8,10},{9,11},{10,... | collective-permute-start | bytes 294920 | tf_op jit(solution)/shard_map/ppermute | solution.py:320
  14.0 7.8 %collective-permute-start.12 = (f32[3,8,1024]{2,1,0:T(8,128)S(1)}, f32[3,8,1024]{2,1,0:T(8,128)S(1)}, u32[]{:S(2)}, u32[]{:S(2)}) collective-permute-start(f32[3,8,1024]{2,1,0:T(8,128)S(1)} %get-tuple-element.87), channel_id=1, source_target_pairs={{2,0},{3,1},{4,2},{5,3},{6,4},{7,5},{8,6},{9,7},{10,8},{11,9},{12,... | collective-permute-start | bytes 294920 | tf_op jit(solution)/shard_map/ppermute | solution.py:320
  16.7 14.0 %copy-start.7 = (s32[256]{0:T(256)S(1)}, s32[256]{0:T(256)}, u32[]{:S(2)}) copy-start(s32[256]{0:T(256)} %param.15) | copy-start | bytes 3076
  18.4 9.4 %collective-permute-start.5 = (f32[10,8,1024]{2,1,0:T(8,128)S(1)}, f32[10,8,1024]{2,1,0:T(8,128)S(1)}, u32[]{:S(2)}, u32[]{:S(2)}) collective-permute-start(f32[10,8,1024]{2,1,0:T(8,128)S(1)} %get-tuple-element.71), channel_id=1, source_target_pairs={{0,2},{1,3},{2,4},{3,5},{4,6},{5,7},{6,8},{7,9},{8,10},{9,11},{10,... | collective-permute-start | bytes 983048 | tf_op jit(solution)/shard_map/ppermute | solution.py:320
  18.4 9.3 %collective-permute-start.6 = (f32[10,8,1024]{2,1,0:T(8,128)S(1)}, f32[10,8,1024]{2,1,0:T(8,128)S(1)}, u32[]{:S(2)}, u32[]{:S(2)}) collective-permute-start(f32[10,8,1024]{2,1,0:T(8,128)S(1)} %get-tuple-element.72), channel_id=1, source_target_pairs={{2,0},{3,1},{4,2},{5,3},{6,4},{7,5},{8,6},{9,7},{10,8},{11,9},{12,... | collective-permute-start | bytes 983048 | tf_op jit(solution)/shard_map/ppermute | solution.py:320
  21.9 13.8 %collective-permute-start.13 = (f32[6,8,1024]{2,1,0:T(8,128)S(1)}, f32[6,8,1024]{2,1,0:T(8,128)S(1)}, u32[]{:S(2)}, u32[]{:S(2)}) collective-permute-start(f32[6,8,1024]{2,1,0:T(8,128)S(1)} %get-tuple-element.88), channel_id=1, source_target_pairs={{0,2},{1,3},{2,4},{3,5},{4,6},{5,7},{6,8},{7,9},{8,10},{9,11},{10,... | collective-permute-start | bytes 589832 | tf_op jit(solution)/shard_map/ppermute | solution.py:320
  22.0 13.7 %collective-permute-start.14 = (f32[6,8,1024]{2,1,0:T(8,128)S(1)}, f32[6,8,1024]{2,1,0:T(8,128)S(1)}, u32[]{:S(2)}, u32[]{:S(2)}) collective-permute-start(f32[6,8,1024]{2,1,0:T(8,128)S(1)} %get-tuple-element.89), channel_id=1, source_target_pairs={{2,0},{3,1},{4,2},{5,3},{6,4},{7,5},{8,6},{9,7},{10,8},{11,9},{12,... | collective-permute-start | bytes 589832 | tf_op jit(solution)/shard_map/ppermute | solution.py:320
  27.9 10.5 %collective-permute-start.7 = (f32[10,8,1024]{2,1,0:T(8,128)S(1)}, f32[10,8,1024]{2,1,0:T(8,128)S(1)}, u32[]{:S(2)}, u32[]{:S(2)}) collective-permute-start(f32[10,8,1024]{2,1,0:T(8,128)S(1)} %get-tuple-element.73), channel_id=1, source_target_pairs={{0,2},{1,3},{2,4},{3,5},{4,6},{5,7},{6,8},{7,9},{8,10},{9,11},{10,... | collective-permute-start | bytes 983048 | tf_op jit(solution)/shard_map/ppermute | solution.py:320
  28.7 9.7 %collective-permute-start.8 = (f32[10,8,1024]{2,1,0:T(8,128)S(1)}, f32[10,8,1024]{2,1,0:T(8,128)S(1)}, u32[]{:S(2)}, u32[]{:S(2)}) collective-permute-start(f32[10,8,1024]{2,1,0:T(8,128)S(1)} %get-tuple-element.74), channel_id=1, source_target_pairs={{2,0},{3,1},{4,2},{5,3},{6,4},{7,5},{8,6},{9,7},{10,8},{11,9},{12,... | collective-permute-start | bytes 983048 | tf_op jit(solution)/shard_map/ppermute | solution.py:320
  31.3 17.2 %collective-permute-start.2 = (f32[16,8,1024]{2,1,0:T(8,128)S(1)}, f32[16,8,1024]{2,1,0:T(8,128)S(1)}, u32[]{:S(2)}, u32[]{:S(2)}) collective-permute-start(f32[16,8,1024]{2,1,0:T(8,128)S(1)} %get-tuple-element.55), channel_id=1, source_target_pairs={{0,1},{1,0},{2,3},{3,2},{4,5},{5,4},{6,7},{7,6},{8,9},{9,8},{10,11... | collective-permute-start | bytes 1572872 | tf_op jit(solution)/shard_map/ppermute | solution.py:320
  35.7 8.3 %collective-permute-start.15 = (f32[6,8,1024]{2,1,0:T(8,128)S(1)}, f32[6,8,1024]{2,1,0:T(8,128)S(1)}, u32[]{:S(2)}, u32[]{:S(2)}) collective-permute-start(f32[6,8,1024]{2,1,0:T(8,128)S(1)} %get-tuple-element.90), channel_id=1, source_target_pairs={{0,2},{1,3},{2,4},{3,5},{4,6},{5,7},{6,8},{7,9},{8,10},{9,11},{10,... | collective-permute-start | bytes 589832 | tf_op jit(solution)/shard_map/ppermute | solution.py:320
  36.5 7.5 %collective-permute-start.16 = (f32[6,8,1024]{2,1,0:T(8,128)S(1)}, f32[6,8,1024]{2,1,0:T(8,128)S(1)}, u32[]{:S(2)}, u32[]{:S(2)}) collective-permute-start(f32[6,8,1024]{2,1,0:T(8,128)S(1)} %get-tuple-element.91), channel_id=1, source_target_pairs={{2,0},{3,1},{4,2},{5,3},{6,4},{7,5},{8,6},{9,7},{10,8},{11,9},{12,... | collective-permute-start | bytes 589832 | tf_op jit(solution)/shard_map/ppermute | solution.py:320
  38.6 11.9 %collective-permute-start.10 = (f32[10,8,1024]{2,1,0:T(8,128)S(1)}, f32[10,8,1024]{2,1,0:T(8,128)S(1)}, u32[]{:S(2)}, u32[]{:S(2)}) collective-permute-start(f32[10,8,1024]{2,1,0:T(8,128)S(1)} %get-tuple-element.76), channel_id=1, source_target_pairs={{2,0},{3,1},{4,2},{5,3},{6,4},{7,5},{8,6},{9,7},{10,8},{11,9},{12,... | collective-permute-start | bytes 983048 | tf_op jit(solution)/shard_map/ppermute | solution.py:320
  40.6 9.9 %collective-permute-start.9 = (f32[10,8,1024]{2,1,0:T(8,128)S(1)}, f32[10,8,1024]{2,1,0:T(8,128)S(1)}, u32[]{:S(2)}, u32[]{:S(2)}) collective-permute-start(f32[10,8,1024]{2,1,0:T(8,128)S(1)} %get-tuple-element.75), channel_id=1, source_target_pairs={{0,2},{1,3},{2,4},{3,5},{4,6},{5,7},{6,8},{7,9},{8,10},{9,11},{10,... | collective-permute-start | bytes 983048 | tf_op jit(solution)/shard_map/ppermute | solution.py:320
  44.8 13.0 %collective-permute-start.17 = (f32[6,8,1024]{2,1,0:T(8,128)}, f32[6,8,1024]{2,1,0:T(8,128)S(1)}, u32[]{:S(2)}, u32[]{:S(2)}) collective-permute-start(f32[6,8,1024]{2,1,0:T(8,128)} %get-tuple-element.92), channel_id=1, source_target_pairs={{0,2},{1,3},{2,4},{3,5},{4,6},{5,7},{6,8},{7,9},{8,10},{9,11},{10,... | collective-permute-start | bytes 589832 | tf_op jit(solution)/shard_map/ppermute | solution.py:320
  45.9 11.9 %collective-permute-start.18 = (f32[6,8,1024]{2,1,0:T(8,128)}, f32[6,8,1024]{2,1,0:T(8,128)S(1)}, u32[]{:S(2)}, u32[]{:S(2)}) collective-permute-start(f32[6,8,1024]{2,1,0:T(8,128)} %get-tuple-element.93), channel_id=1, source_target_pairs={{2,0},{3,1},{4,2},{5,3},{6,4},{7,5},{8,6},{9,7},{10,8},{11,9},{12,... | collective-permute-start | bytes 589832 | tf_op jit(solution)/shard_map/ppermute | solution.py:320
  50.5 3.4 %copy-start.1 = (bf16[256,128,128]{2,1,0:T(8,128)(2,1)S(1)}, bf16[256,128,128]{2,1,0:T(8,128)(2,1)}, u32[]{:S(2)}) copy-start(bf16[256,128,128]{2,1,0:T(8,128)(2,1)} %adjacency.1) | copy-start | bytes 25165828
  59.9 32.0 %copy-start.8 = (f32[256]{0:T(256)S(1)}, f32[256]{0:T(256)}, u32[]{:S(2)}) copy-start(f32[256]{0:T(256)} %param.18) | copy-start | bytes 3076
  59.9 32.1 %copy-start.10 = (s32[32]{0:T(128)S(1)}, s32[32]{0:T(128)}, u32[]{:S(2)}) copy-start(s32[32]{0:T(128)} %param.22) | copy-start | bytes 388
  59.9 32.2 %copy-start.6 = (s32[32,8]{0,1:T(8,128)S(1)}, s32[32,8]{0,1:T(8,128)}, u32[]{:S(2)}) copy-start(s32[32,8]{0,1:T(8,128)} %param.23) | copy-start | bytes 3076
  59.9 39.8 %copy-start.3 = (bf16[256,172]{0,1:T(8,128)(2,1)S(1)}, bf16[256,172]{0,1:T(8,128)(2,1)}, u32[]{:S(2)}) copy-start(bf16[256,172]{0,1:T(8,128)(2,1)} %param.19) | copy-start | bytes 264196
  59.9 39.8 %copy-start.4 = (bf16[256,172]{0,1:T(8,128)(2,1)S(1)}, bf16[256,172]{0,1:T(8,128)(2,1)}, u32[]{:S(2)}) copy-start(bf16[256,172]{0,1:T(8,128)(2,1)} %param.20) | copy-start | bytes 264196
  59.9 39.8 %copy-start.5 = (f32[172]{0:T(256)S(1)}, f32[172]{0:T(256)}, u32[]{:S(2)}) copy-start(f32[172]{0:T(256)} %param.21) | copy-start | bytes 2068
  81.1 18.6 %all-to-all-start.1 = ((f32[16,8,128]{2,1,0:T(8,128)}), f32[16,8,128]{2,1,0:T(8,128)S(1)}, u32[]{:S(2)}, u32[]{:S(2)}) async-start(f32[16,8,128]{2,1,0:T(8,128)} %combine.1), calls=%async_computation.1 | async-start | bytes 131072 | tf_op jit(solution)/shard_map/all_to_all | solution.py:361

commit v7 on v6

--- a/solution.py
+++ b/solution.py
@@ -1,3 +1,5 @@
+import functools
+
 import jax
 import jax.numpy as jnp
 from jax import lax
@@ -13,6 +15,7 @@
 GROUP = 16
 NT = (((1,), (1,)), ((), ()))
 VMEM = pl.BlockSpec(memory_space=pltpu.VMEM)
+SMEM = pl.BlockSpec(memory_space=pltpu.SMEM)
 
 UNITS = 2 * RUNS
 
@@ -37,12 +40,12 @@
     hidden = ordered.shape[0]
     shapes = [
         jax.ShapeDtypeStruct((strips * UNITS, TILE, rows // RUNS), jnp.float32)
-        for strips in (1, CHIPS - 2, 1)
+        for strips in (1, CHIPS - 1)
     ] * 2
     return pl.pallas_call(
         project_kernel,
         in_specs=[VMEM] * 2,
-        out_specs=[VMEM] * 6,
+        out_specs=[VMEM] * 4,
         out_shape=shapes,
         name="project",
         compiler_params=pltpu.CompilerParams(vmem_limit_bytes=8 * 2**20),
@@ -70,35 +73,53 @@
     )
 
 
+def lists_kernel(early, count, target, source, out):
+    slots = target.shape[1]
+    slot = lax.broadcasted_iota(jnp.int32, (1, slots), 1)
+    late = (source[...] >= early).astype(jnp.int32)
+    key = jnp.where(slot < count[0], late, 2) * slots + slot
+    across = jnp.broadcast_to(key, (slots, slots))
+    rank = jnp.sum((across.T < across).astype(jnp.float32), axis=0, keepdims=True)
+    first = jnp.sum((key < slots).astype(jnp.float32), axis=1, keepdims=True)
+    place = 2 * target[...] - target[...] % CHIPS
+    row = lax.broadcasted_iota(jnp.int32, (out.shape[0], slots), 0)
+    values = jnp.zeros(row.shape, jnp.float32)
+    for k, value in enumerate((place, source[...], slot, first, count[0].astype(jnp.float32))):
+        if k < 3:
+            value = value.astype(jnp.float32)
+        values = jnp.where(row == k, value, values)
+    at = lax.broadcasted_iota(jnp.int32, (out.shape[1], slots), 0).astype(jnp.float32) == rank
+    out[...] = lax.dot_general(
+        values.astype(jnp.bfloat16),
+        at.astype(jnp.bfloat16),
+        NT,
+        preferred_element_type=jnp.float32,
+    ).astype(jnp.int32)
+
+
 def block_lists(target_block, source_block, block_count, early):
-    place = 2 * target_block - target_block % CHIPS
     slots = target_block.shape[0]
-    slot = jnp.arange(slots, dtype=jnp.int32)
-    live = slot < block_count[0]
-    key = jnp.where(live, (source_block >= early).astype(jnp.int32), 2)
-    key = key * slots + slot
-    rank = jnp.sum((key[None, :] < key[:, None]).astype(jnp.int32), axis=1)
-    at = rank[None, :] == slot[:, None]
-    lists = [
-        jnp.sum(jnp.where(at, values[None, :], 0), axis=1)
-        for values in (place, source_block, slot)
-    ]
-    first = jnp.sum((key < slots).astype(jnp.int32))[None]
-    spare = jnp.zeros((GROUP,), jnp.int32)
-    pieces = [piece for values in lists for piece in (values, spare)]
-    return jnp.concatenate([*pieces, first, block_count])
-
-
-def block_products(late, own, paired, up, down, adjacency, out, held, table, start, end, loaded):
+    return pl.pallas_call(
+        functools.partial(lists_kernel, early),
+        in_specs=[SMEM] + [VMEM] * 2,
+        out_specs=VMEM,
+        out_shape=jax.ShapeDtypeStruct((TILE, slots + 128), jnp.int32),
+        name="block_lists",
+        compiler_params=pltpu.CompilerParams(vmem_limit_bytes=4 * 2**20),
+    )(block_count, target_block[None, :], source_block[None, :])
+
+
+def block_products(late, table, own, paired, up, down, adjacency, out, held):
     size = adjacency.shape[1]
     lanes = own.shape[2]
+    base = own.shape[0] - UNITS
     begin = SPANS[late][0]
     for b in range(begin // 2 * lanes // size, SPANS[late][1] // 2 * lanes // size):
         run, at = divmod(b * size, lanes)
         at = slice(at, at + size)
         total = jnp.concatenate(
             [
-                (own[unit, :, at] + paired[unit, :, at])
+                (own[base + unit, :, at] + paired[base + unit, :, at])
                 + (up[unit - begin, :, at] + down[unit - begin, :, at])
                 for unit in (2 * run, 2 * run + 1)
             ],
@@ -107,16 +128,15 @@
         upper = total.astype(jnp.bfloat16)
         held[b, : 2 * TILE] = upper
         held[b, 2 * TILE :] = (total - upper.astype(jnp.float32)).astype(jnp.bfloat16)
-    loaded()
-    start, end = start(), end()
-    step = (table.shape[0] - 2) // 3
+    start = table[3, 0] if late else 0
+    end = table[4 if late else 3, 0]
 
     def products(first):
         values = []
         for k in range(0, GROUP, 2):
-            left = [held[table[step + first + k + j]] for j in range(2)]
+            left = [held[table[1, first + k + j]] for j in range(2)]
             right = [
-                adjacency[first - start + k + j if late else table[2 * step + first + k + j]]
+                adjacency[first - start + k + j if late else table[2, first + k + j]]
                 for j in range(2)
             ]
             value = lax.dot_general(
@@ -132,7 +152,7 @@
 
     def add(first, values):
         for k in range(GROUP):
-            place = table[first + k]
+            place = table[0, first + k]
             value = jnp.where(first + k < end, values[k], 0.0)
             out[place] += value[:TILE]
             out[place + CHIPS] += value[TILE:]
@@ -147,53 +167,33 @@
     add(start + (jnp.maximum(groups, 1) - 1) * GROUP, last)
 
 
-def early_kernel(lists, own, paired, up, down, adjacency, out, kept, held, table, landed):
-    copy = pltpu.make_async_copy(lists, table, landed)
-    copy.start()
+def early_kernel(table, own, paired, up, down, adjacency, out, kept, held):
     out[...] = jnp.zeros_like(out)
-    step = (table.shape[0] - 2) // 3
-    block_products(
-        0, own, paired, up, down, adjacency, out, held, table,
-        lambda: 0, lambda: table[3 * step], copy.wait,
-    )
+    block_products(0, table, own, paired, up, down, adjacency, out, held)
 
     def keep(i, carry):
-        kept[i - table[3 * step]] = adjacency[table[2 * step + i]]
+        kept[i - table[3, 0]] = adjacency[table[2, i]]
         return carry
 
-    lax.fori_loop(table[3 * step], table[3 * step + 1], keep, 0)
-
-
-def late_kernel(before, lists, own, paired, up, down, kept, out, held, table, landed):
-    copy = pltpu.make_async_copy(lists, table, landed)
-    copy.start()
+    lax.fori_loop(table[3, 0], table[4, 0], keep, 0)
+
+
+def late_kernel(before, table, own, paired, up, down, kept, out, held):
     out[...] = before[...]
-    step = (table.shape[0] - 2) // 3
-    block_products(
-        1, own, paired, up, down, kept, out, held, table,
-        lambda: table[3 * step], lambda: table[3 * step + 1], copy.wait,
-    )
-
-
-def scratch_for(lists, own, size):
-    return [
-        pltpu.VMEM((RUNS * own.shape[2] // size, 4 * TILE, size), jnp.bfloat16),
-        pltpu.SMEM(lists.shape, jnp.int32),
-        pltpu.SemaphoreType.DMA,
-    ]
+    block_products(1, table, own, paired, up, down, kept, out, held)
 
 
 def early_blocks(lists, own, paired, stream, adjacency, target_blocks):
     slots, size, _ = adjacency.shape
     return pl.pallas_call(
         early_kernel,
-        in_specs=[pl.BlockSpec(memory_space=pl.ANY)] + [VMEM] * 5,
+        in_specs=[SMEM] + [VMEM] * 5,
         out_specs=[VMEM] * 2,
         out_shape=[
             jax.ShapeDtypeStruct((2 * target_blocks, TILE, size), jnp.float32),
             jax.ShapeDtypeStruct((slots + GROUP, size, size), adjacency.dtype),
         ],
-        scratch_shapes=scratch_for(lists, own, size),
+        scratch_shapes=[pltpu.VMEM((RUNS * own.shape[2] // size, 4 * TILE, size), jnp.bfloat16)],
         name="early_blocks",
         compiler_params=pltpu.CompilerParams(vmem_limit_bytes=8 * 2**20),
         cost_estimate=pl.CostEstimate(
@@ -208,10 +208,10 @@
     slots, size, _ = kept.shape
     return pl.pallas_call(
         late_kernel,
-        in_specs=[VMEM, pl.BlockSpec(memory_space=pl.ANY)] + [VMEM] * 5,
+        in_specs=[VMEM, SMEM] + [VMEM] * 5,
         out_specs=VMEM,
         out_shape=jax.ShapeDtypeStruct(before.shape, jnp.float32),
-        scratch_shapes=scratch_for(lists, own, size),
+        scratch_shapes=[pltpu.VMEM((RUNS * own.shape[2] // size, 4 * TILE, size), jnp.bfloat16)],
         name="late_blocks",
         compiler_params=pltpu.CompilerParams(vmem_limit_bytes=8 * 2**20),
         cost_estimate=pl.CostEstimate(
@@ -250,15 +250,16 @@
     for k in range(parts.shape[0]):
         rows += [parts[k], pltpu.roll(parts[k], T_DEV, 1)]
     sums = jnp.concatenate(rows, axis=0)
-    hidden = jnp.maximum(sums + bias_one[...], 0.0).astype(jnp.bfloat16)
-    count, fan = neighbors.shape
-    positions = lax.broadcasted_iota(jnp.int32, (count, hidden.shape[1]), 1)
+    bias = jnp.broadcast_to(bias_one[...], (sums.shape[1], sums.shape[0])).T
+    hidden = jnp.maximum(sums + bias, 0.0).astype(jnp.bfloat16)
+    fan, count = neighbors.shape
+    positions = lax.broadcasted_iota(jnp.int32, (hidden.shape[1], count), 0)
     pick_self = (positions == seeds[...]).astype(jnp.float32)
     tally = jnp.zeros(positions.shape, jnp.float32)
     for k in range(fan):
-        tally += (positions == neighbors[:, k : k + 1]).astype(jnp.float32)
+        tally += (positions == neighbors[k : k + 1]).astype(jnp.float32)
     picked = lax.dot_general(
-        jnp.concatenate([pick_self, tally / fan], axis=0).astype(jnp.bfloat16),
+        jnp.concatenate([pick_self.T, tally.T / fan], axis=0).astype(jnp.bfloat16),
         hidden,
         NT,
         preferred_element_type=jnp.float32,
@@ -284,12 +285,12 @@
         compiler_params=pltpu.CompilerParams(vmem_limit_bytes=8 * 2**20),
     )(
         parts,
-        bias_one[:, None],
+        bias_one[None, :],
         self_weight.T,
         neigh_weight.T,
         bias_two[None, :],
-        seeds[:, None],
-        neighbors,
+        seeds[None, :],
+        neighbors.T,
     )
 
 
@@ -320,12 +321,9 @@
         return lax.ppermute(value, "feat", route)
 
     tie = lax.optimization_barrier
-    opposite, rest, near, opposite_own, rest_own, near_own = project(
-        in_hop_order(layer_one), features
-    )
+    opposite, rest, opposite_own, rest_own = project(in_hop_order(layer_one), features)
     opposite, rest = tie((send(opposite, pair), rest))
-    rest, near = tie((send(rest, pair), near))
-    near = send(near, pair)
+    rest = send(rest, pair)
 
     order = block_count
     streams = []
@@ -353,8 +351,8 @@
 
     early = SPANS[0][1] // 2 * (features.shape[0] // RUNS) // size
     lists = block_lists(target_block, source_block, block_count, early)
-    partial, kept = early_blocks(lists, near_own, near, streams[0], adjacency, target_blocks)
-    partial = late_blocks(partial, lists, near_own, near, streams[1], kept)
+    partial, kept = early_blocks(lists, rest_own, rest, streams[0], adjacency, target_blocks)
+    partial = late_blocks(partial, lists, rest_own, rest, streams[1], kept)
 
     partial = partial.reshape(node_count, 2 * CHIPS, TILE, size)
     parts = combine(lax.all_to_all(partial, "node", 0, 0))

time: 101 us -> 95.2 us (0.943)
  blocking collectives: 20.4 us -> 39 us
  starting transfers between devices: 41.3 us -> 27 us
  local copies, waits for them, and re-layouts: 7.42 us -> 3.11 us
  waiting for transfers between devices: 19.1 us -> 15.6 us
  other arithmetic: 2.42 us -> 0.64 us
    all_to_all x0 -> x1, blocking collectives: none -> 20.4 us  [on_device(): parts = lax.all_to_all(parts, 'feat', 0, 0)]
    all_to_all x1 -> x0, starting transfers between devices: 10.8 us -> none  [on_device(): parts = lax.all_to_all(parts, 'feat', 0, 0)]
    all_to_all x1 -> x0, waiting for transfers between devices: 7.48 us -> none  [on_device(): parts = lax.all_to_all(parts, 'feat', 0, 0)]
    ppermute x19 -> x18, waiting for transfers between devices: 11.7 us -> 15.6 us  [send(): return lax.ppermute(value, 'feat', route)]
    ppermute x19 -> x18, starting transfers between devices: 30.5 us -> 27 us  [send(): return lax.ppermute(value, 'feat', route)]
    unnamed x23 -> x24, local copies, waits for them, and re-layouts: 6.56 us -> 3.11 us
    all_to_all x1, blocking collectives: 20.4 us -> 18.7 us  [on_device(): parts = combine(lax.all_to_all(partial, 'node', 0, 0))]
    reduce_sum x3 -> x0, other arithmetic: 1.03 us -> none  [the longest x1 0.63 us: block_lists(): first = jnp.sum((key < slots).astype(jnp.int32))[None]]
  transfers between devices with their start and end apart: 20 -> 18, of which waited for: 6 -> 8; matrix products, arithmetic and copies ran while one was open for 3% -> 1% of each run, Pallas kernels for 4% -> 4%
where the time goes in v7:
time: 95.2 us; the launch traced here: 95.1 us
  blocking collectives  39 us (41%)
  starting transfers between devices  27 us (28%)
  waiting for transfers between devices  15.6 us (16%)
  Pallas kernels  8.58 us (9%)
  local copies, waits for them, and re-layouts  3.11 us (3%)
    ppermute x18, starting transfers between devices, send(): return lax.ppermute(value, 'feat', route)  27 us
    all_to_all x1, blocking collectives, on_device(): parts = lax.all_to_all(parts, 'feat', 0, 0)  20.4 us
    all_to_all x1, blocking collectives, on_device(): parts = combine(lax.all_to_all(partial, 'node', 0, 0))  18.7 us
    ppermute x18, waiting for transfers between devices, send(): return lax.ppermute(value, 'feat', route)  15.6 us
    pallas_call x1, Pallas kernels, early_blocks(): pl.pallas_call(early_kernel, in_specs=[SMEM] + [VMEM] * 5, out_specs=[VME...  3.77 us
    unnamed x24, local copies, waits for them, and re-layouts  3.11 us
    pallas_call x1, Pallas kernels, late_blocks(): pl.pallas_call(late_kernel, in_specs=[VMEM, SMEM] + [VMEM] * 5, out_specs...  2.09 us
  transfers between devices with their start and end apart: 18, of which 8 were waited for; matrix products, arithmetic and copies ran while one was open for 1% of the time, Pallas kernels for 4%

profile of v7, /device:TPU:1, one launch (start us, length us, event | category | flops | bytes accessed | tf_op | source)
XLA Modules:
  0.0 95.1 jit_solution(14153541887050615800)
XLA Ops:
  0.0 0.9 copy-done
  0.9 0.2 convolution_convert_fusion.ordered
  1.2 2.2 %copy-done.1 = bf16[8192,256]{1,0:T(8,128)(2,1)S(1)} copy-done((bf16[8192,256]{1,0:T(8,128)(2,1)S(1)}, bf16[8192,256]{1,0:T(8,128)(2,1)}, u32[]{:S(2)}) %copy-start.1) | copy-done | bytes 4194328
  3.3 1.3 %project.1 = (f32[16,8,1024]{2,1,0:T(8,128)S(1)}, f32[112,8,1024]{2,1,0:T(8,128)S(1)}, f32[16,8,1024]{2,1,0:T(8,128)S(1)}, f32[112,8,1024]{2,1,0:T(8,128)S(1)}) custom-call(bf16[256,256]{1,0:T(8,128)(2,1)S(1)} %convolution_convert_fusion.ordered, bf16[8192,256]{1,0:T(8,128)(2,1)S(1)} %copy-done.1), custom_call_target="tpu_custom_call" | custom-call | flops 1073741824 | bytes 12582912 | tf_op jit(solution)/shard_map/project/pallas_call | solution.py:45
  4.6 3.3 %collective-permute-start = (f32[16,8,1024]{2,1,0:T(8,128)S(1)}, f32[16,8,1024]{2,1,0:T(8,128)S(1)}, u32[]{:S(2)}, u32[]{:S(2)}) collective-permute-start(f32[16,8,1024]{2,1,0:T(8,128)S(1)} %get-tuple-element.46), channel_id=1, source_target_pairs={{0,1},{1,0},{2,3},{3,2},{4,5},{5,4},{6,7},{7,6},{8,9},{9,8},{10,11... | collective-permute-start | bytes 1572872 | tf_op jit(solution)/shard_map/ppermute | solution.py:321
  7.9 1.5 %collective-permute-done = f32[16,8,1024]{2,1,0:T(8,128)S(1)} collective-permute-done((f32[16,8,1024]{2,1,0:T(8,128)S(1)}, f32[16,8,1024]{2,1,0:T(8,128)S(1)}, u32[]{:S(2)}, u32[]{:S(2)}) %collective-permute-start) | collective-permute-done | bytes 524320 | tf_op jit(solution)/shard_map/ppermute | solution.py:321
  9.5 0.4 collective-permute-start.1
  10.0 3.9 %collective-permute-start.3 = (f32[5,8,1024]{2,1,0:T(8,128)S(1)}, f32[5,8,1024]{2,1,0:T(8,128)S(1)}, u32[]{:S(2)}, u32[]{:S(2)}) collective-permute-start(f32[5,8,1024]{2,1,0:T(8,128)S(1)} %get-tuple-element.64), channel_id=1, source_target_pairs={{2,0},{3,1},{4,2},{5,3},{6,4},{7,5},{8,6},{9,7},{10,8},{11,9},{12,... | collective-permute-start | bytes 491528 | tf_op jit(solution)/shard_map/ppermute | solution.py:321
  14.0 2.7 %collective-permute-start.11 = (f32[3,8,1024]{2,1,0:T(8,128)S(1)}, f32[3,8,1024]{2,1,0:T(8,128)S(1)}, u32[]{:S(2)}, u32[]{:S(2)}) collective-permute-start(f32[3,8,1024]{2,1,0:T(8,128)S(1)} %get-tuple-element.79), channel_id=1, source_target_pairs={{2,0},{3,1},{4,2},{5,3},{6,4},{7,5},{8,6},{9,7},{10,8},{11,9},{12,... | collective-permute-start | bytes 294920 | tf_op jit(solution)/shard_map/ppermute | solution.py:321
  16.7 1.6 %collective-permute-done.2 = f32[5,8,1024]{2,1,0:T(8,128)S(1)} collective-permute-done((f32[5,8,1024]{2,1,0:T(8,128)S(1)}, f32[5,8,1024]{2,1,0:T(8,128)S(1)}, u32[]{:S(2)}, u32[]{:S(2)}) %collective-permute-start.2) | collective-permute-done | bytes 163872 | tf_op jit(solution)/shard_map/ppermute | solution.py:321
  18.5 2.7 %collective-permute-start.5 = (f32[10,8,1024]{2,1,0:T(8,128)S(1)}, f32[10,8,1024]{2,1,0:T(8,128)S(1)}, u32[]{:S(2)}, u32[]{:S(2)}) collective-permute-start(f32[10,8,1024]{2,1,0:T(8,128)S(1)} %get-tuple-element.66), channel_id=1, source_target_pairs={{2,0},{3,1},{4,2},{5,3},{6,4},{7,5},{8,6},{9,7},{10,8},{11,9},{12,... | collective-permute-start | bytes 983048 | tf_op jit(solution)/shard_map/ppermute | solution.py:321
  21.3 2.7 %collective-permute-start.13 = (f32[6,8,1024]{2,1,0:T(8,128)S(1)}, f32[6,8,1024]{2,1,0:T(8,128)S(1)}, u32[]{:S(2)}, u32[]{:S(2)}) collective-permute-start(f32[6,8,1024]{2,1,0:T(8,128)S(1)} %get-tuple-element.81), channel_id=1, source_target_pairs={{2,0},{3,1},{4,2},{5,3},{6,4},{7,5},{8,6},{9,7},{10,8},{11,9},{12,... | collective-permute-start | bytes 589832 | tf_op jit(solution)/shard_map/ppermute | solution.py:321
  24.0 3.8 %collective-permute-done.4 = f32[10,8,1024]{2,1,0:T(8,128)S(1)} collective-permute-done((f32[10,8,1024]{2,1,0:T(8,128)S(1)}, f32[10,8,1024]{2,1,0:T(8,128)S(1)}, u32[]{:S(2)}, u32[]{:S(2)}) %collective-permute-start.4) | collective-permute-done | bytes 327712 | tf_op jit(solution)/shard_map/ppermute | solution.py:321
  27.9 0.8 collective-permute-start.6
  28.8 1.9 %collective-permute-start.7 = (f32[10,8,1024]{2,1,0:T(8,128)S(1)}, f32[10,8,1024]{2,1,0:T(8,128)S(1)}, u32[]{:S(2)}, u32[]{:S(2)}) collective-permute-start(f32[10,8,1024]{2,1,0:T(8,128)S(1)} %get-tuple-element.68), channel_id=1, source_target_pairs={{2,0},{3,1},{4,2},{5,3},{6,4},{7,5},{8,6},{9,7},{10,8},{11,9},{12,... | collective-permute-start | bytes 983048 | tf_op jit(solution)/shard_map/ppermute | solution.py:321
  30.7 1.3 %collective-permute-done.12 = f32[6,8,1024]{2,1,0:T(8,128)S(1)} collective-permute-done((f32[6,8,1024]{2,1,0:T(8,128)S(1)}, f32[6,8,1024]{2,1,0:T(8,128)S(1)}, u32[]{:S(2)}, u32[]{:S(2)}) %collective-permute-start.12) | collective-permute-done | bytes 196640 | tf_op jit(solution)/shard_map/ppermute | solution.py:321
  32.1 0.8 collective-permute-start.14
  32.9 1.9 %collective-permute-start.15 = (f32[6,8,1024]{2,1,0:T(8,128)S(1)}, f32[6,8,1024]{2,1,0:T(8,128)S(1)}, u32[]{:S(2)}, u32[]{:S(2)}) collective-permute-start(f32[6,8,1024]{2,1,0:T(8,128)S(1)} %get-tuple-element.83), channel_id=1, source_target_pairs={{2,0},{3,1},{4,2},{5,3},{6,4},{7,5},{8,6},{9,7},{10,8},{11,9},{12,... | collective-permute-start | bytes 589832 | tf_op jit(solution)/shard_map/ppermute | solution.py:321
  34.8 3.3 %collective-permute-done.6 = f32[10,8,1024]{2,1,0:T(8,128)S(1)} collective-permute-done((f32[10,8,1024]{2,1,0:T(8,128)S(1)}, f32[10,8,1024]{2,1,0:T(8,128)S(1)}, u32[]{:S(2)}, u32[]{:S(2)}) %collective-permute-start.6) | collective-permute-done | bytes 327712 | tf_op jit(solution)/shard_map/ppermute | solution.py:321
  38.3 0.7 collective-permute-start.8
  39.0 2.0 %collective-permute-start.9 = (f32[10,8,1024]{2,1,0:T(8,128)S(1)}, f32[10,8,1024]{2,1,0:T(8,128)S(1)}, u32[]{:S(2)}, u32[]{:S(2)}) collective-permute-start(f32[10,8,1024]{2,1,0:T(8,128)S(1)} %get-tuple-element.70), channel_id=1, source_target_pairs={{2,0},{3,1},{4,2},{5,3},{6,4},{7,5},{8,6},{9,7},{10,8},{11,9},{12,... | collective-permute-start | bytes 983048 | tf_op jit(solution)/shard_map/ppermute | solution.py:321
  41.0 1.3 %collective-permute-done.14 = f32[6,8,1024]{2,1,0:T(8,128)S(1)} collective-permute-done((f32[6,8,1024]{2,1,0:T(8,128)S(1)}, f32[6,8,1024]{2,1,0:T(8,128)S(1)}, u32[]{:S(2)}, u32[]{:S(2)}) %collective-permute-start.14) | collective-permute-done | bytes 196640 | tf_op jit(solution)/shard_map/ppermute | solution.py:321
  42.4 0.7 collective-permute-start.16
  43.1 2.0 %collective-permute-start.17 = (f32[6,8,1024]{2,1,0:T(8,128)S(1)}, f32[6,8,1024]{2,1,0:T(8,128)S(1)}, u32[]{:S(2)}, u32[]{:S(2)}) collective-permute-start(f32[6,8,1024]{2,1,0:T(8,128)S(1)} %get-tuple-element.85), channel_id=1, source_target_pairs={{2,0},{3,1},{4,2},{5,3},{6,4},{7,5},{8,6},{9,7},{10,8},{11,9},{12,... | collective-permute-start | bytes 589832 | tf_op jit(solution)/shard_map/ppermute | solution.py:321
  45.8 0.3 block_lists.1.table
  46.1 2.4 %collective-permute-done.8.up = f32[10,8,1024]{2,1,0:T(8,128)S(1)} collective-permute-done((f32[10,8,1024]{2,1,0:T(8,128)S(1)}, f32[10,8,1024]{2,1,0:T(8,128)S(1)}, u32[]{:S(2)}, u32[]{:S(2)}) %collective-permute-start.8) | collective-permute-done | bytes 327712 | tf_op jit(solution)/shard_map/ppermute | solution.py:321
  48.5 3.8 %early_blocks.1 = (f32[256,8,128]{2,1,0:T(8,128)S(1)}, bf16[272,128,128]{2,1,0:T(8,128)(2,1)S(1)}) custom-call(s32[8,384]{1,0:T(8,128)S(1)} %block_lists.1.table, f32[112,8,1024]{2,1,0:T(8,128)S(1)} %get-tuple-element.72.own, f32[112,8,1024]{2,1,0:T(8,128)S(1)} %collective-permute-done.1.paired, f32[10,8,1024]{2,1,0:T(8,128)S(1)} %collective-permute-done.8.up, ...), custom_call_target="tpu_custom_call" | custom-call | flops 268435456 | bytes 4194304 | tf_op jit(solution)/shard_map/early_blocks/pallas_call | solution.py:188
  52.3 0.4 collective-permute-done.16.up
  52.8 2.1 %late_blocks.1 = f32[256,8,128]{2,1,0:T(8,128)S(1)} custom-call(f32[256,8,128]{2,1,0:T(8,128)S(1)} %get-tuple-element.71.before, s32[8,384]{1,0:T(8,128)S(1)} %block_lists.1.table, f32[112,8,1024]{2,1,0:T(8,128)S(1)} %get-tuple-element.72.own, f32[112,8,1024]{2,1,0:T(8,128)S(1)} %collective-permute-done.1.paired, ...), custom_call_target="tpu_custom_call" | custom-call | flops 285212672 | bytes 4456448 | tf_op jit(solution)/shard_map/late_blocks/pallas_call | solution.py:209
  54.9 18.7 %all_to_all.10.parts = f32[16,16,8,128]{3,2,1,0:T(8,128)S(1)} all-to-all(f32[16,16,8,128]{3,2,1,0:T(8,128)S(1)} %bitcast.12), channel_id=1, replica_groups=mesh['node'=16,'feat'=16] {'node'}, dimensions={0} | all-to-all | bytes 2097152 | tf_op jit(solution)/shard_map/all_to_all | solution.py:358
  73.6 20.4 %all_to_all.11.parts = f32[16,8,128]{2,1,0:T(8,128)S(1)} all-to-all(f32[16,8,128]{2,1,0:T(8,128)S(1)} %combine.1), channel_id=1, replica_groups=mesh['node'=16,'feat'=16] {'feat'}, dimensions={0} | all-to-all | bytes 131072 | tf_op jit(solution)/shard_map/all_to_all | solution.py:359
  94.1 1.0 %second.1 = f32[32,172]{1,0:T(8,128)} custom-call(f32[16,8,128]{2,1,0:T(8,128)S(1)} %all_to_all.11.parts, f32[1,256]{1,0:T(1,128)S(1)} %bitcast.16, bf16[172,256]{1,0:T(8,128)(2,1)S(1)} %bitcast.13, bf16[172,256]{1,0:T(8,128)(2,1)S(1)} %bitcast.14, f32[1,172]{1,0:T(1,128)S(1)} %bitcast.17, s32[1,32]{1,0:T(1,128)S(1)} %bitcast.20, s32[8,32]{1,0:T(8,128)S(1)} %bitcast.15), custom_call_target="tpu_custom_call" | custom-call | tf_op jit(solution)/shard_map/second/pallas_call | solution.py:279
  (47 shorter events, 1.2 us)
Async XLA Ops:
  0.0 0.9 copy-start
  1.1 2.2 %copy-start.1 = (bf16[8192,256]{1,0:T(8,128)(2,1)S(1)}, bf16[8192,256]{1,0:T(8,128)(2,1)}, u32[]{:S(2)}) copy-start(bf16[8192,256]{1,0:T(8,128)(2,1)} %features.1) | copy-start | bytes 12582916
  3.3 45.2 %slice-start = ((s8[8388608]{0:T(1024)(128)(4,1)}), s8[4194304]{0:T(1024)(128)(4,1)S(1)}, s32[]{:S(2)}) async-start(s8[8388608]{0:T(1024)(128)(4,1)} %bitcast.10), calls=%async_computation.2 | async-start | bytes 8388608
  4.6 4.9 %collective-permute-start = (f32[16,8,1024]{2,1,0:T(8,128)S(1)}, f32[16,8,1024]{2,1,0:T(8,128)S(1)}, u32[]{:S(2)}, u32[]{:S(2)}) collective-permute-start(f32[16,8,1024]{2,1,0:T(8,128)S(1)} %get-tuple-element.46), channel_id=1, source_target_pairs={{0,1},{1,0},{2,3},{3,2},{4,5},{5,4},{6,7},{7,6},{8,9},{9,8},{10,11... | collective-permute-start | bytes 1572872 | tf_op jit(solution)/shard_map/ppermute | solution.py:321
  9.5 7.2 %collective-permute-start.1 = (f32[112,8,1024]{2,1,0:T(8,128)S(1)}, f32[112,8,1024]{2,1,0:T(8,128)S(1)}, u32[]{:S(2)}, u32[]{:S(2)}) collective-permute-start(f32[112,8,1024]{2,1,0:T(8,128)S(1)} %get-tuple-element.48), channel_id=1, source_target_pairs={{0,1},{1,0},{2,3},{3,2},{4,5},{5,4},{6,7},{7,6},{8,9},{9,8},{10,11... | collective-permute-start | bytes 11010056 | tf_op jit(solution)/shard_map/ppermute | solution.py:321
  9.9 8.4 %collective-permute-start.2 = (f32[5,8,1024]{2,1,0:T(8,128)S(1)}, f32[5,8,1024]{2,1,0:T(8,128)S(1)}, u32[]{:S(2)}, u32[]{:S(2)}) collective-permute-start(f32[5,8,1024]{2,1,0:T(8,128)S(1)} %get-tuple-element.63), channel_id=1, source_target_pairs={{0,2},{1,3},{2,4},{3,5},{4,6},{5,7},{6,8},{7,9},{8,10},{9,11},{10,... | collective-permute-start | bytes 491528 | tf_op jit(solution)/shard_map/ppermute | solution.py:321
  10.0 8.3 %collective-permute-start.3 = (f32[5,8,1024]{2,1,0:T(8,128)S(1)}, f32[5,8,1024]{2,1,0:T(8,128)S(1)}, u32[]{:S(2)}, u32[]{:S(2)}) collective-permute-start(f32[5,8,1024]{2,1,0:T(8,128)S(1)} %get-tuple-element.64), channel_id=1, source_target_pairs={{2,0},{3,1},{4,2},{5,3},{6,4},{7,5},{8,6},{9,7},{10,8},{11,9},{12,... | collective-permute-start | bytes 491528 | tf_op jit(solution)/shard_map/ppermute | solution.py:321
  13.9 7.2 %collective-permute-start.10 = (f32[3,8,1024]{2,1,0:T(8,128)S(1)}, f32[3,8,1024]{2,1,0:T(8,128)S(1)}, u32[]{:S(2)}, u32[]{:S(2)}) collective-permute-start(f32[3,8,1024]{2,1,0:T(8,128)S(1)} %get-tuple-element.78), channel_id=1, source_target_pairs={{0,2},{1,3},{2,4},{3,5},{4,6},{5,7},{6,8},{7,9},{8,10},{9,11},{10,... | collective-permute-start | bytes 294920 | tf_op jit(solution)/shard_map/ppermute | solution.py:321
  14.0 7.1 %collective-permute-start.11 = (f32[3,8,1024]{2,1,0:T(8,128)S(1)}, f32[3,8,1024]{2,1,0:T(8,128)S(1)}, u32[]{:S(2)}, u32[]{:S(2)}) collective-permute-start(f32[3,8,1024]{2,1,0:T(8,128)S(1)} %get-tuple-element.79), channel_id=1, source_target_pairs={{2,0},{3,1},{4,2},{5,3},{6,4},{7,5},{8,6},{9,7},{10,8},{11,9},{12,... | collective-permute-start | bytes 294920 | tf_op jit(solution)/shard_map/ppermute | solution.py:321
  18.4 30.1 %slice-start.1 = ((s8[8388608]{0:T(1024)(128)(4,1)}), s8[4194304]{0:T(1024)(128)(4,1)S(1)}, s32[]{:S(2)}) async-start(s8[8388608]{0:T(1024)(128)(4,1)} %bitcast.10), calls=%async_computation.3 | async-start | bytes 8388608
  18.4 9.4 %collective-permute-start.4 = (f32[10,8,1024]{2,1,0:T(8,128)S(1)}, f32[10,8,1024]{2,1,0:T(8,128)S(1)}, u32[]{:S(2)}, u32[]{:S(2)}) collective-permute-start(f32[10,8,1024]{2,1,0:T(8,128)S(1)} %get-tuple-element.65), channel_id=1, source_target_pairs={{0,2},{1,3},{2,4},{3,5},{4,6},{5,7},{6,8},{7,9},{8,10},{9,11},{10,... | collective-permute-start | bytes 983048 | tf_op jit(solution)/shard_map/ppermute | solution.py:321
  18.5 9.3 %collective-permute-start.5 = (f32[10,8,1024]{2,1,0:T(8,128)S(1)}, f32[10,8,1024]{2,1,0:T(8,128)S(1)}, u32[]{:S(2)}, u32[]{:S(2)}) collective-permute-start(f32[10,8,1024]{2,1,0:T(8,128)S(1)} %get-tuple-element.66), channel_id=1, source_target_pairs={{2,0},{3,1},{4,2},{5,3},{6,4},{7,5},{8,6},{9,7},{10,8},{11,9},{12,... | collective-permute-start | bytes 983048 | tf_op jit(solution)/shard_map/ppermute | solution.py:321
  21.2 24.6 %copy-start.7 = (s32[256]{0:T(256)S(1)}, s32[256]{0:T(256)}, u32[]{:S(2)}) copy-start(s32[256]{0:T(256)} %param.14) | copy-start | bytes 3076
  21.2 24.6 %copy-start.8 = (s32[256]{0:T(256)S(1)}, s32[256]{0:T(256)}, u32[]{:S(2)}) copy-start(s32[256]{0:T(256)} %param.15) | copy-start | bytes 3076
  21.2 10.8 %collective-permute-start.12 = (f32[6,8,1024]{2,1,0:T(8,128)S(1)}, f32[6,8,1024]{2,1,0:T(8,128)S(1)}, u32[]{:S(2)}, u32[]{:S(2)}) collective-permute-start(f32[6,8,1024]{2,1,0:T(8,128)S(1)} %get-tuple-element.80), channel_id=1, source_target_pairs={{0,2},{1,3},{2,4},{3,5},{4,6},{5,7},{6,8},{7,9},{8,10},{9,11},{10,... | collective-permute-start | bytes 589832 | tf_op jit(solution)/shard_map/ppermute | solution.py:321
  21.3 10.7 %collective-permute-start.13 = (f32[6,8,1024]{2,1,0:T(8,128)S(1)}, f32[6,8,1024]{2,1,0:T(8,128)S(1)}, u32[]{:S(2)}, u32[]{:S(2)}) collective-permute-start(f32[6,8,1024]{2,1,0:T(8,128)S(1)} %get-tuple-element.81), channel_id=1, source_target_pairs={{2,0},{3,1},{4,2},{5,3},{6,4},{7,5},{8,6},{9,7},{10,8},{11,9},{12,... | collective-permute-start | bytes 589832 | tf_op jit(solution)/shard_map/ppermute | solution.py:321
  27.9 10.2 %collective-permute-start.6 = (f32[10,8,1024]{2,1,0:T(8,128)S(1)}, f32[10,8,1024]{2,1,0:T(8,128)S(1)}, u32[]{:S(2)}, u32[]{:S(2)}) collective-permute-start(f32[10,8,1024]{2,1,0:T(8,128)S(1)} %get-tuple-element.67), channel_id=1, source_target_pairs={{0,2},{1,3},{2,4},{3,5},{4,6},{5,7},{6,8},{7,9},{8,10},{9,11},{10,... | collective-permute-start | bytes 983048 | tf_op jit(solution)/shard_map/ppermute | solution.py:321
  28.8 9.3 %collective-permute-start.7 = (f32[10,8,1024]{2,1,0:T(8,128)S(1)}, f32[10,8,1024]{2,1,0:T(8,128)S(1)}, u32[]{:S(2)}, u32[]{:S(2)}) collective-permute-start(f32[10,8,1024]{2,1,0:T(8,128)S(1)} %get-tuple-element.68), channel_id=1, source_target_pairs={{2,0},{3,1},{4,2},{5,3},{6,4},{7,5},{8,6},{9,7},{10,8},{11,9},{12,... | collective-permute-start | bytes 983048 | tf_op jit(solution)/shard_map/ppermute | solution.py:321
  32.1 10.2 %collective-permute-start.14 = (f32[6,8,1024]{2,1,0:T(8,128)S(1)}, f32[6,8,1024]{2,1,0:T(8,128)S(1)}, u32[]{:S(2)}, u32[]{:S(2)}) collective-permute-start(f32[6,8,1024]{2,1,0:T(8,128)S(1)} %get-tuple-element.82), channel_id=1, source_target_pairs={{0,2},{1,3},{2,4},{3,5},{4,6},{5,7},{6,8},{7,9},{8,10},{9,11},{10,... | collective-permute-start | bytes 589832 | tf_op jit(solution)/shard_map/ppermute | solution.py:321
  32.9 9.4 %collective-permute-start.15 = (f32[6,8,1024]{2,1,0:T(8,128)S(1)}, f32[6,8,1024]{2,1,0:T(8,128)S(1)}, u32[]{:S(2)}, u32[]{:S(2)}) collective-permute-start(f32[6,8,1024]{2,1,0:T(8,128)S(1)} %get-tuple-element.83), channel_id=1, source_target_pairs={{2,0},{3,1},{4,2},{5,3},{6,4},{7,5},{8,6},{9,7},{10,8},{11,9},{12,... | collective-permute-start | bytes 589832 | tf_op jit(solution)/shard_map/ppermute | solution.py:321
  38.3 10.2 %collective-permute-start.8 = (f32[10,8,1024]{2,1,0:T(8,128)S(1)}, f32[10,8,1024]{2,1,0:T(8,128)S(1)}, u32[]{:S(2)}, u32[]{:S(2)}) collective-permute-start(f32[10,8,1024]{2,1,0:T(8,128)S(1)} %get-tuple-element.69), channel_id=1, source_target_pairs={{0,2},{1,3},{2,4},{3,5},{4,6},{5,7},{6,8},{7,9},{8,10},{9,11},{10,... | collective-permute-start | bytes 983048 | tf_op jit(solution)/shard_map/ppermute | solution.py:321
  39.0 9.5 %collective-permute-start.9 = (f32[10,8,1024]{2,1,0:T(8,128)S(1)}, f32[10,8,1024]{2,1,0:T(8,128)S(1)}, u32[]{:S(2)}, u32[]{:S(2)}) collective-permute-start(f32[10,8,1024]{2,1,0:T(8,128)S(1)} %get-tuple-element.70), channel_id=1, source_target_pairs={{2,0},{3,1},{4,2},{5,3},{6,4},{7,5},{8,6},{9,7},{10,8},{11,9},{12,... | collective-permute-start | bytes 983048 | tf_op jit(solution)/shard_map/ppermute | solution.py:321
  42.4 10.3 %collective-permute-start.16 = (f32[6,8,1024]{2,1,0:T(8,128)S(1)}, f32[6,8,1024]{2,1,0:T(8,128)S(1)}, u32[]{:S(2)}, u32[]{:S(2)}) collective-permute-start(f32[6,8,1024]{2,1,0:T(8,128)S(1)} %get-tuple-element.84), channel_id=1, source_target_pairs={{0,2},{1,3},{2,4},{3,5},{4,6},{5,7},{6,8},{7,9},{8,10},{9,11},{10,... | collective-permute-start | bytes 589832 | tf_op jit(solution)/shard_map/ppermute | solution.py:321
  43.1 9.6 %collective-permute-start.17 = (f32[6,8,1024]{2,1,0:T(8,128)S(1)}, f32[6,8,1024]{2,1,0:T(8,128)S(1)}, u32[]{:S(2)}, u32[]{:S(2)}) collective-permute-start(f32[6,8,1024]{2,1,0:T(8,128)S(1)} %get-tuple-element.85), channel_id=1, source_target_pairs={{2,0},{3,1},{4,2},{5,3},{6,4},{7,5},{8,6},{9,7},{10,8},{11,9},{12,... | collective-permute-start | bytes 589832 | tf_op jit(solution)/shard_map/ppermute | solution.py:321
  52.7 41.3 %copy-start.2 = (bf16[256,172]{0,1:T(8,128)(2,1)S(1)}, bf16[256,172]{0,1:T(8,128)(2,1)}, u32[]{:S(2)}) copy-start(bf16[256,172]{0,1:T(8,128)(2,1)} %param.19) | copy-start | bytes 264196
  52.7 41.3 %copy-start.3 = (bf16[256,172]{0,1:T(8,128)(2,1)S(1)}, bf16[256,172]{0,1:T(8,128)(2,1)}, u32[]{:S(2)}) copy-start(bf16[256,172]{0,1:T(8,128)(2,1)} %param.20) | copy-start | bytes 264196
  52.7 41.3 %copy-start.4 = (s32[32,8]{0,1:T(8,128)S(1)}, s32[32,8]{0,1:T(8,128)}, u32[]{:S(2)}) copy-start(s32[32,8]{0,1:T(8,128)} %param.23) | copy-start | bytes 3076
  52.7 41.3 %copy-start.5 = (f32[256]{0:T(256)S(1)}, f32[256]{0:T(256)}, u32[]{:S(2)}) copy-start(f32[256]{0:T(256)} %param.18) | copy-start | bytes 3076
  52.7 41.3 %copy-start.6 = (f32[172]{0:T(256)S(1)}, f32[172]{0:T(256)}, u32[]{:S(2)}) copy-start(f32[172]{0:T(256)} %param.21) | copy-start | bytes 2068
  52.7 41.3 %copy-start.9 = (s32[32]{0:T(128)S(1)}, s32[32]{0:T(128)}, u32[]{:S(2)}) copy-start(s32[32]{0:T(128)} %param.22) | copy-start | bytes 388

commit v8 on v7

--- a/solution.py
+++ b/solution.py
@@ -11,7 +11,7 @@
 CHIPS = 8
 TILE = 8
 RUNS = 8
-SPANS = ((0, 10), (10, 16))
+SPANS = ((0, 8), (8, 16))
 GROUP = 16
 NT = (((1,), (1,)), ((), ()))
 VMEM = pl.BlockSpec(memory_space=pltpu.VMEM)
@@ -135,10 +135,7 @@
         values = []
         for k in range(0, GROUP, 2):
             left = [held[table[1, first + k + j]] for j in range(2)]
-            right = [
-                adjacency[first - start + k + j if late else table[2, first + k + j]]
-                for j in range(2)
-            ]
+            right = [adjacency[table[2, first + k + j]] for j in range(2)]
             value = lax.dot_general(
                 jnp.concatenate(left, axis=0),
                 jnp.concatenate(right, axis=0),
@@ -167,59 +164,33 @@
     add(start + (jnp.maximum(groups, 1) - 1) * GROUP, last)
 
 
-def early_kernel(table, own, paired, up, down, adjacency, out, kept, held):
+def early_kernel(table, own, paired, up, down, adjacency, out, held):
     out[...] = jnp.zeros_like(out)
     block_products(0, table, own, paired, up, down, adjacency, out, held)
 
-    def keep(i, carry):
-        kept[i - table[3, 0]] = adjacency[table[2, i]]
-        return carry
-
-    lax.fori_loop(table[3, 0], table[4, 0], keep, 0)
-
-
-def late_kernel(before, table, own, paired, up, down, kept, out, held):
+
+def late_kernel(before, table, own, paired, up, down, adjacency, out, held):
     out[...] = before[...]
-    block_products(1, table, own, paired, up, down, kept, out, held)
-
-
-def early_blocks(lists, own, paired, stream, adjacency, target_blocks):
+    block_products(1, table, own, paired, up, down, adjacency, out, held)
+
+
+def blocks(before, lists, own, paired, stream, adjacency, target_blocks):
     slots, size, _ = adjacency.shape
-    return pl.pallas_call(
-        early_kernel,
-        in_specs=[SMEM] + [VMEM] * 5,
-        out_specs=[VMEM] * 2,
-        out_shape=[
-            jax.ShapeDtypeStruct((2 * target_blocks, TILE, size), jnp.float32),
-            jax.ShapeDtypeStruct((slots + GROUP, size, size), adjacency.dtype),
-        ],
+    late = before is not None
+    return pl.pallas_call(
+        late_kernel if late else early_kernel,
+        in_specs=[VMEM] * late + [SMEM] + [VMEM] * 5,
+        out_specs=VMEM,
+        out_shape=jax.ShapeDtypeStruct((2 * target_blocks, TILE, size), jnp.float32),
         scratch_shapes=[pltpu.VMEM((RUNS * own.shape[2] // size, 4 * TILE, size), jnp.bfloat16)],
-        name="early_blocks",
+        name="late_blocks" if late else "early_blocks",
         compiler_params=pltpu.CompilerParams(vmem_limit_bytes=8 * 2**20),
         cost_estimate=pl.CostEstimate(
             flops=4 * slots * size * size * UNITS,
             bytes_accessed=slots * size * size,
             transcendentals=0,
         ),
-    )(lists, own, paired, *stream, adjacency)
-
-
-def late_blocks(before, lists, own, paired, stream, kept):
-    slots, size, _ = kept.shape
-    return pl.pallas_call(
-        late_kernel,
-        in_specs=[VMEM, SMEM] + [VMEM] * 5,
-        out_specs=VMEM,
-        out_shape=jax.ShapeDtypeStruct(before.shape, jnp.float32),
-        scratch_shapes=[pltpu.VMEM((RUNS * own.shape[2] // size, 4 * TILE, size), jnp.bfloat16)],
-        name="late_blocks",
-        compiler_params=pltpu.CompilerParams(vmem_limit_bytes=8 * 2**20),
-        cost_estimate=pl.CostEstimate(
-            flops=4 * slots * size * size * UNITS,
-            bytes_accessed=slots * size * size,
-            transcendentals=0,
-        ),
-    )(before, lists, own, paired, *stream, kept)
+    )(*([before] if late else []), lists, own, paired, *stream, adjacency)
 
 
 def combine_kernel(parts, out):
@@ -351,8 +322,9 @@
 
     early = SPANS[0][1] // 2 * (features.shape[0] // RUNS) // size
     lists = block_lists(target_block, source_block, block_count, early)
-    partial, kept = early_blocks(lists, rest_own, rest, streams[0], adjacency, target_blocks)
-    partial = late_blocks(partial, lists, rest_own, rest, streams[1], kept)
+    partial = None
+    for stream in streams:
+        partial = blocks(partial, lists, rest_own, rest, stream, adjacency, target_blocks)
 
     partial = partial.reshape(node_count, 2 * CHIPS, TILE, size)
     parts = combine(lax.all_to_all(partial, "node", 0, 0))

time: 95.2 us -> 96.6 us (1.015)
  waiting for transfers between devices: 15.6 us -> 18.1 us
  Pallas kernels: 8.58 us -> 7.2 us
    all_to_all x1, blocking collectives: 18.7 us -> 23.4 us  [on_device(): parts = combine(lax.all_to_all(partial, 'node', 0, 0))]
    all_to_all x1, blocking collectives: 20.4 us -> 15.7 us  [on_device(): parts = lax.all_to_all(parts, 'feat', 0, 0)]
    ppermute x18, waiting for transfers between devices: 15.6 us -> 18.1 us  [send(): return lax.ppermute(value, 'feat', route)]
    pallas_call x2, Pallas kernels: 5.86 us -> 4.47 us  [blocks(): pl.pallas_call(late_kernel if late else early_kernel, in_specs=[VMEM] * l...]
  transfers between devices with their start and end apart: 18 -> 18, of which waited for: 8 -> 8; matrix products, arithmetic and copies ran while one was open for 1% -> 1% of each run, Pallas kernels for 4% -> 3%
where the time goes in v8:
time: 96.6 us; the launch traced here: 96.4 us
  blocking collectives  39.1 us (40%)
  starting transfers between devices  27 us (28%)
  waiting for transfers between devices  18.1 us (19%)
  Pallas kernels  7.2 us (7%)
  local copies, waits for them, and re-layouts  3.12 us (3%)
    ppermute x18, starting transfers between devices, send(): return lax.ppermute(value, 'feat', route)  27 us
    all_to_all x1, blocking collectives, on_device(): parts = combine(lax.all_to_all(partial, 'node', 0, 0))  23.4 us
    ppermute x18, waiting for transfers between devices, send(): return lax.ppermute(value, 'feat', route)  18.1 us
    all_to_all x1, blocking collectives, on_device(): parts = lax.all_to_all(parts, 'feat', 0, 0)  15.7 us
    pallas_call x2, Pallas kernels, blocks(): pl.pallas_call(late_kernel if late else early_kernel, in_specs=[VMEM] * l...  4.47 us
    unnamed x24, local copies, waits for them, and re-layouts  3.12 us
  transfers between devices with their start and end apart: 18, of which 8 were waited for; matrix products, arithmetic and copies ran while one was open for 1% of the time, Pallas kernels for 3%

profile of v8, /device:TPU:1, one launch (start us, length us, event | category | flops | bytes accessed | tf_op | source)
XLA Modules:
  0.0 96.4 jit_solution(15823595624440224758)
XLA Ops:
  0.0 0.9 copy-done
  0.9 0.2 convolution_convert_fusion.ordered
  1.2 2.2 %copy-done.1 = bf16[8192,256]{1,0:T(8,128)(2,1)S(1)} copy-done((bf16[8192,256]{1,0:T(8,128)(2,1)S(1)}, bf16[8192,256]{1,0:T(8,128)(2,1)}, u32[]{:S(2)}) %copy-start.1) | copy-done | bytes 4194328
  3.3 1.3 %project.1 = (f32[16,8,1024]{2,1,0:T(8,128)S(1)}, f32[112,8,1024]{2,1,0:T(8,128)S(1)}, f32[16,8,1024]{2,1,0:T(8,128)S(1)}, f32[112,8,1024]{2,1,0:T(8,128)S(1)}) custom-call(bf16[256,256]{1,0:T(8,128)(2,1)S(1)} %convolution_convert_fusion.ordered, bf16[8192,256]{1,0:T(8,128)(2,1)S(1)} %copy-done.1), custom_call_target="tpu_custom_call" | custom-call | flops 1073741824 | bytes 12582912 | tf_op jit(solution)/shard_map/project/pallas_call | solution.py:45
  4.6 3.3 %collective-permute-start = (f32[16,8,1024]{2,1,0:T(8,128)S(1)}, f32[16,8,1024]{2,1,0:T(8,128)S(1)}, u32[]{:S(2)}, u32[]{:S(2)}) collective-permute-start(f32[16,8,1024]{2,1,0:T(8,128)S(1)} %get-tuple-element.44), channel_id=1, source_target_pairs={{0,1},{1,0},{2,3},{3,2},{4,5},{5,4},{6,7},{7,6},{8,9},{9,8},{10,11... | collective-permute-start | bytes 1572872 | tf_op jit(solution)/shard_map/ppermute | solution.py:292
  7.9 1.5 %collective-permute-done = f32[16,8,1024]{2,1,0:T(8,128)S(1)} collective-permute-done((f32[16,8,1024]{2,1,0:T(8,128)S(1)}, f32[16,8,1024]{2,1,0:T(8,128)S(1)}, u32[]{:S(2)}, u32[]{:S(2)}) %collective-permute-start) | collective-permute-done | bytes 524320 | tf_op jit(solution)/shard_map/ppermute | solution.py:292
  9.5 0.4 collective-permute-start.1
  10.0 3.9 %collective-permute-start.3 = (f32[4,8,1024]{2,1,0:T(8,128)S(1)}, f32[4,8,1024]{2,1,0:T(8,128)S(1)}, u32[]{:S(2)}, u32[]{:S(2)}) collective-permute-start(f32[4,8,1024]{2,1,0:T(8,128)S(1)} %get-tuple-element.62), channel_id=1, source_target_pairs={{2,0},{3,1},{4,2},{5,3},{6,4},{7,5},{8,6},{9,7},{10,8},{11,9},{12,... | collective-permute-start | bytes 393224 | tf_op jit(solution)/shard_map/ppermute | solution.py:292
  14.0 2.7 %collective-permute-start.11 = (f32[4,8,1024]{2,1,0:T(8,128)S(1)}, f32[4,8,1024]{2,1,0:T(8,128)S(1)}, u32[]{:S(2)}, u32[]{:S(2)}) collective-permute-start(f32[4,8,1024]{2,1,0:T(8,128)S(1)} %get-tuple-element.76), channel_id=1, source_target_pairs={{2,0},{3,1},{4,2},{5,3},{6,4},{7,5},{8,6},{9,7},{10,8},{11,9},{12,... | collective-permute-start | bytes 393224 | tf_op jit(solution)/shard_map/ppermute | solution.py:292
  16.7 0.8 collective-permute-done.2
  17.8 2.7 %collective-permute-start.5 = (f32[8,8,1024]{2,1,0:T(8,128)S(1)}, f32[8,8,1024]{2,1,0:T(8,128)S(1)}, u32[]{:S(2)}, u32[]{:S(2)}) collective-permute-start(f32[8,8,1024]{2,1,0:T(8,128)S(1)} %get-tuple-element.64), channel_id=1, source_target_pairs={{2,0},{3,1},{4,2},{5,3},{6,4},{7,5},{8,6},{9,7},{10,8},{11,9},{12,... | collective-permute-start | bytes 786440 | tf_op jit(solution)/shard_map/ppermute | solution.py:292
  20.6 2.7 %collective-permute-start.13 = (f32[8,8,1024]{2,1,0:T(8,128)S(1)}, f32[8,8,1024]{2,1,0:T(8,128)S(1)}, u32[]{:S(2)}, u32[]{:S(2)}) collective-permute-start(f32[8,8,1024]{2,1,0:T(8,128)S(1)} %get-tuple-element.78), channel_id=1, source_target_pairs={{2,0},{3,1},{4,2},{5,3},{6,4},{7,5},{8,6},{9,7},{10,8},{11,9},{12,... | collective-permute-start | bytes 786440 | tf_op jit(solution)/shard_map/ppermute | solution.py:292
  23.3 2.8 %collective-permute-done.4 = f32[8,8,1024]{2,1,0:T(8,128)S(1)} collective-permute-done((f32[8,8,1024]{2,1,0:T(8,128)S(1)}, f32[8,8,1024]{2,1,0:T(8,128)S(1)}, u32[]{:S(2)}, u32[]{:S(2)}) %collective-permute-start.4) | collective-permute-done | bytes 262176 | tf_op jit(solution)/shard_map/ppermute | solution.py:292
  26.2 1.1 %collective-permute-start.6 = (f32[8,8,1024]{2,1,0:T(8,128)S(1)}, f32[8,8,1024]{2,1,0:T(8,128)S(1)}, u32[]{:S(2)}, u32[]{:S(2)}) collective-permute-start(f32[8,8,1024]{2,1,0:T(8,128)S(1)} %get-tuple-element.65), channel_id=1, source_target_pairs={{0,2},{1,3},{2,4},{3,5},{4,6},{5,7},{6,8},{7,9},{8,10},{9,11},{10,... | collective-permute-start | bytes 786440 | tf_op jit(solution)/shard_map/ppermute | solution.py:292
  27.3 1.7 %collective-permute-start.7 = (f32[8,8,1024]{2,1,0:T(8,128)S(1)}, f32[8,8,1024]{2,1,0:T(8,128)S(1)}, u32[]{:S(2)}, u32[]{:S(2)}) collective-permute-start(f32[8,8,1024]{2,1,0:T(8,128)S(1)} %get-tuple-element.66), channel_id=1, source_target_pairs={{2,0},{3,1},{4,2},{5,3},{6,4},{7,5},{8,6},{9,7},{10,8},{11,9},{12,... | collective-permute-start | bytes 786440 | tf_op jit(solution)/shard_map/ppermute | solution.py:292
  29.0 2.7 %collective-permute-done.12 = f32[8,8,1024]{2,1,0:T(8,128)S(1)} collective-permute-done((f32[8,8,1024]{2,1,0:T(8,128)S(1)}, f32[8,8,1024]{2,1,0:T(8,128)S(1)}, u32[]{:S(2)}, u32[]{:S(2)}) %collective-permute-start.12) | collective-permute-done | bytes 262176 | tf_op jit(solution)/shard_map/ppermute | solution.py:292
  31.8 1.1 %collective-permute-start.14 = (f32[8,8,1024]{2,1,0:T(8,128)S(1)}, f32[8,8,1024]{2,1,0:T(8,128)S(1)}, u32[]{:S(2)}, u32[]{:S(2)}) collective-permute-start(f32[8,8,1024]{2,1,0:T(8,128)S(1)} %get-tuple-element.79), channel_id=1, source_target_pairs={{0,2},{1,3},{2,4},{3,5},{4,6},{5,7},{6,8},{7,9},{8,10},{9,11},{10,... | collective-permute-start | bytes 786440 | tf_op jit(solution)/shard_map/ppermute | solution.py:292
  32.9 1.7 %collective-permute-start.15 = (f32[8,8,1024]{2,1,0:T(8,128)S(1)}, f32[8,8,1024]{2,1,0:T(8,128)S(1)}, u32[]{:S(2)}, u32[]{:S(2)}) collective-permute-start(f32[8,8,1024]{2,1,0:T(8,128)S(1)} %get-tuple-element.80), channel_id=1, source_target_pairs={{2,0},{3,1},{4,2},{5,3},{6,4},{7,5},{8,6},{9,7},{10,8},{11,9},{12,... | collective-permute-start | bytes 786440 | tf_op jit(solution)/shard_map/ppermute | solution.py:292
  34.6 2.7 %collective-permute-done.6 = f32[8,8,1024]{2,1,0:T(8,128)S(1)} collective-permute-done((f32[8,8,1024]{2,1,0:T(8,128)S(1)}, f32[8,8,1024]{2,1,0:T(8,128)S(1)}, u32[]{:S(2)}, u32[]{:S(2)}) %collective-permute-start.6) | collective-permute-done | bytes 262176 | tf_op jit(solution)/shard_map/ppermute | solution.py:292
  37.5 0.8 collective-permute-start.8
  38.3 1.9 %collective-permute-start.9 = (f32[8,8,1024]{2,1,0:T(8,128)S(1)}, f32[8,8,1024]{2,1,0:T(8,128)S(1)}, u32[]{:S(2)}, u32[]{:S(2)}) collective-permute-start(f32[8,8,1024]{2,1,0:T(8,128)S(1)} %get-tuple-element.68), channel_id=1, source_target_pairs={{2,0},{3,1},{4,2},{5,3},{6,4},{7,5},{8,6},{9,7},{10,8},{11,9},{12,... | collective-permute-start | bytes 786440 | tf_op jit(solution)/shard_map/ppermute | solution.py:292
  40.2 2.7 %collective-permute-done.14 = f32[8,8,1024]{2,1,0:T(8,128)S(1)} collective-permute-done((f32[8,8,1024]{2,1,0:T(8,128)S(1)}, f32[8,8,1024]{2,1,0:T(8,128)S(1)}, u32[]{:S(2)}, u32[]{:S(2)}) %collective-permute-start.14) | collective-permute-done | bytes 262176 | tf_op jit(solution)/shard_map/ppermute | solution.py:292
  43.1 0.8 collective-permute-start.16
  43.9 1.9 %collective-permute-start.17 = (f32[8,8,1024]{2,1,0:T(8,128)S(1)}, f32[8,8,1024]{2,1,0:T(8,128)S(1)}, u32[]{:S(2)}, u32[]{:S(2)}) collective-permute-start(f32[8,8,1024]{2,1,0:T(8,128)S(1)} %get-tuple-element.82), channel_id=1, source_target_pairs={{2,0},{3,1},{4,2},{5,3},{6,4},{7,5},{8,6},{9,7},{10,8},{11,9},{12,... | collective-permute-start | bytes 786440 | tf_op jit(solution)/shard_map/ppermute | solution.py:292
  46.5 0.3 block_lists.1.table
  46.8 1.8 %collective-permute-done.8.up = f32[8,8,1024]{2,1,0:T(8,128)S(1)} collective-permute-done((f32[8,8,1024]{2,1,0:T(8,128)S(1)}, f32[8,8,1024]{2,1,0:T(8,128)S(1)}, u32[]{:S(2)}, u32[]{:S(2)}) %collective-permute-start.8) | collective-permute-done | bytes 262176 | tf_op jit(solution)/shard_map/ppermute | solution.py:292
  48.6 2.6 %early_blocks.1.before = f32[256,8,128]{2,1,0:T(8,128)S(1)} custom-call(s32[8,384]{1,0:T(8,128)S(1)} %block_lists.1.table, f32[112,8,1024]{2,1,0:T(8,128)S(1)} %get-tuple-element.69.own, f32[112,8,1024]{2,1,0:T(8,128)S(1)} %collective-permute-done.1.paired, f32[8,8,1024]{2,1,0:T(8,128)S(1)} %collective-permute-done.8.up, ...), custom_call_target="tpu_custom_call" | custom-call | flops 268435456 | bytes 4194304 | tf_op jit(solution)/shard_map/early_blocks/pallas_call | solution.py:180
  51.2 3.0 %collective-permute-done.16.up = f32[8,8,1024]{2,1,0:T(8,128)S(1)} collective-permute-done((f32[8,8,1024]{2,1,0:T(8,128)S(1)}, f32[8,8,1024]{2,1,0:T(8,128)S(1)}, u32[]{:S(2)}, u32[]{:S(2)}) %collective-permute-start.16) | collective-permute-done | bytes 262176 | tf_op jit(solution)/shard_map/ppermute | solution.py:292
  54.2 1.9 %late_blocks.1 = f32[256,8,128]{2,1,0:T(8,128)S(1)} custom-call(f32[256,8,128]{2,1,0:T(8,128)S(1)} %early_blocks.1.before, s32[8,384]{1,0:T(8,128)S(1)} %block_lists.1.table, f32[112,8,1024]{2,1,0:T(8,128)S(1)} %get-tuple-element.69.own, f32[112,8,1024]{2,1,0:T(8,128)S(1)} %collective-permute-done.1.paired, f32[8,8,1024]{2,1,0:T(8,128)S(1)} %collective-permute-done.16.up, ...), custom_call_target="tpu_custom_call" | custom-call | flops 268435456 | bytes 4194304 | tf_op jit(solution)/shard_map/late_blocks/pallas_call | solution.py:180
  56.1 23.4 %all_to_all.10.parts = f32[16,16,8,128]{3,2,1,0:T(8,128)S(1)} all-to-all(f32[16,16,8,128]{3,2,1,0:T(8,128)S(1)} %bitcast.12), channel_id=1, replica_groups=mesh['node'=16,'feat'=16] {'node'}, dimensions={0} | all-to-all | bytes 2097152 | tf_op jit(solution)/shard_map/all_to_all | solution.py:330
  79.7 15.7 %all_to_all.11.parts = f32[16,8,128]{2,1,0:T(8,128)S(1)} all-to-all(f32[16,8,128]{2,1,0:T(8,128)S(1)} %combine.1), channel_id=1, replica_groups=mesh['node'=16,'feat'=16] {'feat'}, dimensions={0} | all-to-all | bytes 131072 | tf_op jit(solution)/shard_map/all_to_all | solution.py:331
  95.4 1.0 %second.1 = f32[32,172]{1,0:T(8,128)} custom-call(f32[16,8,128]{2,1,0:T(8,128)S(1)} %all_to_all.11.parts, f32[1,256]{1,0:T(1,128)S(1)} %bitcast.16, bf16[172,256]{1,0:T(8,128)(2,1)S(1)} %bitcast.13, bf16[172,256]{1,0:T(8,128)(2,1)S(1)} %bitcast.14, f32[1,172]{1,0:T(1,128)S(1)} %bitcast.17, s32[1,32]{1,0:T(1,128)S(1)} %bitcast.20, s32[8,32]{1,0:T(8,128)S(1)} %bitcast.15), custom_call_target="tpu_custom_call" | custom-call | tf_op jit(solution)/shard_map/second/pallas_call | solution.py:250
  (47 shorter events, 1.3 us)
Async XLA Ops:
  0.0 0.9 copy-start
  1.1 2.2 %copy-start.1 = (bf16[8192,256]{1,0:T(8,128)(2,1)S(1)}, bf16[8192,256]{1,0:T(8,128)(2,1)}, u32[]{:S(2)}) copy-start(bf16[8192,256]{1,0:T(8,128)(2,1)} %features.1) | copy-start | bytes 12582916
  3.3 45.2 %slice-start = ((s8[8388608]{0:T(1024)(128)(4,1)}), s8[4194304]{0:T(1024)(128)(4,1)S(1)}, s32[]{:S(2)}) async-start(s8[8388608]{0:T(1024)(128)(4,1)} %bitcast.10), calls=%async_computation.2 | async-start | bytes 8388608
  4.6 4.9 %collective-permute-start = (f32[16,8,1024]{2,1,0:T(8,128)S(1)}, f32[16,8,1024]{2,1,0:T(8,128)S(1)}, u32[]{:S(2)}, u32[]{:S(2)}) collective-permute-start(f32[16,8,1024]{2,1,0:T(8,128)S(1)} %get-tuple-element.44), channel_id=1, source_target_pairs={{0,1},{1,0},{2,3},{3,2},{4,5},{5,4},{6,7},{7,6},{8,9},{9,8},{10,11... | collective-permute-start | bytes 1572872 | tf_op jit(solution)/shard_map/ppermute | solution.py:292
  9.5 7.2 %collective-permute-start.1 = (f32[112,8,1024]{2,1,0:T(8,128)S(1)}, f32[112,8,1024]{2,1,0:T(8,128)S(1)}, u32[]{:S(2)}, u32[]{:S(2)}) collective-permute-start(f32[112,8,1024]{2,1,0:T(8,128)S(1)} %get-tuple-element.46), channel_id=1, source_target_pairs={{0,1},{1,0},{2,3},{3,2},{4,5},{5,4},{6,7},{7,6},{8,9},{9,8},{10,11... | collective-permute-start | bytes 11010056 | tf_op jit(solution)/shard_map/ppermute | solution.py:292
  9.9 7.7 %collective-permute-start.2 = (f32[4,8,1024]{2,1,0:T(8,128)S(1)}, f32[4,8,1024]{2,1,0:T(8,128)S(1)}, u32[]{:S(2)}, u32[]{:S(2)}) collective-permute-start(f32[4,8,1024]{2,1,0:T(8,128)S(1)} %get-tuple-element.61), channel_id=1, source_target_pairs={{0,2},{1,3},{2,4},{3,5},{4,6},{5,7},{6,8},{7,9},{8,10},{9,11},{10,... | collective-permute-start | bytes 393224 | tf_op jit(solution)/shard_map/ppermute | solution.py:292
  10.0 7.6 %collective-permute-start.3 = (f32[4,8,1024]{2,1,0:T(8,128)S(1)}, f32[4,8,1024]{2,1,0:T(8,128)S(1)}, u32[]{:S(2)}, u32[]{:S(2)}) collective-permute-start(f32[4,8,1024]{2,1,0:T(8,128)S(1)} %get-tuple-element.62), channel_id=1, source_target_pairs={{2,0},{3,1},{4,2},{5,3},{6,4},{7,5},{8,6},{9,7},{10,8},{11,9},{12,... | collective-permute-start | bytes 393224 | tf_op jit(solution)/shard_map/ppermute | solution.py:292
  14.0 6.5 %collective-permute-start.10 = (f32[4,8,1024]{2,1,0:T(8,128)S(1)}, f32[4,8,1024]{2,1,0:T(8,128)S(1)}, u32[]{:S(2)}, u32[]{:S(2)}) collective-permute-start(f32[4,8,1024]{2,1,0:T(8,128)S(1)} %get-tuple-element.75), channel_id=1, source_target_pairs={{0,2},{1,3},{2,4},{3,5},{4,6},{5,7},{6,8},{7,9},{8,10},{9,11},{10,... | collective-permute-start | bytes 393224 | tf_op jit(solution)/shard_map/ppermute | solution.py:292
  14.0 6.4 %collective-permute-start.11 = (f32[4,8,1024]{2,1,0:T(8,128)S(1)}, f32[4,8,1024]{2,1,0:T(8,128)S(1)}, u32[]{:S(2)}, u32[]{:S(2)}) collective-permute-start(f32[4,8,1024]{2,1,0:T(8,128)S(1)} %get-tuple-element.76), channel_id=1, source_target_pairs={{2,0},{3,1},{4,2},{5,3},{6,4},{7,5},{8,6},{9,7},{10,8},{11,9},{12,... | collective-permute-start | bytes 393224 | tf_op jit(solution)/shard_map/ppermute | solution.py:292
  17.7 30.9 %slice-start.1 = ((s8[8388608]{0:T(1024)(128)(4,1)}), s8[4194304]{0:T(1024)(128)(4,1)S(1)}, s32[]{:S(2)}) async-start(s8[8388608]{0:T(1024)(128)(4,1)} %bitcast.10), calls=%async_computation.3 | async-start | bytes 8388608
  17.7 8.4 %collective-permute-start.4 = (f32[8,8,1024]{2,1,0:T(8,128)S(1)}, f32[8,8,1024]{2,1,0:T(8,128)S(1)}, u32[]{:S(2)}, u32[]{:S(2)}) collective-permute-start(f32[8,8,1024]{2,1,0:T(8,128)S(1)} %get-tuple-element.63), channel_id=1, source_target_pairs={{0,2},{1,3},{2,4},{3,5},{4,6},{5,7},{6,8},{7,9},{8,10},{9,11},{10,... | collective-permute-start | bytes 786440 | tf_op jit(solution)/shard_map/ppermute | solution.py:292
  17.8 8.3 %collective-permute-start.5 = (f32[8,8,1024]{2,1,0:T(8,128)S(1)}, f32[8,8,1024]{2,1,0:T(8,128)S(1)}, u32[]{:S(2)}, u32[]{:S(2)}) collective-permute-start(f32[8,8,1024]{2,1,0:T(8,128)S(1)} %get-tuple-element.64), channel_id=1, source_target_pairs={{2,0},{3,1},{4,2},{5,3},{6,4},{7,5},{8,6},{9,7},{10,8},{11,9},{12,... | collective-permute-start | bytes 786440 | tf_op jit(solution)/shard_map/ppermute | solution.py:292
  20.5 11.2 %collective-permute-start.12 = (f32[8,8,1024]{2,1,0:T(8,128)S(1)}, f32[8,8,1024]{2,1,0:T(8,128)S(1)}, u32[]{:S(2)}, u32[]{:S(2)}) collective-permute-start(f32[8,8,1024]{2,1,0:T(8,128)S(1)} %get-tuple-element.77), channel_id=1, source_target_pairs={{0,2},{1,3},{2,4},{3,5},{4,6},{5,7},{6,8},{7,9},{8,10},{9,11},{10,... | collective-permute-start | bytes 786440 | tf_op jit(solution)/shard_map/ppermute | solution.py:292
  20.6 11.1 %collective-permute-start.13 = (f32[8,8,1024]{2,1,0:T(8,128)S(1)}, f32[8,8,1024]{2,1,0:T(8,128)S(1)}, u32[]{:S(2)}, u32[]{:S(2)}) collective-permute-start(f32[8,8,1024]{2,1,0:T(8,128)S(1)} %get-tuple-element.78), channel_id=1, source_target_pairs={{2,0},{3,1},{4,2},{5,3},{6,4},{7,5},{8,6},{9,7},{10,8},{11,9},{12,... | collective-permute-start | bytes 786440 | tf_op jit(solution)/shard_map/ppermute | solution.py:292
  26.2 20.3 %copy-start.7 = (s32[256]{0:T(256)S(1)}, s32[256]{0:T(256)}, u32[]{:S(2)}) copy-start(s32[256]{0:T(256)} %param.14) | copy-start | bytes 3076
  26.2 20.3 %copy-start.8 = (s32[256]{0:T(256)S(1)}, s32[256]{0:T(256)}, u32[]{:S(2)}) copy-start(s32[256]{0:T(256)} %param.15) | copy-start | bytes 3076
  26.2 11.1 %collective-permute-start.6 = (f32[8,8,1024]{2,1,0:T(8,128)S(1)}, f32[8,8,1024]{2,1,0:T(8,128)S(1)}, u32[]{:S(2)}, u32[]{:S(2)}) collective-permute-start(f32[8,8,1024]{2,1,0:T(8,128)S(1)} %get-tuple-element.65), channel_id=1, source_target_pairs={{0,2},{1,3},{2,4},{3,5},{4,6},{5,7},{6,8},{7,9},{8,10},{9,11},{10,... | collective-permute-start | bytes 786440 | tf_op jit(solution)/shard_map/ppermute | solution.py:292
  27.3 10.0 %collective-permute-start.7 = (f32[8,8,1024]{2,1,0:T(8,128)S(1)}, f32[8,8,1024]{2,1,0:T(8,128)S(1)}, u32[]{:S(2)}, u32[]{:S(2)}) collective-permute-start(f32[8,8,1024]{2,1,0:T(8,128)S(1)} %get-tuple-element.66), channel_id=1, source_target_pairs={{2,0},{3,1},{4,2},{5,3},{6,4},{7,5},{8,6},{9,7},{10,8},{11,9},{12,... | collective-permute-start | bytes 786440 | tf_op jit(solution)/shard_map/ppermute | solution.py:292
  31.8 11.1 %collective-permute-start.14 = (f32[8,8,1024]{2,1,0:T(8,128)S(1)}, f32[8,8,1024]{2,1,0:T(8,128)S(1)}, u32[]{:S(2)}, u32[]{:S(2)}) collective-permute-start(f32[8,8,1024]{2,1,0:T(8,128)S(1)} %get-tuple-element.79), channel_id=1, source_target_pairs={{0,2},{1,3},{2,4},{3,5},{4,6},{5,7},{6,8},{7,9},{8,10},{9,11},{10,... | collective-permute-start | bytes 786440 | tf_op jit(solution)/shard_map/ppermute | solution.py:292
  32.9 10.0 %collective-permute-start.15 = (f32[8,8,1024]{2,1,0:T(8,128)S(1)}, f32[8,8,1024]{2,1,0:T(8,128)S(1)}, u32[]{:S(2)}, u32[]{:S(2)}) collective-permute-start(f32[8,8,1024]{2,1,0:T(8,128)S(1)} %get-tuple-element.80), channel_id=1, source_target_pairs={{2,0},{3,1},{4,2},{5,3},{6,4},{7,5},{8,6},{9,7},{10,8},{11,9},{12,... | collective-permute-start | bytes 786440 | tf_op jit(solution)/shard_map/ppermute | solution.py:292
  37.5 11.1 %collective-permute-start.8 = (f32[8,8,1024]{2,1,0:T(8,128)S(1)}, f32[8,8,1024]{2,1,0:T(8,128)S(1)}, u32[]{:S(2)}, u32[]{:S(2)}) collective-permute-start(f32[8,8,1024]{2,1,0:T(8,128)S(1)} %get-tuple-element.67), channel_id=1, source_target_pairs={{0,2},{1,3},{2,4},{3,5},{4,6},{5,7},{6,8},{7,9},{8,10},{9,11},{10,... | collective-permute-start | bytes 786440 | tf_op jit(solution)/shard_map/ppermute | solution.py:292
  38.3 10.3 %collective-permute-start.9 = (f32[8,8,1024]{2,1,0:T(8,128)S(1)}, f32[8,8,1024]{2,1,0:T(8,128)S(1)}, u32[]{:S(2)}, u32[]{:S(2)}) collective-permute-start(f32[8,8,1024]{2,1,0:T(8,128)S(1)} %get-tuple-element.68), channel_id=1, source_target_pairs={{2,0},{3,1},{4,2},{5,3},{6,4},{7,5},{8,6},{9,7},{10,8},{11,9},{12,... | collective-permute-start | bytes 786440 | tf_op jit(solution)/shard_map/ppermute | solution.py:292
  43.1 11.1 %collective-permute-start.16 = (f32[8,8,1024]{2,1,0:T(8,128)S(1)}, f32[8,8,1024]{2,1,0:T(8,128)S(1)}, u32[]{:S(2)}, u32[]{:S(2)}) collective-permute-start(f32[8,8,1024]{2,1,0:T(8,128)S(1)} %get-tuple-element.81), channel_id=1, source_target_pairs={{0,2},{1,3},{2,4},{3,5},{4,6},{5,7},{6,8},{7,9},{8,10},{9,11},{10,... | collective-permute-start | bytes 786440 | tf_op jit(solution)/shard_map/ppermute | solution.py:292
  43.9 10.3 %collective-permute-start.17 = (f32[8,8,1024]{2,1,0:T(8,128)S(1)}, f32[8,8,1024]{2,1,0:T(8,128)S(1)}, u32[]{:S(2)}, u32[]{:S(2)}) collective-permute-start(f32[8,8,1024]{2,1,0:T(8,128)S(1)} %get-tuple-element.82), channel_id=1, source_target_pairs={{2,0},{3,1},{4,2},{5,3},{6,4},{7,5},{8,6},{9,7},{10,8},{11,9},{12,... | collective-permute-start | bytes 786440 | tf_op jit(solution)/shard_map/ppermute | solution.py:292
  51.1 44.2 %copy-start.2 = (bf16[256,172]{0,1:T(8,128)(2,1)S(1)}, bf16[256,172]{0,1:T(8,128)(2,1)}, u32[]{:S(2)}) copy-start(bf16[256,172]{0,1:T(8,128)(2,1)} %param.19) | copy-start | bytes 264196
  51.2 44.2 %copy-start.3 = (bf16[256,172]{0,1:T(8,128)(2,1)S(1)}, bf16[256,172]{0,1:T(8,128)(2,1)}, u32[]{:S(2)}) copy-start(bf16[256,172]{0,1:T(8,128)(2,1)} %param.20) | copy-start | bytes 264196
  51.2 44.2 %copy-start.4 = (s32[32,8]{0,1:T(8,128)S(1)}, s32[32,8]{0,1:T(8,128)}, u32[]{:S(2)}) copy-start(s32[32,8]{0,1:T(8,128)} %param.23) | copy-start | bytes 3076
  51.2 44.2 %copy-start.5 = (f32[256]{0:T(256)S(1)}, f32[256]{0:T(256)}, u32[]{:S(2)}) copy-start(f32[256]{0:T(256)} %param.18) | copy-start | bytes 3076
  51.2 44.2 %copy-start.6 = (f32[172]{0:T(256)S(1)}, f32[172]{0:T(256)}, u32[]{:S(2)}) copy-start(f32[172]{0:T(256)} %param.21) | copy-start | bytes 2068
  51.2 44.2 %copy-start.9 = (s32[32]{0:T(128)S(1)}, s32[32]{0:T(128)}, u32[]{:S(2)}) copy-start(s32[32]{0:T(128)} %param.22) | copy-start | bytes 388

commit v9 on v8

v9 whole, which is shorter than its diff:
```python
import functools

import jax
import jax.numpy as jnp
from jax import lax
from jax.experimental import pallas as pl
from jax.experimental.pallas import tpu as pltpu
from jax.sharding import PartitionSpec as P

T_DEV = 64
CHIPS = 8
TILE = 8
RUNS = 8
GROUP = 16
NT = (((1,), (1,)), ((), ()))
VMEM = pl.BlockSpec(memory_space=pltpu.VMEM)
SMEM = pl.BlockSpec(memory_space=pltpu.SMEM)

UNITS = 2 * RUNS


def project_kernel(ordered, features, *outs):
    lanes = outs[0].shape[2]
    tile = min(512, lanes)
    for i in range(features.shape[0] // tile):
        rows = features[i * tile : (i + 1) * tile]
        product = lax.dot_general(ordered[...], rows, NT, preferred_element_type=jnp.float32)
        run, at = divmod(i * tile, lanes)
        take = 0
        for out in outs:
            for k in range(out.shape[0] // RUNS):
                out[k * RUNS + run, :, at : at + tile] = product[take : take + TILE]
                take += TILE


def project(ordered, features):
    rows, columns = features.shape
    hidden = ordered.shape[0]
    shapes = [
        jax.ShapeDtypeStruct((strips * UNITS, TILE, rows // RUNS), jnp.float32)
        for strips in (1, 2, CHIPS - 3)
    ] * 2
    return pl.pallas_call(
        project_kernel,
        in_specs=[VMEM] * 2,
        out_specs=[VMEM] * 6,
        out_shape=shapes,
        name="project",
        compiler_params=pltpu.CompilerParams(vmem_limit_bytes=8 * 2**20),
        cost_estimate=pl.CostEstimate(
            flops=2 * rows * columns * hidden,
            bytes_accessed=rows * columns * 2 + rows * hidden * 4,
            transcendentals=0,
        ),
    )(ordered, features)


def in_hop_order(layer_one):
    hidden = layer_one.shape[1]
    feat = lax.axis_index("feat")
    row = jnp.arange(hidden, dtype=jnp.int32)
    place = row % (hidden // 2) // (2 * TILE)
    hop = (place + 1) // 2
    hop = CHIPS // 2 + jnp.where(place % 2 == 1, -hop, hop)
    chip = ((feat >> 1) + hop) % CHIPS
    core = ((feat & 1) + (row < hidden // 2)) % 2
    wanted = (chip * 2 + core) * (2 * TILE) + row % (2 * TILE)
    pick = (jnp.arange(hidden, dtype=jnp.int32)[None, :] == wanted[:, None]).astype(jnp.bfloat16)
    return lax.dot_general(pick, layer_one, NT, preferred_element_type=jnp.float32).astype(
        jnp.bfloat16
    )


def blocks_kernel(stream, target, source, count, own, paired, up, down, adjacency, out, held):
    out[...] = jnp.zeros_like(out)
    size = adjacency.shape[1]
    lanes = own.shape[2]
    base = own.shape[0] - UNITS + stream * RUNS
    for b in range(held.shape[0]):
        run, at = divmod(b * size, lanes)
        at = slice(at, at + size)
        total = (own[base + run, :, at] + paired[base + run, :, at]) + (
            up[run, :, at] + down[run, :, at]
        )
        upper = total.astype(jnp.bfloat16).astype(jnp.float32)
        held[b] = jnp.concatenate([upper, total - upper], axis=0).astype(jnp.bfloat16)
    slots = adjacency.shape[0]
    live = count[0]

    def products(first):
        values = []
        for k in range(0, GROUP, 2):
            pair = [jnp.minimum(first + k + j, slots - 1) for j in range(2)]
            value = lax.dot_general(
                jnp.concatenate([held[source[s]] for s in pair], axis=0),
                jnp.concatenate([adjacency[s] for s in pair], axis=0),
                NT,
                preferred_element_type=jnp.float32,
            )
            values.append(value[:TILE, :size] + value[TILE : 2 * TILE, :size])
            values.append(value[2 * TILE : 3 * TILE, size:] + value[3 * TILE :, size:])
        return values

    def add(first, values):
        for k in range(GROUP):
            slot = jnp.minimum(first + k, slots - 1)
            out[target[slot]] += jnp.where(first + k < live, values[k], 0.0)

    def whole(i, before):
        after = products(i * GROUP)
        add((i - 1) * GROUP, before)
        return after

    groups = (live + GROUP - 1) // GROUP
    last = lax.fori_loop(1, groups, whole, products(0))
    add((jnp.maximum(groups, 1) - 1) * GROUP, last)


def blocks(stream, lists, own, paired, sums, adjacency, target_blocks):
    slots, size, _ = adjacency.shape
    return pl.pallas_call(
        functools.partial(blocks_kernel, stream),
        in_specs=[SMEM] * 3 + [VMEM] * 5,
        out_specs=VMEM,
        out_shape=jax.ShapeDtypeStruct((target_blocks, TILE, size), jnp.float32),
        scratch_shapes=[pltpu.VMEM((RUNS * own.shape[2] // size, 2 * TILE, size), jnp.bfloat16)],
        name="first_blocks" if stream == 0 else "second_blocks",
        compiler_params=pltpu.CompilerParams(vmem_limit_bytes=8 * 2**20),
        cost_estimate=pl.CostEstimate(
            flops=4 * slots * size * size * UNITS,
            bytes_accessed=slots * size * size,
            transcendentals=0,
        ),
    )(*lists, own, paired, *sums, adjacency)


def combine_kernel(first, second, out):
    size = first.shape[3]
    low = lax.broadcasted_iota(jnp.int32, (TILE, size), 1) < T_DEV
    for chip in range(CHIPS):
        left, right = first[0, chip], second[0, chip]
        for n in range(1, first.shape[0]):
            left += first[n, chip]
            right += second[n, chip]
        out[2 * chip] = jnp.where(low, left, pltpu.roll(right, T_DEV, 1))
        out[2 * chip + 1] = jnp.where(low, pltpu.roll(left, T_DEV, 1), right)


def combine(first, second):
    return pl.pallas_call(
        combine_kernel,
        in_specs=[VMEM] * 2,
        out_specs=VMEM,
        out_shape=jax.ShapeDtypeStruct((2 * CHIPS, *first.shape[2:]), jnp.float32),
        name="combine",
        compiler_params=pltpu.CompilerParams(vmem_limit_bytes=4 * 2**20),
    )(first, second)


def second_kernel(parts, bias_one, self_weight, neigh_weight, bias_two, seeds, neighbors, out):
    rows = []
    for k in range(parts.shape[0]):
        rows += [parts[k], pltpu.roll(parts[k], T_DEV, 1)]
    sums = jnp.concatenate(rows, axis=0)
    bias = jnp.broadcast_to(bias_one[...], (sums.shape[1], sums.shape[0])).T
    hidden = jnp.maximum(sums + bias, 0.0).astype(jnp.bfloat16)
    fan, count = neighbors.shape
    positions = lax.broadcasted_iota(jnp.int32, (hidden.shape[1], count), 0)
    pick_self = (positions == seeds[...]).astype(jnp.float32)
    tally = jnp.zeros(positions.shape, jnp.float32)
    for k in range(fan):
        tally += (positions == neighbors[k : k + 1]).astype(jnp.float32)
    picked = lax.dot_general(
        jnp.concatenate([pick_self.T, tally.T / fan], axis=0).astype(jnp.bfloat16),
        hidden,
        NT,
        preferred_element_type=jnp.float32,
    ).astype(jnp.bfloat16)
    out[...] = (
        lax.dot_general(
            picked[:count], self_weight[...], NT, preferred_element_type=jnp.float32
        )
        + lax.dot_general(
            picked[count:], neigh_weight[...], NT, preferred_element_type=jnp.float32
        )
        + bias_two[...]
    )


def second(parts, bias_one, self_weight, neigh_weight, bias_two, seeds, neighbors):
    return pl.pallas_call(
        second_kernel,
        in_specs=[VMEM] * 7,
        out_specs=VMEM,
        out_shape=jax.ShapeDtypeStruct((seeds.shape[0], bias_two.shape[0]), jnp.float32),
        name="second",
        compiler_params=pltpu.CompilerParams(vmem_limit_bytes=8 * 2**20),
    )(
        parts,
        bias_one[None, :],
        self_weight.T,
        neigh_weight.T,
        bias_two[None, :],
        seeds[None, :],
        neighbors.T,
    )


def on_device(
    features,
    adjacency,
    target_block,
    source_block,
    block_count,
    layer_one,
    bias_one,
    self_weight,
    neigh_weight,
    bias_two,
    seed_ids,
    neighbor_ids,
):
    size = adjacency.shape[1]
    node_count = lax.axis_size("node")
    feat_count = lax.axis_size("feat")
    target_blocks = T_DEV * node_count * feat_count // size

    pair = [(i, i ^ 1) for i in range(feat_count)]
    up = [(i, (i + 2) % feat_count) for i in range(feat_count)]
    down = [((i + 2) % feat_count, i) for i in range(feat_count)]

    def send(value, route):
        return lax.ppermute(value, "feat", route)

    tie = lax.optimization_barrier
    opposite, three, rest, opposite_own, three_own, rest_own = project(
        in_hop_order(layer_one), features
    )
    opposite, three, rest = tie((send(opposite, pair), three, rest))
    three, rest = send(three, pair), send(rest, pair)

    half = RUNS // 2
    lists = target_block, source_block
    order = block_count
    streams = [None, None]

    def advance(k, turn, order, *parts):
        opposite, opposite_own, three, three_own, rest, rest_own = parts
        if turn == 0:
            opposite, opposite_own, order = tie((opposite, opposite_own, order))
            begin = k * RUNS
            middle = begin + half
            onward = opposite_own[begin:middle] + opposite[begin:middle]
            back = opposite_own[middle : middle + half] + opposite[middle : middle + half]
        else:
            onward, back = streams[k]
            if turn == 1:
                zero = jnp.float32(0)
                onward = lax.pad(onward, zero, ((0, half, 0), (0, 0, 0), (0, 0, 0)))
                back = lax.pad(back, zero, ((half, 0, 0), (0, 0, 0), (0, 0, 0)))
                three, three_own, order = tie((three, three_own, order))
                here, there, at = three_own, three, k * RUNS
            else:
                rest, rest_own, order = tie((rest, rest_own, order))
                here, there, at = rest_own, rest, 2 * (turn - 2) * UNITS + k * RUNS
            onward = here[at : at + RUNS] + there[at : at + RUNS] + onward
            at += UNITS
            back = here[at : at + RUNS] + there[at : at + RUNS] + back
        onward, back, order = tie((onward, back, order))
        streams[k] = send(onward, up), send(back, down)
        return order, opposite, opposite_own, three, three_own, rest, rest_own

    state = order, opposite, opposite_own, three, three_own, rest, rest_own
    for k, turn in ((0, 0), (0, 1), (0, 2), (1, 0), (0, 3), (1, 1)):
        state = advance(k, turn, *state)
    first = blocks(
        0, (*lists, state[0]), rest_own, rest, streams[0], adjacency, target_blocks
    )
    first, order = tie((first, state[0]))
    state = advance(1, 2, order, *state[1:])
    first, order = tie((first, state[0]))
    first = lax.all_to_all(first.reshape(node_count, CHIPS, TILE, size), "node", 0, 0)
    order, *_ = advance(1, 3, order, *state[1:])
    last = blocks(1, (*lists, order), rest_own, rest, streams[1], adjacency, target_blocks)
    last = lax.all_to_all(last.reshape(node_count, CHIPS, TILE, size), "node", 0, 0)

    parts = combine(first, last)
    parts = lax.all_to_all(parts, "feat", 0, 0)
    return second(
        parts, bias_one, self_weight, neigh_weight, bias_two, seed_ids, neighbor_ids
    )


def solution(mesh):
    placed = (
        P("node", "feat"),
        P("node", None, None),
        P("node"),
        P("node"),
        P("node"),
        P("feat", None),
        P(),
        P(),
        P(),
        P(),
        P(("node", "feat")),
        P(("node", "feat"), None),
    )
    return jax.shard_map(
        on_device, mesh=mesh, in_specs=placed, out_specs=P(("node", "feat"), None), check_vma=False
    )
```

time: 96.6 us -> 115 us (1.19); the launches traced: 96.4 us -> 116 us
  starting transfers between devices: 27 us -> 33.5 us
  local copies, waits for them, and re-layouts: 3.12 us -> 8.24 us
  Pallas kernels: 7.2 us -> 11.7 us
  other arithmetic: 0.77 us -> 2.47 us
  waiting for transfers between devices: 18.1 us -> 19.6 us
    all_to_all x0 -> x1, starting transfers between devices: none -> 7.7 us  [on_device(): lax.all_to_all(first.reshape(node_count, CHIPS, TILE, size), 'node', 0, 0)]
    all_to_all x1, blocking collectives: 15.7 us -> 22.8 us  [on_device(): parts = lax.all_to_all(parts, 'feat', 0, 0)]
    all_to_all x1, blocking collectives: 23.4 us -> 16.9 us  [on_device(): lax.all_to_all(last.reshape(node_count, CHIPS, TILE, size), 'node', 0, 0)]
    unnamed x24 -> x28, local copies, waits for them, and re-layouts: 3.12 us -> 8.24 us
    pallas_call x5 -> x4, Pallas kernels: 6.17 us -> 10.6 us  [the longest x2 8.19 us: blocks(): pl.pallas_call(functools.partial(blocks_kernel, stream), in_specs=[SMEM]...]
    add x8, other arithmetic: 0.74 us -> 2.44 us  [the longest x6 2.38 us: advance(): back = here[at:at + RUNS] + there[at:at + RUNS] + back]
    ppermute x18 -> x19, waiting for transfers between devices: 18.1 us -> 19.6 us  [send(): return lax.ppermute(value, 'feat', route)]
    ppermute x18 -> x19, starting transfers between devices: 27 us -> 25.8 us  [send(): return lax.ppermute(value, 'feat', route)]
  transfers between devices with their start and end apart: 18 -> 20, of which waited for: 8 -> 9; matrix products, arithmetic and copies ran while one was open for 1% -> 1% of each run, Pallas kernels for 3% -> 7%
where the time goes in v9:
time: 115 us; the launch traced here: 116 us
  blocking collectives  39.7 us (35%)
  starting transfers between devices  33.5 us (29%)
  waiting for transfers between devices  19.6 us (17%)
  Pallas kernels  11.7 us (10%)
  local copies, waits for them, and re-layouts  8.24 us (7%)
  other arithmetic  2.47 us (2%)
    ppermute x19, starting transfers between devices, send(): return lax.ppermute(value, 'feat', route)  25.8 us
    all_to_all x1, blocking collectives, on_device(): parts = lax.all_to_all(parts, 'feat', 0, 0)  22.8 us
    ppermute x19, waiting for transfers between devices, send(): return lax.ppermute(value, 'feat', route)  19.6 us
    all_to_all x1, blocking collectives, on_device(): lax.all_to_all(last.reshape(node_count, CHIPS, TILE, size), 'node', 0, 0)  16.9 us
    unnamed x28, local copies, waits for them, and re-layouts  8.24 us
    pallas_call x2, Pallas kernels, blocks(): pl.pallas_call(functools.partial(blocks_kernel, stream), in_specs=[SMEM]...  8.19 us
    all_to_all x1, starting transfers between devices, on_device(): lax.all_to_all(first.reshape(node_count, CHIPS, TILE, size), 'node', 0, 0)  7.7 us
    add x6, other arithmetic, advance(): back = here[at:at + RUNS] + there[at:at + RUNS] + back  2.38 us
  transfers between devices with their start and end apart: 20, of which 9 were waited for; matrix products, arithmetic and copies ran while one was open for 1% of the time, Pallas kernels for 7%

profile of v9, /device:TPU:1, one launch (start us, length us, event | category | flops | bytes accessed | tf_op | source)
XLA Modules:
  0.0 116.3 jit_solution(1166621853607335154)
XLA Ops:
  0.0 0.9 copy-done
  1.2 2.2 %copy-done.5 = bf16[8192,256]{1,0:T(8,128)(2,1)S(1)} copy-done((bf16[8192,256]{1,0:T(8,128)(2,1)S(1)}, bf16[8192,256]{1,0:T(8,128)(2,1)}, u32[]{:S(2)}) %copy-start.5) | copy-done | bytes 4194328
  3.3 1.3 %project.1 = (f32[16,8,1024]{2,1,0:T(8,128)S(1)}, f32[32,8,1024]{2,1,0:T(8,128)S(1)}, f32[80,8,1024]{2,1,0:T(8,128)S(1)}, f32[16,8,1024]{2,1,0:T(8,128)S(1)}, f3...) custom-call(bf16[256,256]{1,0:T(8,128)(2,1)S(1)} %convolution_convert_fusion.ordered, bf16[8192,256]{1,0:T(8,128)(2,1)S(1)} %copy-done.5), custom_call_target="tpu_custom_call" | custom-call | flops 1073741824 | bytes 12582912 | tf_op jit(solution)/shard_map/project/pallas_call | solution.py:43
  4.6 3.3 %collective-permute-start = (f32[16,8,1024]{2,1,0:T(8,128)S(1)}, f32[16,8,1024]{2,1,0:T(8,128)S(1)}, u32[]{:S(2)}, u32[]{:S(2)}) collective-permute-start(f32[16,8,1024]{2,1,0:T(8,128)S(1)} %get-tuple-element.66), channel_id=1, source_target_pairs={{0,1},{1,0},{2,3},{3,2},{4,5},{5,4},{6,7},{7,6},{8,9},{9,8},{10,11... | collective-permute-start | bytes 1572872 | tf_op jit(solution)/shard_map/ppermute | solution.py:233
  7.9 1.5 %collective-permute-done = f32[16,8,1024]{2,1,0:T(8,128)S(1)} collective-permute-done((f32[16,8,1024]{2,1,0:T(8,128)S(1)}, f32[16,8,1024]{2,1,0:T(8,128)S(1)}, u32[]{:S(2)}, u32[]{:S(2)}) %collective-permute-start) | collective-permute-done | bytes 524320 | tf_op jit(solution)/shard_map/ppermute | solution.py:233
  10.1 3.9 %collective-permute-start.4 = (f32[4,8,1024]{2,1,0:T(8,128)S(1)}, f32[4,8,1024]{2,1,0:T(8,128)S(1)}, u32[]{:S(2)}, u32[]{:S(2)}) collective-permute-start(f32[4,8,1024]{2,1,0:T(8,128)S(1)} %get-tuple-element.82), channel_id=1, source_target_pairs={{2,0},{3,1},{4,2},{5,3},{6,4},{7,5},{8,6},{9,7},{10,8},{11,9},{12,... | collective-permute-start | bytes 393224 | tf_op jit(solution)/shard_map/ppermute | solution.py:233
  14.0 1.9 %collective-permute-done.1 = f32[32,8,1024]{2,1,0:T(8,128)S(1)} collective-permute-done((f32[32,8,1024]{2,1,0:T(8,128)S(1)}, f32[32,8,1024]{2,1,0:T(8,128)S(1)}, u32[]{:S(2)}, u32[]{:S(2)}) %collective-permute-start.1) | collective-permute-done | bytes 1048608 | tf_op jit(solution)/shard_map/ppermute | solution.py:233
  15.9 1.6 %collective-permute-done.3 = f32[4,8,1024]{2,1,0:T(8,128)S(1)} collective-permute-done((f32[4,8,1024]{2,1,0:T(8,128)S(1)}, f32[4,8,1024]{2,1,0:T(8,128)S(1)}, u32[]{:S(2)}, u32[]{:S(2)}) %collective-permute-start.3) | collective-permute-done | bytes 131104 | tf_op jit(solution)/shard_map/ppermute | solution.py:233
  17.7 2.7 %collective-permute-start.6 = (f32[8,8,1024]{2,1,0:T(8,128)S(1)}, f32[8,8,1024]{2,1,0:T(8,128)S(1)}, u32[]{:S(2)}, u32[]{:S(2)}) collective-permute-start(f32[8,8,1024]{2,1,0:T(8,128)S(1)} %get-tuple-element.88), channel_id=1, source_target_pairs={{2,0},{3,1},{4,2},{5,3},{6,4},{7,5},{8,6},{9,7},{10,8},{11,9},{12,... | collective-permute-start | bytes 786440 | tf_op jit(solution)/shard_map/ppermute | solution.py:233
  20.4 5.5 %collective-permute-done.5 = f32[8,8,1024]{2,1,0:T(8,128)S(1)} collective-permute-done((f32[8,8,1024]{2,1,0:T(8,128)S(1)}, f32[8,8,1024]{2,1,0:T(8,128)S(1)}, u32[]{:S(2)}, u32[]{:S(2)}) %collective-permute-start.5) | collective-permute-done | bytes 262176 | tf_op jit(solution)/shard_map/ppermute | solution.py:233
  25.9 1.0 collective-permute-start.7
  26.9 1.8 %collective-permute-start.8 = (f32[8,8,1024]{2,1,0:T(8,128)S(1)}, f32[8,8,1024]{2,1,0:T(8,128)S(1)}, u32[]{:S(2)}, u32[]{:S(2)}) collective-permute-start(f32[8,8,1024]{2,1,0:T(8,128)S(1)} %get-tuple-element.98), channel_id=1, source_target_pairs={{2,0},{3,1},{4,2},{5,3},{6,4},{7,5},{8,6},{9,7},{10,8},{11,9},{12,... | collective-permute-start | bytes 786440 | tf_op jit(solution)/shard_map/ppermute | solution.py:233
  28.7 1.2 %collective-permute-start.10 = (f32[4,8,1024]{2,1,0:T(8,128)S(1)}, f32[4,8,1024]{2,1,0:T(8,128)S(1)}, u32[]{:S(2)}, u32[]{:S(2)}) collective-permute-start(f32[4,8,1024]{2,1,0:T(8,128)S(1)} %get-tuple-element.104), channel_id=1, source_target_pairs={{2,0},{3,1},{4,2},{5,3},{6,4},{7,5},{8,6},{9,7},{10,8},{11,9},{12,... | collective-permute-start | bytes 393224 | tf_op jit(solution)/shard_map/ppermute | solution.py:233
  30.3 3.0 %collective-permute-done.7 = f32[8,8,1024]{2,1,0:T(8,128)S(1)} collective-permute-done((f32[8,8,1024]{2,1,0:T(8,128)S(1)}, f32[8,8,1024]{2,1,0:T(8,128)S(1)}, u32[]{:S(2)}, u32[]{:S(2)}) %collective-permute-start.7) | collective-permute-done | bytes 262176 | tf_op jit(solution)/shard_map/ppermute | solution.py:233
  33.4 0.8 collective-permute-start.11
  34.2 1.9 %collective-permute-start.12 = (f32[8,8,1024]{2,1,0:T(8,128)S(1)}, f32[8,8,1024]{2,1,0:T(8,128)S(1)}, u32[]{:S(2)}, u32[]{:S(2)}) collective-permute-start(f32[8,8,1024]{2,1,0:T(8,128)S(1)} %get-tuple-element.108), channel_id=1, source_target_pairs={{2,0},{3,1},{4,2},{5,3},{6,4},{7,5},{8,6},{9,7},{10,8},{11,9},{12,... | collective-permute-start | bytes 786440 | tf_op jit(solution)/shard_map/ppermute | solution.py:233
  36.9 2.7 %collective-permute-start.14 = (f32[8,8,1024]{2,1,0:T(8,128)S(1)}, f32[8,8,1024]{2,1,0:T(8,128)S(1)}, u32[]{:S(2)}, u32[]{:S(2)}) collective-permute-start(f32[8,8,1024]{2,1,0:T(8,128)S(1)} %get-tuple-element.114), channel_id=1, source_target_pairs={{2,0},{3,1},{4,2},{5,3},{6,4},{7,5},{8,6},{9,7},{10,8},{11,9},{12,... | collective-permute-start | bytes 786440 | tf_op jit(solution)/shard_map/ppermute | solution.py:233
  40.2 0.9 collective-permute-done.11.up
  41.2 4.6 %first_blocks.1 = f32[128,8,128]{2,1,0:T(8,128)} custom-call(s32[256]{0:T(256)S(1)} %copy-done.9, s32[256]{0:T(256)S(1)} %copy-done.10, s32[1]{0:T(128)S(6)} %copy.13.count, f32[80,8,1024]{2,1,0:T(8,128)S(1)} %get-tuple-element.119.own, f32[80,8,1024]{2,1,0:T(8,128)S(1)} %collective-permute-done.2.paired, f32[8,8,1024]{2,1,0:T(8,128)S(1)} %collective-permute-done.11.up, ...), custom_call_target="tpu_custom_call" | custom-call | flops 268435456 | bytes 4194304 | tf_op jit(solution)/shard_map/first_blocks/pallas_call | solution.py:121
  45.8 0.8 collective-permute-done.13
  47.8 2.3 %collective-permute-start.16 = (f32[8,8,1024]{2,1,0:T(8,128)S(1)}, f32[8,8,1024]{2,1,0:T(8,128)}, u32[]{:S(2)}, u32[]{:S(2)}) collective-permute-start(f32[8,8,1024]{2,1,0:T(8,128)S(1)} %get-tuple-element.122), channel_id=1, source_target_pairs={{2,0},{3,1},{4,2},{5,3},{6,4},{7,5},{8,6},{9,7},{10,8},{11,9},{12,... | collective-permute-start | bytes 786440 | tf_op jit(solution)/shard_map/ppermute | solution.py:233
  50.1 7.7 %all-to-all-start = ((f32[16,8,8,128]{3,2,1,0:T(8,128)}), f32[16,8,8,128]{3,2,1,0:T(8,128)}, u32[]{:S(2)}, u32[]{:S(2)}) async-start(f32[16,8,8,128]{3,2,1,0:T(8,128)} %bitcast), calls=%async_computation | async-start | bytes 1048576 | tf_op jit(solution)/shard_map/all_to_all | solution.py:282
  57.8 1.3 %add_add_fusion = (f32[8,8,1024]{2,1,0:T(8,128)S(1)}, f32[8,8,1024]{2,1,0:T(8,128)S(1)}) fusion(f32[8,8,1024]{2,1,0:T(8,128)} %collective-permute-done.16, f32[80,8,1024]{2,1,0:T(8,128)} %copy-done.3, f32[80,8,1024]{2,1,0:T(8,128)S(1)} %get-tuple-element.119.own, f32[8,8,1024]{2,1,0:T(8,128)S(1)} %collective-permute-done.15), kind=kLoop, calls=%fused_computation.1 | loop fusion | flops 262144 | bytes 2097152 | tf_op jit(solution)/shard_map/add | solution.py:268
  59.2 2.7 %collective-permute-start.18 = (f32[8,8,1024]{2,1,0:T(8,128)S(1)}, f32[8,8,1024]{2,1,0:T(8,128)S(1)}, u32[]{:S(2)}, u32[]{:S(2)}) collective-permute-start(f32[8,8,1024]{2,1,0:T(8,128)S(1)} %get-tuple-element.126), channel_id=1, source_target_pairs={{2,0},{3,1},{4,2},{5,3},{6,4},{7,5},{8,6},{9,7},{10,8},{11,9},{12,... | collective-permute-start | bytes 786440 | tf_op jit(solution)/shard_map/ppermute | solution.py:233
  61.9 3.8 %collective-permute-done.17.up = f32[8,8,1024]{2,1,0:T(8,128)S(1)} collective-permute-done((f32[8,8,1024]{2,1,0:T(8,128)S(1)}, f32[8,8,1024]{2,1,0:T(8,128)S(1)}, u32[]{:S(2)}, u32[]{:S(2)}) %collective-permute-start.17) | collective-permute-done | bytes 262176 | tf_op jit(solution)/shard_map/ppermute | solution.py:233
  65.7 3.4 %copy-done.2 = bf16[256,128,128]{2,1,0:T(8,128)(2,1)S(1)} copy-done((bf16[256,128,128]{2,1,0:T(8,128)(2,1)S(1)}, bf16[256,128,128]{2,1,0:T(8,128)(2,1)}, u32[]{:S(2)}) %copy-start.2) | copy-done | bytes 8388632
  69.1 1.7 %copy-done.4 = f32[80,8,1024]{2,1,0:T(8,128)S(1)} copy-done((f32[80,8,1024]{2,1,0:T(8,128)S(1)}, f32[80,8,1024]{2,1,0:T(8,128)}, u32[]{:S(2)}) %copy-start.4) | copy-done | bytes 2621464
  70.8 3.6 %second_blocks.1 = f32[128,8,128]{2,1,0:T(8,128)S(1)} custom-call(s32[256]{0:T(256)S(1)} %copy-done.9, s32[256]{0:T(256)S(1)} %copy-done.10, s32[1]{0:T(128)S(6)} %copy.13.count, f32[80,8,1024]{2,1,0:T(8,128)S(1)} %get-tuple-element.119.own, f32[80,8,1024]{2,1,0:T(8,128)S(1)} %copy-done.4, f32[8,8,1024]{2,1,0:T(8,128)S(1)} %collective-permute-done.17.up, ...), custom_call_target="tpu_custom_call" | custom-call | flops 268435456 | bytes 4194304 | tf_op jit(solution)/shard_map/second_blocks/pallas_call | solution.py:121
  74.4 16.9 %all_to_all.15.second = f32[16,8,8,128]{3,2,1,0:T(8,128)S(1)} all-to-all(f32[16,8,8,128]{3,2,1,0:T(8,128)S(1)} %bitcast.9), channel_id=1, replica_groups=mesh['node'=16,'feat'=16] {'node'}, dimensions={0} | all-to-all | bytes 1048576 | tf_op jit(solution)/shard_map/all_to_all | solution.py:285
  91.3 1.2 %combine.1 = f32[16,8,128]{2,1,0:T(8,128)S(1)} custom-call(f32[16,8,8,128]{3,2,1,0:T(8,128)} %all-to-all-done.first, f32[16,8,8,128]{3,2,1,0:T(8,128)S(1)} %all_to_all.15.second), custom_call_target="tpu_custom_call" | custom-call | tf_op jit(solution)/shard_map/combine/pallas_call | solution.py:150
  92.4 22.8 %all_to_all.16.parts = f32[16,8,128]{2,1,0:T(8,128)S(1)} all-to-all(f32[16,8,128]{2,1,0:T(8,128)S(1)} %combine.1), channel_id=1, replica_groups=mesh['node'=16,'feat'=16] {'feat'}, dimensions={0} | all-to-all | bytes 131072 | tf_op jit(solution)/shard_map/all_to_all | solution.py:288
  115.3 1.0 second.1
  (53 shorter events, 3.8 us)
Async XLA Ops:
  1.1 2.2 %copy-start.5 = (bf16[8192,256]{1,0:T(8,128)(2,1)S(1)}, bf16[8192,256]{1,0:T(8,128)(2,1)}, u32[]{:S(2)}) copy-start(bf16[8192,256]{1,0:T(8,128)(2,1)} %features.1) | copy-start | bytes 12582916
  4.6 4.9 %collective-permute-start = (f32[16,8,1024]{2,1,0:T(8,128)S(1)}, f32[16,8,1024]{2,1,0:T(8,128)S(1)}, u32[]{:S(2)}, u32[]{:S(2)}) collective-permute-start(f32[16,8,1024]{2,1,0:T(8,128)S(1)} %get-tuple-element.66), channel_id=1, source_target_pairs={{0,1},{1,0},{2,3},{3,2},{4,5},{5,4},{6,7},{7,6},{8,9},{9,8},{10,11... | collective-permute-start | bytes 1572872 | tf_op jit(solution)/shard_map/ppermute | solution.py:233
  9.5 10.9 %collective-permute-start.2 = (f32[80,8,1024]{2,1,0:T(8,128)S(1)}, f32[80,8,1024]{2,1,0:T(8,128)S(1)}, u32[]{:S(2)}, u32[]{:S(2)}) collective-permute-start(f32[80,8,1024]{2,1,0:T(8,128)S(1)} %get-tuple-element.79), channel_id=1, source_target_pairs={{0,1},{1,0},{2,3},{3,2},{4,5},{5,4},{6,7},{7,6},{8,9},{9,8},{10,11... | collective-permute-start | bytes 7864328 | tf_op jit(solution)/shard_map/ppermute | solution.py:233
  9.9 6.0 %collective-permute-start.1 = (f32[32,8,1024]{2,1,0:T(8,128)S(1)}, f32[32,8,1024]{2,1,0:T(8,128)S(1)}, u32[]{:S(2)}, u32[]{:S(2)}) collective-permute-start(f32[32,8,1024]{2,1,0:T(8,128)S(1)} %get-tuple-element.69), channel_id=1, source_target_pairs={{0,1},{1,0},{2,3},{3,2},{4,5},{5,4},{6,7},{7,6},{8,9},{9,8},{10,11... | collective-permute-start | bytes 3145736 | tf_op jit(solution)/shard_map/ppermute | solution.py:233
  10.0 7.5 %collective-permute-start.3 = (f32[4,8,1024]{2,1,0:T(8,128)S(1)}, f32[4,8,1024]{2,1,0:T(8,128)S(1)}, u32[]{:S(2)}, u32[]{:S(2)}) collective-permute-start(f32[4,8,1024]{2,1,0:T(8,128)S(1)} %get-tuple-element.81), channel_id=1, source_target_pairs={{0,2},{1,3},{2,4},{3,5},{4,6},{5,7},{6,8},{7,9},{8,10},{9,11},{10,... | collective-permute-start | bytes 393224 | tf_op jit(solution)/shard_map/ppermute | solution.py:233
  10.1 7.4 %collective-permute-start.4 = (f32[4,8,1024]{2,1,0:T(8,128)S(1)}, f32[4,8,1024]{2,1,0:T(8,128)S(1)}, u32[]{:S(2)}, u32[]{:S(2)}) collective-permute-start(f32[4,8,1024]{2,1,0:T(8,128)S(1)} %get-tuple-element.82), channel_id=1, source_target_pairs={{2,0},{3,1},{4,2},{5,3},{6,4},{7,5},{8,6},{9,7},{10,8},{11,9},{12,... | collective-permute-start | bytes 393224 | tf_op jit(solution)/shard_map/ppermute | solution.py:233
  17.5 23.7 %copy-start.1 = (bf16[256,128,128]{2,1,0:T(8,128)(2,1)S(1)}, bf16[256,128,128]{2,1,0:T(8,128)(2,1)}, u32[]{:S(2)}) copy-start(bf16[256,128,128]{2,1,0:T(8,128)(2,1)} %adjacency.3) | copy-start | bytes 25165828
  17.6 8.2 %collective-permute-start.5 = (f32[8,8,1024]{2,1,0:T(8,128)S(1)}, f32[8,8,1024]{2,1,0:T(8,128)S(1)}, u32[]{:S(2)}, u32[]{:S(2)}) collective-permute-start(f32[8,8,1024]{2,1,0:T(8,128)S(1)} %get-tuple-element.87), channel_id=1, source_target_pairs={{0,2},{1,3},{2,4},{3,5},{4,6},{5,7},{6,8},{7,9},{8,10},{9,11},{10,... | collective-permute-start | bytes 786440 | tf_op jit(solution)/shard_map/ppermute | solution.py:233
  17.7 8.1 %collective-permute-start.6 = (f32[8,8,1024]{2,1,0:T(8,128)S(1)}, f32[8,8,1024]{2,1,0:T(8,128)S(1)}, u32[]{:S(2)}, u32[]{:S(2)}) collective-permute-start(f32[8,8,1024]{2,1,0:T(8,128)S(1)} %get-tuple-element.88), channel_id=1, source_target_pairs={{2,0},{3,1},{4,2},{5,3},{6,4},{7,5},{8,6},{9,7},{10,8},{11,9},{12,... | collective-permute-start | bytes 786440 | tf_op jit(solution)/shard_map/ppermute | solution.py:233
  20.4 26.3 %copy-start.3 = (f32[80,8,1024]{2,1,0:T(8,128)}, f32[80,8,1024]{2,1,0:T(8,128)S(1)}, u32[]{:S(2)}) copy-start(f32[80,8,1024]{2,1,0:T(8,128)S(1)} %collective-permute-done.2.paired) | copy-start | bytes 7864324
  25.9 15.3 %copy-start.9 = (s32[256]{0:T(256)S(1)}, s32[256]{0:T(256)}, u32[]{:S(2)}) copy-start(s32[256]{0:T(256)} %target.3) | copy-start | bytes 3076
  25.9 15.3 %copy-start.10 = (s32[256]{0:T(256)S(1)}, s32[256]{0:T(256)}, u32[]{:S(2)}) copy-start(s32[256]{0:T(256)} %source.3) | copy-start | bytes 3076
  25.9 7.3 %collective-permute-start.7 = (f32[8,8,1024]{2,1,0:T(8,128)S(1)}, f32[8,8,1024]{2,1,0:T(8,128)S(1)}, u32[]{:S(2)}, u32[]{:S(2)}) collective-permute-start(f32[8,8,1024]{2,1,0:T(8,128)S(1)} %get-tuple-element.97), channel_id=1, source_target_pairs={{0,2},{1,3},{2,4},{3,5},{4,6},{5,7},{6,8},{7,9},{8,10},{9,11},{10,... | collective-permute-start | bytes 786440 | tf_op jit(solution)/shard_map/ppermute | solution.py:233
  26.9 6.4 %collective-permute-start.8 = (f32[8,8,1024]{2,1,0:T(8,128)S(1)}, f32[8,8,1024]{2,1,0:T(8,128)S(1)}, u32[]{:S(2)}, u32[]{:S(2)}) collective-permute-start(f32[8,8,1024]{2,1,0:T(8,128)S(1)} %get-tuple-element.98), channel_id=1, source_target_pairs={{2,0},{3,1},{4,2},{5,3},{6,4},{7,5},{8,6},{9,7},{10,8},{11,9},{12,... | collective-permute-start | bytes 786440 | tf_op jit(solution)/shard_map/ppermute | solution.py:233
  28.7 7.4 %collective-permute-start.10 = (f32[4,8,1024]{2,1,0:T(8,128)S(1)}, f32[4,8,1024]{2,1,0:T(8,128)S(1)}, u32[]{:S(2)}, u32[]{:S(2)}) collective-permute-start(f32[4,8,1024]{2,1,0:T(8,128)S(1)} %get-tuple-element.104), channel_id=1, source_target_pairs={{2,0},{3,1},{4,2},{5,3},{6,4},{7,5},{8,6},{9,7},{10,8},{11,9},{12,... | collective-permute-start | bytes 393224 | tf_op jit(solution)/shard_map/ppermute | solution.py:233
  30.0 6.8 %collective-permute-start.9 = (f32[4,8,1024]{2,1,0:T(8,128)S(1)}, f32[4,8,1024]{2,1,0:T(8,128)S(1)}, u32[]{:S(2)}, u32[]{:S(2)}) collective-permute-start(f32[4,8,1024]{2,1,0:T(8,128)S(1)} %get-tuple-element.103), channel_id=1, source_target_pairs={{0,2},{1,3},{2,4},{3,5},{4,6},{5,7},{6,8},{7,9},{8,10},{9,11},{10,... | collective-permute-start | bytes 393224 | tf_op jit(solution)/shard_map/ppermute | solution.py:233
  33.4 7.8 %collective-permute-start.11 = (f32[8,8,1024]{2,1,0:T(8,128)S(1)}, f32[8,8,1024]{2,1,0:T(8,128)S(1)}, u32[]{:S(2)}, u32[]{:S(2)}) collective-permute-start(f32[8,8,1024]{2,1,0:T(8,128)S(1)} %get-tuple-element.107), channel_id=1, source_target_pairs={{0,2},{1,3},{2,4},{3,5},{4,6},{5,7},{6,8},{7,9},{8,10},{9,11},{10,... | collective-permute-start | bytes 786440 | tf_op jit(solution)/shard_map/ppermute | solution.py:233
  34.2 7.0 %collective-permute-start.12 = (f32[8,8,1024]{2,1,0:T(8,128)S(1)}, f32[8,8,1024]{2,1,0:T(8,128)S(1)}, u32[]{:S(2)}, u32[]{:S(2)}) collective-permute-start(f32[8,8,1024]{2,1,0:T(8,128)S(1)} %get-tuple-element.108), channel_id=1, source_target_pairs={{2,0},{3,1},{4,2},{5,3},{6,4},{7,5},{8,6},{9,7},{10,8},{11,9},{12,... | collective-permute-start | bytes 786440 | tf_op jit(solution)/shard_map/ppermute | solution.py:233
  36.8 9.8 %collective-permute-start.13 = (f32[8,8,1024]{2,1,0:T(8,128)S(1)}, f32[8,8,1024]{2,1,0:T(8,128)S(1)}, u32[]{:S(2)}, u32[]{:S(2)}) collective-permute-start(f32[8,8,1024]{2,1,0:T(8,128)S(1)} %get-tuple-element.113), channel_id=1, source_target_pairs={{0,2},{1,3},{2,4},{3,5},{4,6},{5,7},{6,8},{7,9},{8,10},{9,11},{10,... | collective-permute-start | bytes 786440 | tf_op jit(solution)/shard_map/ppermute | solution.py:233
  36.9 9.7 %collective-permute-start.14 = (f32[8,8,1024]{2,1,0:T(8,128)S(1)}, f32[8,8,1024]{2,1,0:T(8,128)S(1)}, u32[]{:S(2)}, u32[]{:S(2)}) collective-permute-start(f32[8,8,1024]{2,1,0:T(8,128)S(1)} %get-tuple-element.114), channel_id=1, source_target_pairs={{2,0},{3,1},{4,2},{5,3},{6,4},{7,5},{8,6},{9,7},{10,8},{11,9},{12,... | collective-permute-start | bytes 786440 | tf_op jit(solution)/shard_map/ppermute | solution.py:233
  47.4 10.4 %collective-permute-start.15 = (f32[8,8,1024]{2,1,0:T(8,128)}, f32[8,8,1024]{2,1,0:T(8,128)S(1)}, u32[]{:S(2)}, u32[]{:S(2)}) collective-permute-start(f32[8,8,1024]{2,1,0:T(8,128)} %get-tuple-element.121), channel_id=1, source_target_pairs={{0,2},{1,3},{2,4},{3,5},{4,6},{5,7},{6,8},{7,9},{8,10},{9,11},{10,... | collective-permute-start | bytes 786440 | tf_op jit(solution)/shard_map/ppermute | solution.py:233
  47.8 10.0 %collective-permute-start.16 = (f32[8,8,1024]{2,1,0:T(8,128)S(1)}, f32[8,8,1024]{2,1,0:T(8,128)}, u32[]{:S(2)}, u32[]{:S(2)}) collective-permute-start(f32[8,8,1024]{2,1,0:T(8,128)S(1)} %get-tuple-element.122), channel_id=1, source_target_pairs={{2,0},{3,1},{4,2},{5,3},{6,4},{7,5},{8,6},{9,7},{10,8},{11,9},{12,... | collective-permute-start | bytes 786440 | tf_op jit(solution)/shard_map/ppermute | solution.py:233
  50.1 24.3 %all-to-all-start = ((f32[16,8,8,128]{3,2,1,0:T(8,128)}), f32[16,8,8,128]{3,2,1,0:T(8,128)}, u32[]{:S(2)}, u32[]{:S(2)}) async-start(f32[16,8,8,128]{3,2,1,0:T(8,128)} %bitcast), calls=%async_computation | async-start | bytes 1048576 | tf_op jit(solution)/shard_map/all_to_all | solution.py:282
  57.8 57.5 %copy-start.6 = (bf16[256,172]{0,1:T(8,128)(2,1)S(1)}, bf16[256,172]{0,1:T(8,128)(2,1)}, u32[]{:S(2)}) copy-start(bf16[256,172]{0,1:T(8,128)(2,1)} %param.19) | copy-start | bytes 264196
  57.8 57.4 %copy-start.7 = (bf16[256,172]{0,1:T(8,128)(2,1)S(1)}, bf16[256,172]{0,1:T(8,128)(2,1)}, u32[]{:S(2)}) copy-start(bf16[256,172]{0,1:T(8,128)(2,1)} %param.20) | copy-start | bytes 264196
  57.8 57.4 %copy-start.8 = (s32[32,8]{0,1:T(8,128)S(1)}, s32[32,8]{0,1:T(8,128)}, u32[]{:S(2)}) copy-start(s32[32,8]{0,1:T(8,128)} %param.23) | copy-start | bytes 3076
  59.1 56.2 %copy-start.12 = (f32[172]{0:T(256)S(1)}, f32[172]{0:T(256)}, u32[]{:S(2)}) copy-start(f32[172]{0:T(256)} %param.21) | copy-start | bytes 2068
  59.1 56.2 %copy-start.11 = (f32[256]{0:T(256)S(1)}, f32[256]{0:T(256)}, u32[]{:S(2)}) copy-start(f32[256]{0:T(256)} %param.18) | copy-start | bytes 3076
  59.1 56.2 %copy-start.13 = (s32[32]{0:T(128)S(1)}, s32[32]{0:T(128)}, u32[]{:S(2)}) copy-start(s32[32]{0:T(128)} %param.22) | copy-start | bytes 388
  59.2 6.5 %collective-permute-start.17 = (f32[8,8,1024]{2,1,0:T(8,128)S(1)}, f32[8,8,1024]{2,1,0:T(8,128)S(1)}, u32[]{:S(2)}, u32[]{:S(2)}) collective-permute-start(f32[8,8,1024]{2,1,0:T(8,128)S(1)} %get-tuple-element.125), channel_id=1, source_target_pairs={{0,2},{1,3},{2,4},{3,5},{4,6},{5,7},{6,8},{7,9},{8,10},{9,11},{10,... | collective-permute-start | bytes 786440 | tf_op jit(solution)/shard_map/ppermute | solution.py:233
  59.2 6.4 %collective-permute-start.18 = (f32[8,8,1024]{2,1,0:T(8,128)S(1)}, f32[8,8,1024]{2,1,0:T(8,128)S(1)}, u32[]{:S(2)}, u32[]{:S(2)}) collective-permute-start(f32[8,8,1024]{2,1,0:T(8,128)S(1)} %get-tuple-element.126), channel_id=1, source_target_pairs={{2,0},{3,1},{4,2},{5,3},{6,4},{7,5},{8,6},{9,7},{10,8},{11,9},{12,... | collective-permute-start | bytes 786440 | tf_op jit(solution)/shard_map/ppermute | solution.py:233
  65.7 3.4 %copy-start.2 = (bf16[256,128,128]{2,1,0:T(8,128)(2,1)S(1)}, bf16[256,128,128]{2,1,0:T(8,128)(2,1)}, u32[]{:S(2)}) copy-start(bf16[256,128,128]{2,1,0:T(8,128)(2,1)} %adjacency.3) | copy-start | bytes 25165828
  (2 other events, 2.6 us)

commit v10 on v8

--- a/solution.py
+++ b/solution.py
@@ -30,7 +30,11 @@
         take = 0
         for out in outs:
             for k in range(out.shape[0] // RUNS):
-                unit = k // 2 * UNITS + 2 * run + k % 2
+                if out.shape[0] == UNITS:
+                    stream, place = divmod(run, RUNS // 2)
+                    unit = place // 2 * RUNS + stream * RUNS // 2 + place % 2 * 2 + k
+                else:
+                    unit = k // 2 * UNITS + 2 * run + k % 2
                 out[unit, :, at : at + tile] = product[take : take + TILE]
                 take += TILE
 
@@ -40,12 +44,12 @@
     hidden = ordered.shape[0]
     shapes = [
         jax.ShapeDtypeStruct((strips * UNITS, TILE, rows // RUNS), jnp.float32)
-        for strips in (1, CHIPS - 1)
+        for strips in (1, 2, CHIPS - 3)
     ] * 2
     return pl.pallas_call(
         project_kernel,
         in_specs=[VMEM] * 2,
-        out_specs=[VMEM] * 4,
+        out_specs=[VMEM] * 6,
         out_shape=shapes,
         name="project",
         compiler_params=pltpu.CompilerParams(vmem_limit_bytes=8 * 2**20),
@@ -292,36 +296,39 @@
         return lax.ppermute(value, "feat", route)
 
     tie = lax.optimization_barrier
-    opposite, rest, opposite_own, rest_own = project(in_hop_order(layer_one), features)
-    opposite, rest = tie((send(opposite, pair), rest))
+    opposite, three, rest, opposite_own, three_own, rest_own = project(
+        in_hop_order(layer_one), features
+    )
+    opposite, three = tie((send(opposite, pair), three))
+    three = send(three, pair)
+
+    half = RUNS // 2
+    onward = send(opposite_own[:RUNS] + opposite[:RUNS], up)
+    back = send(opposite_own[RUNS:] + opposite[RUNS:], down)
+    onward, back, three, rest = tie((onward, back, three, rest))
     rest = send(rest, pair)
-
+    streams = [(onward[:half], back[:half]), (onward[half:], back[half:])]
     order = block_count
-    streams = []
-    for begin, end in SPANS:
-        middle = (end - begin) // 2
-        opposite, opposite_own, order = tie((opposite, opposite_own, order))
-        onward = opposite_own[begin : begin + middle] + opposite[begin : begin + middle]
-        back = opposite_own[begin + middle : end] + opposite[begin + middle : end]
-        onward, back, order = tie((onward, back, order))
-        streams.append((send(onward, up), send(back, down)))
     for turn in range(3):
         for k, (begin, end) in enumerate(SPANS):
             onward, back = streams[k]
             if turn == 0:
                 zero = jnp.float32(0)
-                onward = lax.pad(onward, zero, ((0, (end - begin) // 2, 0), (0, 0, 0), (0, 0, 0)))
-                back = lax.pad(back, zero, (((end - begin) // 2, 0, 0), (0, 0, 0), (0, 0, 0)))
-            rest, rest_own, order = tie((rest, rest_own, order))
-            at = 2 * turn * UNITS
-            onward = rest_own[at + begin : at + end] + rest[at + begin : at + end] + onward
+                onward = lax.pad(onward, zero, ((0, half, 0), (0, 0, 0), (0, 0, 0)))
+                back = lax.pad(back, zero, ((half, 0, 0), (0, 0, 0), (0, 0, 0)))
+                three, three_own, order = tie((three, three_own, order))
+                here, there, at = three_own, three, 0
+            else:
+                rest, rest_own, order = tie((rest, rest_own, order))
+                here, there, at = rest_own, rest, 2 * (turn - 1) * UNITS
+            onward = here[at + begin : at + end] + there[at + begin : at + end] + onward
             at += UNITS
-            back = rest_own[at + begin : at + end] + rest[at + begin : at + end] + back
+            back = here[at + begin : at + end] + there[at + begin : at + end] + back
             onward, back, order = tie((onward, back, order))
             streams[k] = send(onward, up), send(back, down)
 
     early = SPANS[0][1] // 2 * (features.shape[0] // RUNS) // size
-    lists = block_lists(target_block, source_block, block_count, early)
+    lists = block_lists(target_block, source_block, order, early)
     partial = None
     for stream in streams:
         partial = blocks(partial, lists, rest_own, rest, stream, adjacency, target_blocks)

time: 96.6 us -> 99.9 us (1.034)
  waiting for transfers between devices: 18.1 us -> 21.3 us
  Pallas kernels: 7.2 us -> 9.2 us
  blocking collectives: 39.1 us -> 37.5 us
    all_to_all x1, blocking collectives: 23.4 us -> 20 us  [on_device(): parts = combine(lax.all_to_all(partial, 'node', 0, 0))]
    ppermute x18 -> x17, waiting for transfers between devices: 18.1 us -> 21.3 us  [send(): return lax.ppermute(value, 'feat', route)]
    pallas_call x2, Pallas kernels: 4.47 us -> 6.48 us  [blocks(): pl.pallas_call(late_kernel if late else early_kernel, in_specs=[VMEM] * l...]
    all_to_all x1, blocking collectives: 15.7 us -> 17.6 us  [on_device(): parts = lax.all_to_all(parts, 'feat', 0, 0)]
    ppermute x18 -> x17, starting transfers between devices: 27 us -> 26.5 us  [send(): return lax.ppermute(value, 'feat', route)]
    unnamed x24 -> x26, local copies, waits for them, and re-layouts: 3.12 us -> 3.12 us
  transfers between devices with their start and end apart: 18 -> 17, of which waited for: 8 -> 9; matrix products, arithmetic and copies ran while one was open for 1% -> 1% of each run, Pallas kernels for 3% -> 4%
where the time goes in v10:
time: 99.9 us; the launch traced here: 99.5 us
  blocking collectives  37.5 us (38%)
  starting transfers between devices  26.5 us (27%)
  waiting for transfers between devices  21.3 us (21%)
  Pallas kernels  9.2 us (9%)
  local copies, waits for them, and re-layouts  3.15 us (3%)
    ppermute x17, starting transfers between devices, send(): return lax.ppermute(value, 'feat', route)  26.5 us
    ppermute x17, waiting for transfers between devices, send(): return lax.ppermute(value, 'feat', route)  21.3 us
    all_to_all x1, blocking collectives, on_device(): parts = combine(lax.all_to_all(partial, 'node', 0, 0))  20 us
    all_to_all x1, blocking collectives, on_device(): parts = lax.all_to_all(parts, 'feat', 0, 0)  17.6 us
    pallas_call x2, Pallas kernels, blocks(): pl.pallas_call(late_kernel if late else early_kernel, in_specs=[VMEM] * l...  6.48 us
    unnamed x26, local copies, waits for them, and re-layouts  3.12 us
  transfers between devices with their start and end apart: 17, of which 9 were waited for; matrix products, arithmetic and copies ran while one was open for 1% of the time, Pallas kernels for 4%

profile of v10, /device:TPU:1, one launch (start us, length us, event | category | flops | bytes accessed | tf_op | source)
XLA Modules:
  0.0 99.5 jit_solution(15499774887508108594)
XLA Ops:
  0.0 0.9 copy-done
  0.9 0.2 convolution_convert_fusion.ordered
  1.2 2.2 %copy-done.1 = bf16[8192,256]{1,0:T(8,128)(2,1)S(1)} copy-done((bf16[8192,256]{1,0:T(8,128)(2,1)S(1)}, bf16[8192,256]{1,0:T(8,128)(2,1)}, u32[]{:S(2)}) %copy-start.1) | copy-done | bytes 4194328
  3.3 1.3 %project.1 = (f32[16,8,1024]{2,1,0:T(8,128)S(1)}, f32[32,8,1024]{2,1,0:T(8,128)S(1)}, f32[80,8,1024]{2,1,0:T(8,128)S(1)}, f32[16,8,1024]{2,1,0:T(8,128)S(1)}, f3...) custom-call(bf16[256,256]{1,0:T(8,128)(2,1)S(1)} %convolution_convert_fusion.ordered, bf16[8192,256]{1,0:T(8,128)(2,1)S(1)} %copy-done.1), custom_call_target="tpu_custom_call" | custom-call | flops 1073741824 | bytes 12582912 | tf_op jit(solution)/shard_map/project/pallas_call | solution.py:49
  4.6 3.3 %collective-permute-start = (f32[16,8,1024]{2,1,0:T(8,128)S(1)}, f32[16,8,1024]{2,1,0:T(8,128)S(1)}, u32[]{:S(2)}, u32[]{:S(2)}) collective-permute-start(f32[16,8,1024]{2,1,0:T(8,128)S(1)} %get-tuple-element.54), channel_id=1, source_target_pairs={{0,1},{1,0},{2,3},{3,2},{4,5},{5,4},{6,7},{7,6},{8,9},{9,8},{10,11... | collective-permute-start | bytes 1572872 | tf_op jit(solution)/shard_map/ppermute | solution.py:296
  8.0 1.5 %collective-permute-done = f32[16,8,1024]{2,1,0:T(8,128)S(1)} collective-permute-done((f32[16,8,1024]{2,1,0:T(8,128)S(1)}, f32[16,8,1024]{2,1,0:T(8,128)S(1)}, u32[]{:S(2)}, u32[]{:S(2)}) %collective-permute-start) | collective-permute-done | bytes 524320 | tf_op jit(solution)/shard_map/ppermute | solution.py:296
  9.5 0.4 collective-permute-start.3
  10.0 3.9 %collective-permute-start.2 = (f32[8,8,1024]{2,1,0:T(8,128)S(1)}, f32[8,8,1024]{2,1,0:T(8,128)S(1)}, u32[]{:S(2)}, u32[]{:S(2)}) collective-permute-start(f32[8,8,1024]{2,1,0:T(8,128)S(1)} %get-tuple-element.113), channel_id=1, source_target_pairs={{2,0},{3,1},{4,2},{5,3},{6,4},{7,5},{8,6},{9,7},{10,8},{11,9},{12,... | collective-permute-start | bytes 786440 | tf_op jit(solution)/shard_map/ppermute | solution.py:296
  13.9 6.5 %collective-permute-done.1 = f32[8,8,1024]{2,1,0:T(8,128)S(1)} collective-permute-done((f32[8,8,1024]{2,1,0:T(8,128)S(1)}, f32[8,8,1024]{2,1,0:T(8,128)S(1)}, u32[]{:S(2)}, u32[]{:S(2)}) %collective-permute-start.1) | collective-permute-done | bytes 262176 | tf_op jit(solution)/shard_map/ppermute | solution.py:296
  20.4 0.7 collective-permute-start.4
  21.4 2.8 %collective-permute-start.6 = (f32[8,8,1024]{2,1,0:T(8,128)S(1)}, f32[8,8,1024]{2,1,0:T(8,128)S(1)}, u32[]{:S(2)}, u32[]{:S(2)}) collective-permute-start(f32[8,8,1024]{2,1,0:T(8,128)S(1)} %get-tuple-element.76), channel_id=1, source_target_pairs={{2,0},{3,1},{4,2},{5,3},{6,4},{7,5},{8,6},{9,7},{10,8},{11,9},{12,... | collective-permute-start | bytes 786440 | tf_op jit(solution)/shard_map/ppermute | solution.py:296
  24.4 2.7 %collective-permute-start.8 = (f32[8,8,1024]{2,1,0:T(8,128)S(1)}, f32[8,8,1024]{2,1,0:T(8,128)S(1)}, u32[]{:S(2)}, u32[]{:S(2)}) collective-permute-start(f32[8,8,1024]{2,1,0:T(8,128)S(1)} %get-tuple-element.82), channel_id=1, source_target_pairs={{2,0},{3,1},{4,2},{5,3},{6,4},{7,5},{8,6},{9,7},{10,8},{11,9},{12,... | collective-permute-start | bytes 786440 | tf_op jit(solution)/shard_map/ppermute | solution.py:296
  27.1 3.6 %collective-permute-done.5 = f32[8,8,1024]{2,1,0:T(8,128)S(1)} collective-permute-done((f32[8,8,1024]{2,1,0:T(8,128)S(1)}, f32[8,8,1024]{2,1,0:T(8,128)S(1)}, u32[]{:S(2)}, u32[]{:S(2)}) %collective-permute-start.5) | collective-permute-done | bytes 262176 | tf_op jit(solution)/shard_map/ppermute | solution.py:296
  30.8 2.6 %collective-permute-start.10 = (f32[8,8,1024]{2,1,0:T(8,128)S(1)}, f32[8,8,1024]{2,1,0:T(8,128)S(1)}, u32[]{:S(2)}, u32[]{:S(2)}) collective-permute-start(f32[8,8,1024]{2,1,0:T(8,128)S(1)} %get-tuple-element.88), channel_id=1, source_target_pairs={{2,0},{3,1},{4,2},{5,3},{6,4},{7,5},{8,6},{9,7},{10,8},{11,9},{12,... | collective-permute-start | bytes 786440 | tf_op jit(solution)/shard_map/ppermute | solution.py:296
  33.4 2.9 %collective-permute-done.7 = f32[8,8,1024]{2,1,0:T(8,128)S(1)} collective-permute-done((f32[8,8,1024]{2,1,0:T(8,128)S(1)}, f32[8,8,1024]{2,1,0:T(8,128)S(1)}, u32[]{:S(2)}, u32[]{:S(2)}) %collective-permute-start.7) | collective-permute-done | bytes 262176 | tf_op jit(solution)/shard_map/ppermute | solution.py:296
  36.4 2.1 %collective-permute-start.11 = (f32[8,8,1024]{2,1,0:T(8,128)S(1)}, f32[8,8,1024]{2,1,0:T(8,128)S(1)}, u32[]{:S(2)}, u32[]{:S(2)}) collective-permute-start(f32[8,8,1024]{2,1,0:T(8,128)S(1)} %get-tuple-element.93), channel_id=1, source_target_pairs={{0,2},{1,3},{2,4},{3,5},{4,6},{5,7},{6,8},{7,9},{8,10},{9,11},{10,... | collective-permute-start | bytes 786440 | tf_op jit(solution)/shard_map/ppermute | solution.py:296
  38.5 0.7 collective-permute-start.12
  39.2 2.1 %collective-permute-done.10 = f32[8,8,1024]{2,1,0:T(8,128)S(1)} collective-permute-done((f32[8,8,1024]{2,1,0:T(8,128)S(1)}, f32[8,8,1024]{2,1,0:T(8,128)S(1)}, u32[]{:S(2)}, u32[]{:S(2)}) %collective-permute-start.10) | collective-permute-done | bytes 262176 | tf_op jit(solution)/shard_map/ppermute | solution.py:296
  41.3 2.7 %collective-permute-start.13 = (f32[8,8,1024]{2,1,0:T(8,128)S(1)}, f32[8,8,1024]{2,1,0:T(8,128)S(1)}, u32[]{:S(2)}, u32[]{:S(2)}) collective-permute-start(f32[8,8,1024]{2,1,0:T(8,128)S(1)} %get-tuple-element.97), channel_id=1, source_target_pairs={{0,2},{1,3},{2,4},{3,5},{4,6},{5,7},{6,8},{7,9},{8,10},{9,11},{10,... | collective-permute-start | bytes 786440 | tf_op jit(solution)/shard_map/ppermute | solution.py:296
  44.1 0.8 collective-permute-start.14
  44.9 1.4 %collective-permute-done.11 = f32[8,8,1024]{2,1,0:T(8,128)S(1)} collective-permute-done((f32[8,8,1024]{2,1,0:T(8,128)S(1)}, f32[8,8,1024]{2,1,0:T(8,128)S(1)}, u32[]{:S(2)}, u32[]{:S(2)}) %collective-permute-start.11) | collective-permute-done | bytes 262176 | tf_op jit(solution)/shard_map/ppermute | solution.py:296
  46.2 0.4 collective-permute-done.12
  46.7 2.7 %collective-permute-start.15 = (f32[8,8,1024]{2,1,0:T(8,128)S(1)}, f32[8,8,1024]{2,1,0:T(8,128)S(1)}, u32[]{:S(2)}, u32[]{:S(2)}) collective-permute-start(f32[8,8,1024]{2,1,0:T(8,128)S(1)} %get-tuple-element.99), channel_id=1, source_target_pairs={{0,2},{1,3},{2,4},{3,5},{4,6},{5,7},{6,8},{7,9},{8,10},{9,11},{10,... | collective-permute-start | bytes 786440 | tf_op jit(solution)/shard_map/ppermute | solution.py:296
  49.4 0.9 collective-permute-start.16
  51.0 0.3 block_lists.1.table
  51.3 0.6 collective-permute-done.13.up
  51.9 3.2 %early_blocks.1.before = f32[256,8,128]{2,1,0:T(8,128)S(1)} custom-call(s32[8,384]{1,0:T(8,128)S(1)} %block_lists.1.table, f32[80,8,1024]{2,1,0:T(8,128)S(1)} %get-tuple-element.91.own, f32[80,8,1024]{2,1,0:T(8,128)S(1)} %collective-permute-done.4.paired, f32[8,8,1024]{2,1,0:T(8,128)S(1)} %collective-permute-done.13.up, ...), custom_call_target="tpu_custom_call" | custom-call | flops 268435456 | bytes 4194304 | tf_op jit(solution)/shard_map/early_blocks/pallas_call | solution.py:184
  55.1 2.4 %collective-permute-done.15.up = f32[8,8,1024]{2,1,0:T(8,128)S(1)} collective-permute-done((f32[8,8,1024]{2,1,0:T(8,128)S(1)}, f32[8,8,1024]{2,1,0:T(8,128)S(1)}, u32[]{:S(2)}, u32[]{:S(2)}) %collective-permute-start.15) | collective-permute-done | bytes 262176 | tf_op jit(solution)/shard_map/ppermute | solution.py:296
  57.5 3.3 %late_blocks.1 = f32[256,8,128]{2,1,0:T(8,128)S(1)} custom-call(f32[256,8,128]{2,1,0:T(8,128)S(1)} %early_blocks.1.before, s32[8,384]{1,0:T(8,128)S(1)} %block_lists.1.table, f32[80,8,1024]{2,1,0:T(8,128)S(1)} %get-tuple-element.91.own, f32[80,8,1024]{2,1,0:T(8,128)S(1)} %collective-permute-done.4.paired, f32[8,8,1024]{2,1,0:T(8,128)S(1)} %collective-permute-done.15.up, ...), custom_call_target="tpu_custom_call" | custom-call | flops 268435456 | bytes 4194304 | tf_op jit(solution)/shard_map/late_blocks/pallas_call | solution.py:184
  60.8 20.0 %all_to_all.10.parts = f32[16,16,8,128]{3,2,1,0:T(8,128)S(1)} all-to-all(f32[16,16,8,128]{3,2,1,0:T(8,128)S(1)} %bitcast.12), channel_id=1, replica_groups=mesh['node'=16,'feat'=16] {'node'}, dimensions={0} | all-to-all | bytes 2097152 | tf_op jit(solution)/shard_map/all_to_all | solution.py:337
  80.9 17.6 %all_to_all.11.parts = f32[16,8,128]{2,1,0:T(8,128)S(1)} all-to-all(f32[16,8,128]{2,1,0:T(8,128)S(1)} %combine.1), channel_id=1, replica_groups=mesh['node'=16,'feat'=16] {'feat'}, dimensions={0} | all-to-all | bytes 131072 | tf_op jit(solution)/shard_map/all_to_all | solution.py:338
  98.5 1.0 %second.1 = f32[32,172]{1,0:T(8,128)} custom-call(f32[16,8,128]{2,1,0:T(8,128)S(1)} %all_to_all.11.parts, f32[1,256]{1,0:T(1,128)S(1)} %bitcast.16, bf16[172,256]{1,0:T(8,128)(2,1)S(1)} %bitcast.13, bf16[172,256]{1,0:T(8,128)(2,1)S(1)} %bitcast.14, f32[1,172]{1,0:T(1,128)S(1)} %bitcast.17, s32[1,32]{1,0:T(1,128)S(1)} %bitcast.20, s32[8,32]{1,0:T(8,128)S(1)} %bitcast.15), custom_call_target="tpu_custom_call" | custom-call | tf_op jit(solution)/shard_map/second/pallas_call | solution.py:254
  (48 shorter events, 1.2 us)
Async XLA Ops:
  0.0 0.9 copy-start
  1.1 2.2 %copy-start.1 = (bf16[8192,256]{1,0:T(8,128)(2,1)S(1)}, bf16[8192,256]{1,0:T(8,128)(2,1)}, u32[]{:S(2)}) copy-start(bf16[8192,256]{1,0:T(8,128)(2,1)} %features.1) | copy-start | bytes 12582916
  3.3 17.8 %copy-start.10 = (pred[8]{0:T(512)(128)(4,1)S(1)}, pred[8]{0:T(512)(128)(4,1)}, u32[]{:S(2)}) copy-start(pred[8]{0:T(512)(128)(4,1)} %constant.87.clone.1) | copy-start | bytes 28
  3.3 48.5 %slice-start = ((s8[8388608]{0:T(1024)(128)(4,1)}), s8[4194304]{0:T(1024)(128)(4,1)S(1)}, s32[]{:S(2)}) async-start(s8[8388608]{0:T(1024)(128)(4,1)} %bitcast.10), calls=%async_computation.2 | async-start | bytes 8388608
  4.6 4.9 %collective-permute-start = (f32[16,8,1024]{2,1,0:T(8,128)S(1)}, f32[16,8,1024]{2,1,0:T(8,128)S(1)}, u32[]{:S(2)}, u32[]{:S(2)}) collective-permute-start(f32[16,8,1024]{2,1,0:T(8,128)S(1)} %get-tuple-element.54), channel_id=1, source_target_pairs={{0,1},{1,0},{2,3},{3,2},{4,5},{5,4},{6,7},{7,6},{8,9},{9,8},{10,11... | collective-permute-start | bytes 1572872 | tf_op jit(solution)/shard_map/ppermute | solution.py:296
  9.5 10.9 %collective-permute-start.3 = (f32[32,8,1024]{2,1,0:T(8,128)S(1)}, f32[32,8,1024]{2,1,0:T(8,128)S(1)}, u32[]{:S(2)}, u32[]{:S(2)}) collective-permute-start(f32[32,8,1024]{2,1,0:T(8,128)S(1)} %get-tuple-element.57), channel_id=1, source_target_pairs={{0,1},{1,0},{2,3},{3,2},{4,5},{5,4},{6,7},{7,6},{8,9},{9,8},{10,11... | collective-permute-start | bytes 3145736 | tf_op jit(solution)/shard_map/ppermute | solution.py:296
  9.9 10.5 %collective-permute-start.1 = (f32[8,8,1024]{2,1,0:T(8,128)S(1)}, f32[8,8,1024]{2,1,0:T(8,128)S(1)}, u32[]{:S(2)}, u32[]{:S(2)}) collective-permute-start(f32[8,8,1024]{2,1,0:T(8,128)S(1)} %get-tuple-element.114), channel_id=1, source_target_pairs={{0,2},{1,3},{2,4},{3,5},{4,6},{5,7},{6,8},{7,9},{8,10},{9,11},{10,... | collective-permute-start | bytes 786440 | tf_op jit(solution)/shard_map/ppermute | solution.py:296
  10.0 10.4 %collective-permute-start.2 = (f32[8,8,1024]{2,1,0:T(8,128)S(1)}, f32[8,8,1024]{2,1,0:T(8,128)S(1)}, u32[]{:S(2)}, u32[]{:S(2)}) collective-permute-start(f32[8,8,1024]{2,1,0:T(8,128)S(1)} %get-tuple-element.113), channel_id=1, source_target_pairs={{2,0},{3,1},{4,2},{5,3},{6,4},{7,5},{8,6},{9,7},{10,8},{11,9},{12,... | collective-permute-start | bytes 786440 | tf_op jit(solution)/shard_map/ppermute | solution.py:296
  20.4 6.7 %collective-permute-start.4 = (f32[80,8,1024]{2,1,0:T(8,128)S(1)}, f32[80,8,1024]{2,1,0:T(8,128)S(1)}, u32[]{:S(2)}, u32[]{:S(2)}) collective-permute-start(f32[80,8,1024]{2,1,0:T(8,128)S(1)} %get-tuple-element.59), channel_id=1, source_target_pairs={{0,1},{1,0},{2,3},{3,2},{4,5},{5,4},{6,7},{7,6},{8,9},{9,8},{10,11... | collective-permute-start | bytes 7864328 | tf_op jit(solution)/shard_map/ppermute | solution.py:296
  21.3 9.4 %collective-permute-start.5 = (f32[8,8,1024]{2,1,0:T(8,128)S(1)}, f32[8,8,1024]{2,1,0:T(8,128)S(1)}, u32[]{:S(2)}, u32[]{:S(2)}) collective-permute-start(f32[8,8,1024]{2,1,0:T(8,128)S(1)} %get-tuple-element.75), channel_id=1, source_target_pairs={{0,2},{1,3},{2,4},{3,5},{4,6},{5,7},{6,8},{7,9},{8,10},{9,11},{10,... | collective-permute-start | bytes 786440 | tf_op jit(solution)/shard_map/ppermute | solution.py:296
  21.4 9.3 %collective-permute-start.6 = (f32[8,8,1024]{2,1,0:T(8,128)S(1)}, f32[8,8,1024]{2,1,0:T(8,128)S(1)}, u32[]{:S(2)}, u32[]{:S(2)}) collective-permute-start(f32[8,8,1024]{2,1,0:T(8,128)S(1)} %get-tuple-element.76), channel_id=1, source_target_pairs={{2,0},{3,1},{4,2},{5,3},{6,4},{7,5},{8,6},{9,7},{10,8},{11,9},{12,... | collective-permute-start | bytes 786440 | tf_op jit(solution)/shard_map/ppermute | solution.py:296
  24.2 27.6 %slice-start.1 = ((s8[8388608]{0:T(1024)(128)(4,1)}), s8[4194304]{0:T(1024)(128)(4,1)S(1)}, s32[]{:S(2)}) async-start(s8[8388608]{0:T(1024)(128)(4,1)} %bitcast.10), calls=%async_computation.3 | async-start | bytes 8388608
  24.3 12.0 %collective-permute-start.7 = (f32[8,8,1024]{2,1,0:T(8,128)S(1)}, f32[8,8,1024]{2,1,0:T(8,128)S(1)}, u32[]{:S(2)}, u32[]{:S(2)}) collective-permute-start(f32[8,8,1024]{2,1,0:T(8,128)S(1)} %get-tuple-element.81), channel_id=1, source_target_pairs={{0,2},{1,3},{2,4},{3,5},{4,6},{5,7},{6,8},{7,9},{8,10},{9,11},{10,... | collective-permute-start | bytes 786440 | tf_op jit(solution)/shard_map/ppermute | solution.py:296
  24.4 11.9 %collective-permute-start.8 = (f32[8,8,1024]{2,1,0:T(8,128)S(1)}, f32[8,8,1024]{2,1,0:T(8,128)S(1)}, u32[]{:S(2)}, u32[]{:S(2)}) collective-permute-start(f32[8,8,1024]{2,1,0:T(8,128)S(1)} %get-tuple-element.82), channel_id=1, source_target_pairs={{2,0},{3,1},{4,2},{5,3},{6,4},{7,5},{8,6},{9,7},{10,8},{11,9},{12,... | collective-permute-start | bytes 786440 | tf_op jit(solution)/shard_map/ppermute | solution.py:296
  30.8 10.4 %collective-permute-start.10 = (f32[8,8,1024]{2,1,0:T(8,128)S(1)}, f32[8,8,1024]{2,1,0:T(8,128)S(1)}, u32[]{:S(2)}, u32[]{:S(2)}) collective-permute-start(f32[8,8,1024]{2,1,0:T(8,128)S(1)} %get-tuple-element.88), channel_id=1, source_target_pairs={{2,0},{3,1},{4,2},{5,3},{6,4},{7,5},{8,6},{9,7},{10,8},{11,9},{12,... | collective-permute-start | bytes 786440 | tf_op jit(solution)/shard_map/ppermute | solution.py:296
  33.4 7.9 %collective-permute-start.9 = (f32[8,8,1024]{2,1,0:T(8,128)S(1)}, f32[8,8,1024]{2,1,0:T(8,128)S(1)}, u32[]{:S(2)}, u32[]{:S(2)}) collective-permute-start(f32[8,8,1024]{2,1,0:T(8,128)S(1)} %get-tuple-element.87), channel_id=1, source_target_pairs={{0,2},{1,3},{2,4},{3,5},{4,6},{5,7},{6,8},{7,9},{8,10},{9,11},{10,... | collective-permute-start | bytes 786440 | tf_op jit(solution)/shard_map/ppermute | solution.py:296
  36.4 14.6 %copy-start.7 = (s32[256]{0:T(256)S(1)}, s32[256]{0:T(256)}, u32[]{:S(2)}) copy-start(s32[256]{0:T(256)} %param.14) | copy-start | bytes 3076
  36.4 14.6 %copy-start.8 = (s32[256]{0:T(256)S(1)}, s32[256]{0:T(256)}, u32[]{:S(2)}) copy-start(s32[256]{0:T(256)} %param.15) | copy-start | bytes 3076
  36.4 9.8 %collective-permute-start.11 = (f32[8,8,1024]{2,1,0:T(8,128)S(1)}, f32[8,8,1024]{2,1,0:T(8,128)S(1)}, u32[]{:S(2)}, u32[]{:S(2)}) collective-permute-start(f32[8,8,1024]{2,1,0:T(8,128)S(1)} %get-tuple-element.93), channel_id=1, source_target_pairs={{0,2},{1,3},{2,4},{3,5},{4,6},{5,7},{6,8},{7,9},{8,10},{9,11},{10,... | collective-permute-start | bytes 786440 | tf_op jit(solution)/shard_map/ppermute | solution.py:296
  38.5 8.1 %collective-permute-start.12 = (f32[8,8,1024]{2,1,0:T(8,128)S(1)}, f32[8,8,1024]{2,1,0:T(8,128)S(1)}, u32[]{:S(2)}, u32[]{:S(2)}) collective-permute-start(f32[8,8,1024]{2,1,0:T(8,128)S(1)} %get-tuple-element.94), channel_id=1, source_target_pairs={{2,0},{3,1},{4,2},{5,3},{6,4},{7,5},{8,6},{9,7},{10,8},{11,9},{12,... | collective-permute-start | bytes 786440 | tf_op jit(solution)/shard_map/ppermute | solution.py:296
  41.3 10.5 %collective-permute-start.13 = (f32[8,8,1024]{2,1,0:T(8,128)S(1)}, f32[8,8,1024]{2,1,0:T(8,128)S(1)}, u32[]{:S(2)}, u32[]{:S(2)}) collective-permute-start(f32[8,8,1024]{2,1,0:T(8,128)S(1)} %get-tuple-element.97), channel_id=1, source_target_pairs={{0,2},{1,3},{2,4},{3,5},{4,6},{5,7},{6,8},{7,9},{8,10},{9,11},{10,... | collective-permute-start | bytes 786440 | tf_op jit(solution)/shard_map/ppermute | solution.py:296
  44.1 7.8 %collective-permute-start.14 = (f32[8,8,1024]{2,1,0:T(8,128)S(1)}, f32[8,8,1024]{2,1,0:T(8,128)S(1)}, u32[]{:S(2)}, u32[]{:S(2)}) collective-permute-start(f32[8,8,1024]{2,1,0:T(8,128)S(1)} %get-tuple-element.98), channel_id=1, source_target_pairs={{2,0},{3,1},{4,2},{5,3},{6,4},{7,5},{8,6},{9,7},{10,8},{11,9},{12,... | collective-permute-start | bytes 786440 | tf_op jit(solution)/shard_map/ppermute | solution.py:296
  46.7 10.7 %collective-permute-start.15 = (f32[8,8,1024]{2,1,0:T(8,128)S(1)}, f32[8,8,1024]{2,1,0:T(8,128)S(1)}, u32[]{:S(2)}, u32[]{:S(2)}) collective-permute-start(f32[8,8,1024]{2,1,0:T(8,128)S(1)} %get-tuple-element.99), channel_id=1, source_target_pairs={{0,2},{1,3},{2,4},{3,5},{4,6},{5,7},{6,8},{7,9},{8,10},{9,11},{10,... | collective-permute-start | bytes 786440 | tf_op jit(solution)/shard_map/ppermute | solution.py:296
  49.4 8.0 %collective-permute-start.16 = (f32[8,8,1024]{2,1,0:T(8,128)S(1)}, f32[8,8,1024]{2,1,0:T(8,128)S(1)}, u32[]{:S(2)}, u32[]{:S(2)}) collective-permute-start(f32[8,8,1024]{2,1,0:T(8,128)S(1)} %get-tuple-element.100), channel_id=1, source_target_pairs={{2,0},{3,1},{4,2},{5,3},{6,4},{7,5},{8,6},{9,7},{10,8},{11,9},{12,... | collective-permute-start | bytes 786440 | tf_op jit(solution)/shard_map/ppermute | solution.py:296
  60.7 37.7 %copy-start.2 = (bf16[256,172]{0,1:T(8,128)(2,1)S(1)}, bf16[256,172]{0,1:T(8,128)(2,1)}, u32[]{:S(2)}) copy-start(bf16[256,172]{0,1:T(8,128)(2,1)} %param.19) | copy-start | bytes 264196
  60.8 37.7 %copy-start.3 = (bf16[256,172]{0,1:T(8,128)(2,1)S(1)}, bf16[256,172]{0,1:T(8,128)(2,1)}, u32[]{:S(2)}) copy-start(bf16[256,172]{0,1:T(8,128)(2,1)} %param.20) | copy-start | bytes 264196
  60.8 37.7 %copy-start.4 = (s32[32,8]{0,1:T(8,128)S(1)}, s32[32,8]{0,1:T(8,128)}, u32[]{:S(2)}) copy-start(s32[32,8]{0,1:T(8,128)} %param.23) | copy-start | bytes 3076
  60.8 37.7 %copy-start.5 = (f32[256]{0:T(256)S(1)}, f32[256]{0:T(256)}, u32[]{:S(2)}) copy-start(f32[256]{0:T(256)} %param.18) | copy-start | bytes 3076
  60.8 37.7 %copy-start.6 = (f32[172]{0:T(256)S(1)}, f32[172]{0:T(256)}, u32[]{:S(2)}) copy-start(f32[172]{0:T(256)} %param.21) | copy-start | bytes 2068
  60.8 37.7 %copy-start.9 = (s32[32]{0:T(128)S(1)}, s32[32]{0:T(128)}, u32[]{:S(2)}) copy-start(s32[32]{0:T(128)} %param.22) | copy-start | bytes 388

commit v11 on v8

--- a/solution.py
+++ b/solution.py
@@ -11,7 +11,7 @@
 CHIPS = 8
 TILE = 8
 RUNS = 8
-SPANS = ((0, 8), (8, 16))
+SPANS = ((0, 10), (10, 16))
 GROUP = 16
 NT = (((1,), (1,)), ((), ()))
 VMEM = pl.BlockSpec(memory_space=pltpu.VMEM)

time: 96.6 us -> 95.7 us (level)
  waiting for transfers between devices: 18.1 us -> 16.3 us
    all_to_all x1, blocking collectives: 15.7 us -> 20.3 us  [on_device(): parts = lax.all_to_all(parts, 'feat', 0, 0)]
    all_to_all x1, blocking collectives: 23.4 us -> 19.6 us  [on_device(): parts = combine(lax.all_to_all(partial, 'node', 0, 0))]
    ppermute x18, waiting for transfers between devices: 18.1 us -> 16.3 us  [send(): return lax.ppermute(value, 'feat', route)]
where the time goes in v11:
time: 95.7 us; the launch traced here: 96 us
  blocking collectives  39.9 us (42%)
  starting transfers between devices  27 us (28%)
  waiting for transfers between devices  16.3 us (17%)
  Pallas kernels  7.86 us (8%)
  local copies, waits for them, and re-layouts  3.12 us (3%)
    ppermute x18, starting transfers between devices, send(): return lax.ppermute(value, 'feat', route)  27 us
    all_to_all x1, blocking collectives, on_device(): parts = lax.all_to_all(parts, 'feat', 0, 0)  20.3 us
    all_to_all x1, blocking collectives, on_device(): parts = combine(lax.all_to_all(partial, 'node', 0, 0))  19.6 us
    ppermute x18, waiting for transfers between devices, send(): return lax.ppermute(value, 'feat', route)  16.3 us
    pallas_call x2, Pallas kernels, blocks(): pl.pallas_call(late_kernel if late else early_kernel, in_specs=[VMEM] * l...  5.13 us
    unnamed x24, local copies, waits for them, and re-layouts  3.12 us
  transfers between devices with their start and end apart: 18, of which 8 were waited for; matrix products, arithmetic and copies ran while one was open for 1% of the time, Pallas kernels for 3%

profile of v11, /device:TPU:1, one launch (start us, length us, event | category | flops | bytes accessed | tf_op | source)
XLA Modules:
  0.0 96.0 jit_solution(2545669648575959080)
XLA Ops:
  0.0 0.9 copy-done
  0.9 0.2 convolution_convert_fusion.ordered
  1.2 2.2 %copy-done.1 = bf16[8192,256]{1,0:T(8,128)(2,1)S(1)} copy-done((bf16[8192,256]{1,0:T(8,128)(2,1)S(1)}, bf16[8192,256]{1,0:T(8,128)(2,1)}, u32[]{:S(2)}) %copy-start.1) | copy-done | bytes 4194328
  3.3 1.3 %project.1 = (f32[16,8,1024]{2,1,0:T(8,128)S(1)}, f32[112,8,1024]{2,1,0:T(8,128)S(1)}, f32[16,8,1024]{2,1,0:T(8,128)S(1)}, f32[112,8,1024]{2,1,0:T(8,128)S(1)}) custom-call(bf16[256,256]{1,0:T(8,128)(2,1)S(1)} %convolution_convert_fusion.ordered, bf16[8192,256]{1,0:T(8,128)(2,1)S(1)} %copy-done.1), custom_call_target="tpu_custom_call" | custom-call | flops 1073741824 | bytes 12582912 | tf_op jit(solution)/shard_map/project/pallas_call | solution.py:45
  4.6 3.3 %collective-permute-start = (f32[16,8,1024]{2,1,0:T(8,128)S(1)}, f32[16,8,1024]{2,1,0:T(8,128)S(1)}, u32[]{:S(2)}, u32[]{:S(2)}) collective-permute-start(f32[16,8,1024]{2,1,0:T(8,128)S(1)} %get-tuple-element.44), channel_id=1, source_target_pairs={{0,1},{1,0},{2,3},{3,2},{4,5},{5,4},{6,7},{7,6},{8,9},{9,8},{10,11... | collective-permute-start | bytes 1572872 | tf_op jit(solution)/shard_map/ppermute | solution.py:292
  7.9 1.5 %collective-permute-done = f32[16,8,1024]{2,1,0:T(8,128)S(1)} collective-permute-done((f32[16,8,1024]{2,1,0:T(8,128)S(1)}, f32[16,8,1024]{2,1,0:T(8,128)S(1)}, u32[]{:S(2)}, u32[]{:S(2)}) %collective-permute-start) | collective-permute-done | bytes 524320 | tf_op jit(solution)/shard_map/ppermute | solution.py:292
  9.5 0.4 collective-permute-start.1
  10.0 3.9 %collective-permute-start.3 = (f32[5,8,1024]{2,1,0:T(8,128)S(1)}, f32[5,8,1024]{2,1,0:T(8,128)S(1)}, u32[]{:S(2)}, u32[]{:S(2)}) collective-permute-start(f32[5,8,1024]{2,1,0:T(8,128)S(1)} %get-tuple-element.62), channel_id=1, source_target_pairs={{2,0},{3,1},{4,2},{5,3},{6,4},{7,5},{8,6},{9,7},{10,8},{11,9},{12,... | collective-permute-start | bytes 491528 | tf_op jit(solution)/shard_map/ppermute | solution.py:292
  14.0 2.7 %collective-permute-start.11 = (f32[3,8,1024]{2,1,0:T(8,128)S(1)}, f32[3,8,1024]{2,1,0:T(8,128)S(1)}, u32[]{:S(2)}, u32[]{:S(2)}) collective-permute-start(f32[3,8,1024]{2,1,0:T(8,128)S(1)} %get-tuple-element.76), channel_id=1, source_target_pairs={{2,0},{3,1},{4,2},{5,3},{6,4},{7,5},{8,6},{9,7},{10,8},{11,9},{12,... | collective-permute-start | bytes 294920 | tf_op jit(solution)/shard_map/ppermute | solution.py:292
  16.7 1.6 %collective-permute-done.2 = f32[5,8,1024]{2,1,0:T(8,128)S(1)} collective-permute-done((f32[5,8,1024]{2,1,0:T(8,128)S(1)}, f32[5,8,1024]{2,1,0:T(8,128)S(1)}, u32[]{:S(2)}, u32[]{:S(2)}) %collective-permute-start.2) | collective-permute-done | bytes 163872 | tf_op jit(solution)/shard_map/ppermute | solution.py:292
  18.5 2.7 %collective-permute-start.5 = (f32[10,8,1024]{2,1,0:T(8,128)S(1)}, f32[10,8,1024]{2,1,0:T(8,128)S(1)}, u32[]{:S(2)}, u32[]{:S(2)}) collective-permute-start(f32[10,8,1024]{2,1,0:T(8,128)S(1)} %get-tuple-element.64), channel_id=1, source_target_pairs={{2,0},{3,1},{4,2},{5,3},{6,4},{7,5},{8,6},{9,7},{10,8},{11,9},{12,... | collective-permute-start | bytes 983048 | tf_op jit(solution)/shard_map/ppermute | solution.py:292
  21.3 2.7 %collective-permute-start.13 = (f32[6,8,1024]{2,1,0:T(8,128)S(1)}, f32[6,8,1024]{2,1,0:T(8,128)S(1)}, u32[]{:S(2)}, u32[]{:S(2)}) collective-permute-start(f32[6,8,1024]{2,1,0:T(8,128)S(1)} %get-tuple-element.78), channel_id=1, source_target_pairs={{2,0},{3,1},{4,2},{5,3},{6,4},{7,5},{8,6},{9,7},{10,8},{11,9},{12,... | collective-permute-start | bytes 589832 | tf_op jit(solution)/shard_map/ppermute | solution.py:292
  24.0 3.8 %collective-permute-done.4 = f32[10,8,1024]{2,1,0:T(8,128)S(1)} collective-permute-done((f32[10,8,1024]{2,1,0:T(8,128)S(1)}, f32[10,8,1024]{2,1,0:T(8,128)S(1)}, u32[]{:S(2)}, u32[]{:S(2)}) %collective-permute-start.4) | collective-permute-done | bytes 327712 | tf_op jit(solution)/shard_map/ppermute | solution.py:292
  28.0 0.8 collective-permute-start.6
  28.8 1.9 %collective-permute-start.7 = (f32[10,8,1024]{2,1,0:T(8,128)S(1)}, f32[10,8,1024]{2,1,0:T(8,128)S(1)}, u32[]{:S(2)}, u32[]{:S(2)}) collective-permute-start(f32[10,8,1024]{2,1,0:T(8,128)S(1)} %get-tuple-element.66), channel_id=1, source_target_pairs={{2,0},{3,1},{4,2},{5,3},{6,4},{7,5},{8,6},{9,7},{10,8},{11,9},{12,... | collective-permute-start | bytes 983048 | tf_op jit(solution)/shard_map/ppermute | solution.py:292
  30.8 1.3 %collective-permute-done.12 = f32[6,8,1024]{2,1,0:T(8,128)S(1)} collective-permute-done((f32[6,8,1024]{2,1,0:T(8,128)S(1)}, f32[6,8,1024]{2,1,0:T(8,128)S(1)}, u32[]{:S(2)}, u32[]{:S(2)}) %collective-permute-start.12) | collective-permute-done | bytes 196640 | tf_op jit(solution)/shard_map/ppermute | solution.py:292
  32.1 0.8 collective-permute-start.14
  33.0 1.9 %collective-permute-start.15 = (f32[6,8,1024]{2,1,0:T(8,128)S(1)}, f32[6,8,1024]{2,1,0:T(8,128)S(1)}, u32[]{:S(2)}, u32[]{:S(2)}) collective-permute-start(f32[6,8,1024]{2,1,0:T(8,128)S(1)} %get-tuple-element.80), channel_id=1, source_target_pairs={{2,0},{3,1},{4,2},{5,3},{6,4},{7,5},{8,6},{9,7},{10,8},{11,9},{12,... | collective-permute-start | bytes 589832 | tf_op jit(solution)/shard_map/ppermute | solution.py:292
  34.9 3.2 %collective-permute-done.6 = f32[10,8,1024]{2,1,0:T(8,128)S(1)} collective-permute-done((f32[10,8,1024]{2,1,0:T(8,128)S(1)}, f32[10,8,1024]{2,1,0:T(8,128)S(1)}, u32[]{:S(2)}, u32[]{:S(2)}) %collective-permute-start.6) | collective-permute-done | bytes 327712 | tf_op jit(solution)/shard_map/ppermute | solution.py:292
  38.3 0.7 collective-permute-start.8
  39.0 2.0 %collective-permute-start.9 = (f32[10,8,1024]{2,1,0:T(8,128)S(1)}, f32[10,8,1024]{2,1,0:T(8,128)S(1)}, u32[]{:S(2)}, u32[]{:S(2)}) collective-permute-start(f32[10,8,1024]{2,1,0:T(8,128)S(1)} %get-tuple-element.68), channel_id=1, source_target_pairs={{2,0},{3,1},{4,2},{5,3},{6,4},{7,5},{8,6},{9,7},{10,8},{11,9},{12,... | collective-permute-start | bytes 983048 | tf_op jit(solution)/shard_map/ppermute | solution.py:292
  41.0 1.3 %collective-permute-done.14 = f32[6,8,1024]{2,1,0:T(8,128)S(1)} collective-permute-done((f32[6,8,1024]{2,1,0:T(8,128)S(1)}, f32[6,8,1024]{2,1,0:T(8,128)S(1)}, u32[]{:S(2)}, u32[]{:S(2)}) %collective-permute-start.14) | collective-permute-done | bytes 196640 | tf_op jit(solution)/shard_map/ppermute | solution.py:292
  42.4 0.7 collective-permute-start.16
  43.1 2.0 %collective-permute-start.17 = (f32[6,8,1024]{2,1,0:T(8,128)S(1)}, f32[6,8,1024]{2,1,0:T(8,128)S(1)}, u32[]{:S(2)}, u32[]{:S(2)}) collective-permute-start(f32[6,8,1024]{2,1,0:T(8,128)S(1)} %get-tuple-element.82), channel_id=1, source_target_pairs={{2,0},{3,1},{4,2},{5,3},{6,4},{7,5},{8,6},{9,7},{10,8},{11,9},{12,... | collective-permute-start | bytes 589832 | tf_op jit(solution)/shard_map/ppermute | solution.py:292
  45.8 0.3 block_lists.1.table
  46.1 2.3 %collective-permute-done.8.up = f32[10,8,1024]{2,1,0:T(8,128)S(1)} collective-permute-done((f32[10,8,1024]{2,1,0:T(8,128)S(1)}, f32[10,8,1024]{2,1,0:T(8,128)S(1)}, u32[]{:S(2)}, u32[]{:S(2)}) %collective-permute-start.8) | collective-permute-done | bytes 327712 | tf_op jit(solution)/shard_map/ppermute | solution.py:292
  48.5 2.9 %early_blocks.1.before = f32[256,8,128]{2,1,0:T(8,128)S(1)} custom-call(s32[8,384]{1,0:T(8,128)S(1)} %block_lists.1.table, f32[112,8,1024]{2,1,0:T(8,128)S(1)} %get-tuple-element.69.own, f32[112,8,1024]{2,1,0:T(8,128)S(1)} %collective-permute-done.1.paired, f32[10,8,1024]{2,1,0:T(8,128)S(1)} %collective-permute-done.8.up, ...), custom_call_target="tpu_custom_call" | custom-call | flops 268435456 | bytes 4194304 | tf_op jit(solution)/shard_map/early_blocks/pallas_call | solution.py:180
  51.4 1.2 %collective-permute-done.16.up = f32[6,8,1024]{2,1,0:T(8,128)S(1)} collective-permute-done((f32[6,8,1024]{2,1,0:T(8,128)S(1)}, f32[6,8,1024]{2,1,0:T(8,128)S(1)}, u32[]{:S(2)}, u32[]{:S(2)}) %collective-permute-start.16) | collective-permute-done | bytes 196640 | tf_op jit(solution)/shard_map/ppermute | solution.py:292
  52.7 2.2 %late_blocks.1 = f32[256,8,128]{2,1,0:T(8,128)S(1)} custom-call(f32[256,8,128]{2,1,0:T(8,128)S(1)} %early_blocks.1.before, s32[8,384]{1,0:T(8,128)S(1)} %block_lists.1.table, f32[112,8,1024]{2,1,0:T(8,128)S(1)} %get-tuple-element.69.own, f32[112,8,1024]{2,1,0:T(8,128)S(1)} %collective-permute-done.1.paired, f32[6,8,1024]{2,1,0:T(8,128)S(1)} %collective-permute-done.16.up, ...), custom_call_target="tpu_custom_call" | custom-call | flops 268435456 | bytes 4194304 | tf_op jit(solution)/shard_map/late_blocks/pallas_call | solution.py:180
  54.9 19.6 %all_to_all.10.parts = f32[16,16,8,128]{3,2,1,0:T(8,128)S(1)} all-to-all(f32[16,16,8,128]{3,2,1,0:T(8,128)S(1)} %bitcast.12), channel_id=1, replica_groups=mesh['node'=16,'feat'=16] {'node'}, dimensions={0} | all-to-all | bytes 2097152 | tf_op jit(solution)/shard_map/all_to_all | solution.py:330
  74.7 20.3 %all_to_all.11.parts = f32[16,8,128]{2,1,0:T(8,128)S(1)} all-to-all(f32[16,8,128]{2,1,0:T(8,128)S(1)} %combine.1), channel_id=1, replica_groups=mesh['node'=16,'feat'=16] {'feat'}, dimensions={0} | all-to-all | bytes 131072 | tf_op jit(solution)/shard_map/all_to_all | solution.py:331
  95.0 1.0 %second.1 = f32[32,172]{1,0:T(8,128)} custom-call(f32[16,8,128]{2,1,0:T(8,128)S(1)} %all_to_all.11.parts, f32[1,256]{1,0:T(1,128)S(1)} %bitcast.16, bf16[172,256]{1,0:T(8,128)(2,1)S(1)} %bitcast.13, bf16[172,256]{1,0:T(8,128)(2,1)S(1)} %bitcast.14, f32[1,172]{1,0:T(1,128)S(1)} %bitcast.17, s32[1,32]{1,0:T(1,128)S(1)} %bitcast.20, s32[8,32]{1,0:T(8,128)S(1)} %bitcast.15), custom_call_target="tpu_custom_call" | custom-call | tf_op jit(solution)/shard_map/second/pallas_call | solution.py:250
  (47 shorter events, 1.3 us)
Async XLA Ops:
  0.0 0.9 copy-start
  1.1 2.2 %copy-start.1 = (bf16[8192,256]{1,0:T(8,128)(2,1)S(1)}, bf16[8192,256]{1,0:T(8,128)(2,1)}, u32[]{:S(2)}) copy-start(bf16[8192,256]{1,0:T(8,128)(2,1)} %features.1) | copy-start | bytes 12582916
  3.3 45.1 %slice-start = ((s8[8388608]{0:T(1024)(128)(4,1)}), s8[4194304]{0:T(1024)(128)(4,1)S(1)}, s32[]{:S(2)}) async-start(s8[8388608]{0:T(1024)(128)(4,1)} %bitcast.10), calls=%async_computation.2 | async-start | bytes 8388608
  4.6 4.9 %collective-permute-start = (f32[16,8,1024]{2,1,0:T(8,128)S(1)}, f32[16,8,1024]{2,1,0:T(8,128)S(1)}, u32[]{:S(2)}, u32[]{:S(2)}) collective-permute-start(f32[16,8,1024]{2,1,0:T(8,128)S(1)} %get-tuple-element.44), channel_id=1, source_target_pairs={{0,1},{1,0},{2,3},{3,2},{4,5},{5,4},{6,7},{7,6},{8,9},{9,8},{10,11... | collective-permute-start | bytes 1572872 | tf_op jit(solution)/shard_map/ppermute | solution.py:292
  9.5 7.2 %collective-permute-start.1 = (f32[112,8,1024]{2,1,0:T(8,128)S(1)}, f32[112,8,1024]{2,1,0:T(8,128)S(1)}, u32[]{:S(2)}, u32[]{:S(2)}) collective-permute-start(f32[112,8,1024]{2,1,0:T(8,128)S(1)} %get-tuple-element.46), channel_id=1, source_target_pairs={{0,1},{1,0},{2,3},{3,2},{4,5},{5,4},{6,7},{7,6},{8,9},{9,8},{10,11... | collective-permute-start | bytes 11010056 | tf_op jit(solution)/shard_map/ppermute | solution.py:292
  9.9 8.4 %collective-permute-start.2 = (f32[5,8,1024]{2,1,0:T(8,128)S(1)}, f32[5,8,1024]{2,1,0:T(8,128)S(1)}, u32[]{:S(2)}, u32[]{:S(2)}) collective-permute-start(f32[5,8,1024]{2,1,0:T(8,128)S(1)} %get-tuple-element.61), channel_id=1, source_target_pairs={{0,2},{1,3},{2,4},{3,5},{4,6},{5,7},{6,8},{7,9},{8,10},{9,11},{10,... | collective-permute-start | bytes 491528 | tf_op jit(solution)/shard_map/ppermute | solution.py:292
  10.0 8.3 %collective-permute-start.3 = (f32[5,8,1024]{2,1,0:T(8,128)S(1)}, f32[5,8,1024]{2,1,0:T(8,128)S(1)}, u32[]{:S(2)}, u32[]{:S(2)}) collective-permute-start(f32[5,8,1024]{2,1,0:T(8,128)S(1)} %get-tuple-element.62), channel_id=1, source_target_pairs={{2,0},{3,1},{4,2},{5,3},{6,4},{7,5},{8,6},{9,7},{10,8},{11,9},{12,... | collective-permute-start | bytes 491528 | tf_op jit(solution)/shard_map/ppermute | solution.py:292
  13.9 7.2 %collective-permute-start.10 = (f32[3,8,1024]{2,1,0:T(8,128)S(1)}, f32[3,8,1024]{2,1,0:T(8,128)S(1)}, u32[]{:S(2)}, u32[]{:S(2)}) collective-permute-start(f32[3,8,1024]{2,1,0:T(8,128)S(1)} %get-tuple-element.75), channel_id=1, source_target_pairs={{0,2},{1,3},{2,4},{3,5},{4,6},{5,7},{6,8},{7,9},{8,10},{9,11},{10,... | collective-permute-start | bytes 294920 | tf_op jit(solution)/shard_map/ppermute | solution.py:292
  14.0 7.1 %collective-permute-start.11 = (f32[3,8,1024]{2,1,0:T(8,128)S(1)}, f32[3,8,1024]{2,1,0:T(8,128)S(1)}, u32[]{:S(2)}, u32[]{:S(2)}) collective-permute-start(f32[3,8,1024]{2,1,0:T(8,128)S(1)} %get-tuple-element.76), channel_id=1, source_target_pairs={{2,0},{3,1},{4,2},{5,3},{6,4},{7,5},{8,6},{9,7},{10,8},{11,9},{12,... | collective-permute-start | bytes 294920 | tf_op jit(solution)/shard_map/ppermute | solution.py:292
  18.4 30.1 %slice-start.1 = ((s8[8388608]{0:T(1024)(128)(4,1)}), s8[4194304]{0:T(1024)(128)(4,1)S(1)}, s32[]{:S(2)}) async-start(s8[8388608]{0:T(1024)(128)(4,1)} %bitcast.10), calls=%async_computation.3 | async-start | bytes 8388608
  18.4 9.4 %collective-permute-start.4 = (f32[10,8,1024]{2,1,0:T(8,128)S(1)}, f32[10,8,1024]{2,1,0:T(8,128)S(1)}, u32[]{:S(2)}, u32[]{:S(2)}) collective-permute-start(f32[10,8,1024]{2,1,0:T(8,128)S(1)} %get-tuple-element.63), channel_id=1, source_target_pairs={{0,2},{1,3},{2,4},{3,5},{4,6},{5,7},{6,8},{7,9},{8,10},{9,11},{10,... | collective-permute-start | bytes 983048 | tf_op jit(solution)/shard_map/ppermute | solution.py:292
  18.5 9.3 %collective-permute-start.5 = (f32[10,8,1024]{2,1,0:T(8,128)S(1)}, f32[10,8,1024]{2,1,0:T(8,128)S(1)}, u32[]{:S(2)}, u32[]{:S(2)}) collective-permute-start(f32[10,8,1024]{2,1,0:T(8,128)S(1)} %get-tuple-element.64), channel_id=1, source_target_pairs={{2,0},{3,1},{4,2},{5,3},{6,4},{7,5},{8,6},{9,7},{10,8},{11,9},{12,... | collective-permute-start | bytes 983048 | tf_op jit(solution)/shard_map/ppermute | solution.py:292
  21.2 24.6 %copy-start.7 = (s32[256]{0:T(256)S(1)}, s32[256]{0:T(256)}, u32[]{:S(2)}) copy-start(s32[256]{0:T(256)} %param.14) | copy-start | bytes 3076
  21.2 24.6 %copy-start.8 = (s32[256]{0:T(256)S(1)}, s32[256]{0:T(256)}, u32[]{:S(2)}) copy-start(s32[256]{0:T(256)} %param.15) | copy-start | bytes 3076
  21.3 10.8 %collective-permute-start.12 = (f32[6,8,1024]{2,1,0:T(8,128)S(1)}, f32[6,8,1024]{2,1,0:T(8,128)S(1)}, u32[]{:S(2)}, u32[]{:S(2)}) collective-permute-start(f32[6,8,1024]{2,1,0:T(8,128)S(1)} %get-tuple-element.77), channel_id=1, source_target_pairs={{0,2},{1,3},{2,4},{3,5},{4,6},{5,7},{6,8},{7,9},{8,10},{9,11},{10,... | collective-permute-start | bytes 589832 | tf_op jit(solution)/shard_map/ppermute | solution.py:292
  21.3 10.7 %collective-permute-start.13 = (f32[6,8,1024]{2,1,0:T(8,128)S(1)}, f32[6,8,1024]{2,1,0:T(8,128)S(1)}, u32[]{:S(2)}, u32[]{:S(2)}) collective-permute-start(f32[6,8,1024]{2,1,0:T(8,128)S(1)} %get-tuple-element.78), channel_id=1, source_target_pairs={{2,0},{3,1},{4,2},{5,3},{6,4},{7,5},{8,6},{9,7},{10,8},{11,9},{12,... | collective-permute-start | bytes 589832 | tf_op jit(solution)/shard_map/ppermute | solution.py:292
  28.0 10.1 %collective-permute-start.6 = (f32[10,8,1024]{2,1,0:T(8,128)S(1)}, f32[10,8,1024]{2,1,0:T(8,128)S(1)}, u32[]{:S(2)}, u32[]{:S(2)}) collective-permute-start(f32[10,8,1024]{2,1,0:T(8,128)S(1)} %get-tuple-element.65), channel_id=1, source_target_pairs={{0,2},{1,3},{2,4},{3,5},{4,6},{5,7},{6,8},{7,9},{8,10},{9,11},{10,... | collective-permute-start | bytes 983048 | tf_op jit(solution)/shard_map/ppermute | solution.py:292
  28.8 9.3 %collective-permute-start.7 = (f32[10,8,1024]{2,1,0:T(8,128)S(1)}, f32[10,8,1024]{2,1,0:T(8,128)S(1)}, u32[]{:S(2)}, u32[]{:S(2)}) collective-permute-start(f32[10,8,1024]{2,1,0:T(8,128)S(1)} %get-tuple-element.66), channel_id=1, source_target_pairs={{2,0},{3,1},{4,2},{5,3},{6,4},{7,5},{8,6},{9,7},{10,8},{11,9},{12,... | collective-permute-start | bytes 983048 | tf_op jit(solution)/shard_map/ppermute | solution.py:292
  32.1 10.2 %collective-permute-start.14 = (f32[6,8,1024]{2,1,0:T(8,128)S(1)}, f32[6,8,1024]{2,1,0:T(8,128)S(1)}, u32[]{:S(2)}, u32[]{:S(2)}) collective-permute-start(f32[6,8,1024]{2,1,0:T(8,128)S(1)} %get-tuple-element.79), channel_id=1, source_target_pairs={{0,2},{1,3},{2,4},{3,5},{4,6},{5,7},{6,8},{7,9},{8,10},{9,11},{10,... | collective-permute-start | bytes 589832 | tf_op jit(solution)/shard_map/ppermute | solution.py:292
  33.0 9.4 %collective-permute-start.15 = (f32[6,8,1024]{2,1,0:T(8,128)S(1)}, f32[6,8,1024]{2,1,0:T(8,128)S(1)}, u32[]{:S(2)}, u32[]{:S(2)}) collective-permute-start(f32[6,8,1024]{2,1,0:T(8,128)S(1)} %get-tuple-element.80), channel_id=1, source_target_pairs={{2,0},{3,1},{4,2},{5,3},{6,4},{7,5},{8,6},{9,7},{10,8},{11,9},{12,... | collective-permute-start | bytes 589832 | tf_op jit(solution)/shard_map/ppermute | solution.py:292
  38.3 10.2 %collective-permute-start.8 = (f32[10,8,1024]{2,1,0:T(8,128)S(1)}, f32[10,8,1024]{2,1,0:T(8,128)S(1)}, u32[]{:S(2)}, u32[]{:S(2)}) collective-permute-start(f32[10,8,1024]{2,1,0:T(8,128)S(1)} %get-tuple-element.67), channel_id=1, source_target_pairs={{0,2},{1,3},{2,4},{3,5},{4,6},{5,7},{6,8},{7,9},{8,10},{9,11},{10,... | collective-permute-start | bytes 983048 | tf_op jit(solution)/shard_map/ppermute | solution.py:292
  39.0 9.4 %collective-permute-start.9 = (f32[10,8,1024]{2,1,0:T(8,128)S(1)}, f32[10,8,1024]{2,1,0:T(8,128)S(1)}, u32[]{:S(2)}, u32[]{:S(2)}) collective-permute-start(f32[10,8,1024]{2,1,0:T(8,128)S(1)} %get-tuple-element.68), channel_id=1, source_target_pairs={{2,0},{3,1},{4,2},{5,3},{6,4},{7,5},{8,6},{9,7},{10,8},{11,9},{12,... | collective-permute-start | bytes 983048 | tf_op jit(solution)/shard_map/ppermute | solution.py:292
  42.4 10.3 %collective-permute-start.16 = (f32[6,8,1024]{2,1,0:T(8,128)S(1)}, f32[6,8,1024]{2,1,0:T(8,128)S(1)}, u32[]{:S(2)}, u32[]{:S(2)}) collective-permute-start(f32[6,8,1024]{2,1,0:T(8,128)S(1)} %get-tuple-element.81), channel_id=1, source_target_pairs={{0,2},{1,3},{2,4},{3,5},{4,6},{5,7},{6,8},{7,9},{8,10},{9,11},{10,... | collective-permute-start | bytes 589832 | tf_op jit(solution)/shard_map/ppermute | solution.py:292
  43.1 9.5 %collective-permute-start.17 = (f32[6,8,1024]{2,1,0:T(8,128)S(1)}, f32[6,8,1024]{2,1,0:T(8,128)S(1)}, u32[]{:S(2)}, u32[]{:S(2)}) collective-permute-start(f32[6,8,1024]{2,1,0:T(8,128)S(1)} %get-tuple-element.82), channel_id=1, source_target_pairs={{2,0},{3,1},{4,2},{5,3},{6,4},{7,5},{8,6},{9,7},{10,8},{11,9},{12,... | collective-permute-start | bytes 589832 | tf_op jit(solution)/shard_map/ppermute | solution.py:292
  51.4 43.6 %copy-start.2 = (bf16[256,172]{0,1:T(8,128)(2,1)S(1)}, bf16[256,172]{0,1:T(8,128)(2,1)}, u32[]{:S(2)}) copy-start(bf16[256,172]{0,1:T(8,128)(2,1)} %param.19) | copy-start | bytes 264196
  51.4 43.6 %copy-start.3 = (bf16[256,172]{0,1:T(8,128)(2,1)S(1)}, bf16[256,172]{0,1:T(8,128)(2,1)}, u32[]{:S(2)}) copy-start(bf16[256,172]{0,1:T(8,128)(2,1)} %param.20) | copy-start | bytes 264196
  51.4 43.6 %copy-start.4 = (s32[32,8]{0,1:T(8,128)S(1)}, s32[32,8]{0,1:T(8,128)}, u32[]{:S(2)}) copy-start(s32[32,8]{0,1:T(8,128)} %param.23) | copy-start | bytes 3076
  51.4 43.6 %copy-start.5 = (f32[256]{0:T(256)S(1)}, f32[256]{0:T(256)}, u32[]{:S(2)}) copy-start(f32[256]{0:T(256)} %param.18) | copy-start | bytes 3076
  51.4 43.6 %copy-start.6 = (f32[172]{0:T(256)S(1)}, f32[172]{0:T(256)}, u32[]{:S(2)}) copy-start(f32[172]{0:T(256)} %param.21) | copy-start | bytes 2068
  51.4 43.5 %copy-start.9 = (s32[32]{0:T(128)S(1)}, s32[32]{0:T(128)}, u32[]{:S(2)}) copy-start(s32[32]{0:T(128)} %param.22) | copy-start | bytes 388

commit v12 on v11

--- a/solution.py
+++ b/solution.py
@@ -20,38 +20,54 @@
 UNITS = 2 * RUNS
 
 
-def project_kernel(ordered, features, *outs):
+def project_kernel(first, ordered, features, *outs):
+    hidden = ordered.shape[0]
     lanes = outs[0].shape[2]
     tile = min(512, lanes)
+    width = 2 * TILE
+    strips = 1 if first else CHIPS - 1
+    rows = [
+        ordered[half + (0 if first else width) : half + (width if first else hidden // 2)]
+        for half in (0, hidden // 2)
+    ]
+    rows = jnp.concatenate(rows, axis=0)
     for i in range(features.shape[0] // tile):
-        rows = features[i * tile : (i + 1) * tile]
-        product = lax.dot_general(ordered[...], rows, NT, preferred_element_type=jnp.float32)
+        product = lax.dot_general(
+            rows, features[i * tile : (i + 1) * tile], NT, preferred_element_type=jnp.float32
+        )
         run, at = divmod(i * tile, lanes)
+        at = slice(at, at + tile)
         take = 0
-        for out in outs:
-            for k in range(out.shape[0] // RUNS):
-                unit = k // 2 * UNITS + 2 * run + k % 2
-                out[unit, :, at : at + tile] = product[take : take + TILE]
-                take += TILE
-
-
-def project(ordered, features):
+        for core in range(2):
+            for strip in range(strips):
+                for k in range(2):
+                    unit = 2 * run + k
+                    if first:
+                        stream = int(unit >= SPANS[1][0])
+                        out, unit = outs[2 * core + stream], unit - SPANS[stream][0]
+                    else:
+                        out, unit = outs[core], strip * UNITS + unit
+                    out[unit, :, at] = product[take : take + TILE]
+                    take += TILE
+
+
+def project(first, ordered, features):
     rows, columns = features.shape
     hidden = ordered.shape[0]
+    units = [end - begin for begin, end in SPANS] if first else [(CHIPS - 1) * UNITS]
     shapes = [
-        jax.ShapeDtypeStruct((strips * UNITS, TILE, rows // RUNS), jnp.float32)
-        for strips in (1, CHIPS - 1)
+        jax.ShapeDtypeStruct((count, TILE, rows // RUNS), jnp.float32) for count in units
     ] * 2
     return pl.pallas_call(
-        project_kernel,
+        functools.partial(project_kernel, first),
         in_specs=[VMEM] * 2,
-        out_specs=[VMEM] * 4,
+        out_specs=[VMEM] * len(shapes),
         out_shape=shapes,
-        name="project",
+        name="project_first" if first else "project_rest",
         compiler_params=pltpu.CompilerParams(vmem_limit_bytes=8 * 2**20),
         cost_estimate=pl.CostEstimate(
             flops=2 * rows * columns * hidden,
-            bytes_accessed=rows * columns * 2 + rows * hidden * 4,
+            bytes_accessed=rows * columns * 2,
             transcendentals=0,
         ),
     )(ordered, features)
@@ -292,17 +308,21 @@
         return lax.ppermute(value, "feat", route)
 
     tie = lax.optimization_barrier
-    opposite, rest, opposite_own, rest_own = project(in_hop_order(layer_one), features)
-    opposite, rest = tie((send(opposite, pair), rest))
+    ordered = in_hop_order(layer_one)
+    *opposite, own_first, own_second = project(True, ordered, features)
+    opposite_own = own_first, own_second
+    rest, rest_own = project(False, ordered, features)
+    second_part = send(opposite[1], pair)
+    first_part, rest = tie((send(opposite[0], pair), rest))
+    opposite = first_part, second_part
     rest = send(rest, pair)
 
     order = block_count
     streams = []
-    for begin, end in SPANS:
-        middle = (end - begin) // 2
-        opposite, opposite_own, order = tie((opposite, opposite_own, order))
-        onward = opposite_own[begin : begin + middle] + opposite[begin : begin + middle]
-        back = opposite_own[begin + middle : end] + opposite[begin + middle : end]
+    for own, other in zip(opposite_own, opposite):
+        middle = own.shape[0] // 2
+        onward = own[:middle] + other[:middle]
+        back = own[middle:] + other[middle:]
         onward, back, order = tie((onward, back, order))
         streams.append((send(onward, up), send(back, down)))
     for turn in range(3):

time: 95.7 us -> 98.2 us (1.026)
  starting transfers between devices: 27 us -> 28.6 us
  Pallas kernels: 7.86 us -> 8.99 us
    ppermute x18 -> x19, starting transfers between devices: 27 us -> 28.6 us  [send(): return lax.ppermute(value, 'feat', route)]
    pallas_call x1 -> x2, Pallas kernels: 1.28 us -> 2.78 us  [project(): pl.pallas_call(functools.partial(project_kernel, first), in_specs=[VMEM]...]
    ppermute x18 -> x19, waiting for transfers between devices: 16.3 us -> 16 us  [send(): return lax.ppermute(value, 'feat', route)]
  transfers between devices with their start and end apart: 18 -> 19, of which waited for: 8 -> 8; matrix products, arithmetic and copies ran while one was open for 1% -> 1% of each run, Pallas kernels for 3% -> 5%
where the time goes in v12:
time: 98.2 us; the launch traced here: 98 us
  blocking collectives  39.5 us (40%)
  starting transfers between devices  28.6 us (29%)
  waiting for transfers between devices  16 us (16%)
  Pallas kernels  8.99 us (9%)
  local copies, waits for them, and re-layouts  3.12 us (3%)
    ppermute x19, starting transfers between devices, send(): return lax.ppermute(value, 'feat', route)  28.6 us
    all_to_all x1, blocking collectives, on_device(): parts = combine(lax.all_to_all(partial, 'node', 0, 0))  20.2 us
    all_to_all x1, blocking collectives, on_device(): parts = lax.all_to_all(parts, 'feat', 0, 0)  19.4 us
    ppermute x19, waiting for transfers between devices, send(): return lax.ppermute(value, 'feat', route)  16 us
    pallas_call x2, Pallas kernels, blocks(): pl.pallas_call(late_kernel if late else early_kernel, in_specs=[VMEM] * l...  4.78 us
    unnamed x24, local copies, waits for them, and re-layouts  3.12 us
    pallas_call x2, Pallas kernels, project(): pl.pallas_call(functools.partial(project_kernel, first), in_specs=[VMEM]...  2.78 us
  transfers between devices with their start and end apart: 19, of which 8 were waited for; matrix products, arithmetic and copies ran while one was open for 1% of the time, Pallas kernels for 5%

profile of v12, /device:TPU:1, one launch (start us, length us, event | category | flops | bytes accessed | tf_op | source)
XLA Modules:
  0.0 98.0 jit_solution(14718830670918361810)
XLA Ops:
  0.0 0.9 copy-done
  0.9 0.2 convolution_convert_fusion.ordered
  1.2 2.2 %copy-done.1 = bf16[8192,256]{1,0:T(8,128)(2,1)S(1)} copy-done((bf16[8192,256]{1,0:T(8,128)(2,1)S(1)}, bf16[8192,256]{1,0:T(8,128)(2,1)}, u32[]{:S(2)}) %copy-start.1) | copy-done | bytes 4194328
  3.3 1.3 %project_first.1 = (f32[10,8,1024]{2,1,0:T(8,128)S(1)}, f32[6,8,1024]{2,1,0:T(8,128)S(1)}, f32[10,8,1024]{2,1,0:T(8,128)S(1)}, f32[6,8,1024]{2,1,0:T(8,128)S(1)}) custom-call(bf16[256,256]{1,0:T(8,128)(2,1)S(1)} %convolution_convert_fusion.ordered, bf16[8192,256]{1,0:T(8,128)(2,1)S(1)} %copy-done.1), custom_call_target="tpu_custom_call" | custom-call | flops 1073741824 | bytes 4194304 | tf_op jit(solution)/shard_map/project_first/pallas_call | solution.py:61
  4.6 3.3 %collective-permute-start = (f32[10,8,1024]{2,1,0:T(8,128)S(1)}, f32[10,8,1024]{2,1,0:T(8,128)S(1)}, u32[]{:S(2)}, u32[]{:S(2)}) collective-permute-start(f32[10,8,1024]{2,1,0:T(8,128)S(1)} %get-tuple-element.41), channel_id=1, source_target_pairs={{0,1},{1,0},{2,3},{3,2},{4,5},{5,4},{6,7},{7,6},{8,9},{9,8},{10,11... | collective-permute-start | bytes 983048 | tf_op jit(solution)/shard_map/ppermute | solution.py:308
  7.9 1.5 %project_rest.1 = (f32[112,8,1024]{2,1,0:T(8,128)S(1)}, f32[112,8,1024]{2,1,0:T(8,128)S(1)}) custom-call(bf16[256,256]{1,0:T(8,128)(2,1)S(1)} %convolution_convert_fusion.ordered, bf16[8192,256]{1,0:T(8,128)(2,1)S(1)} %copy-done.1), custom_call_target="tpu_custom_call" | custom-call | flops 1073741824 | bytes 4194304 | tf_op jit(solution)/shard_map/project_rest/pallas_call | solution.py:61
  9.4 0.2 collective-permute-start.1
  9.6 0.4 collective-permute-start.10
  10.1 3.9 %collective-permute-start.3 = (f32[5,8,1024]{2,1,0:T(8,128)S(1)}, f32[5,8,1024]{2,1,0:T(8,128)S(1)}, u32[]{:S(2)}, u32[]{:S(2)}) collective-permute-start(f32[5,8,1024]{2,1,0:T(8,128)S(1)} %get-tuple-element.56), channel_id=1, source_target_pairs={{2,0},{3,1},{4,2},{5,3},{6,4},{7,5},{8,6},{9,7},{10,8},{11,9},{12,... | collective-permute-start | bytes 491528 | tf_op jit(solution)/shard_map/ppermute | solution.py:308
  14.1 2.1 %collective-permute-done.10 = f32[6,8,1024]{2,1,0:T(8,128)S(1)} collective-permute-done((f32[6,8,1024]{2,1,0:T(8,128)S(1)}, f32[6,8,1024]{2,1,0:T(8,128)S(1)}, u32[]{:S(2)}, u32[]{:S(2)}) %collective-permute-start.10) | collective-permute-done | bytes 196640 | tf_op jit(solution)/shard_map/ppermute | solution.py:308
  16.3 3.9 %collective-permute-start.12 = (f32[3,8,1024]{2,1,0:T(8,128)S(1)}, f32[3,8,1024]{2,1,0:T(8,128)S(1)}, u32[]{:S(2)}, u32[]{:S(2)}) collective-permute-start(f32[3,8,1024]{2,1,0:T(8,128)S(1)} %get-tuple-element.70), channel_id=1, source_target_pairs={{2,0},{3,1},{4,2},{5,3},{6,4},{7,5},{8,6},{9,7},{10,8},{11,9},{12,... | collective-permute-start | bytes 294920 | tf_op jit(solution)/shard_map/ppermute | solution.py:308
  20.4 2.7 %collective-permute-start.5 = (f32[10,8,1024]{2,1,0:T(8,128)S(1)}, f32[10,8,1024]{2,1,0:T(8,128)S(1)}, u32[]{:S(2)}, u32[]{:S(2)}) collective-permute-start(f32[10,8,1024]{2,1,0:T(8,128)S(1)} %get-tuple-element.58), channel_id=1, source_target_pairs={{2,0},{3,1},{4,2},{5,3},{6,4},{7,5},{8,6},{9,7},{10,8},{11,9},{12,... | collective-permute-start | bytes 983048 | tf_op jit(solution)/shard_map/ppermute | solution.py:308
  23.3 2.7 %collective-permute-start.14 = (f32[6,8,1024]{2,1,0:T(8,128)S(1)}, f32[6,8,1024]{2,1,0:T(8,128)S(1)}, u32[]{:S(2)}, u32[]{:S(2)}) collective-permute-start(f32[6,8,1024]{2,1,0:T(8,128)S(1)} %get-tuple-element.72), channel_id=1, source_target_pairs={{2,0},{3,1},{4,2},{5,3},{6,4},{7,5},{8,6},{9,7},{10,8},{11,9},{12,... | collective-permute-start | bytes 589832 | tf_op jit(solution)/shard_map/ppermute | solution.py:308
  26.0 4.5 %collective-permute-done.4 = f32[10,8,1024]{2,1,0:T(8,128)S(1)} collective-permute-done((f32[10,8,1024]{2,1,0:T(8,128)S(1)}, f32[10,8,1024]{2,1,0:T(8,128)S(1)}, u32[]{:S(2)}, u32[]{:S(2)}) %collective-permute-start.4) | collective-permute-done | bytes 327712 | tf_op jit(solution)/shard_map/ppermute | solution.py:308
  30.5 0.1 add_add_fusion.1
  30.7 2.7 %collective-permute-start.7 = (f32[10,8,1024]{2,1,0:T(8,128)S(1)}, f32[10,8,1024]{2,1,0:T(8,128)S(1)}, u32[]{:S(2)}, u32[]{:S(2)}) collective-permute-start(f32[10,8,1024]{2,1,0:T(8,128)S(1)} %get-tuple-element.60), channel_id=1, source_target_pairs={{2,0},{3,1},{4,2},{5,3},{6,4},{7,5},{8,6},{9,7},{10,8},{11,9},{12,... | collective-permute-start | bytes 983048 | tf_op jit(solution)/shard_map/ppermute | solution.py:308
  33.4 1.3 %collective-permute-done.13 = f32[6,8,1024]{2,1,0:T(8,128)S(1)} collective-permute-done((f32[6,8,1024]{2,1,0:T(8,128)S(1)}, f32[6,8,1024]{2,1,0:T(8,128)S(1)}, u32[]{:S(2)}, u32[]{:S(2)}) %collective-permute-start.13) | collective-permute-done | bytes 196640 | tf_op jit(solution)/shard_map/ppermute | solution.py:308
  34.8 0.3 collective-permute-start.15
  35.0 2.7 %collective-permute-start.16 = (f32[6,8,1024]{2,1,0:T(8,128)S(1)}, f32[6,8,1024]{2,1,0:T(8,128)S(1)}, u32[]{:S(2)}, u32[]{:S(2)}) collective-permute-start(f32[6,8,1024]{2,1,0:T(8,128)S(1)} %get-tuple-element.74), channel_id=1, source_target_pairs={{2,0},{3,1},{4,2},{5,3},{6,4},{7,5},{8,6},{9,7},{10,8},{11,9},{12,... | collective-permute-start | bytes 589832 | tf_op jit(solution)/shard_map/ppermute | solution.py:308
  37.7 3.1 %collective-permute-done.6 = f32[10,8,1024]{2,1,0:T(8,128)S(1)} collective-permute-done((f32[10,8,1024]{2,1,0:T(8,128)S(1)}, f32[10,8,1024]{2,1,0:T(8,128)S(1)}, u32[]{:S(2)}, u32[]{:S(2)}) %collective-permute-start.6) | collective-permute-done | bytes 327712 | tf_op jit(solution)/shard_map/ppermute | solution.py:308
  40.8 0.1 add_add_fusion
  41.1 2.7 %collective-permute-start.9 = (f32[10,8,1024]{2,1,0:T(8,128)S(1)}, f32[10,8,1024]{2,1,0:T(8,128)S(1)}, u32[]{:S(2)}, u32[]{:S(2)}) collective-permute-start(f32[10,8,1024]{2,1,0:T(8,128)S(1)} %get-tuple-element.62), channel_id=1, source_target_pairs={{2,0},{3,1},{4,2},{5,3},{6,4},{7,5},{8,6},{9,7},{10,8},{11,9},{12,... | collective-permute-start | bytes 983048 | tf_op jit(solution)/shard_map/ppermute | solution.py:308
  43.7 1.3 %collective-permute-done.15 = f32[6,8,1024]{2,1,0:T(8,128)S(1)} collective-permute-done((f32[6,8,1024]{2,1,0:T(8,128)S(1)}, f32[6,8,1024]{2,1,0:T(8,128)S(1)}, u32[]{:S(2)}, u32[]{:S(2)}) %collective-permute-start.15) | collective-permute-done | bytes 196640 | tf_op jit(solution)/shard_map/ppermute | solution.py:308
  45.2 2.7 %collective-permute-start.18 = (f32[6,8,1024]{2,1,0:T(8,128)S(1)}, f32[6,8,1024]{2,1,0:T(8,128)S(1)}, u32[]{:S(2)}, u32[]{:S(2)}) collective-permute-start(f32[6,8,1024]{2,1,0:T(8,128)S(1)} %get-tuple-element.76), channel_id=1, source_target_pairs={{2,0},{3,1},{4,2},{5,3},{6,4},{7,5},{8,6},{9,7},{10,8},{11,9},{12,... | collective-permute-start | bytes 589832 | tf_op jit(solution)/shard_map/ppermute | solution.py:308
  48.5 0.3 block_lists.1.table
  48.8 2.3 %collective-permute-done.8.up = f32[10,8,1024]{2,1,0:T(8,128)S(1)} collective-permute-done((f32[10,8,1024]{2,1,0:T(8,128)S(1)}, f32[10,8,1024]{2,1,0:T(8,128)S(1)}, u32[]{:S(2)}, u32[]{:S(2)}) %collective-permute-start.8) | collective-permute-done | bytes 327712 | tf_op jit(solution)/shard_map/ppermute | solution.py:308
  51.2 2.9 %early_blocks.1.before = f32[256,8,128]{2,1,0:T(8,128)S(1)} custom-call(s32[8,384]{1,0:T(8,128)S(1)} %block_lists.1.table, f32[112,8,1024]{2,1,0:T(8,128)S(1)} %get-tuple-element.63.own, f32[112,8,1024]{2,1,0:T(8,128)S(1)} %collective-permute-done.1.paired, f32[10,8,1024]{2,1,0:T(8,128)S(1)} %collective-permute-done.8.up, ...), custom_call_target="tpu_custom_call" | custom-call | flops 268435456 | bytes 4194304 | tf_op jit(solution)/shard_map/early_blocks/pallas_call | solution.py:196
  54.1 1.2 %collective-permute-done.17.up = f32[6,8,1024]{2,1,0:T(8,128)S(1)} collective-permute-done((f32[6,8,1024]{2,1,0:T(8,128)S(1)}, f32[6,8,1024]{2,1,0:T(8,128)S(1)}, u32[]{:S(2)}, u32[]{:S(2)}) %collective-permute-start.17) | collective-permute-done | bytes 196640 | tf_op jit(solution)/shard_map/ppermute | solution.py:308
  55.4 1.9 %late_blocks.1 = f32[256,8,128]{2,1,0:T(8,128)S(1)} custom-call(f32[256,8,128]{2,1,0:T(8,128)S(1)} %early_blocks.1.before, s32[8,384]{1,0:T(8,128)S(1)} %block_lists.1.table, f32[112,8,1024]{2,1,0:T(8,128)S(1)} %get-tuple-element.63.own, f32[112,8,1024]{2,1,0:T(8,128)S(1)} %collective-permute-done.1.paired, f32[6,8,1024]{2,1,0:T(8,128)S(1)} %collective-permute-done.17.up, ...), custom_call_target="tpu_custom_call" | custom-call | flops 268435456 | bytes 4194304 | tf_op jit(solution)/shard_map/late_blocks/pallas_call | solution.py:196
  57.3 20.2 %all_to_all.10.parts = f32[16,16,8,128]{3,2,1,0:T(8,128)S(1)} all-to-all(f32[16,16,8,128]{3,2,1,0:T(8,128)S(1)} %bitcast.12), channel_id=1, replica_groups=mesh['node'=16,'feat'=16] {'node'}, dimensions={0} | all-to-all | bytes 2097152 | tf_op jit(solution)/shard_map/all_to_all | solution.py:350
  77.6 19.4 %all_to_all.11.parts = f32[16,8,128]{2,1,0:T(8,128)S(1)} all-to-all(f32[16,8,128]{2,1,0:T(8,128)S(1)} %combine.1), channel_id=1, replica_groups=mesh['node'=16,'feat'=16] {'feat'}, dimensions={0} | all-to-all | bytes 131072 | tf_op jit(solution)/shard_map/all_to_all | solution.py:351
  97.0 1.0 %second.1 = f32[32,172]{1,0:T(8,128)} custom-call(f32[16,8,128]{2,1,0:T(8,128)S(1)} %all_to_all.11.parts, f32[1,256]{1,0:T(1,128)S(1)} %bitcast.16, bf16[172,256]{1,0:T(8,128)(2,1)S(1)} %bitcast.13, bf16[172,256]{1,0:T(8,128)(2,1)S(1)} %bitcast.14, f32[1,172]{1,0:T(1,128)S(1)} %bitcast.17, s32[1,32]{1,0:T(1,128)S(1)} %bitcast.20, s32[8,32]{1,0:T(8,128)S(1)} %bitcast.15), custom_call_target="tpu_custom_call" | custom-call | tf_op jit(solution)/shard_map/second/pallas_call | solution.py:266
  (50 shorter events, 1.2 us)
Async XLA Ops:
  0.0 0.9 copy-start
  1.1 2.2 %copy-start.1 = (bf16[8192,256]{1,0:T(8,128)(2,1)S(1)}, bf16[8192,256]{1,0:T(8,128)(2,1)}, u32[]{:S(2)}) copy-start(bf16[8192,256]{1,0:T(8,128)(2,1)} %features.3) | copy-start | bytes 12582916
  4.6 4.7 %collective-permute-start = (f32[10,8,1024]{2,1,0:T(8,128)S(1)}, f32[10,8,1024]{2,1,0:T(8,128)S(1)}, u32[]{:S(2)}, u32[]{:S(2)}) collective-permute-start(f32[10,8,1024]{2,1,0:T(8,128)S(1)} %get-tuple-element.41), channel_id=1, source_target_pairs={{0,1},{1,0},{2,3},{3,2},{4,5},{5,4},{6,7},{7,6},{8,9},{9,8},{10,11... | collective-permute-start | bytes 983048 | tf_op jit(solution)/shard_map/ppermute | solution.py:308
  7.9 43.2 %slice-start = ((s8[8388608]{0:T(1024)(128)(4,1)}), s8[4194304]{0:T(1024)(128)(4,1)S(1)}, s32[]{:S(2)}) async-start(s8[8388608]{0:T(1024)(128)(4,1)} %bitcast.10), calls=%async_computation.2 | async-start | bytes 8388608
  9.4 10.8 %collective-permute-start.1 = (f32[112,8,1024]{2,1,0:T(8,128)S(1)}, f32[112,8,1024]{2,1,0:T(8,128)S(1)}, u32[]{:S(2)}, u32[]{:S(2)}) collective-permute-start(f32[112,8,1024]{2,1,0:T(8,128)S(1)} %get-tuple-element.43), channel_id=1, source_target_pairs={{0,1},{1,0},{2,3},{3,2},{4,5},{5,4},{6,7},{7,6},{8,9},{9,8},{10,11... | collective-permute-start | bytes 11010056 | tf_op jit(solution)/shard_map/ppermute | solution.py:308
  9.6 6.6 %collective-permute-start.10 = (f32[6,8,1024]{2,1,0:T(8,128)S(1)}, f32[6,8,1024]{2,1,0:T(8,128)S(1)}, u32[]{:S(2)}, u32[]{:S(2)}) collective-permute-start(f32[6,8,1024]{2,1,0:T(8,128)S(1)} %get-tuple-element.68), channel_id=1, source_target_pairs={{0,1},{1,0},{2,3},{3,2},{4,5},{5,4},{6,7},{7,6},{8,9},{9,8},{10,11... | collective-permute-start | bytes 589832 | tf_op jit(solution)/shard_map/ppermute | solution.py:308
  10.0 10.2 %collective-permute-start.2 = (f32[5,8,1024]{2,1,0:T(8,128)S(1)}, f32[5,8,1024]{2,1,0:T(8,128)S(1)}, u32[]{:S(2)}, u32[]{:S(2)}) collective-permute-start(f32[5,8,1024]{2,1,0:T(8,128)S(1)} %get-tuple-element.55), channel_id=1, source_target_pairs={{0,2},{1,3},{2,4},{3,5},{4,6},{5,7},{6,8},{7,9},{8,10},{9,11},{10,... | collective-permute-start | bytes 491528 | tf_op jit(solution)/shard_map/ppermute | solution.py:308
  10.1 10.1 %collective-permute-start.3 = (f32[5,8,1024]{2,1,0:T(8,128)S(1)}, f32[5,8,1024]{2,1,0:T(8,128)S(1)}, u32[]{:S(2)}, u32[]{:S(2)}) collective-permute-start(f32[5,8,1024]{2,1,0:T(8,128)S(1)} %get-tuple-element.56), channel_id=1, source_target_pairs={{2,0},{3,1},{4,2},{5,3},{6,4},{7,5},{8,6},{9,7},{10,8},{11,9},{12,... | collective-permute-start | bytes 491528 | tf_op jit(solution)/shard_map/ppermute | solution.py:308
  16.2 7.0 %collective-permute-start.11 = (f32[3,8,1024]{2,1,0:T(8,128)S(1)}, f32[3,8,1024]{2,1,0:T(8,128)S(1)}, u32[]{:S(2)}, u32[]{:S(2)}) collective-permute-start(f32[3,8,1024]{2,1,0:T(8,128)S(1)} %get-tuple-element.69), channel_id=1, source_target_pairs={{0,2},{1,3},{2,4},{3,5},{4,6},{5,7},{6,8},{7,9},{8,10},{9,11},{10,... | collective-permute-start | bytes 294920 | tf_op jit(solution)/shard_map/ppermute | solution.py:308
  16.3 6.9 %collective-permute-start.12 = (f32[3,8,1024]{2,1,0:T(8,128)S(1)}, f32[3,8,1024]{2,1,0:T(8,128)S(1)}, u32[]{:S(2)}, u32[]{:S(2)}) collective-permute-start(f32[3,8,1024]{2,1,0:T(8,128)S(1)} %get-tuple-element.70), channel_id=1, source_target_pairs={{2,0},{3,1},{4,2},{5,3},{6,4},{7,5},{8,6},{9,7},{10,8},{11,9},{12,... | collective-permute-start | bytes 294920 | tf_op jit(solution)/shard_map/ppermute | solution.py:308
  20.3 30.8 %slice-start.1 = ((s8[8388608]{0:T(1024)(128)(4,1)}), s8[4194304]{0:T(1024)(128)(4,1)S(1)}, s32[]{:S(2)}) async-start(s8[8388608]{0:T(1024)(128)(4,1)} %bitcast.10), calls=%async_computation.3 | async-start | bytes 8388608
  20.3 10.1 %collective-permute-start.4 = (f32[10,8,1024]{2,1,0:T(8,128)S(1)}, f32[10,8,1024]{2,1,0:T(8,128)S(1)}, u32[]{:S(2)}, u32[]{:S(2)}) collective-permute-start(f32[10,8,1024]{2,1,0:T(8,128)S(1)} %get-tuple-element.57), channel_id=1, source_target_pairs={{0,2},{1,3},{2,4},{3,5},{4,6},{5,7},{6,8},{7,9},{8,10},{9,11},{10,... | collective-permute-start | bytes 983048 | tf_op jit(solution)/shard_map/ppermute | solution.py:308
  20.4 10.1 %collective-permute-start.5 = (f32[10,8,1024]{2,1,0:T(8,128)S(1)}, f32[10,8,1024]{2,1,0:T(8,128)S(1)}, u32[]{:S(2)}, u32[]{:S(2)}) collective-permute-start(f32[10,8,1024]{2,1,0:T(8,128)S(1)} %get-tuple-element.58), channel_id=1, source_target_pairs={{2,0},{3,1},{4,2},{5,3},{6,4},{7,5},{8,6},{9,7},{10,8},{11,9},{12,... | collective-permute-start | bytes 983048 | tf_op jit(solution)/shard_map/ppermute | solution.py:308
  23.2 25.3 %copy-start.7 = (s32[256]{0:T(256)S(1)}, s32[256]{0:T(256)}, u32[]{:S(2)}) copy-start(s32[256]{0:T(256)} %param.14) | copy-start | bytes 3076
  23.2 25.3 %copy-start.8 = (s32[256]{0:T(256)S(1)}, s32[256]{0:T(256)}, u32[]{:S(2)}) copy-start(s32[256]{0:T(256)} %param.15) | copy-start | bytes 3076
  23.2 11.5 %collective-permute-start.13 = (f32[6,8,1024]{2,1,0:T(8,128)S(1)}, f32[6,8,1024]{2,1,0:T(8,128)S(1)}, u32[]{:S(2)}, u32[]{:S(2)}) collective-permute-start(f32[6,8,1024]{2,1,0:T(8,128)S(1)} %get-tuple-element.71), channel_id=1, source_target_pairs={{0,2},{1,3},{2,4},{3,5},{4,6},{5,7},{6,8},{7,9},{8,10},{9,11},{10,... | collective-permute-start | bytes 589832 | tf_op jit(solution)/shard_map/ppermute | solution.py:308
  23.3 11.4 %collective-permute-start.14 = (f32[6,8,1024]{2,1,0:T(8,128)S(1)}, f32[6,8,1024]{2,1,0:T(8,128)S(1)}, u32[]{:S(2)}, u32[]{:S(2)}) collective-permute-start(f32[6,8,1024]{2,1,0:T(8,128)S(1)} %get-tuple-element.72), channel_id=1, source_target_pairs={{2,0},{3,1},{4,2},{5,3},{6,4},{7,5},{8,6},{9,7},{10,8},{11,9},{12,... | collective-permute-start | bytes 589832 | tf_op jit(solution)/shard_map/ppermute | solution.py:308
  30.6 10.2 %collective-permute-start.6 = (f32[10,8,1024]{2,1,0:T(8,128)S(1)}, f32[10,8,1024]{2,1,0:T(8,128)S(1)}, u32[]{:S(2)}, u32[]{:S(2)}) collective-permute-start(f32[10,8,1024]{2,1,0:T(8,128)S(1)} %get-tuple-element.59), channel_id=1, source_target_pairs={{0,2},{1,3},{2,4},{3,5},{4,6},{5,7},{6,8},{7,9},{8,10},{9,11},{10,... | collective-permute-start | bytes 983048 | tf_op jit(solution)/shard_map/ppermute | solution.py:308
  30.7 10.1 %collective-permute-start.7 = (f32[10,8,1024]{2,1,0:T(8,128)S(1)}, f32[10,8,1024]{2,1,0:T(8,128)S(1)}, u32[]{:S(2)}, u32[]{:S(2)}) collective-permute-start(f32[10,8,1024]{2,1,0:T(8,128)S(1)} %get-tuple-element.60), channel_id=1, source_target_pairs={{2,0},{3,1},{4,2},{5,3},{6,4},{7,5},{8,6},{9,7},{10,8},{11,9},{12,... | collective-permute-start | bytes 983048 | tf_op jit(solution)/shard_map/ppermute | solution.py:308
  34.8 10.3 %collective-permute-start.15 = (f32[6,8,1024]{2,1,0:T(8,128)S(1)}, f32[6,8,1024]{2,1,0:T(8,128)S(1)}, u32[]{:S(2)}, u32[]{:S(2)}) collective-permute-start(f32[6,8,1024]{2,1,0:T(8,128)S(1)} %get-tuple-element.73), channel_id=1, source_target_pairs={{0,2},{1,3},{2,4},{3,5},{4,6},{5,7},{6,8},{7,9},{8,10},{9,11},{10,... | collective-permute-start | bytes 589832 | tf_op jit(solution)/shard_map/ppermute | solution.py:308
  35.0 10.0 %collective-permute-start.16 = (f32[6,8,1024]{2,1,0:T(8,128)S(1)}, f32[6,8,1024]{2,1,0:T(8,128)S(1)}, u32[]{:S(2)}, u32[]{:S(2)}) collective-permute-start(f32[6,8,1024]{2,1,0:T(8,128)S(1)} %get-tuple-element.74), channel_id=1, source_target_pairs={{2,0},{3,1},{4,2},{5,3},{6,4},{7,5},{8,6},{9,7},{10,8},{11,9},{12,... | collective-permute-start | bytes 589832 | tf_op jit(solution)/shard_map/ppermute | solution.py:308
  41.0 10.2 %collective-permute-start.8 = (f32[10,8,1024]{2,1,0:T(8,128)S(1)}, f32[10,8,1024]{2,1,0:T(8,128)S(1)}, u32[]{:S(2)}, u32[]{:S(2)}) collective-permute-start(f32[10,8,1024]{2,1,0:T(8,128)S(1)} %get-tuple-element.61), channel_id=1, source_target_pairs={{0,2},{1,3},{2,4},{3,5},{4,6},{5,7},{6,8},{7,9},{8,10},{9,11},{10,... | collective-permute-start | bytes 983048 | tf_op jit(solution)/shard_map/ppermute | solution.py:308
  41.1 10.1 %collective-permute-start.9 = (f32[10,8,1024]{2,1,0:T(8,128)S(1)}, f32[10,8,1024]{2,1,0:T(8,128)S(1)}, u32[]{:S(2)}, u32[]{:S(2)}) collective-permute-start(f32[10,8,1024]{2,1,0:T(8,128)S(1)} %get-tuple-element.62), channel_id=1, source_target_pairs={{2,0},{3,1},{4,2},{5,3},{6,4},{7,5},{8,6},{9,7},{10,8},{11,9},{12,... | collective-permute-start | bytes 983048 | tf_op jit(solution)/shard_map/ppermute | solution.py:308
  45.1 10.2 %collective-permute-start.17 = (f32[6,8,1024]{2,1,0:T(8,128)S(1)}, f32[6,8,1024]{2,1,0:T(8,128)S(1)}, u32[]{:S(2)}, u32[]{:S(2)}) collective-permute-start(f32[6,8,1024]{2,1,0:T(8,128)S(1)} %get-tuple-element.75), channel_id=1, source_target_pairs={{0,2},{1,3},{2,4},{3,5},{4,6},{5,7},{6,8},{7,9},{8,10},{9,11},{10,... | collective-permute-start | bytes 589832 | tf_op jit(solution)/shard_map/ppermute | solution.py:308
  45.2 10.2 %collective-permute-start.18 = (f32[6,8,1024]{2,1,0:T(8,128)S(1)}, f32[6,8,1024]{2,1,0:T(8,128)S(1)}, u32[]{:S(2)}, u32[]{:S(2)}) collective-permute-start(f32[6,8,1024]{2,1,0:T(8,128)S(1)} %get-tuple-element.76), channel_id=1, source_target_pairs={{2,0},{3,1},{4,2},{5,3},{6,4},{7,5},{8,6},{9,7},{10,8},{11,9},{12,... | collective-permute-start | bytes 589832 | tf_op jit(solution)/shard_map/ppermute | solution.py:308
  54.1 42.9 %copy-start.2 = (bf16[256,172]{0,1:T(8,128)(2,1)S(1)}, bf16[256,172]{0,1:T(8,128)(2,1)}, u32[]{:S(2)}) copy-start(bf16[256,172]{0,1:T(8,128)(2,1)} %param.19) | copy-start | bytes 264196
  54.1 42.9 %copy-start.3 = (bf16[256,172]{0,1:T(8,128)(2,1)S(1)}, bf16[256,172]{0,1:T(8,128)(2,1)}, u32[]{:S(2)}) copy-start(bf16[256,172]{0,1:T(8,128)(2,1)} %param.20) | copy-start | bytes 264196
  54.1 42.9 %copy-start.4 = (s32[32,8]{0,1:T(8,128)S(1)}, s32[32,8]{0,1:T(8,128)}, u32[]{:S(2)}) copy-start(s32[32,8]{0,1:T(8,128)} %param.23) | copy-start | bytes 3076
  54.1 42.8 %copy-start.5 = (f32[256]{0:T(256)S(1)}, f32[256]{0:T(256)}, u32[]{:S(2)}) copy-start(f32[256]{0:T(256)} %param.18) | copy-start | bytes 3076
  54.1 42.8 %copy-start.6 = (f32[172]{0:T(256)S(1)}, f32[172]{0:T(256)}, u32[]{:S(2)}) copy-start(f32[172]{0:T(256)} %param.21) | copy-start | bytes 2068
  54.1 42.8 %copy-start.9 = (s32[32]{0:T(128)S(1)}, s32[32]{0:T(128)}, u32[]{:S(2)}) copy-start(s32[32]{0:T(128)} %param.22) | copy-start | bytes 388

commit v13 on v11

--- a/solution.py
+++ b/solution.py
@@ -12,7 +12,7 @@
 TILE = 8
 RUNS = 8
 SPANS = ((0, 10), (10, 16))
-GROUP = 16
+GROUP = 8
 NT = (((1,), (1,)), ((), ()))
 VMEM = pl.BlockSpec(memory_space=pltpu.VMEM)
 SMEM = pl.BlockSpec(memory_space=pltpu.SMEM)

time: 95.7 us -> 97.3 us (1.017); the launches traced: 96 us -> 96.2 us
  transfers between devices with their start and end apart: 18 -> 18, of which waited for: 8 -> 8; matrix products, arithmetic and copies ran while one was open for 1% -> 1% of each run, Pallas kernels for 3% -> 4%
where the time goes in v13:
time: 97.3 us; the launch traced here: 96.2 us
  blocking collectives  39.8 us (41%)
  starting transfers between devices  27 us (28%)
  waiting for transfers between devices  15.7 us (16%)
  Pallas kernels  8.8 us (9%)
  local copies, waits for them, and re-layouts  3.12 us (3%)
    ppermute x18, starting transfers between devices, send(): return lax.ppermute(value, 'feat', route)  27 us
    all_to_all x1, blocking collectives, on_device(): parts = lax.all_to_all(parts, 'feat', 0, 0)  20.5 us
    all_to_all x1, blocking collectives, on_device(): parts = combine(lax.all_to_all(partial, 'node', 0, 0))  19.3 us
    ppermute x18, waiting for transfers between devices, send(): return lax.ppermute(value, 'feat', route)  15.7 us
    pallas_call x2, Pallas kernels, blocks(): pl.pallas_call(late_kernel if late else early_kernel, in_specs=[VMEM] * l...  6.07 us
    unnamed x24, local copies, waits for them, and re-layouts  3.12 us
  transfers between devices with their start and end apart: 18, of which 8 were waited for; matrix products, arithmetic and copies ran while one was open for 1% of the time, Pallas kernels for 4%

profile of v13, /device:TPU:1, one launch (start us, length us, event | category | flops | bytes accessed | tf_op | source)
XLA Modules:
  0.0 96.2 jit_solution(17959485161482507107)
XLA Ops:
  0.0 0.9 copy-done
  0.9 0.2 convolution_convert_fusion.ordered
  1.2 2.2 %copy-done.1 = bf16[8192,256]{1,0:T(8,128)(2,1)S(1)} copy-done((bf16[8192,256]{1,0:T(8,128)(2,1)S(1)}, bf16[8192,256]{1,0:T(8,128)(2,1)}, u32[]{:S(2)}) %copy-start.1) | copy-done | bytes 4194328
  3.3 1.3 %project.1 = (f32[16,8,1024]{2,1,0:T(8,128)S(1)}, f32[112,8,1024]{2,1,0:T(8,128)S(1)}, f32[16,8,1024]{2,1,0:T(8,128)S(1)}, f32[112,8,1024]{2,1,0:T(8,128)S(1)}) custom-call(bf16[256,256]{1,0:T(8,128)(2,1)S(1)} %convolution_convert_fusion.ordered, bf16[8192,256]{1,0:T(8,128)(2,1)S(1)} %copy-done.1), custom_call_target="tpu_custom_call" | custom-call | flops 1073741824 | bytes 12582912 | tf_op jit(solution)/shard_map/project/pallas_call | solution.py:45
  4.6 3.3 %collective-permute-start = (f32[16,8,1024]{2,1,0:T(8,128)S(1)}, f32[16,8,1024]{2,1,0:T(8,128)S(1)}, u32[]{:S(2)}, u32[]{:S(2)}) collective-permute-start(f32[16,8,1024]{2,1,0:T(8,128)S(1)} %get-tuple-element.44), channel_id=1, source_target_pairs={{0,1},{1,0},{2,3},{3,2},{4,5},{5,4},{6,7},{7,6},{8,9},{9,8},{10,11... | collective-permute-start | bytes 1572872 | tf_op jit(solution)/shard_map/ppermute | solution.py:292
  7.9 1.5 %collective-permute-done = f32[16,8,1024]{2,1,0:T(8,128)S(1)} collective-permute-done((f32[16,8,1024]{2,1,0:T(8,128)S(1)}, f32[16,8,1024]{2,1,0:T(8,128)S(1)}, u32[]{:S(2)}, u32[]{:S(2)}) %collective-permute-start) | collective-permute-done | bytes 524320 | tf_op jit(solution)/shard_map/ppermute | solution.py:292
  9.5 0.4 collective-permute-start.1
  10.0 3.9 %collective-permute-start.3 = (f32[5,8,1024]{2,1,0:T(8,128)S(1)}, f32[5,8,1024]{2,1,0:T(8,128)S(1)}, u32[]{:S(2)}, u32[]{:S(2)}) collective-permute-start(f32[5,8,1024]{2,1,0:T(8,128)S(1)} %get-tuple-element.62), channel_id=1, source_target_pairs={{2,0},{3,1},{4,2},{5,3},{6,4},{7,5},{8,6},{9,7},{10,8},{11,9},{12,... | collective-permute-start | bytes 491528 | tf_op jit(solution)/shard_map/ppermute | solution.py:292
  14.0 2.7 %collective-permute-start.11 = (f32[3,8,1024]{2,1,0:T(8,128)S(1)}, f32[3,8,1024]{2,1,0:T(8,128)S(1)}, u32[]{:S(2)}, u32[]{:S(2)}) collective-permute-start(f32[3,8,1024]{2,1,0:T(8,128)S(1)} %get-tuple-element.76), channel_id=1, source_target_pairs={{2,0},{3,1},{4,2},{5,3},{6,4},{7,5},{8,6},{9,7},{10,8},{11,9},{12,... | collective-permute-start | bytes 294920 | tf_op jit(solution)/shard_map/ppermute | solution.py:292
  16.7 1.6 %collective-permute-done.2 = f32[5,8,1024]{2,1,0:T(8,128)S(1)} collective-permute-done((f32[5,8,1024]{2,1,0:T(8,128)S(1)}, f32[5,8,1024]{2,1,0:T(8,128)S(1)}, u32[]{:S(2)}, u32[]{:S(2)}) %collective-permute-start.2) | collective-permute-done | bytes 163872 | tf_op jit(solution)/shard_map/ppermute | solution.py:292
  18.5 2.7 %collective-permute-start.5 = (f32[10,8,1024]{2,1,0:T(8,128)S(1)}, f32[10,8,1024]{2,1,0:T(8,128)S(1)}, u32[]{:S(2)}, u32[]{:S(2)}) collective-permute-start(f32[10,8,1024]{2,1,0:T(8,128)S(1)} %get-tuple-element.64), channel_id=1, source_target_pairs={{2,0},{3,1},{4,2},{5,3},{6,4},{7,5},{8,6},{9,7},{10,8},{11,9},{12,... | collective-permute-start | bytes 983048 | tf_op jit(solution)/shard_map/ppermute | solution.py:292
  21.3 2.7 %collective-permute-start.13 = (f32[6,8,1024]{2,1,0:T(8,128)S(1)}, f32[6,8,1024]{2,1,0:T(8,128)S(1)}, u32[]{:S(2)}, u32[]{:S(2)}) collective-permute-start(f32[6,8,1024]{2,1,0:T(8,128)S(1)} %get-tuple-element.78), channel_id=1, source_target_pairs={{2,0},{3,1},{4,2},{5,3},{6,4},{7,5},{8,6},{9,7},{10,8},{11,9},{12,... | collective-permute-start | bytes 589832 | tf_op jit(solution)/shard_map/ppermute | solution.py:292
  24.0 3.8 %collective-permute-done.4 = f32[10,8,1024]{2,1,0:T(8,128)S(1)} collective-permute-done((f32[10,8,1024]{2,1,0:T(8,128)S(1)}, f32[10,8,1024]{2,1,0:T(8,128)S(1)}, u32[]{:S(2)}, u32[]{:S(2)}) %collective-permute-start.4) | collective-permute-done | bytes 327712 | tf_op jit(solution)/shard_map/ppermute | solution.py:292
  28.0 0.8 collective-permute-start.6
  28.8 1.9 %collective-permute-start.7 = (f32[10,8,1024]{2,1,0:T(8,128)S(1)}, f32[10,8,1024]{2,1,0:T(8,128)S(1)}, u32[]{:S(2)}, u32[]{:S(2)}) collective-permute-start(f32[10,8,1024]{2,1,0:T(8,128)S(1)} %get-tuple-element.66), channel_id=1, source_target_pairs={{2,0},{3,1},{4,2},{5,3},{6,4},{7,5},{8,6},{9,7},{10,8},{11,9},{12,... | collective-permute-start | bytes 983048 | tf_op jit(solution)/shard_map/ppermute | solution.py:292
  30.8 1.3 %collective-permute-done.12 = f32[6,8,1024]{2,1,0:T(8,128)S(1)} collective-permute-done((f32[6,8,1024]{2,1,0:T(8,128)S(1)}, f32[6,8,1024]{2,1,0:T(8,128)S(1)}, u32[]{:S(2)}, u32[]{:S(2)}) %collective-permute-start.12) | collective-permute-done | bytes 196640 | tf_op jit(solution)/shard_map/ppermute | solution.py:292
  32.1 0.8 collective-permute-start.14
  33.0 1.9 %collective-permute-start.15 = (f32[6,8,1024]{2,1,0:T(8,128)S(1)}, f32[6,8,1024]{2,1,0:T(8,128)S(1)}, u32[]{:S(2)}, u32[]{:S(2)}) collective-permute-start(f32[6,8,1024]{2,1,0:T(8,128)S(1)} %get-tuple-element.80), channel_id=1, source_target_pairs={{2,0},{3,1},{4,2},{5,3},{6,4},{7,5},{8,6},{9,7},{10,8},{11,9},{12,... | collective-permute-start | bytes 589832 | tf_op jit(solution)/shard_map/ppermute | solution.py:292
  34.9 3.2 %collective-permute-done.6 = f32[10,8,1024]{2,1,0:T(8,128)S(1)} collective-permute-done((f32[10,8,1024]{2,1,0:T(8,128)S(1)}, f32[10,8,1024]{2,1,0:T(8,128)S(1)}, u32[]{:S(2)}, u32[]{:S(2)}) %collective-permute-start.6) | collective-permute-done | bytes 327712 | tf_op jit(solution)/shard_map/ppermute | solution.py:292
  38.3 0.7 collective-permute-start.8
  39.0 2.0 %collective-permute-start.9 = (f32[10,8,1024]{2,1,0:T(8,128)S(1)}, f32[10,8,1024]{2,1,0:T(8,128)S(1)}, u32[]{:S(2)}, u32[]{:S(2)}) collective-permute-start(f32[10,8,1024]{2,1,0:T(8,128)S(1)} %get-tuple-element.68), channel_id=1, source_target_pairs={{2,0},{3,1},{4,2},{5,3},{6,4},{7,5},{8,6},{9,7},{10,8},{11,9},{12,... | collective-permute-start | bytes 983048 | tf_op jit(solution)/shard_map/ppermute | solution.py:292
  41.0 1.3 %collective-permute-done.14 = f32[6,8,1024]{2,1,0:T(8,128)S(1)} collective-permute-done((f32[6,8,1024]{2,1,0:T(8,128)S(1)}, f32[6,8,1024]{2,1,0:T(8,128)S(1)}, u32[]{:S(2)}, u32[]{:S(2)}) %collective-permute-start.14) | collective-permute-done | bytes 196640 | tf_op jit(solution)/shard_map/ppermute | solution.py:292
  42.4 0.7 collective-permute-start.16
  43.1 2.0 %collective-permute-start.17 = (f32[6,8,1024]{2,1,0:T(8,128)S(1)}, f32[6,8,1024]{2,1,0:T(8,128)S(1)}, u32[]{:S(2)}, u32[]{:S(2)}) collective-permute-start(f32[6,8,1024]{2,1,0:T(8,128)S(1)} %get-tuple-element.82), channel_id=1, source_target_pairs={{2,0},{3,1},{4,2},{5,3},{6,4},{7,5},{8,6},{9,7},{10,8},{11,9},{12,... | collective-permute-start | bytes 589832 | tf_op jit(solution)/shard_map/ppermute | solution.py:292
  45.8 0.3 block_lists.1.table
  46.1 2.3 %collective-permute-done.8.up = f32[10,8,1024]{2,1,0:T(8,128)S(1)} collective-permute-done((f32[10,8,1024]{2,1,0:T(8,128)S(1)}, f32[10,8,1024]{2,1,0:T(8,128)S(1)}, u32[]{:S(2)}, u32[]{:S(2)}) %collective-permute-start.8) | collective-permute-done | bytes 327712 | tf_op jit(solution)/shard_map/ppermute | solution.py:292
  48.5 3.5 %early_blocks.1.before = f32[256,8,128]{2,1,0:T(8,128)S(1)} custom-call(s32[8,384]{1,0:T(8,128)S(1)} %block_lists.1.table, f32[112,8,1024]{2,1,0:T(8,128)S(1)} %get-tuple-element.69.own, f32[112,8,1024]{2,1,0:T(8,128)S(1)} %collective-permute-done.1.paired, f32[10,8,1024]{2,1,0:T(8,128)S(1)} %collective-permute-done.8.up, ...), custom_call_target="tpu_custom_call" | custom-call | flops 268435456 | bytes 4194304 | tf_op jit(solution)/shard_map/early_blocks/pallas_call | solution.py:180
  52.1 0.6 collective-permute-done.16.up
  52.7 2.6 %late_blocks.1 = f32[256,8,128]{2,1,0:T(8,128)S(1)} custom-call(f32[256,8,128]{2,1,0:T(8,128)S(1)} %early_blocks.1.before, s32[8,384]{1,0:T(8,128)S(1)} %block_lists.1.table, f32[112,8,1024]{2,1,0:T(8,128)S(1)} %get-tuple-element.69.own, f32[112,8,1024]{2,1,0:T(8,128)S(1)} %collective-permute-done.1.paired, f32[6,8,1024]{2,1,0:T(8,128)S(1)} %collective-permute-done.16.up, ...), custom_call_target="tpu_custom_call" | custom-call | flops 268435456 | bytes 4194304 | tf_op jit(solution)/shard_map/late_blocks/pallas_call | solution.py:180
  55.2 19.3 %all_to_all.10.parts = f32[16,16,8,128]{3,2,1,0:T(8,128)S(1)} all-to-all(f32[16,16,8,128]{3,2,1,0:T(8,128)S(1)} %bitcast.12), channel_id=1, replica_groups=mesh['node'=16,'feat'=16] {'node'}, dimensions={0} | all-to-all | bytes 2097152 | tf_op jit(solution)/shard_map/all_to_all | solution.py:330
  74.7 20.5 %all_to_all.11.parts = f32[16,8,128]{2,1,0:T(8,128)S(1)} all-to-all(f32[16,8,128]{2,1,0:T(8,128)S(1)} %combine.1), channel_id=1, replica_groups=mesh['node'=16,'feat'=16] {'feat'}, dimensions={0} | all-to-all | bytes 131072 | tf_op jit(solution)/shard_map/all_to_all | solution.py:331
  95.2 1.0 %second.1 = f32[32,172]{1,0:T(8,128)} custom-call(f32[16,8,128]{2,1,0:T(8,128)S(1)} %all_to_all.11.parts, f32[1,256]{1,0:T(1,128)S(1)} %bitcast.16, bf16[172,256]{1,0:T(8,128)(2,1)S(1)} %bitcast.13, bf16[172,256]{1,0:T(8,128)(2,1)S(1)} %bitcast.14, f32[1,172]{1,0:T(1,128)S(1)} %bitcast.17, s32[1,32]{1,0:T(1,128)S(1)} %bitcast.20, s32[8,32]{1,0:T(8,128)S(1)} %bitcast.15), custom_call_target="tpu_custom_call" | custom-call | tf_op jit(solution)/shard_map/second/pallas_call | solution.py:250
  (47 shorter events, 1.3 us)
Async XLA Ops:
  0.0 0.9 copy-start
  1.1 2.2 %copy-start.1 = (bf16[8192,256]{1,0:T(8,128)(2,1)S(1)}, bf16[8192,256]{1,0:T(8,128)(2,1)}, u32[]{:S(2)}) copy-start(bf16[8192,256]{1,0:T(8,128)(2,1)} %features.1) | copy-start | bytes 12582916
  3.3 45.1 %slice-start = ((s8[8388608]{0:T(1024)(128)(4,1)}), s8[4194304]{0:T(1024)(128)(4,1)S(1)}, s32[]{:S(2)}) async-start(s8[8388608]{0:T(1024)(128)(4,1)} %bitcast.10), calls=%async_computation.2 | async-start | bytes 8388608
  4.6 4.9 %collective-permute-start = (f32[16,8,1024]{2,1,0:T(8,128)S(1)}, f32[16,8,1024]{2,1,0:T(8,128)S(1)}, u32[]{:S(2)}, u32[]{:S(2)}) collective-permute-start(f32[16,8,1024]{2,1,0:T(8,128)S(1)} %get-tuple-element.44), channel_id=1, source_target_pairs={{0,1},{1,0},{2,3},{3,2},{4,5},{5,4},{6,7},{7,6},{8,9},{9,8},{10,11... | collective-permute-start | bytes 1572872 | tf_op jit(solution)/shard_map/ppermute | solution.py:292
  9.5 7.2 %collective-permute-start.1 = (f32[112,8,1024]{2,1,0:T(8,128)S(1)}, f32[112,8,1024]{2,1,0:T(8,128)S(1)}, u32[]{:S(2)}, u32[]{:S(2)}) collective-permute-start(f32[112,8,1024]{2,1,0:T(8,128)S(1)} %get-tuple-element.46), channel_id=1, source_target_pairs={{0,1},{1,0},{2,3},{3,2},{4,5},{5,4},{6,7},{7,6},{8,9},{9,8},{10,11... | collective-permute-start | bytes 11010056 | tf_op jit(solution)/shard_map/ppermute | solution.py:292
  9.9 8.4 %collective-permute-start.2 = (f32[5,8,1024]{2,1,0:T(8,128)S(1)}, f32[5,8,1024]{2,1,0:T(8,128)S(1)}, u32[]{:S(2)}, u32[]{:S(2)}) collective-permute-start(f32[5,8,1024]{2,1,0:T(8,128)S(1)} %get-tuple-element.61), channel_id=1, source_target_pairs={{0,2},{1,3},{2,4},{3,5},{4,6},{5,7},{6,8},{7,9},{8,10},{9,11},{10,... | collective-permute-start | bytes 491528 | tf_op jit(solution)/shard_map/ppermute | solution.py:292
  10.0 8.3 %collective-permute-start.3 = (f32[5,8,1024]{2,1,0:T(8,128)S(1)}, f32[5,8,1024]{2,1,0:T(8,128)S(1)}, u32[]{:S(2)}, u32[]{:S(2)}) collective-permute-start(f32[5,8,1024]{2,1,0:T(8,128)S(1)} %get-tuple-element.62), channel_id=1, source_target_pairs={{2,0},{3,1},{4,2},{5,3},{6,4},{7,5},{8,6},{9,7},{10,8},{11,9},{12,... | collective-permute-start | bytes 491528 | tf_op jit(solution)/shard_map/ppermute | solution.py:292
  13.9 7.2 %collective-permute-start.10 = (f32[3,8,1024]{2,1,0:T(8,128)S(1)}, f32[3,8,1024]{2,1,0:T(8,128)S(1)}, u32[]{:S(2)}, u32[]{:S(2)}) collective-permute-start(f32[3,8,1024]{2,1,0:T(8,128)S(1)} %get-tuple-element.75), channel_id=1, source_target_pairs={{0,2},{1,3},{2,4},{3,5},{4,6},{5,7},{6,8},{7,9},{8,10},{9,11},{10,... | collective-permute-start | bytes 294920 | tf_op jit(solution)/shard_map/ppermute | solution.py:292
  14.0 7.1 %collective-permute-start.11 = (f32[3,8,1024]{2,1,0:T(8,128)S(1)}, f32[3,8,1024]{2,1,0:T(8,128)S(1)}, u32[]{:S(2)}, u32[]{:S(2)}) collective-permute-start(f32[3,8,1024]{2,1,0:T(8,128)S(1)} %get-tuple-element.76), channel_id=1, source_target_pairs={{2,0},{3,1},{4,2},{5,3},{6,4},{7,5},{8,6},{9,7},{10,8},{11,9},{12,... | collective-permute-start | bytes 294920 | tf_op jit(solution)/shard_map/ppermute | solution.py:292
  18.4 30.1 %slice-start.1 = ((s8[8388608]{0:T(1024)(128)(4,1)}), s8[4194304]{0:T(1024)(128)(4,1)S(1)}, s32[]{:S(2)}) async-start(s8[8388608]{0:T(1024)(128)(4,1)} %bitcast.10), calls=%async_computation.3 | async-start | bytes 8388608
  18.4 9.4 %collective-permute-start.4 = (f32[10,8,1024]{2,1,0:T(8,128)S(1)}, f32[10,8,1024]{2,1,0:T(8,128)S(1)}, u32[]{:S(2)}, u32[]{:S(2)}) collective-permute-start(f32[10,8,1024]{2,1,0:T(8,128)S(1)} %get-tuple-element.63), channel_id=1, source_target_pairs={{0,2},{1,3},{2,4},{3,5},{4,6},{5,7},{6,8},{7,9},{8,10},{9,11},{10,... | collective-permute-start | bytes 983048 | tf_op jit(solution)/shard_map/ppermute | solution.py:292
  18.5 9.3 %collective-permute-start.5 = (f32[10,8,1024]{2,1,0:T(8,128)S(1)}, f32[10,8,1024]{2,1,0:T(8,128)S(1)}, u32[]{:S(2)}, u32[]{:S(2)}) collective-permute-start(f32[10,8,1024]{2,1,0:T(8,128)S(1)} %get-tuple-element.64), channel_id=1, source_target_pairs={{2,0},{3,1},{4,2},{5,3},{6,4},{7,5},{8,6},{9,7},{10,8},{11,9},{12,... | collective-permute-start | bytes 983048 | tf_op jit(solution)/shard_map/ppermute | solution.py:292
  21.2 24.6 %copy-start.7 = (s32[256]{0:T(256)S(1)}, s32[256]{0:T(256)}, u32[]{:S(2)}) copy-start(s32[256]{0:T(256)} %param.14) | copy-start | bytes 3076
  21.2 24.6 %copy-start.8 = (s32[256]{0:T(256)S(1)}, s32[256]{0:T(256)}, u32[]{:S(2)}) copy-start(s32[256]{0:T(256)} %param.15) | copy-start | bytes 3076
  21.3 10.8 %collective-permute-start.12 = (f32[6,8,1024]{2,1,0:T(8,128)S(1)}, f32[6,8,1024]{2,1,0:T(8,128)S(1)}, u32[]{:S(2)}, u32[]{:S(2)}) collective-permute-start(f32[6,8,1024]{2,1,0:T(8,128)S(1)} %get-tuple-element.77), channel_id=1, source_target_pairs={{0,2},{1,3},{2,4},{3,5},{4,6},{5,7},{6,8},{7,9},{8,10},{9,11},{10,... | collective-permute-start | bytes 589832 | tf_op jit(solution)/shard_map/ppermute | solution.py:292
  21.3 10.7 %collective-permute-start.13 = (f32[6,8,1024]{2,1,0:T(8,128)S(1)}, f32[6,8,1024]{2,1,0:T(8,128)S(1)}, u32[]{:S(2)}, u32[]{:S(2)}) collective-permute-start(f32[6,8,1024]{2,1,0:T(8,128)S(1)} %get-tuple-element.78), channel_id=1, source_target_pairs={{2,0},{3,1},{4,2},{5,3},{6,4},{7,5},{8,6},{9,7},{10,8},{11,9},{12,... | collective-permute-start | bytes 589832 | tf_op jit(solution)/shard_map/ppermute | solution.py:292
  28.0 10.1 %collective-permute-start.6 = (f32[10,8,1024]{2,1,0:T(8,128)S(1)}, f32[10,8,1024]{2,1,0:T(8,128)S(1)}, u32[]{:S(2)}, u32[]{:S(2)}) collective-permute-start(f32[10,8,1024]{2,1,0:T(8,128)S(1)} %get-tuple-element.65), channel_id=1, source_target_pairs={{0,2},{1,3},{2,4},{3,5},{4,6},{5,7},{6,8},{7,9},{8,10},{9,11},{10,... | collective-permute-start | bytes 983048 | tf_op jit(solution)/shard_map/ppermute | solution.py:292
  28.8 9.3 %collective-permute-start.7 = (f32[10,8,1024]{2,1,0:T(8,128)S(1)}, f32[10,8,1024]{2,1,0:T(8,128)S(1)}, u32[]{:S(2)}, u32[]{:S(2)}) collective-permute-start(f32[10,8,1024]{2,1,0:T(8,128)S(1)} %get-tuple-element.66), channel_id=1, source_target_pairs={{2,0},{3,1},{4,2},{5,3},{6,4},{7,5},{8,6},{9,7},{10,8},{11,9},{12,... | collective-permute-start | bytes 983048 | tf_op jit(solution)/shard_map/ppermute | solution.py:292
  32.1 10.2 %collective-permute-start.14 = (f32[6,8,1024]{2,1,0:T(8,128)S(1)}, f32[6,8,1024]{2,1,0:T(8,128)S(1)}, u32[]{:S(2)}, u32[]{:S(2)}) collective-permute-start(f32[6,8,1024]{2,1,0:T(8,128)S(1)} %get-tuple-element.79), channel_id=1, source_target_pairs={{0,2},{1,3},{2,4},{3,5},{4,6},{5,7},{6,8},{7,9},{8,10},{9,11},{10,... | collective-permute-start | bytes 589832 | tf_op jit(solution)/shard_map/ppermute | solution.py:292
  33.0 9.4 %collective-permute-start.15 = (f32[6,8,1024]{2,1,0:T(8,128)S(1)}, f32[6,8,1024]{2,1,0:T(8,128)S(1)}, u32[]{:S(2)}, u32[]{:S(2)}) collective-permute-start(f32[6,8,1024]{2,1,0:T(8,128)S(1)} %get-tuple-element.80), channel_id=1, source_target_pairs={{2,0},{3,1},{4,2},{5,3},{6,4},{7,5},{8,6},{9,7},{10,8},{11,9},{12,... | collective-permute-start | bytes 589832 | tf_op jit(solution)/shard_map/ppermute | solution.py:292
  38.3 10.2 %collective-permute-start.8 = (f32[10,8,1024]{2,1,0:T(8,128)S(1)}, f32[10,8,1024]{2,1,0:T(8,128)S(1)}, u32[]{:S(2)}, u32[]{:S(2)}) collective-permute-start(f32[10,8,1024]{2,1,0:T(8,128)S(1)} %get-tuple-element.67), channel_id=1, source_target_pairs={{0,2},{1,3},{2,4},{3,5},{4,6},{5,7},{6,8},{7,9},{8,10},{9,11},{10,... | collective-permute-start | bytes 983048 | tf_op jit(solution)/shard_map/ppermute | solution.py:292
  39.0 9.4 %collective-permute-start.9 = (f32[10,8,1024]{2,1,0:T(8,128)S(1)}, f32[10,8,1024]{2,1,0:T(8,128)S(1)}, u32[]{:S(2)}, u32[]{:S(2)}) collective-permute-start(f32[10,8,1024]{2,1,0:T(8,128)S(1)} %get-tuple-element.68), channel_id=1, source_target_pairs={{2,0},{3,1},{4,2},{5,3},{6,4},{7,5},{8,6},{9,7},{10,8},{11,9},{12,... | collective-permute-start | bytes 983048 | tf_op jit(solution)/shard_map/ppermute | solution.py:292
  42.4 10.3 %collective-permute-start.16 = (f32[6,8,1024]{2,1,0:T(8,128)S(1)}, f32[6,8,1024]{2,1,0:T(8,128)S(1)}, u32[]{:S(2)}, u32[]{:S(2)}) collective-permute-start(f32[6,8,1024]{2,1,0:T(8,128)S(1)} %get-tuple-element.81), channel_id=1, source_target_pairs={{0,2},{1,3},{2,4},{3,5},{4,6},{5,7},{6,8},{7,9},{8,10},{9,11},{10,... | collective-permute-start | bytes 589832 | tf_op jit(solution)/shard_map/ppermute | solution.py:292
  43.1 9.5 %collective-permute-start.17 = (f32[6,8,1024]{2,1,0:T(8,128)S(1)}, f32[6,8,1024]{2,1,0:T(8,128)S(1)}, u32[]{:S(2)}, u32[]{:S(2)}) collective-permute-start(f32[6,8,1024]{2,1,0:T(8,128)S(1)} %get-tuple-element.82), channel_id=1, source_target_pairs={{2,0},{3,1},{4,2},{5,3},{6,4},{7,5},{8,6},{9,7},{10,8},{11,9},{12,... | collective-permute-start | bytes 589832 | tf_op jit(solution)/shard_map/ppermute | solution.py:292
  52.0 43.1 %copy-start.2 = (bf16[256,172]{0,1:T(8,128)(2,1)S(1)}, bf16[256,172]{0,1:T(8,128)(2,1)}, u32[]{:S(2)}) copy-start(bf16[256,172]{0,1:T(8,128)(2,1)} %param.19) | copy-start | bytes 264196
  52.0 43.1 %copy-start.3 = (bf16[256,172]{0,1:T(8,128)(2,1)S(1)}, bf16[256,172]{0,1:T(8,128)(2,1)}, u32[]{:S(2)}) copy-start(bf16[256,172]{0,1:T(8,128)(2,1)} %param.20) | copy-start | bytes 264196
  52.0 43.1 %copy-start.4 = (s32[32,8]{0,1:T(8,128)S(1)}, s32[32,8]{0,1:T(8,128)}, u32[]{:S(2)}) copy-start(s32[32,8]{0,1:T(8,128)} %param.23) | copy-start | bytes 3076
  52.0 43.1 %copy-start.5 = (f32[256]{0:T(256)S(1)}, f32[256]{0:T(256)}, u32[]{:S(2)}) copy-start(f32[256]{0:T(256)} %param.18) | copy-start | bytes 3076
  52.0 43.1 %copy-start.6 = (f32[172]{0:T(256)S(1)}, f32[172]{0:T(256)}, u32[]{:S(2)}) copy-start(f32[172]{0:T(256)} %param.21) | copy-start | bytes 2068
  52.1 43.1 %copy-start.9 = (s32[32]{0:T(128)S(1)}, s32[32]{0:T(128)}, u32[]{:S(2)}) copy-start(s32[32]{0:T(128)} %param.22) | copy-start | bytes 388
